TPU v7x, 32 devices: a whole 2x2x4 slice. The times are simulated.
32 devices in a mesh: side: 2 (over x), row: 4 (over z), col: 4 (over y, core).
Axes of the slice: x: 2, y: 2, z: 4, core: 2. Of those that a mesh axis runs over, the one named last changes fastest.
Arguments:
- query: bfloat16 [2, 8, 4096], P(None, 'row'), may hold values from -32 to 32
- new_keys: bfloat16 [2, 8, 512], P(None, 'row'), may hold values from -6 to 6
- new_values: bfloat16 [2, 8, 512], P(None, 'row'), may hold values from -12 to 12
- key_cache: bfloat16 [8, 1536, 512], P('row', 'col'), may hold values from -4 to 4
- value_cache: bfloat16 [8, 1536, 512], P('row', 'col'), may hold values from -12 to 12
- lengths: int32 [8], P('row'), may hold values from 256 to 1536, as said below
- residual: bfloat16 [2, 8, 8192], P(None, None, 'row'), may hold values from -32 to 32
- out_weight: bfloat16 [4096, 8192], P('col', 'row'), may hold values from -0.5 to 0.5
- norm_gain: bfloat16 [8192], P('row'), may hold values from 0.099609375 to 1.8984375
- gate_weight: bfloat16 [8192, 14336], P('row', 'col'), may hold values from -0.0625 to 0.0625
- up_weight: bfloat16 [8192, 14336], P('row', 'col'), may hold values from -0.0625 to 0.0625
- down_weight: bfloat16 [14336, 8192], P('col', 'row'), may hold values from -0.046875 to 0.046875
Outputs:
- hidden_out: bfloat16 [2, 8, 8192], P(None, None, 'row')
Inputs may be any that keep to these rules, and one draw needn't show every extreme that they name: `lengths`: every value from 256 to 1536 can occur; in every draw some row has exactly 1536 and some row exactly 256.
All inputs are finite; a program needn't handle non-finite values.
Results may differ from a plain program's by a relative error of at most 0.0059.
Values may be sent and summed in bfloat16 or wider, within the bound.
No kernel may reach another device: no remote copies, remote signals or barrier semaphores. Data moves between devices by JAX's collectives and lax.ppermute only.
A program may use at most 128 MiB of HBM per device.

v0:
```python
import math

import jax
import jax.numpy as jnp
from jax import lax
from jax.sharding import PartitionSpec as P

D = 8192
HEADS = 32
KV_HEADS = 4
HD = 128


very_low = -1e30


def partner(value, axis, bit):
    mask = 2**bit
    pairs = [(source, source ^ mask) for source in range(lax.axis_size(axis))]
    return lax.ppermute(value, axis, pairs)


def joined(part, axis, combine):
    gathered = jax.tree.map(lambda a: lax.all_gather(a, axis), part)

    def take(source):
        return jax.tree.map(lambda a: lax.dynamic_index_in_dim(a, source, 0, False), gathered)

    return lax.fori_loop(
        1, lax.axis_size(axis), lambda source, state: combine(state, take(source)), take(0)
    )


def combine(first, second):
    peak_a, total_a, summed_a = first
    peak_b, total_b, summed_b = second
    peak = jnp.maximum(peak_a, peak_b)
    scale_a = jnp.exp(peak_a - peak)
    scale_b = jnp.exp(peak_b - peak)
    return (
        peak,
        total_a * scale_a + total_b * scale_b,
        summed_a * scale_a[..., None] + summed_b * scale_b[..., None],
    )


def cross(value):
    return partner(value, "side", 0)


def tile_sum(value):
    return lax.psum(value, "col")


def partial_softmax(queries, keys_part, values_part, live_part):
    scores = jnp.einsum(
        "bkgd,bpkd->bkgp", queries, keys_part, preferred_element_type=jnp.float32
    ) * (1.0 / math.sqrt(queries.shape[-1]))
    scores = jnp.where(live_part[:, None, None, :], scores, very_low)
    peak = jnp.max(scores, axis=-1)
    weights = jnp.where(live_part[:, None, None, :], jnp.exp(scores - peak[..., None]), 0.0)
    summed = jnp.einsum(
        "bkgp,bpkd->bkgd", weights, values_part.astype(jnp.float32), precision=lax.Precision.HIGHEST
    )
    return (peak, jnp.sum(weights, axis=-1), summed)


def shards(
    query,
    new_keys,
    new_values,
    key_cache,
    value_cache,
    lengths,
    residual,
    out_weight,
    norm_gain,
    gate_weight,
    up_weight,
    down_weight,
):
    side_index = lax.axis_index("side")
    serving = side_index == 0
    ffn_side = jnp.logical_not(serving)
    column = lax.axis_index("col")
    columns = lax.axis_size("col")
    group = HEADS // KV_HEADS
    head_block = HEADS // columns
    feature_block = head_block * HD
    inv_root = 1.0 / math.sqrt(HD)
    rows_here, span, kv_width = key_cache.shape
    total_rows = residual.shape[1]
    width_share = residual.shape[2]
    hidden_share = gate_weight.shape[1]
    positions = column * span + lax.iota(jnp.int32, span)
    live = positions[None, :] < lengths[:, None]
    cached_keys = key_cache.reshape(rows_here, span, KV_HEADS, HD)
    cached_values = value_cache.reshape(rows_here, span, KV_HEADS, HD)
    gains = norm_gain.astype(jnp.float32)
    finished = []
    for step in range(2):
        queries = query[step].reshape(rows_here, KV_HEADS, group, HD)

        def local_part():
            return partial_softmax(queries, cached_keys, cached_values, live)

        def empty_part():
            return (
                jnp.full((rows_here, KV_HEADS, group), very_low, jnp.float32),
                jnp.zeros((rows_here, KV_HEADS, group), jnp.float32),
                jnp.zeros((rows_here, KV_HEADS, group, HD), jnp.float32),
            )

        peak, total, summed = lax.cond(serving, local_part, empty_part)
        fresh_keys = new_keys[: step + 1].reshape(step + 1, rows_here, KV_HEADS, HD)
        fresh_values = (
            new_values[: step + 1].reshape(step + 1, rows_here, KV_HEADS, HD).astype(jnp.float32)
        )
        fresh_scores = (
            jnp.einsum("bkgd,tbkd->bkgt", queries, fresh_keys, preferred_element_type=jnp.float32)
            * inv_root
        )
        peak, total, summed = joined((peak, total, summed), "col", combine)
        top = jnp.maximum(peak, jnp.max(fresh_scores, axis=-1))
        rescale = jnp.exp(peak - top)
        fresh_weights = jnp.exp(fresh_scores - top[..., None])
        total = total * rescale + jnp.sum(fresh_weights, axis=-1)
        summed = summed * rescale[..., None] + jnp.einsum(
            "bkgt,tbkd->bkgd", fresh_weights, fresh_values, precision=lax.Precision.HIGHEST
        )
        attended = (summed / total[..., None]).reshape(rows_here, HEADS * HD).astype(jnp.bfloat16)
        piece = lax.dynamic_slice_in_dim(attended, column * feature_block, feature_block, 1)
        arrived = cross(piece)
        part = lax.all_gather(arrived, "row", axis=0, tiled=True)
        partial_value = lax.cond(
            ffn_side,
            lambda: jnp.dot(part, out_weight, preferred_element_type=jnp.float32),
            lambda: jnp.zeros((part.shape[0], width_share), jnp.float32),
        )
        mid = residual[step].astype(jnp.float32) + tile_sum(partial_value)
        lifted = (mid * gains).astype(jnp.bfloat16)

        def lift_products():
            return (
                jnp.dot(lifted, gate_weight, preferred_element_type=jnp.float32),
                jnp.dot(lifted, up_weight, preferred_element_type=jnp.float32),
            )

        def lift_empty():
            return (
                jnp.zeros((total_rows, hidden_share), jnp.float32),
                jnp.zeros((total_rows, hidden_share), jnp.float32),
            )

        gate_part, up_part = lax.cond(ffn_side, lift_products, lift_empty)
        gate, up, squares = lax.psum((gate_part, up_part, jnp.sum(mid * mid, axis=1)), "row")
        inv = lax.rsqrt(squares / D + 1e-05)[:, None]
        act = (jax.nn.silu(gate * inv) * (up * inv)).astype(jnp.bfloat16)
        down_part = lax.cond(
            ffn_side,
            lambda: jnp.dot(act, down_weight, preferred_element_type=jnp.float32),
            lambda: jnp.zeros((total_rows, width_share), jnp.float32),
        )
        result = (mid + tile_sum(down_part)).astype(jnp.bfloat16)
        finished.append(result)
    stacked = jnp.stack(finished)
    returned = cross(stacked)
    stacked = jnp.where(serving, returned, stacked)
    return stacked


def solution(mesh):
    in_specs = (
        P(None, "row", None),
        P(None, "row", None),
        P(None, "row", None),
        P("row", "col", None),
        P("row", "col", None),
        P("row"),
        P(None, None, "row"),
        P("col", "row"),
        P("row"),
        P("row", "col"),
        P("row", "col"),
        P("col", "row"),
    )
    out_specs = P(None, None, "row")
    return jax.shard_map(shards, mesh=mesh, in_specs=in_specs, out_specs=out_specs, check_vma=False)
```

profile of v0, /device:TPU:0, one launch (start us, length us, event | category | flops | bytes accessed | tf_op | source)
XLA Modules:
  0.0 246.6 jit_solution(9161006681990997496)
XLA Ops:
  6.5 0.7 slice.26
  7.3 0.7 slice_convert_fusion
  8.0 0.8 slice_bitcast_fusion.1
  8.7 1.5 copy.23
  10.2 1.5 copy.24
  11.8 0.7 broadcast_compare_fusion
  12.5 0.1 fusion.47
  12.6 3.5 %conditional.8 = (f32[2,4,8]{2,1,0:T(4,128)}, f32[2,4,8]{2,1,0:T(4,128)S(1)}, f32[2,4,8,128]{3,2,1,0:T(8,128)S(1)}) conditional(s32[]{:T(128)} %convert_element_type.64, () %tuple.106, (pred[2,384]{1,0:T(4,128)(4,1)S(1)}, bf16[2,4,8,128]{3,2,1,0:T(8,128)(2,1)S(1)}, bf16[2,384,4,128]{1,3,2,0:T(8,128)(2,1)S(1)}, ...), branch_computations={%region_0.0_spmd, %region_1.4_spmd} | conditional | flops 44236672 | bytes 1920280 | solution.py:114
  12.6 0.9 fusion.36
  13.5 1.6 fusion.1
  15.2 0.9 fusion.2
  16.1 6.3 %all-gather = f32[8,4,8]{2,1,0:T(4,128)S(1)} all-gather(f32[2,4,8]{2,1,0:T(4,128)} %get-tuple-element.449), channel_id=2, replica_groups=mesh['side'=2,'row'=4,'col'=4] {'col'}, dimensions={0}, use_global_device_ids=true | all-gather | bytes 1280 | tf_op jit(solution)/shard_map/all_gather | solution.py:24
  22.4 5.4 %all-gather.1 = f32[8,4,8]{2,1,0:T(4,128)S(1)} all-gather(f32[2,4,8]{2,1,0:T(4,128)S(1)} %get-tuple-element.450), channel_id=3, replica_groups=mesh['side'=2,'row'=4,'col'=4] {'col'}, dimensions={0}, use_global_device_ids=true | all-gather | bytes 1280 | tf_op jit(solution)/shard_map/all_gather | solution.py:24
  27.8 5.4 %all-gather.2 = f32[8,4,8,128]{3,2,1,0:T(8,128)S(1)} all-gather(f32[2,4,8,128]{3,2,1,0:T(8,128)S(1)} %get-tuple-element.451), channel_id=4, replica_groups=mesh['side'=2,'row'=4,'col'=4] {'col'}, dimensions={0}, use_global_device_ids=true | all-gather | bytes 163840 | tf_op jit(solution)/shard_map/all_gather | solution.py:24
  33.2 0.4 while.38
  33.4 0.1 fusion.77
  33.5 0.1 fusion.77
  33.6 0.1 fusion.25
  33.8 0.7 reshape.67
  34.5 0.7 reshape.68
  35.2 0.1 fusion.38
  35.4 3.5 %conditional.12 = (f32[2,4,8]{2,1,0:T(4,128)}, f32[2,4,8]{2,1,0:T(4,128)S(1)}, f32[2,4,8,128]{3,2,1,0:T(8,128)S(1)}) conditional(s32[]{:T(128)} %convert_element_type.64, () %tuple.115, (pred[2,384]{1,0:T(4,128)(4,1)S(1)}, bf16[2,4,8,128]{3,2,1,0:T(8,128)(2,1)S(1)}, bf16[2,384,4,128]{1,3,2,0:T(8,128)(2,1)S(1)}, ...), branch_computations={%region_18.19_spmd, %region_19.22_spmd} | conditional | flops 44236672 | bytes 1920280 | solution.py:114
  35.4 0.9 fusion.37
  36.3 1.6 fusion.11
  38.0 0.9 fusion.12
  38.8 5.4 %all-gather.3 = f32[8,4,8]{2,1,0:T(4,128)S(1)} all-gather(f32[2,4,8]{2,1,0:T(4,128)} %get-tuple-element.457), channel_id=5, replica_groups=mesh['side'=2,'row'=4,'col'=4] {'col'}, dimensions={0}, use_global_device_ids=true | all-gather | bytes 1280 | tf_op jit(solution)/shard_map/all_gather | solution.py:24
  44.2 5.2 %all-gather.4 = f32[8,4,8]{2,1,0:T(4,128)S(1)} all-gather(f32[2,4,8]{2,1,0:T(4,128)S(1)} %get-tuple-element.458), channel_id=6, replica_groups=mesh['side'=2,'row'=4,'col'=4] {'col'}, dimensions={0}, use_global_device_ids=true | all-gather | bytes 1280 | tf_op jit(solution)/shard_map/all_gather | solution.py:24
  49.4 5.4 %all-gather.5 = f32[8,4,8,128]{3,2,1,0:T(8,128)S(1)} all-gather(f32[2,4,8,128]{3,2,1,0:T(8,128)S(1)} %get-tuple-element.459), channel_id=7, replica_groups=mesh['side'=2,'row'=4,'col'=4] {'col'}, dimensions={0}, use_global_device_ids=true | all-gather | bytes 163840 | tf_op jit(solution)/shard_map/all_gather | solution.py:24
  54.8 0.4 while.39
  55.3 0.2 fusion.22
  55.6 13.5 %all-gather.6 = bf16[4,2,1024]{2,1,0:T(2,128)(2,1)S(1)} all-gather(bf16[1,2,1024]{2,1,0:T(2,128)(2,1)S(1)} %bitcast.145), channel_id=1, replica_groups=mesh['side'=2,'row'=4,'col'=4] {'row'}, dimensions={0}, use_global_device_ids=true | all-gather | bytes 20480 | tf_op jit(solution)/shard_map/all_gather | solution.py:134
  69.2 13.1 %all-gather.7 = bf16[4,2,1024]{2,1,0:T(2,128)(2,1)S(1)} all-gather(bf16[1,2,1024]{2,1,0:T(2,128)(2,1)S(1)} %bitcast.146), channel_id=1, replica_groups=mesh['side'=2,'row'=4,'col'=4] {'row'}, dimensions={0}, use_global_device_ids=true | all-gather | bytes 20480 | tf_op jit(solution)/shard_map/all_gather | solution.py:134
  82.4 0.6 copy-done.6
  83.1 38.8 %all-reduce.10.cloned.1.call-done = (f32[8,2048]{1,0:T(8,128)}, f32[8,2048]{1,0:T(8,128)}) async-done(((f32[8,2048]{1,0:T(8,128)}, f32[8,2048]{1,0:T(8,128)}), (f32[8,2048]{1,0:T(8,128)}, f32[8,2048]{1,0:T(8,128)})) %all-reduce.10.cloned.1.call-update) | async-done | bytes 131088 | tf_op jit(solution)/shard_map/psum | solution.py:52
  121.9 1.0 multiply_reduce_fusion.1
  123.0 0.6 copy-done.2
  123.7 0.6 copy-done.4
  124.5 11.7 %all-reduce.2 = (f32[8]{0:T(128)S(1)}, f32[8]{0:T(128)S(1)}) all-reduce(f32[8]{0:T(128)S(1)} %get-tuple-element.484, f32[8]{0:T(128)S(1)} %get-tuple-element.483), channel_id=1, replica_groups=mesh['side'=2,'row'=4,'col'=4] {'row'}, use_global_device_ids=true, to_apply=%region_33.34 | all-reduce | flops 16 | bytes 128 | tf_op jit(solution)/shard_map/psum | solution.py:156
  136.2 49.2 %all-reduce.12.cloned.1.call-done = (f32[8,3584]{1,0:T(8,128)}, f32[8,3584]{1,0:T(8,128)}, f32[8,3584]{1,0:T(8,128)}, f32[8,3584]{1,0:T(8,128)}) async-done(((f32[8,3584]{1,0:T(8,128)}, f32[8,3584]{1,0:T(8,128)}, f32[8,3584]{1,0:T(8,128)}, f32[8,3584]{1,0:T(8,128)}), (f32[8,3584]{1,0:T(8,128)}, f32[8,3584]{1,0:T(8,128)}, f32[8,3584]{1,0:T(8,128)}, f32[8,3584]{1,0:T(8,128)})) %all-reduce.12.cloned.1.call-update) | async-done | bytes 458768 | tf_op jit(solution)/shard_map/psum | solution.py:156
  185.3 1.1 multiply_convert_fusion
  186.4 1.1 multiply_convert_fusion.1
  187.5 0.2 conditional.15
  187.8 0.6 copy-done.8
  188.4 45.7 %all-reduce.8.cloned.1.call-done = (f32[8,2048]{1,0:T(8,128)}, f32[8,2048]{1,0:T(8,128)}) async-done(((f32[8,2048]{1,0:T(8,128)}, f32[8,2048]{1,0:T(8,128)}), (f32[8,2048]{1,0:T(8,128)}, f32[8,2048]{1,0:T(8,128)})) %all-reduce.8.cloned.1.call-update) | async-done | bytes 131088 | tf_op jit(solution)/shard_map/psum | solution.py:52
  234.1 0.9 fusion.23
  235.0 1.5 collective-permute-start.2
  236.6 2.8 %collective-permute-done.2 = bf16[2,8,2048]{2,1,0:T(8,128)(2,1)S(1)} collective-permute-done((bf16[2,8,2048]{2,1,0:T(8,128)(2,1)S(1)}, bf16[2,8,2048]{2,1,0:T(8,128)(2,1)S(1)}, u32[]{:S(2)}, u32[]{:S(2)}) %collective-permute-start.2) | collective-permute-done | bytes 65568 | tf_op jit(solution)/shard_map/ppermute | solution.py:20
  239.4 0.6 broadcast_select_fusion
  (75 shorter events, 1.4 us)
Async XLA Ops:
  6.5 76.5 %copy-start.13 = (bf16[2048]{0:T(1024)(128)(2,1)S(1)}, bf16[2048]{0:T(1024)(128)(2,1)}, u32[]{:S(2)}) copy-start(bf16[2048]{0:T(1024)(128)(2,1)} %param.40) | copy-start | bytes 12292
  6.5 115.4 %copy-start.10 = (bf16[2,8,2048]{2,1,0:T(8,128)(2,1)S(1)}, bf16[2,8,2048]{2,1,0:T(8,128)(2,1)}, u32[]{:S(2)}) copy-start(bf16[2,8,2048]{2,1,0:T(8,128)(2,1)} %param.38) | copy-start | bytes 196612
  6.5 115.3 %all-reduce.10.cloned.1.call-start = ((), (), s32[]{:S(2)}) async-start(), calls=%async_computation.1 | async-start | bytes 262144 | tf_op jit(solution)/shard_map/psum | solution.py:52
  33.8 21.9 %collective-permute-start = (bf16[2,1024]{1,0:T(2,128)(2,1)S(1)}, bf16[2,1024]{1,0:T(2,128)(2,1)S(1)}, u32[]{:S(2)}, u32[]{:S(2)}) collective-permute-start(bf16[2,1024]{1,0:T(2,128)(2,1)S(1)} %constant_dynamic-slice_fusion.1), channel_id=1, source_target_pairs={{0,16},{16,0},{1,17},{17,1},{2,18},{18,2},{3,19},{19,3},{4,20},{20... | collective-permute-start | bytes 12296 | tf_op jit(solution)/shard_map/ppermute | solution.py:20
  55.5 13.6 %collective-permute-start.1 = (bf16[2,1024]{1,0:T(2,128)(2,1)S(1)}, bf16[2,1024]{1,0:T(2,128)(2,1)S(1)}, u32[]{:S(2)}, u32[]{:S(2)}) collective-permute-start(bf16[2,1024]{1,0:T(2,128)(2,1)S(1)} %constant_dynamic-slice_fusion), channel_id=1, source_target_pairs={{0,16},{16,0},{1,17},{17,1},{2,18},{18,2},{3,19},{19,3},{4,20},{20... | collective-permute-start | bytes 12296 | tf_op jit(solution)/shard_map/ppermute | solution.py:20
  82.3 0.6 copy-start.6
  82.4 0.6 copy-start.7
  83.0 102.3 %all-reduce.12.cloned.1.call-start = ((), (), s32[]{:S(2)}) async-start(), calls=%async_computation.2 | async-start | bytes 917504 | tf_op jit(solution)/shard_map/psum | solution.py:156
  123.0 0.6 copy-start.2
  123.0 0.7 copy-start.3
  123.7 0.6 copy-start.4
  123.7 0.7 copy-start.5
  124.4 109.7 %all-reduce.8.cloned.1.call-start = ((), (), s32[]{:S(2)}) async-start(), calls=%async_computation | async-start | bytes 262144 | tf_op jit(solution)/shard_map/psum | solution.py:52
  187.7 0.6 copy-start.8
  187.7 46.4 %copy-start.11 = (f32[8,2048]{1,0:T(8,128)S(1)}, f32[8,2048]{1,0:T(8,128)}, u32[]{:S(2)}) copy-start(f32[8,2048]{1,0:T(8,128)} %get-tuple-element.515) | copy-start | bytes 196612
  187.7 46.4 %copy-start.12 = (f32[8,2048]{1,0:T(8,128)S(1)}, f32[8,2048]{1,0:T(8,128)}, u32[]{:S(2)}) copy-start(f32[8,2048]{1,0:T(8,128)} %get-tuple-element.516) | copy-start | bytes 196612
  187.8 0.6 copy-start.9
  235.0 4.3 %collective-permute-start.2 = (bf16[2,8,2048]{2,1,0:T(8,128)(2,1)S(1)}, bf16[2,8,2048]{2,1,0:T(8,128)(2,1)S(1)}, u32[]{:S(2)}, u32[]{:S(2)}) collective-permute-start(bf16[2,8,2048]{2,1,0:T(8,128)(2,1)S(1)} %pad_maximum_fusion), channel_id=1, source_target_pairs={{0,16},{16,0},{1,17},{17,1},{2,18},{18,2},{3,19},{19,3},{4,20},{20... | collective-permute-start | bytes 196616 | tf_op jit(solution)/shard_map/ppermute | solution.py:20
Sparse Core Ops, SparseCore 0:
  83.1 38.6 all-reduce.9
  124.7 60.6 all-reduce.11
  188.5 45.5 all-reduce.7
where the time goes:
time: 247 us
  waiting for transfers between devices  137 us (55%)
  blocking collectives  71.4 us (29%)
  between operations  13.4 us (5%)
  other arithmetic  8.72 us (4%)
  local copies, waits for them, and re-layouts  8.64 us (3%)
  matrix products  5.65 us (2%)
    psum x2, waiting for transfers between devices, tile_sum(): return lax.psum(value, 'col')  84.5 us
    psum x1, waiting for transfers between devices, shards(): lax.psum((gate_part, up_part, jnp.sum(mid * mid, axis=1)), 'row')  49.2 us
    all_gather x6, blocking collectives, joined(): gathered = jax.tree.map(lambda a: lax.all_gather(a, axis), part)  33.1 us
    all_gather x2, blocking collectives, shards(): part = lax.all_gather(arrived, 'row', axis=0, tiled=True)  26.7 us
    psum x1, blocking collectives, shards(): lax.psum((gate_part, up_part, jnp.sum(mid * mid, axis=1)), 'row')  11.7 us
    unnamed x29, local copies, waits for them, and re-layouts  6.38 us
  transfers between devices with their start and end apart: 6, of which 4 were waited for; matrix products, arithmetic and copies ran while one was open for 2% of the time, Pallas kernels for 0%

commit v1 on v0

v1 whole, which is shorter than its diff:
```python
import functools
import math

import jax
import jax.numpy as jnp
from jax import lax
from jax.experimental import pallas as pl
from jax.experimental.pallas import tpu as pltpu
from jax.sharding import PartitionSpec as P

HEADS = 32
KV_HEADS = 4
HD = 128
GROUP = HEADS // KV_HEADS
TOKENS = 2
very_low = -1e30
MIB = 1024 * 1024
WIRE = jnp.bfloat16
VMEM_SPEC = pl.BlockSpec(memory_space=pltpu.VMEM)
ANY_SPEC = pl.BlockSpec(memory_space=pl.ANY)


def partner(value, axis, k):
    return lax.ppermute(value, axis, [(i, i ^ k) for i in range(lax.axis_size(axis))])


def spread(piece, axis):
    return [piece] + [partner(piece, axis, k) for k in range(1, lax.axis_size(axis))]


def dot(a, b):
    return jnp.dot(a, b, preferred_element_type=jnp.float32)


def dot_t(a, b):
    return lax.dot_general(a, b, (((1,), (1,)), ((), ())), preferred_element_type=jnp.float32)


def call(kernel, out_shape, in_specs, scratch=(), limit=4, name=None, flops=None):
    cost = None
    if flops is not None:
        cost = pl.CostEstimate(flops=flops, bytes_accessed=1024, transcendentals=0)
    return pl.pallas_call(
        kernel,
        out_shape=out_shape,
        in_specs=in_specs,
        out_specs=jax.tree.map(lambda _: VMEM_SPEC, out_shape),
        scratch_shapes=list(scratch),
        compiler_params=pltpu.CompilerParams(vmem_limit_bytes=limit * MIB),
        cost_estimate=cost,
        name=name,
    )


def in_hbm(value):
    return pltpu.with_memory_space_constraint(value, pltpu.HBM)


def in_vmem(value):
    return pltpu.with_memory_space_constraint(value, pltpu.VMEM)


def divide(blocks, bit, keep, send):
    for i in range(keep.shape[0]):
        keep[i] = blocks[2 * i + bit]
        send[i] = blocks[2 * i + 1 - bit]


def attention_kernel(cols, lengths, *rest):
    sources, (keep, send), held, (sized_ref, packed, sems) = rest[:5], rest[5:7], rest[7:12], rest[12:]
    sized = pltpu.make_async_copy(lengths, sized_ref, sems.at[5])
    sized.start()
    lengths = sized_ref
    copies = [
        pltpu.make_async_copy(source, target, sems.at[i])
        for i, (source, target) in enumerate(zip(sources, held))
    ]
    for copy in copies:
        copy.start()
    query, new_keys, new_values, keys, values = held
    column = lax.axis_index("col")
    rows, span, _ = keys.shape
    hb = HEADS // cols
    inv_root = 1.0 / math.sqrt(HD)
    n = TOKENS * GROUP
    pairs = [(b, g) for b in range(rows) for g in range(KV_HEADS)]
    for copy in [sized] + copies[:4]:
        copy.wait()
    q32 = query[...].astype(jnp.float32)
    nk, nv = new_keys[...].astype(jnp.float32), new_values[...].astype(jnp.float32)
    zeros = jnp.zeros((8 - TOKENS, HD), jnp.float32)

    def fresh(block, b, g):
        lanes = slice(g * HD, (g + 1) * HD)
        return jnp.concatenate([block[t, b : b + 1, lanes] for t in range(TOKENS)] + [zeros], axis=0)

    scores, fresh_scores = [], []
    for b, g in pairs:
        q = jnp.concatenate(
            [
                q32[t, b : b + 1, (g * GROUP + h) * HD : (g * GROUP + h + 1) * HD]
                for t in range(TOKENS)
                for h in range(GROUP)
            ],
            axis=0,
        ).astype(jnp.bfloat16)
        s = dot_t(q, keys[b, :, g * HD : (g + 1) * HD]) * inv_root
        position = column * span + lax.broadcasted_iota(jnp.int32, (n, span), 1)
        scores.append(jnp.where(position < lengths[b], s, very_low))
        f = dot_t(q, fresh(nk, b, g).astype(jnp.bfloat16)) * inv_root
        token = lax.broadcasted_iota(jnp.int32, (n, 8), 0) // GROUP
        slot = lax.broadcasted_iota(jnp.int32, (n, 8), 1)
        seen = jnp.logical_and(slot <= token, column == 0)
        fresh_scores.append(jnp.where(seen, f, very_low))
    scores = jnp.concatenate(scores, axis=0)
    fresh_scores = jnp.concatenate(fresh_scores, axis=0)
    peak = jnp.maximum(
        jnp.max(scores, axis=1, keepdims=True), jnp.max(fresh_scores, axis=1, keepdims=True)
    )
    weights = jnp.where(scores > 0.5 * very_low, jnp.exp(scores - peak), 0.0)
    fresh_weights = jnp.where(fresh_scores > 0.5 * very_low, jnp.exp(fresh_scores - peak), 0.0)
    total = jnp.sum(weights, axis=1, keepdims=True) + jnp.sum(fresh_weights, axis=1, keepdims=True)

    def halves(w):
        high = w.astype(jnp.bfloat16)
        low = (w - high.astype(jnp.float32)).astype(jnp.bfloat16)
        return jnp.concatenate([high, low], axis=0)

    lane = lax.broadcasted_iota(jnp.int32, (GROUP, HD), 1)
    stats = [jnp.zeros((GROUP, HD), jnp.float32) for _ in range(KV_HEADS)]
    copies[4].wait()
    for i, (b, g) in enumerate(pairs):
        here = slice(i * n, (i + 1) * n)
        s = dot(halves(weights[here]), values[b, :, g * HD : (g + 1) * HD])
        s = s + dot(halves(fresh_weights[here]), fresh(nv, b, g).astype(jnp.bfloat16))
        s = s[:n] + s[n:]
        for t in range(TOKENS):
            tb = t * rows + b
            part = slice(i * n + t * GROUP, i * n + (t + 1) * GROUP)
            stats[g] = jnp.where(lane == 2 * tb, peak[part], stats[g])
            stats[g] = jnp.where(lane == 2 * tb + 1, total[part], stats[g])
            block = s[t * GROUP : (t + 1) * GROUP]
            if hb >= GROUP:
                at = g * GROUP
                packed[at // hb, tb, at % hb : at % hb + GROUP] = block
            else:
                for j in range(GROUP // hb):
                    packed[g * (GROUP // hb) + j, tb] = block[j * hb : (j + 1) * hb]
    for g in range(KV_HEADS):
        if hb >= GROUP:
            at = g * GROUP
            packed[at // hb, TOKENS * rows, at % hb : at % hb + GROUP] = stats[g]
        else:
            for j in range(GROUP // hb):
                packed[g * (GROUP // hb) + j, TOKENS * rows] = stats[g][j * hb : (j + 1) * hb]
    divide(packed, column & 1, keep, send)


def joined(first, second, i):
    cells = first.shape[1] - 1
    result = []
    for tb in range(cells):
        stats = [p[i, cells] for p in (first, second)]
        peak_a, peak_b = (s[:, 2 * tb : 2 * tb + 1] for s in stats)
        total_a, total_b = (s[:, 2 * tb + 1 : 2 * tb + 2] for s in stats)
        peak = jnp.maximum(peak_a, peak_b)
        scale_a, scale_b = jnp.exp(peak_a - peak), jnp.exp(peak_b - peak)
        total = total_a * scale_a + total_b * scale_b
        result.append((first[i, tb] * scale_a + second[i, tb] * scale_b, total, peak))
    return result


def merge_kernel(level, kept, received, keep, send, packed):
    lane = lax.broadcasted_iota(jnp.int32, kept.shape[2:], 1)
    for i in range(kept.shape[0]):
        stats = jnp.zeros(kept.shape[2:], jnp.float32)
        result = joined(kept, received, i)
        for tb, (summed, total, peak) in enumerate(result):
            packed[i, tb] = summed
            stats = jnp.where(lane == 2 * tb, peak, stats)
            stats = jnp.where(lane == 2 * tb + 1, total, stats)
        packed[i, len(result)] = stats
    divide(packed, (lax.axis_index("col") >> level) & 1, keep, send)


def attended_kernel(kept, received, out):
    attended = [summed / total for summed, total, _ in joined(kept, received, 0)]
    rows = [
        jnp.concatenate([a[h : h + 1] for a in attended], axis=0) for h in range(kept.shape[2])
    ]
    out[...] = jnp.concatenate(rows, axis=1).astype(out.dtype)


def add_kernel(first, second, out):
    out[...] = (first[...].astype(jnp.float32) + second[...].astype(jnp.float32)).astype(out.dtype)


def group_order(value, groups):
    here = value.shape[1] // groups
    return jnp.concatenate(
        [value[t, r * here : (r + 1) * here] for r in range(groups) for t in range(TOKENS)], axis=0
    )


def canonical(parts, canon, me):
    cells = parts[0].shape[0]
    for k, part in enumerate(parts):
        canon[jnp.bitwise_xor(me, k), :cells] = part[...].astype(jnp.float32)
    rows = [canon[r, :cells] for r in range(len(parts))]
    return jnp.concatenate(rows, axis=0).astype(jnp.bfloat16)


def over_columns(width, body):
    size = width // 2 if width % 256 == 0 else width

    def step(j, carry):
        body(pl.multiple_of(j * size, 128), size)
        return carry

    lax.fori_loop(0, width // size, step, 0)


def out_kernel(groups, *refs):
    parts, (weight, out, canon, attended) = refs[:groups], refs[groups:]
    attended[...] = canonical(parts, canon, lax.axis_index("row"))

    def body(at, size):
        out[:, pl.ds(at, size)] = dot(attended[...], weight[:, pl.ds(at, size)]).astype(out.dtype)

    over_columns(out.shape[1], body)


def in_pieces(squares):
    first = squares.astype(WIRE).astype(jnp.float32)
    second = (squares - first).astype(WIRE).astype(jnp.float32)
    third = squares - first - second
    lane = lax.broadcasted_iota(jnp.int32, (squares.shape[0], HD), 1)
    return jnp.where(
        lane == 0, first, jnp.where(lane == 1, second, jnp.where(lane == 2, third, 0.0))
    )


def lift_kernel(groups, split, residual, gains, gate_weight, up_weight, first, second, *refs):
    mid_out, keep, send, lifted, packed = refs
    hidden = gate_weight.shape[1] // split
    start = lax.axis_index("side") * hidden if split > 1 else 0
    half = packed.shape[1] // 2
    mid = first[...].astype(jnp.float32) + second[...].astype(jnp.float32)
    mid = group_order(residual[...].astype(jnp.float32), groups) + mid
    mid_out[...] = mid
    sent = in_pieces(jnp.sum(mid * mid, axis=1, keepdims=True))
    lifted[...] = (mid * gains[...].astype(jnp.float32).reshape(1, mid.shape[1])).astype(jnp.bfloat16)
    for i in range(2):
        piece = sent[i * half : (i + 1) * half]
        packed[i, :, hidden:] = jnp.concatenate([piece, piece], axis=0)

    def body(at, size):
        block = pl.ds(pl.multiple_of(start + at, 128), size)
        gate = dot(lifted[...], gate_weight[:, block])
        up = dot(lifted[...], up_weight[:, block])
        for i in range(2):
            rows = slice(i * half, (i + 1) * half)
            packed[i, :, pl.ds(at, size)] = jnp.concatenate([gate[rows], up[rows]], axis=0)

    over_columns(hidden, body)
    bit = lax.axis_index("row") & 1
    keep[...] = packed[bit].astype(keep.dtype)
    send[...] = packed[1 - bit].astype(send.dtype)


def sum_kernel(first, second, out):
    hidden = out.shape[1] - HD
    total = first[...].astype(jnp.float32) + second[...].astype(jnp.float32)
    out[:, :hidden] = total[:, :hidden].astype(out.dtype)
    squares = jnp.sum(total[:, hidden:], axis=1, keepdims=True)
    out[:, hidden:] = in_pieces(squares).astype(out.dtype)


def act_kernel(model, first, second, out):
    hidden = first.shape[1] - HD
    cells = first.shape[0] // 2
    total = first[...].astype(jnp.float32) + second[...].astype(jnp.float32)
    squares = jnp.sum(total[:cells, hidden:], axis=1, keepdims=True)
    inv = lax.rsqrt(squares / model + 1e-05)
    gate = total[:cells, :hidden] * inv
    up = total[cells:, :hidden] * inv
    out[...] = (gate / (1.0 + jnp.exp(-gate)) * up).astype(out.dtype)


def gather_kernel(own, received, out, packed):
    bit = lax.axis_index("row") & 1
    packed[bit] = own[...].astype(jnp.float32)
    packed[1 - bit] = received[...].astype(jnp.float32)
    out[...] = jnp.concatenate([packed[0], packed[1]], axis=0).astype(out.dtype)


def down_kernel(other, act, weight, *refs):
    out = refs[-1]
    hidden = act.shape[1]
    start = 0
    if weight.shape[0] > hidden:
        start = pl.multiple_of(jnp.bitwise_xor(lax.axis_index("side"), other) * hidden, 128)

    def body(at, size):
        product = dot(act[...], weight[pl.ds(start, hidden), pl.ds(at, size)])
        if len(refs) > 1:
            product = product + refs[0][:, pl.ds(at, size)]
        out[:, pl.ds(at, size)] = product.astype(out.dtype)

    over_columns(out.shape[1], body)


def final_kernel(groups, mid, first, second, out):
    total = first[...].astype(jnp.float32) + second[...].astype(jnp.float32)
    total = mid[...] + total
    here = out.shape[1] // groups
    for t in range(TOKENS):
        block = [
            total[(r * TOKENS + t) * here : (r * TOKENS + t + 1) * here] for r in range(groups)
        ]
        out[t] = jnp.concatenate(block, axis=0).astype(out.dtype)


def shards(
    query,
    new_keys,
    new_values,
    key_cache,
    value_cache,
    lengths,
    residual,
    out_weight,
    norm_gain,
    gate_weight,
    up_weight,
    down_weight,
):
    sides, groups, cols = (lax.axis_size(a) for a in ("side", "row", "col"))
    rows_here = key_cache.shape[0]
    total_rows = residual.shape[1]
    width_share = residual.shape[2]
    hidden_share = gate_weight.shape[1]
    features = out_weight.shape[0]
    model = width_share * groups
    m = TOKENS * total_rows
    cells = TOKENS * rows_here
    hb = HEADS // cols
    split = 2 if sides == 2 and (hidden_share // 2) % 128 == 0 else 1
    hidden = hidden_share // split
    f32, bf16 = jnp.float32, jnp.bfloat16
    shape = jax.ShapeDtypeStruct
    pad = -(-cells // 8) * 8

    def halves(n):
        return [shape((n // 2, cells + 1, hb, HD), f32)] * 2

    sources = [query, new_keys, new_values, key_cache, value_cache]
    keep, send = call(
        functools.partial(attention_kernel, cols),
        halves(cols),
        [ANY_SPEC] * 6,
        [pltpu.VMEM(a.shape, a.dtype) for a in sources]
        + [pltpu.SMEM(lengths.shape, lengths.dtype)]
        + [pltpu.VMEM((cols, cells + 1, hb, HD), f32), pltpu.SemaphoreType.DMA((6,))],
        flops=40 * 10**9,
        name="attention",
    )(*[in_hbm(a) for a in [lengths, *sources]])
    for level in range(1, cols.bit_length() - 1):
        received = partner(send, "col", 1 << (level - 1))
        n = cols >> level
        keep, send = call(
            functools.partial(merge_kernel, level),
            halves(n),
            [VMEM_SPEC] * 2,
            [pltpu.VMEM((n, cells + 1, hb, HD), f32)],
            name="merge",
        )(keep, received)
    attended = call(
        attended_kernel,
        shape((cells, features), bf16),
        [VMEM_SPEC] * 2,
        name="attended",
    )(keep, partner(send, "col", cols // 2))
    gathered = spread(attended, "row")
    partial = call(
        functools.partial(out_kernel, groups),
        shape((m, width_share), WIRE),
        [VMEM_SPEC] * (groups + 1),
        [pltpu.VMEM((groups, pad, features), f32), pltpu.VMEM((m, features), bf16)],
        name="out_projection",
    )(*gathered, in_vmem(out_weight))

    def sum_of_columns(value):
        for level in range(cols.bit_length() - 2):
            value = call(
                add_kernel,
                shape(value.shape, WIRE),
                [VMEM_SPEC] * 2,
                name="add",
            )(value, partner(value, "col", 1 << level))
        return value, partner(value, "col", cols // 2)

    mid, keep, send = call(
        functools.partial(lift_kernel, groups, split),
        [shape((m, width_share), f32)] + [shape((m, hidden + HD), WIRE)] * 2,
        [VMEM_SPEC] * 6,
        [pltpu.VMEM((m, width_share), bf16), pltpu.VMEM((2, m, hidden + HD), f32)],
        name="gate_up",
    )(
        in_vmem(residual), in_vmem(norm_gain), in_vmem(gate_weight), in_vmem(up_weight),
        *sum_of_columns(partial),
    )
    received = partner(send, "row", 1)
    for level in range(1, groups.bit_length() - 1):
        keep = call(
            sum_kernel,
            shape(keep.shape, WIRE),
            [VMEM_SPEC] * 2,
            name="gate_up_sum",
        )(keep, received)
        received = partner(keep, "row", 1 << level)
    act = call(
        functools.partial(act_kernel, model),
        shape((m // 2, hidden), bf16),
        [VMEM_SPEC] * 2,
        name="activation",
    )(keep, received)
    own = call(
        gather_kernel,
        shape((m, hidden), bf16),
        [VMEM_SPEC] * 2,
        [pltpu.VMEM((2, m // 2, hidden), f32)],
        name="gather_act",
    )(act, partner(act, "row", 1))
    down_weight = in_vmem(down_weight)
    first = call(
        functools.partial(down_kernel, 0),
        shape((m, width_share), f32 if split > 1 else WIRE),
        [VMEM_SPEC] * 2,
        name="down_first",
    )(own, down_weight)
    down = first
    if split > 1:
        crossed = partner(own, "side", 1)
        down = call(
            functools.partial(down_kernel, 1),
            shape((m, width_share), WIRE),
            [VMEM_SPEC] * 3,
            name="down_second",
        )(crossed, down_weight, first)
    return call(
        functools.partial(final_kernel, groups),
        shape((TOKENS, total_rows, width_share), bf16),
        [VMEM_SPEC] * 3,
        name="final",
    )(mid, *sum_of_columns(down))


def solution(mesh):
    in_specs = (
        P(None, "row", None),
        P(None, "row", None),
        P(None, "row", None),
        P("row", "col", None),
        P("row", "col", None),
        P("row"),
        P(None, None, "row"),
        P("col", "row"),
        P("row"),
        P("row", "col"),
        P("row", "col"),
        P("col", "row"),
    )
    out_specs = P(None, None, "row")
    return jax.shard_map(shards, mesh=mesh, in_specs=in_specs, out_specs=out_specs, check_vma=False)
```

time: 247 us -> 51.8 us (0.21)
  waiting for transfers between devices: 137 us -> 27 us
  blocking collectives: 71.4 us -> 0 us
  starting transfers between devices: 1.76 us -> 15.5 us
  between operations: 13.4 us -> 0.13 us
  Pallas kernels: 0 us -> 8.98 us
  other arithmetic: 8.72 us -> 0.01 us
  local copies, waits for them, and re-layouts: 8.64 us -> 0.04 us
  matrix products: 5.65 us -> 0 us
    psum x3 -> x0, waiting for transfers between devices: 134 us -> none  [the longest x2 84.5 us: tile_sum(): return lax.psum(value, 'col')]
    all_gather x8 -> x0, blocking collectives: 59.7 us -> none  [the longest x6 33.1 us: joined(): gathered = jax.tree.map(lambda a: lax.all_gather(a, axis), part)]
    ppermute x3 -> x13, waiting for transfers between devices: 2.8 us -> 27 us  [partner(): lax.ppermute(value, axis, [(i, i ^ k) for i in range(lax.axis_size(axis))])]
    ppermute x3 -> x13, starting transfers between devices: 1.68 us -> 15.5 us  [partner(): lax.ppermute(value, axis, [(i, i ^ k) for i in range(lax.axis_size(axis))])]
    psum x1 -> x0, blocking collectives: 11.7 us -> none  [shards(): lax.psum((gate_part, up_part, jnp.sum(mid * mid, axis=1)), 'row')]
    pallas_call x0 -> x13, Pallas kernels: none -> 8.98 us  [the longest x1 2.31 us: shards(): call(functools.partial(lift_kernel, groups, split), [shape((m, width_shar...]
    unnamed x29 -> x18, local copies, waits for them, and re-layouts: 6.38 us -> 0.04 us
    dot_general x7 -> x0, matrix products: 5.65 us -> none  [the longest x2 3.29 us: partial_softmax(): jnp.einsum('bkgp,bpkd->bkgd', weights, values_part.astype(jnp.float32), p...]
  transfers between devices with their start and end apart: 6 -> 13, of which waited for: 4 -> 12; matrix products, arithmetic and copies ran while one was open for 2% -> 0% of each run, Pallas kernels for 0% -> 2%
where the time goes in v1:
time: 51.8 us; the launch traced here: 51.7 us
  waiting for transfers between devices  27 us (52%)
  starting transfers between devices  15.5 us (30%)
  Pallas kernels  8.98 us (17%)
    ppermute x13, waiting for transfers between devices, partner(): lax.ppermute(value, axis, [(i, i ^ k) for i in range(lax.axis_size(axis))])  27 us
    ppermute x13, starting transfers between devices, partner(): lax.ppermute(value, axis, [(i, i ^ k) for i in range(lax.axis_size(axis))])  15.5 us
    pallas_call x1, Pallas kernels, shards(): call(functools.partial(lift_kernel, groups, split), [shape((m, width_shar...  2.31 us
    pallas_call x1, Pallas kernels, shards(): call(functools.partial(attention_kernel, cols), halves(cols), [ANY_SPEC]...  2.25 us
    pallas_call x1, Pallas kernels, shards(): call(functools.partial(down_kernel, 0), shape((m, width_share), f32 if sp...  1.18 us
    pallas_call x1, Pallas kernels, shards(): call(functools.partial(down_kernel, 1), shape((m, width_share), WIRE), [V...  1.17 us
  transfers between devices with their start and end apart: 13, of which 12 were waited for; matrix products, arithmetic and copies ran while one was open for 0% of the time, Pallas kernels for 2%

profile of v1, /device:TPU:0, one launch (start us, length us, event | category | flops | bytes accessed | tf_op | source)
XLA Modules:
  0.0 51.7 jit_solution(12634545297731448954)
XLA Ops:
  0.0 2.3 %attention.1 = (f32[2,5,8,128]{3,2,1,0:T(8,128)S(1)}, f32[2,5,8,128]{3,2,1,0:T(8,128)S(1)}) custom-call(s32[2]{0:T(128)} %lengths.1, bf16[2,2,4096]{2,1,0:T(2,128)(2,1)} %rest_0_.1, bf16[2,2,512]{2,1,0:T(2,128)(2,1)} %rest_1_.1, bf16[2,2,512]{2,1,0:T(2,128)(2,1)} %rest_2_.1, bf16[2,384,512]{2,1,0:T(8,128)(2,1)} %rest_3_.1, bf16[2,384,512]{2,1,0:T(8,128)(2,1)} %rest_4_.1), custom_call_target="tpu_custom_call" | custom-call | flops 40000000000 | bytes 1024 | tf_op jit(solution)/shard_map/attention/pallas_call | solution.py:358
  2.3 0.5 %collective-permute-start = (f32[2,5,8,128]{3,2,1,0:T(8,128)S(1)}, f32[2,5,8,128]{3,2,1,0:T(8,128)S(1)}, u32[]{:S(2)}, u32[]{:S(2)}) collective-permute-start(f32[2,5,8,128]{3,2,1,0:T(8,128)S(1)} %get-tuple-element.13), channel_id=1, source_target_pairs={{0,1},{1,0},{2,3},{3,2},{4,5},{5,4},{6,7},{7,6},{8,9},{9,8},{10,11... | collective-permute-start | bytes 122888 | tf_op jit(solution)/shard_map/ppermute | solution.py:24
  2.8 0.9 %collective-permute-done.received = f32[2,5,8,128]{3,2,1,0:T(8,128)S(1)} collective-permute-done((f32[2,5,8,128]{3,2,1,0:T(8,128)S(1)}, f32[2,5,8,128]{3,2,1,0:T(8,128)S(1)}, u32[]{:S(2)}, u32[]{:S(2)}) %collective-permute-start) | collective-permute-done | bytes 40992 | tf_op jit(solution)/shard_map/ppermute | solution.py:24
  3.7 0.2 merge.1
  3.8 2.9 %collective-permute-start.1 = (f32[1,5,8,128]{3,2,1,0:T(8,128)S(1)}, f32[1,5,8,128]{3,2,1,0:T(8,128)S(1)}, u32[]{:S(2)}, u32[]{:S(2)}) collective-permute-start(f32[1,5,8,128]{3,2,1,0:T(8,128)S(1)} %get-tuple-element.15), channel_id=1, source_target_pairs={{0,2},{1,3},{2,0},{3,1},{4,6},{5,7},{6,4},{7,5},{8,10},{9,11},{10,... | collective-permute-start | bytes 61448 | tf_op jit(solution)/shard_map/ppermute | solution.py:24
  6.8 1.8 %collective-permute-done.1.received = f32[1,5,8,128]{3,2,1,0:T(8,128)S(1)} collective-permute-done((f32[1,5,8,128]{3,2,1,0:T(8,128)S(1)}, f32[1,5,8,128]{3,2,1,0:T(8,128)S(1)}, u32[]{:S(2)}, u32[]{:S(2)}) %collective-permute-start.1) | collective-permute-done | bytes 20512 | tf_op jit(solution)/shard_map/ppermute | solution.py:24
  8.5 0.2 attended.1.refs_0_
  8.7 4.2 %collective-permute-start.4 = (bf16[4,1024]{1,0:T(4,128)(2,1)S(1)}, bf16[4,1024]{1,0:T(4,128)(2,1)S(1)}, u32[]{:S(2)}, u32[]{:S(2)}) collective-permute-start(bf16[4,1024]{1,0:T(4,128)(2,1)S(1)} %attended.1.refs_0_), channel_id=1, source_target_pairs={{0,12},{4,8},{8,4},{12,0},{1,13},{5,9},{9,5},{13,1},{2,14},{6,10},... | collective-permute-start | bytes 24584 | tf_op jit(solution)/shard_map/ppermute | solution.py:24
  12.9 0.0 collective-permute-start.3
  12.9 0.6 %collective-permute-start.2 = (bf16[4,1024]{1,0:T(4,128)(2,1)S(1)}, bf16[4,1024]{1,0:T(4,128)(2,1)S(1)}, u32[]{:S(2)}, u32[]{:S(2)}) collective-permute-start(bf16[4,1024]{1,0:T(4,128)(2,1)S(1)} %attended.1.refs_0_), channel_id=1, source_target_pairs={{0,4},{4,0},{8,12},{12,8},{1,5},{5,1},{9,13},{13,9},{2,6},{6,2},{1... | collective-permute-start | bytes 24584 | tf_op jit(solution)/shard_map/ppermute | solution.py:24
  13.5 1.0 %collective-permute-done.4.refs_3_ = bf16[4,1024]{1,0:T(4,128)(2,1)S(1)} collective-permute-done((bf16[4,1024]{1,0:T(4,128)(2,1)S(1)}, bf16[4,1024]{1,0:T(4,128)(2,1)S(1)}, u32[]{:S(2)}, u32[]{:S(2)}) %collective-permute-start.4) | collective-permute-done | bytes 8224 | tf_op jit(solution)/shard_map/ppermute | solution.py:24
  14.5 2.9 %collective-permute-done.3.refs_2_ = bf16[4,1024]{1,0:T(4,128)(2,1)S(1)} collective-permute-done((bf16[4,1024]{1,0:T(4,128)(2,1)S(1)}, bf16[4,1024]{1,0:T(4,128)(2,1)S(1)}, u32[]{:S(2)}, u32[]{:S(2)}) %collective-permute-start.3) | collective-permute-done | bytes 8224 | tf_op jit(solution)/shard_map/ppermute | solution.py:24
  17.4 0.0 collective-permute-done.2.refs_1_
  17.4 0.0 copy-done.2
  17.4 0.8 %out_projection.1.first = bf16[16,2048]{1,0:T(8,128)(2,1)S(1)} custom-call(bf16[4,1024]{1,0:T(4,128)(2,1)S(1)} %attended.1.refs_0_, bf16[4,1024]{1,0:T(4,128)(2,1)S(1)} %collective-permute-done.2.refs_1_, bf16[4,1024]{1,0:T(4,128)(2,1)S(1)} %collective-permute-done.3.refs_2_, bf16[4,1024]{1,0:T(4,128)(2,1)S(1)} %collective-permute-done.4.refs_3_, ...), custom_call_target="tpu_custom_call" | custom-call | tf_op jit(solution)/shard_map/out_projection/pallas_call | solution.py:385
  18.2 0.0 collective-permute-start.5
  18.2 1.3 %collective-permute-done.5.second = bf16[16,2048]{1,0:T(8,128)(2,1)S(1)} collective-permute-done((bf16[16,2048]{1,0:T(8,128)(2,1)S(1)}, bf16[16,2048]{1,0:T(8,128)(2,1)S(1)}, u32[]{:S(2)}, u32[]{:S(2)}) %collective-permute-start.5) | collective-permute-done | bytes 65568 | tf_op jit(solution)/shard_map/ppermute | solution.py:24
  19.5 0.0 slice-start.1
  19.5 0.0 slice-start.2
  19.5 0.0 slice-start.3
  19.6 1.6 %collective-permute-start.6 = (bf16[16,2048]{1,0:T(8,128)(2,1)S(1)}, bf16[16,2048]{1,0:T(8,128)(2,1)S(1)}, u32[]{:S(2)}, u32[]{:S(2)}) collective-permute-start(bf16[16,2048]{1,0:T(8,128)(2,1)S(1)} %add.2.first), channel_id=1, source_target_pairs={{0,2},{1,3},{2,0},{3,1},{4,6},{5,7},{6,4},{7,5},{8,10},{9,11},{10,... | collective-permute-start | bytes 196616 | tf_op jit(solution)/shard_map/ppermute | solution.py:24
  21.1 2.7 %collective-permute-done.6.second = bf16[16,2048]{1,0:T(8,128)(2,1)S(1)} collective-permute-done((bf16[16,2048]{1,0:T(8,128)(2,1)S(1)}, bf16[16,2048]{1,0:T(8,128)(2,1)S(1)}, u32[]{:S(2)}, u32[]{:S(2)}) %collective-permute-start.6) | collective-permute-done | bytes 65568 | tf_op jit(solution)/shard_map/ppermute | solution.py:24
  23.9 0.0 copy-done.4
  23.9 0.0 copy-done.3
  23.9 0.0 copy-done
  23.9 0.0 copy-done.1
  23.9 2.3 %gate_up.1 = (f32[16,2048]{1,0:T(8,128)S(1)}, bf16[16,1920]{1,0:T(8,128)(2,1)S(1)}, bf16[16,1920]{1,0:T(8,128)(2,1)S(1)}) custom-call(bf16[2,8,2048]{2,1,0:T(8,128)(2,1)S(1)} %copy-done.3, bf16[2048]{0:T(1024)(128)(2,1)S(1)} %copy-done.4, bf16[2048,3584]{1,0:T(8,128)(2,1)S(1)} %copy-done, bf16[2048,3584]{1,0:T(8,128)(2,1)S(1)} %copy-done.1, ...), custom_call_target="tpu_custom_call" | custom-call | tf_op jit(solution)/shard_map/gate_up/pallas_call | solution.py:403
  26.2 0.1 collective-permute-start.7
  26.3 4.2 %collective-permute-done.7.second = bf16[16,1920]{1,0:T(8,128)(2,1)S(1)} collective-permute-done((bf16[16,1920]{1,0:T(8,128)(2,1)S(1)}, bf16[16,1920]{1,0:T(8,128)(2,1)S(1)}, u32[]{:S(2)}, u32[]{:S(2)}) %collective-permute-start.7) | collective-permute-done | bytes 61472 | tf_op jit(solution)/shard_map/ppermute | solution.py:24
  30.5 0.1 gate_up_sum.1.first
  30.6 2.4 %collective-permute-start.8 = (bf16[16,1920]{1,0:T(8,128)(2,1)S(1)}, bf16[16,1920]{1,0:T(8,128)(2,1)S(1)}, u32[]{:S(2)}, u32[]{:S(2)}) collective-permute-start(bf16[16,1920]{1,0:T(8,128)(2,1)S(1)} %gate_up_sum.1.first), channel_id=1, source_target_pairs={{0,8},{4,12},{8,0},{12,4},{1,9},{5,13},{9,1},{13,5},{2,10},{6,14},... | collective-permute-start | bytes 184328 | tf_op jit(solution)/shard_map/ppermute | solution.py:24
  33.0 2.8 %collective-permute-done.8.second = bf16[16,1920]{1,0:T(8,128)(2,1)S(1)} collective-permute-done((bf16[16,1920]{1,0:T(8,128)(2,1)S(1)}, bf16[16,1920]{1,0:T(8,128)(2,1)S(1)}, u32[]{:S(2)}, u32[]{:S(2)}) %collective-permute-start.8) | collective-permute-done | bytes 61472 | tf_op jit(solution)/shard_map/ppermute | solution.py:24
  35.9 0.1 activation.1.own
  36.0 0.1 collective-permute-start.9
  36.1 3.9 %collective-permute-done.9.received = bf16[8,1792]{1,0:T(8,128)(2,1)S(1)} collective-permute-done((bf16[8,1792]{1,0:T(8,128)(2,1)S(1)}, bf16[8,1792]{1,0:T(8,128)(2,1)S(1)}, u32[]{:S(2)}, u32[]{:S(2)}) %collective-permute-start.9) | collective-permute-done | bytes 28704 | tf_op jit(solution)/shard_map/ppermute | solution.py:24
  39.9 1.6 %collective-permute-start.10 = (bf16[16,1792]{1,0:T(8,128)(2,1)S(1)}, bf16[16,1792]{1,0:T(8,128)(2,1)S(1)}, u32[]{:S(2)}, u32[]{:S(2)}) collective-permute-start(bf16[16,1792]{1,0:T(8,128)(2,1)S(1)} %gather_act.1.act), channel_id=1, source_target_pairs={{0,16},{16,0},{1,17},{17,1},{2,18},{18,2},{3,19},{19,3},{4,20},{20... | collective-permute-start | bytes 172040 | tf_op jit(solution)/shard_map/ppermute | solution.py:24
  41.5 0.0 slice-done
  41.5 0.0 slice-done.1
  41.5 0.0 slice-done.2
  41.5 0.0 slice-done.3
  41.5 1.2 %down_first.1.refs_0_ = f32[16,2048]{1,0:T(8,128)S(1)} custom-call(bf16[16,1792]{1,0:T(8,128)(2,1)S(1)} %gather_act.1.act, bf16[3584,2048]{1,0:T(8,128)(2,1)S(1)} %bitcast.1), custom_call_target="tpu_custom_call" | custom-call | tf_op jit(solution)/shard_map/down_first/pallas_call | solution.py:436
  42.7 1.5 %collective-permute-done.10.act = bf16[16,1792]{1,0:T(8,128)(2,1)S(1)} collective-permute-done((bf16[16,1792]{1,0:T(8,128)(2,1)S(1)}, bf16[16,1792]{1,0:T(8,128)(2,1)S(1)}, u32[]{:S(2)}, u32[]{:S(2)}) %collective-permute-start.10) | collective-permute-done | bytes 57376 | tf_op jit(solution)/shard_map/ppermute | solution.py:24
  44.2 1.2 %down_second.1.first = bf16[16,2048]{1,0:T(8,128)(2,1)S(1)} custom-call(bf16[16,1792]{1,0:T(8,128)(2,1)S(1)} %collective-permute-done.10.act, bf16[3584,2048]{1,0:T(8,128)(2,1)S(1)} %bitcast.1, f32[16,2048]{1,0:T(8,128)S(1)} %down_first.1.refs_0_), custom_call_target="tpu_custom_call" | custom-call | tf_op jit(solution)/shard_map/down_second/pallas_call | solution.py:445
  45.4 0.0 collective-permute-start.11
  45.4 1.3 %collective-permute-done.11.second = bf16[16,2048]{1,0:T(8,128)(2,1)S(1)} collective-permute-done((bf16[16,2048]{1,0:T(8,128)(2,1)S(1)}, bf16[16,2048]{1,0:T(8,128)(2,1)S(1)}, u32[]{:S(2)}, u32[]{:S(2)}) %collective-permute-start.11) | collective-permute-done | bytes 65568 | tf_op jit(solution)/shard_map/ppermute | solution.py:24
  46.6 1.6 %collective-permute-start.12 = (bf16[16,2048]{1,0:T(8,128)(2,1)S(1)}, bf16[16,2048]{1,0:T(8,128)(2,1)S(1)}, u32[]{:S(2)}, u32[]{:S(2)}) collective-permute-start(bf16[16,2048]{1,0:T(8,128)(2,1)S(1)} %add.3.first), channel_id=1, source_target_pairs={{0,2},{1,3},{2,0},{3,1},{4,6},{5,7},{6,4},{7,5},{8,10},{9,11},{10,... | collective-permute-start | bytes 196616 | tf_op jit(solution)/shard_map/ppermute | solution.py:24
  48.2 2.7 %collective-permute-done.12.second = bf16[16,2048]{1,0:T(8,128)(2,1)S(1)} collective-permute-done((bf16[16,2048]{1,0:T(8,128)(2,1)S(1)}, bf16[16,2048]{1,0:T(8,128)(2,1)S(1)}, u32[]{:S(2)}, u32[]{:S(2)}) %collective-permute-start.12) | collective-permute-done | bytes 65568 | tf_op jit(solution)/shard_map/ppermute | solution.py:24
  51.0 0.7 %final.1 = bf16[2,8,2048]{2,1,0:T(8,128)(2,1)} custom-call(f32[16,2048]{1,0:T(8,128)S(1)} %get-tuple-element.16.mid, bf16[16,2048]{1,0:T(8,128)(2,1)S(1)} %add.3.first, bf16[16,2048]{1,0:T(8,128)(2,1)S(1)} %collective-permute-done.12.second), custom_call_target="tpu_custom_call" | custom-call | tf_op jit(solution)/shard_map/final/pallas_call | solution.py:451
  (10 shorter events, 0.1 us)
Async XLA Ops:
  0.0 17.4 %copy-start.2 = (bf16[1024,2048]{1,0:T(8,128)(2,1)S(1)}, bf16[1024,2048]{1,0:T(8,128)(2,1)}, u32[]{:S(2)}) copy-start(bf16[1024,2048]{1,0:T(8,128)(2,1)} %refs_4_.1) | copy-start | bytes 12582916
  0.0 23.9 %copy-start.4 = (bf16[2048]{0:T(1024)(128)(2,1)S(1)}, bf16[2048]{0:T(1024)(128)(2,1)}, u32[]{:S(2)}) copy-start(bf16[2048]{0:T(1024)(128)(2,1)} %gains.1) | copy-start | bytes 12292
  0.0 23.9 %copy-start.3 = (bf16[2,8,2048]{2,1,0:T(8,128)(2,1)S(1)}, bf16[2,8,2048]{2,1,0:T(8,128)(2,1)}, u32[]{:S(2)}) copy-start(bf16[2,8,2048]{2,1,0:T(8,128)(2,1)} %residual.1) | copy-start | bytes 196612
  0.0 23.9 %copy-start = (bf16[2048,3584]{1,0:T(8,128)(2,1)S(1)}, bf16[2048,3584]{1,0:T(8,128)(2,1)}, u32[]{:S(2)}) copy-start(bf16[2048,3584]{1,0:T(8,128)(2,1)} %gate_weight.1) | copy-start | bytes 44040196
  0.0 23.9 %copy-start.1 = (bf16[2048,3584]{1,0:T(8,128)(2,1)S(1)}, bf16[2048,3584]{1,0:T(8,128)(2,1)}, u32[]{:S(2)}) copy-start(bf16[2048,3584]{1,0:T(8,128)(2,1)} %up_weight.1) | copy-start | bytes 44040196
  2.3 1.4 %collective-permute-start = (f32[2,5,8,128]{3,2,1,0:T(8,128)S(1)}, f32[2,5,8,128]{3,2,1,0:T(8,128)S(1)}, u32[]{:S(2)}, u32[]{:S(2)}) collective-permute-start(f32[2,5,8,128]{3,2,1,0:T(8,128)S(1)} %get-tuple-element.13), channel_id=1, source_target_pairs={{0,1},{1,0},{2,3},{3,2},{4,5},{5,4},{6,7},{7,6},{8,9},{9,8},{10,11... | collective-permute-start | bytes 122888 | tf_op jit(solution)/shard_map/ppermute | solution.py:24
  3.8 4.7 %collective-permute-start.1 = (f32[1,5,8,128]{3,2,1,0:T(8,128)S(1)}, f32[1,5,8,128]{3,2,1,0:T(8,128)S(1)}, u32[]{:S(2)}, u32[]{:S(2)}) collective-permute-start(f32[1,5,8,128]{3,2,1,0:T(8,128)S(1)} %get-tuple-element.15), channel_id=1, source_target_pairs={{0,2},{1,3},{2,0},{3,1},{4,6},{5,7},{6,4},{7,5},{8,10},{9,11},{10,... | collective-permute-start | bytes 61448 | tf_op jit(solution)/shard_map/ppermute | solution.py:24
  8.7 5.8 %collective-permute-start.4 = (bf16[4,1024]{1,0:T(4,128)(2,1)S(1)}, bf16[4,1024]{1,0:T(4,128)(2,1)S(1)}, u32[]{:S(2)}, u32[]{:S(2)}) collective-permute-start(bf16[4,1024]{1,0:T(4,128)(2,1)S(1)} %attended.1.refs_0_), channel_id=1, source_target_pairs={{0,12},{4,8},{8,4},{12,0},{1,13},{5,9},{9,5},{13,1},{2,14},{6,10},... | collective-permute-start | bytes 24584 | tf_op jit(solution)/shard_map/ppermute | solution.py:24
  12.9 4.5 %collective-permute-start.3 = (bf16[4,1024]{1,0:T(4,128)(2,1)S(1)}, bf16[4,1024]{1,0:T(4,128)(2,1)S(1)}, u32[]{:S(2)}, u32[]{:S(2)}) collective-permute-start(bf16[4,1024]{1,0:T(4,128)(2,1)S(1)} %attended.1.refs_0_), channel_id=1, source_target_pairs={{0,8},{4,12},{8,0},{12,4},{1,9},{5,13},{9,1},{13,5},{2,10},{6,14},... | collective-permute-start | bytes 24584 | tf_op jit(solution)/shard_map/ppermute | solution.py:24
  12.9 4.5 %collective-permute-start.2 = (bf16[4,1024]{1,0:T(4,128)(2,1)S(1)}, bf16[4,1024]{1,0:T(4,128)(2,1)S(1)}, u32[]{:S(2)}, u32[]{:S(2)}) collective-permute-start(bf16[4,1024]{1,0:T(4,128)(2,1)S(1)} %attended.1.refs_0_), channel_id=1, source_target_pairs={{0,4},{4,0},{8,12},{12,8},{1,5},{5,1},{9,13},{13,9},{2,6},{6,2},{1... | collective-permute-start | bytes 24584 | tf_op jit(solution)/shard_map/ppermute | solution.py:24
  18.2 1.3 %collective-permute-start.5 = (bf16[16,2048]{1,0:T(8,128)(2,1)S(1)}, bf16[16,2048]{1,0:T(8,128)(2,1)S(1)}, u32[]{:S(2)}, u32[]{:S(2)}) collective-permute-start(bf16[16,2048]{1,0:T(8,128)(2,1)S(1)} %out_projection.1.first), channel_id=1, source_target_pairs={{0,1},{1,0},{2,3},{3,2},{4,5},{5,4},{6,7},{7,6},{8,9},{9,8},{10,11... | collective-permute-start | bytes 196616 | tf_op jit(solution)/shard_map/ppermute | solution.py:24
  19.5 22.0 %slice-start = ((s8[14680064]{0:T(1024)(128)(4,1)}), s8[4194304]{0:T(1024)(128)(4,1)S(1)}, s32[]{:S(2)}) async-start(s8[14680064]{0:T(1024)(128)(4,1)} %bitcast), calls=%async_computation | async-start | bytes 8388608
  19.5 22.0 %slice-start.1 = ((s8[14680064]{0:T(1024)(128)(4,1)}), s8[4194304]{0:T(1024)(128)(4,1)S(1)}, s32[]{:S(2)}) async-start(s8[14680064]{0:T(1024)(128)(4,1)} %bitcast), calls=%async_computation.1 | async-start | bytes 8388608
  19.5 22.0 %slice-start.2 = ((s8[14680064]{0:T(1024)(128)(4,1)}), s8[4194304]{0:T(1024)(128)(4,1)S(1)}, s32[]{:S(2)}) async-start(s8[14680064]{0:T(1024)(128)(4,1)} %bitcast), calls=%async_computation.2 | async-start | bytes 8388608
  19.5 21.9 %slice-start.3 = ((s8[14680064]{0:T(1024)(128)(4,1)}), s8[2097152]{0:T(1024)(128)(4,1)S(1)}, s32[]{:S(2)}) async-start(s8[14680064]{0:T(1024)(128)(4,1)} %bitcast), calls=%async_computation.3 | async-start | bytes 4194304
  19.6 4.3 %collective-permute-start.6 = (bf16[16,2048]{1,0:T(8,128)(2,1)S(1)}, bf16[16,2048]{1,0:T(8,128)(2,1)S(1)}, u32[]{:S(2)}, u32[]{:S(2)}) collective-permute-start(bf16[16,2048]{1,0:T(8,128)(2,1)S(1)} %add.2.first), channel_id=1, source_target_pairs={{0,2},{1,3},{2,0},{3,1},{4,6},{5,7},{6,4},{7,5},{8,10},{9,11},{10,... | collective-permute-start | bytes 196616 | tf_op jit(solution)/shard_map/ppermute | solution.py:24
  26.2 4.3 %collective-permute-start.7 = (bf16[16,1920]{1,0:T(8,128)(2,1)S(1)}, bf16[16,1920]{1,0:T(8,128)(2,1)S(1)}, u32[]{:S(2)}, u32[]{:S(2)}) collective-permute-start(bf16[16,1920]{1,0:T(8,128)(2,1)S(1)} %get-tuple-element.18), channel_id=1, source_target_pairs={{0,4},{4,0},{8,12},{12,8},{1,5},{5,1},{9,13},{13,9},{2,6},{6,2},{1... | collective-permute-start | bytes 184328 | tf_op jit(solution)/shard_map/ppermute | solution.py:24
  30.6 5.2 %collective-permute-start.8 = (bf16[16,1920]{1,0:T(8,128)(2,1)S(1)}, bf16[16,1920]{1,0:T(8,128)(2,1)S(1)}, u32[]{:S(2)}, u32[]{:S(2)}) collective-permute-start(bf16[16,1920]{1,0:T(8,128)(2,1)S(1)} %gate_up_sum.1.first), channel_id=1, source_target_pairs={{0,8},{4,12},{8,0},{12,4},{1,9},{5,13},{9,1},{13,5},{2,10},{6,14},... | collective-permute-start | bytes 184328 | tf_op jit(solution)/shard_map/ppermute | solution.py:24
  36.0 3.9 %collective-permute-start.9 = (bf16[8,1792]{1,0:T(8,128)(2,1)S(1)}, bf16[8,1792]{1,0:T(8,128)(2,1)S(1)}, u32[]{:S(2)}, u32[]{:S(2)}) collective-permute-start(bf16[8,1792]{1,0:T(8,128)(2,1)S(1)} %activation.1.own), channel_id=1, source_target_pairs={{0,4},{4,0},{8,12},{12,8},{1,5},{5,1},{9,13},{13,9},{2,6},{6,2},{1... | collective-permute-start | bytes 86024 | tf_op jit(solution)/shard_map/ppermute | solution.py:24
  39.9 4.2 %collective-permute-start.10 = (bf16[16,1792]{1,0:T(8,128)(2,1)S(1)}, bf16[16,1792]{1,0:T(8,128)(2,1)S(1)}, u32[]{:S(2)}, u32[]{:S(2)}) collective-permute-start(bf16[16,1792]{1,0:T(8,128)(2,1)S(1)} %gather_act.1.act), channel_id=1, source_target_pairs={{0,16},{16,0},{1,17},{17,1},{2,18},{18,2},{3,19},{19,3},{4,20},{20... | collective-permute-start | bytes 172040 | tf_op jit(solution)/shard_map/ppermute | solution.py:24
  45.4 1.3 %collective-permute-start.11 = (bf16[16,2048]{1,0:T(8,128)(2,1)S(1)}, bf16[16,2048]{1,0:T(8,128)(2,1)S(1)}, u32[]{:S(2)}, u32[]{:S(2)}) collective-permute-start(bf16[16,2048]{1,0:T(8,128)(2,1)S(1)} %down_second.1.first), channel_id=1, source_target_pairs={{0,1},{1,0},{2,3},{3,2},{4,5},{5,4},{6,7},{7,6},{8,9},{9,8},{10,11... | collective-permute-start | bytes 196616 | tf_op jit(solution)/shard_map/ppermute | solution.py:24
  46.6 4.3 %collective-permute-start.12 = (bf16[16,2048]{1,0:T(8,128)(2,1)S(1)}, bf16[16,2048]{1,0:T(8,128)(2,1)S(1)}, u32[]{:S(2)}, u32[]{:S(2)}) collective-permute-start(bf16[16,2048]{1,0:T(8,128)(2,1)S(1)} %add.3.first), channel_id=1, source_target_pairs={{0,2},{1,3},{2,0},{3,1},{4,6},{5,7},{6,4},{7,5},{8,10},{9,11},{10,... | collective-permute-start | bytes 196616 | tf_op jit(solution)/shard_map/ppermute | solution.py:24

commit v2 on v1

--- a/solution.py
+++ b/solution.py
@@ -25,7 +25,17 @@
 
 
 def spread(piece, axis):
-    return [piece] + [partner(piece, axis, k) for k in range(1, lax.axis_size(axis))]
+    return [piece] + [partner(piece, axis, k) for k in reversed(range(1, lax.axis_size(axis)))]
+
+
+def by_distance(pieces):
+    return pieces[:1] + pieces[:0:-1]
+
+
+def tree_sum(values):
+    while len(values) > 1:
+        values = [values[i] + values[i + 1] for i in range(0, len(values), 2)]
+    return values[0]
 
 
 def dot(a, b):
@@ -60,14 +70,9 @@
     return pltpu.with_memory_space_constraint(value, pltpu.VMEM)
 
 
-def divide(blocks, bit, keep, send):
-    for i in range(keep.shape[0]):
-        keep[i] = blocks[2 * i + bit]
-        send[i] = blocks[2 * i + 1 - bit]
-
-
 def attention_kernel(cols, lengths, *rest):
-    sources, (keep, send), held, (sized_ref, packed, sems) = rest[:5], rest[5:7], rest[7:12], rest[12:]
+    sources, outs = rest[:5], rest[5 : 5 + cols]
+    held, (sized_ref, packed, sems) = rest[5 + cols : 10 + cols], rest[10 + cols :]
     sized = pltpu.make_async_copy(lengths, sized_ref, sems.at[5])
     sized.start()
     lengths = sized_ref
@@ -153,46 +158,28 @@
         else:
             for j in range(GROUP // hb):
                 packed[g * (GROUP // hb) + j, TOKENS * rows] = stats[g][j * hb : (j + 1) * hb]
-    divide(packed, column & 1, keep, send)
-
-
-def joined(first, second, i):
-    cells = first.shape[1] - 1
-    result = []
+    for k in range(cols):
+        outs[k][...] = packed[jnp.bitwise_xor(column, k)]
+
+
+def combine_kernel(cols, *refs):
+    parts, out = refs[:cols], refs[cols]
+    cells = parts[0].shape[0] - 1
+    hb = parts[0].shape[1]
+    stats = [p[cells] for p in parts]
+    attended = []
     for tb in range(cells):
-        stats = [p[i, cells] for p in (first, second)]
-        peak_a, peak_b = (s[:, 2 * tb : 2 * tb + 1] for s in stats)
-        total_a, total_b = (s[:, 2 * tb + 1 : 2 * tb + 2] for s in stats)
-        peak = jnp.maximum(peak_a, peak_b)
-        scale_a, scale_b = jnp.exp(peak_a - peak), jnp.exp(peak_b - peak)
-        total = total_a * scale_a + total_b * scale_b
-        result.append((first[i, tb] * scale_a + second[i, tb] * scale_b, total, peak))
-    return result
-
-
-def merge_kernel(level, kept, received, keep, send, packed):
-    lane = lax.broadcasted_iota(jnp.int32, kept.shape[2:], 1)
-    for i in range(kept.shape[0]):
-        stats = jnp.zeros(kept.shape[2:], jnp.float32)
-        result = joined(kept, received, i)
-        for tb, (summed, total, peak) in enumerate(result):
-            packed[i, tb] = summed
-            stats = jnp.where(lane == 2 * tb, peak, stats)
-            stats = jnp.where(lane == 2 * tb + 1, total, stats)
-        packed[i, len(result)] = stats
-    divide(packed, (lax.axis_index("col") >> level) & 1, keep, send)
-
-
-def attended_kernel(kept, received, out):
-    attended = [summed / total for summed, total, _ in joined(kept, received, 0)]
+        peaks = [s[:, 2 * tb : 2 * tb + 1] for s in stats]
+        totals = [s[:, 2 * tb + 1 : 2 * tb + 2] for s in stats]
+        top = functools.reduce(jnp.maximum, peaks)
+        scales = [jnp.exp(p - top) for p in peaks]
+        total = tree_sum([t * s for t, s in zip(totals, scales)])
+        summed = tree_sum([p[tb] * s for p, s in zip(parts, scales)])
+        attended.append(summed / total)
     rows = [
-        jnp.concatenate([a[h : h + 1] for a in attended], axis=0) for h in range(kept.shape[2])
+        jnp.concatenate([attended[tb][h : h + 1] for tb in range(cells)], axis=0) for h in range(hb)
     ]
     out[...] = jnp.concatenate(rows, axis=1).astype(out.dtype)
-
-
-def add_kernel(first, second, out):
-    out[...] = (first[...].astype(jnp.float32) + second[...].astype(jnp.float32)).astype(out.dtype)
 
 
 def group_order(value, groups):
@@ -221,7 +208,7 @@
 
 
 def out_kernel(groups, *refs):
-    parts, (weight, out, canon, attended) = refs[:groups], refs[groups:]
+    parts, (weight, out, canon, attended) = by_distance(refs[:groups]), refs[groups:]
     attended[...] = canonical(parts, canon, lax.axis_index("row"))
 
     def body(at, size):
@@ -240,32 +227,25 @@
     )
 
 
-def lift_kernel(groups, split, residual, gains, gate_weight, up_weight, first, second, *refs):
-    mid_out, keep, send, lifted, packed = refs
+def lift_kernel(groups, split, residual, gains, gate_weight, up_weight, *refs):
+    parts, (mid_out, out, lifted) = by_distance(refs[:-3]), refs[-3:]
     hidden = gate_weight.shape[1] // split
     start = lax.axis_index("side") * hidden if split > 1 else 0
-    half = packed.shape[1] // 2
-    mid = first[...].astype(jnp.float32) + second[...].astype(jnp.float32)
+    mid = tree_sum([p[...].astype(jnp.float32) for p in parts])
     mid = group_order(residual[...].astype(jnp.float32), groups) + mid
     mid_out[...] = mid
     sent = in_pieces(jnp.sum(mid * mid, axis=1, keepdims=True))
     lifted[...] = (mid * gains[...].astype(jnp.float32).reshape(1, mid.shape[1])).astype(jnp.bfloat16)
-    for i in range(2):
-        piece = sent[i * half : (i + 1) * half]
-        packed[i, :, hidden:] = jnp.concatenate([piece, piece], axis=0)
+    out[:, hidden:] = jnp.concatenate([sent, sent], axis=0).astype(out.dtype)
 
     def body(at, size):
         block = pl.ds(pl.multiple_of(start + at, 128), size)
         gate = dot(lifted[...], gate_weight[:, block])
         up = dot(lifted[...], up_weight[:, block])
-        for i in range(2):
-            rows = slice(i * half, (i + 1) * half)
-            packed[i, :, pl.ds(at, size)] = jnp.concatenate([gate[rows], up[rows]], axis=0)
+        both = jnp.concatenate([gate, up], axis=0)
+        out[:, pl.ds(at, size)] = both.astype(out.dtype)
 
     over_columns(hidden, body)
-    bit = lax.axis_index("row") & 1
-    keep[...] = packed[bit].astype(keep.dtype)
-    send[...] = packed[1 - bit].astype(send.dtype)
 
 
 def sum_kernel(first, second, out):
@@ -287,13 +267,6 @@
     out[...] = (gate / (1.0 + jnp.exp(-gate)) * up).astype(out.dtype)
 
 
-def gather_kernel(own, received, out, packed):
-    bit = lax.axis_index("row") & 1
-    packed[bit] = own[...].astype(jnp.float32)
-    packed[1 - bit] = received[...].astype(jnp.float32)
-    out[...] = jnp.concatenate([packed[0], packed[1]], axis=0).astype(out.dtype)
-
-
 def down_kernel(other, act, weight, *refs):
     out = refs[-1]
     hidden = act.shape[1]
@@ -310,9 +283,9 @@
     over_columns(out.shape[1], body)
 
 
-def final_kernel(groups, mid, first, second, out):
-    total = first[...].astype(jnp.float32) + second[...].astype(jnp.float32)
-    total = mid[...] + total
+def final_kernel(groups, mid, *refs):
+    parts, out = by_distance(refs[:-1]), refs[-1]
+    total = mid[...] + tree_sum([p[...].astype(jnp.float32) for p in parts])
     here = out.shape[1] // groups
     for t in range(TOKENS):
         block = [
@@ -351,13 +324,11 @@
     shape = jax.ShapeDtypeStruct
     pad = -(-cells // 8) * 8
 
-    def halves(n):
-        return [shape((n // 2, cells + 1, hb, HD), f32)] * 2
-
     sources = [query, new_keys, new_values, key_cache, value_cache]
-    keep, send = call(
+    message = shape((cells + 1, hb, HD), f32)
+    parts = call(
         functools.partial(attention_kernel, cols),
-        halves(cols),
+        [message] * cols,
         [ANY_SPEC] * 6,
         [pltpu.VMEM(a.shape, a.dtype) for a in sources]
         + [pltpu.SMEM(lengths.shape, lengths.dtype)]
@@ -365,22 +336,13 @@
         flops=40 * 10**9,
         name="attention",
     )(*[in_hbm(a) for a in [lengths, *sources]])
-    for level in range(1, cols.bit_length() - 1):
-        received = partner(send, "col", 1 << (level - 1))
-        n = cols >> level
-        keep, send = call(
-            functools.partial(merge_kernel, level),
-            halves(n),
-            [VMEM_SPEC] * 2,
-            [pltpu.VMEM((n, cells + 1, hb, HD), f32)],
-            name="merge",
-        )(keep, received)
+    parts = [parts[0]] + [partner(parts[k], "col", k) for k in range(1, cols)]
     attended = call(
-        attended_kernel,
+        functools.partial(combine_kernel, cols),
         shape((cells, features), bf16),
-        [VMEM_SPEC] * 2,
-        name="attended",
-    )(keep, partner(send, "col", cols // 2))
+        [VMEM_SPEC] * cols,
+        name="combine",
+    )(*parts)
     gathered = spread(attended, "row")
     partial = call(
         functools.partial(out_kernel, groups),
@@ -389,49 +351,34 @@
         [pltpu.VMEM((groups, pad, features), f32), pltpu.VMEM((m, features), bf16)],
         name="out_projection",
     )(*gathered, in_vmem(out_weight))
-
-    def sum_of_columns(value):
-        for level in range(cols.bit_length() - 2):
-            value = call(
-                add_kernel,
-                shape(value.shape, WIRE),
-                [VMEM_SPEC] * 2,
-                name="add",
-            )(value, partner(value, "col", 1 << level))
-        return value, partner(value, "col", cols // 2)
-
-    mid, keep, send = call(
+    mid, value = call(
         functools.partial(lift_kernel, groups, split),
-        [shape((m, width_share), f32)] + [shape((m, hidden + HD), WIRE)] * 2,
-        [VMEM_SPEC] * 6,
-        [pltpu.VMEM((m, width_share), bf16), pltpu.VMEM((2, m, hidden + HD), f32)],
+        [shape((m, width_share), f32), shape((2 * m, hidden + HD), WIRE)],
+        [VMEM_SPEC] * (cols + 4),
+        [pltpu.VMEM((m, width_share), bf16)],
         name="gate_up",
     )(
         in_vmem(residual), in_vmem(norm_gain), in_vmem(gate_weight), in_vmem(up_weight),
-        *sum_of_columns(partial),
-    )
-    received = partner(send, "row", 1)
-    for level in range(1, groups.bit_length() - 1):
-        keep = call(
+        *spread(partial, "col"),
+    )
+    last = groups // 2
+    for level in range(groups.bit_length() - 2):
+        value = call(
             sum_kernel,
-            shape(keep.shape, WIRE),
+            shape(value.shape, WIRE),
             [VMEM_SPEC] * 2,
             name="gate_up_sum",
-        )(keep, received)
-        received = partner(keep, "row", 1 << level)
-    act = call(
-        functools.partial(act_kernel, model),
-        shape((m // 2, hidden), bf16),
-        [VMEM_SPEC] * 2,
-        name="activation",
-    )(keep, received)
-    own = call(
-        gather_kernel,
-        shape((m, hidden), bf16),
-        [VMEM_SPEC] * 2,
-        [pltpu.VMEM((2, m // 2, hidden), f32)],
-        name="gather_act",
-    )(act, partner(act, "row", 1))
+        )(value, partner(value, "row", 1 << level))
+
+    def activation(first, second):
+        return call(
+            functools.partial(act_kernel, model),
+            shape((m, hidden), bf16),
+            [VMEM_SPEC] * 2,
+            name="activation",
+        )(first, second)
+
+    own = activation(value, partner(value, "row", last))
     down_weight = in_vmem(down_weight)
     first = call(
         functools.partial(down_kernel, 0),
@@ -441,7 +388,9 @@
     )(own, down_weight)
     down = first
     if split > 1:
-        crossed = partner(own, "side", 1)
+        crossed = activation(
+            partner(value, "side", 1), partner(value, ("side", "row"), groups + last)
+        )
         down = call(
             functools.partial(down_kernel, 1),
             shape((m, width_share), WIRE),
@@ -451,9 +400,9 @@
     return call(
         functools.partial(final_kernel, groups),
         shape((TOKENS, total_rows, width_share), bf16),
-        [VMEM_SPEC] * 3,
+        [VMEM_SPEC] * (cols + 1),
         name="final",
-    )(mid, *sum_of_columns(down))
+    )(mid, *spread(down, "col"))
 
 
 def solution(mesh):

time: 51.8 us -> 53 us (1.023)
  waiting for transfers between devices: 27 us -> 27.8 us
    ppermute x13 -> x16, waiting for transfers between devices: 27 us -> 27.8 us  [partner(): lax.ppermute(value, axis, [(i, i ^ k) for i in range(lax.axis_size(axis))])]
    ppermute x13 -> x16, starting transfers between devices: 15.5 us -> 16 us  [partner(): lax.ppermute(value, axis, [(i, i ^ k) for i in range(lax.axis_size(axis))])]
    pallas_call x8 -> x5, Pallas kernels: 2.84 us -> 2.76 us  [the longest x1 2.25 us: shards(): call(functools.partial(attention_kernel, cols), [message] * cols, [ANY_SP...]
  transfers between devices with their start and end apart: 13 -> 16, of which waited for: 12 -> 11; matrix products, arithmetic and copies ran while one was open for 0% -> 0% of each run, Pallas kernels for 2% -> 2%
where the time goes in v2:
time: 53 us; the launch traced here: 52.9 us
  waiting for transfers between devices  27.8 us (52%)
  starting transfers between devices  16 us (30%)
  Pallas kernels  8.95 us (17%)
    ppermute x16, waiting for transfers between devices, partner(): lax.ppermute(value, axis, [(i, i ^ k) for i in range(lax.axis_size(axis))])  27.8 us
    ppermute x16, starting transfers between devices, partner(): lax.ppermute(value, axis, [(i, i ^ k) for i in range(lax.axis_size(axis))])  16 us
    pallas_call x1, Pallas kernels, shards(): call(functools.partial(lift_kernel, groups, split), [shape((m, width_shar...  2.31 us
    pallas_call x1, Pallas kernels, shards(): call(functools.partial(attention_kernel, cols), [message] * cols, [ANY_SP...  2.25 us
    pallas_call x1, Pallas kernels, shards(): call(functools.partial(down_kernel, 1), shape((m, width_share), WIRE), [V...  1.19 us
    pallas_call x1, Pallas kernels, shards(): call(functools.partial(down_kernel, 0), shape((m, width_share), f32 if sp...  1.18 us
  transfers between devices with their start and end apart: 16, of which 11 were waited for; matrix products, arithmetic and copies ran while one was open for 0% of the time, Pallas kernels for 2%

profile of v2, /device:TPU:0, one launch (start us, length us, event | category | flops | bytes accessed | tf_op | source)
XLA Modules:
  0.0 52.9 jit_solution(4588115363176370214)
XLA Ops:
  0.0 2.3 %attention.1 = (f32[5,8,128]{2,1,0:T(8,128)S(1)}, f32[5,8,128]{2,1,0:T(8,128)S(1)}, f32[5,8,128]{2,1,0:T(8,128)S(1)}, f32[5,8,128]{2,1,0:T(8,128)S(1)}) custom-call(s32[2]{0:T(128)} %lengths.1, bf16[2,2,4096]{2,1,0:T(2,128)(2,1)} %rest_0_.1, bf16[2,2,512]{2,1,0:T(2,128)(2,1)} %rest_1_.1, bf16[2,2,512]{2,1,0:T(2,128)(2,1)} %rest_2_.1, ...), custom_call_target="tpu_custom_call" | custom-call | flops 40000000000 | bytes 1024 | tf_op jit(solution)/shard_map/attention/pallas_call | solution.py:329
  2.3 0.5 %collective-permute-start = (f32[5,8,128]{2,1,0:T(8,128)S(1)}, f32[5,8,128]{2,1,0:T(8,128)S(1)}, u32[]{:S(2)}, u32[]{:S(2)}) collective-permute-start(f32[5,8,128]{2,1,0:T(8,128)S(1)} %get-tuple-element.12), channel_id=1, source_target_pairs={{0,1},{1,0},{2,3},{3,2},{4,5},{5,4},{6,7},{7,6},{8,9},{9,8},{10,11... | collective-permute-start | bytes 61448 | tf_op jit(solution)/shard_map/ppermute | solution.py:24
  2.8 2.6 %collective-permute-start.1 = (f32[5,8,128]{2,1,0:T(8,128)S(1)}, f32[5,8,128]{2,1,0:T(8,128)S(1)}, u32[]{:S(2)}, u32[]{:S(2)}) collective-permute-start(f32[5,8,128]{2,1,0:T(8,128)S(1)} %get-tuple-element.13), channel_id=1, source_target_pairs={{0,2},{1,3},{2,0},{3,1},{4,6},{5,7},{6,4},{7,5},{8,10},{9,11},{10,... | collective-permute-start | bytes 61448 | tf_op jit(solution)/shard_map/ppermute | solution.py:24
  5.4 0.1 collective-permute-start.2
  5.5 0.0 collective-permute-done.refs_1_
  5.5 1.7 %collective-permute-done.1.refs_2_ = f32[5,8,128]{2,1,0:T(8,128)S(1)} collective-permute-done((f32[5,8,128]{2,1,0:T(8,128)S(1)}, f32[5,8,128]{2,1,0:T(8,128)S(1)}, u32[]{:S(2)}, u32[]{:S(2)}) %collective-permute-start.1) | collective-permute-done | bytes 20512 | tf_op jit(solution)/shard_map/ppermute | solution.py:24
  7.2 1.4 %collective-permute-done.2.refs_3_ = f32[5,8,128]{2,1,0:T(8,128)S(1)} collective-permute-done((f32[5,8,128]{2,1,0:T(8,128)S(1)}, f32[5,8,128]{2,1,0:T(8,128)S(1)}, u32[]{:S(2)}, u32[]{:S(2)}) %collective-permute-start.2) | collective-permute-done | bytes 20512 | tf_op jit(solution)/shard_map/ppermute | solution.py:24
  8.6 0.2 combine.1.refs_0_
  8.8 3.7 %collective-permute-start.3 = (bf16[4,1024]{1,0:T(4,128)(2,1)S(1)}, bf16[4,1024]{1,0:T(4,128)(2,1)S(1)}, u32[]{:S(2)}, u32[]{:S(2)}) collective-permute-start(bf16[4,1024]{1,0:T(4,128)(2,1)S(1)} %combine.1.refs_0_), channel_id=1, source_target_pairs={{0,12},{4,8},{8,4},{12,0},{1,13},{5,9},{9,5},{13,1},{2,14},{6,10},... | collective-permute-start | bytes 24584 | tf_op jit(solution)/shard_map/ppermute | solution.py:24
  12.5 0.0 collective-permute-start.4
  12.5 0.8 %collective-permute-start.5 = (bf16[4,1024]{1,0:T(4,128)(2,1)S(1)}, bf16[4,1024]{1,0:T(4,128)(2,1)S(1)}, u32[]{:S(2)}, u32[]{:S(2)}) collective-permute-start(bf16[4,1024]{1,0:T(4,128)(2,1)S(1)} %combine.1.refs_0_), channel_id=1, source_target_pairs={{0,4},{4,0},{8,12},{12,8},{1,5},{5,1},{9,13},{13,9},{2,6},{6,2},{1... | collective-permute-start | bytes 24584 | tf_op jit(solution)/shard_map/ppermute | solution.py:24
  13.2 1.1 %collective-permute-done.3.refs_1_ = bf16[4,1024]{1,0:T(4,128)(2,1)S(1)} collective-permute-done((bf16[4,1024]{1,0:T(4,128)(2,1)S(1)}, bf16[4,1024]{1,0:T(4,128)(2,1)S(1)}, u32[]{:S(2)}, u32[]{:S(2)}) %collective-permute-start.3) | collective-permute-done | bytes 8224 | tf_op jit(solution)/shard_map/ppermute | solution.py:24
  14.3 2.7 %collective-permute-done.4.refs_2_ = bf16[4,1024]{1,0:T(4,128)(2,1)S(1)} collective-permute-done((bf16[4,1024]{1,0:T(4,128)(2,1)S(1)}, bf16[4,1024]{1,0:T(4,128)(2,1)S(1)}, u32[]{:S(2)}, u32[]{:S(2)}) %collective-permute-start.4) | collective-permute-done | bytes 8224 | tf_op jit(solution)/shard_map/ppermute | solution.py:24
  17.0 0.0 collective-permute-done.5.refs_3_
  17.0 0.0 copy-done.2
  17.0 0.8 %out_projection.1.refs_0_ = bf16[16,2048]{1,0:T(8,128)(2,1)S(1)} custom-call(bf16[4,1024]{1,0:T(4,128)(2,1)S(1)} %combine.1.refs_0_, bf16[4,1024]{1,0:T(4,128)(2,1)S(1)} %collective-permute-done.3.refs_1_, bf16[4,1024]{1,0:T(4,128)(2,1)S(1)} %collective-permute-done.4.refs_2_, bf16[4,1024]{1,0:T(4,128)(2,1)S(1)} %collective-permute-done.5.refs_3_, ...), custom_call_target="tpu_custom_call" | custom-call | tf_op jit(solution)/shard_map/out_projection/pallas_call | solution.py:347
  17.8 0.1 collective-permute-start.6
  17.9 0.8 %collective-permute-start.7 = (bf16[16,2048]{1,0:T(8,128)(2,1)S(1)}, bf16[16,2048]{1,0:T(8,128)(2,1)S(1)}, u32[]{:S(2)}, u32[]{:S(2)}) collective-permute-start(bf16[16,2048]{1,0:T(8,128)(2,1)S(1)} %out_projection.1.refs_0_), channel_id=1, source_target_pairs={{0,2},{1,3},{2,0},{3,1},{4,6},{5,7},{6,4},{7,5},{8,10},{9,11},{10,... | collective-permute-start | bytes 196616 | tf_op jit(solution)/shard_map/ppermute | solution.py:24
  18.7 1.1 %collective-permute-start.8 = (bf16[16,2048]{1,0:T(8,128)(2,1)S(1)}, bf16[16,2048]{1,0:T(8,128)(2,1)S(1)}, u32[]{:S(2)}, u32[]{:S(2)}) collective-permute-start(bf16[16,2048]{1,0:T(8,128)(2,1)S(1)} %out_projection.1.refs_0_), channel_id=1, source_target_pairs={{0,1},{1,0},{2,3},{3,2},{4,5},{5,4},{6,7},{7,6},{8,9},{9,8},{10,11... | collective-permute-start | bytes 196616 | tf_op jit(solution)/shard_map/ppermute | solution.py:24
  19.8 1.9 %collective-permute-done.6.refs_1_ = bf16[16,2048]{1,0:T(8,128)(2,1)S(1)} collective-permute-done((bf16[16,2048]{1,0:T(8,128)(2,1)S(1)}, bf16[16,2048]{1,0:T(8,128)(2,1)S(1)}, u32[]{:S(2)}, u32[]{:S(2)}) %collective-permute-start.6) | collective-permute-done | bytes 65568 | tf_op jit(solution)/shard_map/ppermute | solution.py:24
  21.7 1.2 %collective-permute-done.7.refs_2_ = bf16[16,2048]{1,0:T(8,128)(2,1)S(1)} collective-permute-done((bf16[16,2048]{1,0:T(8,128)(2,1)S(1)}, bf16[16,2048]{1,0:T(8,128)(2,1)S(1)}, u32[]{:S(2)}, u32[]{:S(2)}) %collective-permute-start.7) | collective-permute-done | bytes 65568 | tf_op jit(solution)/shard_map/ppermute | solution.py:24
  22.9 0.0 collective-permute-done.8.refs_3_
  22.9 0.0 copy-done.3
  22.9 0.0 copy-done.4
  22.9 0.0 copy-done
  22.9 0.0 copy-done.1
  22.9 2.3 %gate_up.1 = (f32[16,2048]{1,0:T(8,128)S(1)}, bf16[32,1920]{1,0:T(8,128)(2,1)S(1)}) custom-call(bf16[2,8,2048]{2,1,0:T(8,128)(2,1)S(1)} %copy-done.3, bf16[2048]{0:T(1024)(128)(2,1)S(1)} %copy-done.4, bf16[2048,3584]{1,0:T(8,128)(2,1)S(1)} %copy-done, bf16[2048,3584]{1,0:T(8,128)(2,1)S(1)} %copy-done.1, bf16[16,2048]{1,0:T(8,128)(2,1)S(1)} %out_projection.1.refs_0_, ...), custom_call_target="tpu_custom_call" | custom-call | tf_op jit(solution)/shard_map/gate_up/pallas_call | solution.py:354
  25.2 0.1 collective-permute-start.9
  25.3 5.3 %collective-permute-done.9.second = bf16[32,1920]{1,0:T(8,128)(2,1)S(1)} collective-permute-done((bf16[32,1920]{1,0:T(8,128)(2,1)S(1)}, bf16[32,1920]{1,0:T(8,128)(2,1)S(1)}, u32[]{:S(2)}, u32[]{:S(2)}) %collective-permute-start.9) | collective-permute-done | bytes 122912 | tf_op jit(solution)/shard_map/ppermute | solution.py:24
  30.6 0.1 gate_up_sum.1.first
  30.7 2.1 %collective-permute-start.12 = (bf16[32,1920]{1,0:T(8,128)(2,1)S(1)}, bf16[32,1920]{1,0:T(8,128)(2,1)S(1)}, u32[]{:S(2)}, u32[]{:S(2)}) collective-permute-start(bf16[32,1920]{1,0:T(8,128)(2,1)S(1)} %gate_up_sum.1.first), channel_id=1, source_target_pairs={{0,8},{4,12},{8,0},{12,4},{1,9},{5,13},{9,1},{13,5},{2,10},{6,14},... | collective-permute-start | bytes 368648 | tf_op jit(solution)/shard_map/ppermute | solution.py:24
  32.8 1.5 %collective-permute-start.10 = (bf16[32,1920]{1,0:T(8,128)(2,1)S(1)}, bf16[32,1920]{1,0:T(8,128)(2,1)S(1)}, u32[]{:S(2)}, u32[]{:S(2)}) collective-permute-start(bf16[32,1920]{1,0:T(8,128)(2,1)S(1)} %gate_up_sum.1.first), channel_id=1, source_target_pairs={{0,16},{16,0},{1,17},{17,1},{2,18},{18,2},{3,19},{19,3},{4,20},{20... | collective-permute-start | bytes 368648 | tf_op jit(solution)/shard_map/ppermute | solution.py:24
  34.3 0.9 %collective-permute-start.11 = (bf16[32,1920]{1,0:T(8,128)(2,1)S(1)}, bf16[32,1920]{1,0:T(8,128)(2,1)S(1)}, u32[]{:S(2)}, u32[]{:S(2)}) collective-permute-start(bf16[32,1920]{1,0:T(8,128)(2,1)S(1)} %gate_up_sum.1.first), channel_id=1, source_target_pairs={{0,24},{4,28},{8,16},{12,20},{16,8},{20,12},{24,0},{28,4},{1,25},{... | collective-permute-start | bytes 368648 | tf_op jit(solution)/shard_map/ppermute | solution.py:24
  35.2 6.4 %collective-permute-done.12.second = bf16[32,1920]{1,0:T(8,128)(2,1)S(1)} collective-permute-done((bf16[32,1920]{1,0:T(8,128)(2,1)S(1)}, bf16[32,1920]{1,0:T(8,128)(2,1)S(1)}, u32[]{:S(2)}, u32[]{:S(2)}) %collective-permute-start.12) | collective-permute-done | bytes 122912 | tf_op jit(solution)/shard_map/ppermute | solution.py:24
  41.6 0.1 activation.3.act
  41.7 0.0 slice-done
  41.8 1.2 %down_first.1.refs_0_ = f32[16,2048]{1,0:T(8,128)S(1)} custom-call(bf16[16,1792]{1,0:T(8,128)(2,1)S(1)} %activation.3.act, bf16[3584,2048]{1,0:T(8,128)(2,1)S(1)} %bitcast.1), custom_call_target="tpu_custom_call" | custom-call | tf_op jit(solution)/shard_map/down_first/pallas_call | solution.py:383
  43.0 0.0 collective-permute-done.10.first
  43.0 2.1 %collective-permute-done.11.second = bf16[32,1920]{1,0:T(8,128)(2,1)S(1)} collective-permute-done((bf16[32,1920]{1,0:T(8,128)(2,1)S(1)}, bf16[32,1920]{1,0:T(8,128)(2,1)S(1)}, u32[]{:S(2)}, u32[]{:S(2)}) %collective-permute-start.11) | collective-permute-done | bytes 122912 | tf_op jit(solution)/shard_map/ppermute | solution.py:24
  45.0 0.1 activation.2.act
  45.2 1.2 %down_second.1.refs_0_ = bf16[16,2048]{1,0:T(8,128)(2,1)S(1)} custom-call(bf16[16,1792]{1,0:T(8,128)(2,1)S(1)} %activation.2.act, bf16[3584,2048]{1,0:T(8,128)(2,1)S(1)} %bitcast.1, f32[16,2048]{1,0:T(8,128)S(1)} %down_first.1.refs_0_), custom_call_target="tpu_custom_call" | custom-call | tf_op jit(solution)/shard_map/down_second/pallas_call | solution.py:394
  46.4 0.8 %collective-permute-start.13 = (bf16[16,2048]{1,0:T(8,128)(2,1)S(1)}, bf16[16,2048]{1,0:T(8,128)(2,1)S(1)}, u32[]{:S(2)}, u32[]{:S(2)}) collective-permute-start(bf16[16,2048]{1,0:T(8,128)(2,1)S(1)} %down_second.1.refs_0_), channel_id=1, source_target_pairs={{0,3},{1,2},{2,1},{3,0},{4,7},{5,6},{6,5},{7,4},{8,11},{9,10},{10,... | collective-permute-start | bytes 196616 | tf_op jit(solution)/shard_map/ppermute | solution.py:24
  47.2 0.8 %collective-permute-start.14 = (bf16[16,2048]{1,0:T(8,128)(2,1)S(1)}, bf16[16,2048]{1,0:T(8,128)(2,1)S(1)}, u32[]{:S(2)}, u32[]{:S(2)}) collective-permute-start(bf16[16,2048]{1,0:T(8,128)(2,1)S(1)} %down_second.1.refs_0_), channel_id=1, source_target_pairs={{0,2},{1,3},{2,0},{3,1},{4,6},{5,7},{6,4},{7,5},{8,10},{9,11},{10,... | collective-permute-start | bytes 196616 | tf_op jit(solution)/shard_map/ppermute | solution.py:24
  48.0 0.3 collective-permute-start.15
  48.2 2.4 %collective-permute-done.13.refs_1_ = bf16[16,2048]{1,0:T(8,128)(2,1)S(1)} collective-permute-done((bf16[16,2048]{1,0:T(8,128)(2,1)S(1)}, bf16[16,2048]{1,0:T(8,128)(2,1)S(1)}, u32[]{:S(2)}, u32[]{:S(2)}) %collective-permute-start.13) | collective-permute-done | bytes 65568 | tf_op jit(solution)/shard_map/ppermute | solution.py:24
  50.6 1.6 %collective-permute-done.14.refs_2_ = bf16[16,2048]{1,0:T(8,128)(2,1)S(1)} collective-permute-done((bf16[16,2048]{1,0:T(8,128)(2,1)S(1)}, bf16[16,2048]{1,0:T(8,128)(2,1)S(1)}, u32[]{:S(2)}, u32[]{:S(2)}) %collective-permute-start.14) | collective-permute-done | bytes 65568 | tf_op jit(solution)/shard_map/ppermute | solution.py:24
  52.2 0.0 collective-permute-done.15.refs_3_
  52.2 0.7 %final.1 = bf16[2,8,2048]{2,1,0:T(8,128)(2,1)} custom-call(f32[16,2048]{1,0:T(8,128)S(1)} %get-tuple-element.15.mid, bf16[16,2048]{1,0:T(8,128)(2,1)S(1)} %down_second.1.refs_0_, bf16[16,2048]{1,0:T(8,128)(2,1)S(1)} %collective-permute-done.13.refs_1_, bf16[16,2048]{1,0:T(8,128)(2,1)S(1)} %collective-permute-done.14.refs_2_, ...), custom_call_target="tpu_custom_call" | custom-call | tf_op jit(solution)/shard_map/final/pallas_call | solution.py:400
  (13 shorter events, 0.0 us)
Async XLA Ops:
  0.0 17.0 %copy-start.2 = (bf16[1024,2048]{1,0:T(8,128)(2,1)S(1)}, bf16[1024,2048]{1,0:T(8,128)(2,1)}, u32[]{:S(2)}) copy-start(bf16[1024,2048]{1,0:T(8,128)(2,1)} %refs_4_.1) | copy-start | bytes 12582916
  0.0 22.9 %copy-start.3 = (bf16[2,8,2048]{2,1,0:T(8,128)(2,1)S(1)}, bf16[2,8,2048]{2,1,0:T(8,128)(2,1)}, u32[]{:S(2)}) copy-start(bf16[2,8,2048]{2,1,0:T(8,128)(2,1)} %residual.1) | copy-start | bytes 196612
  0.0 22.9 %copy-start.4 = (bf16[2048]{0:T(1024)(128)(2,1)S(1)}, bf16[2048]{0:T(1024)(128)(2,1)}, u32[]{:S(2)}) copy-start(bf16[2048]{0:T(1024)(128)(2,1)} %gains.1) | copy-start | bytes 12292
  0.0 22.9 %copy-start = (bf16[2048,3584]{1,0:T(8,128)(2,1)S(1)}, bf16[2048,3584]{1,0:T(8,128)(2,1)}, u32[]{:S(2)}) copy-start(bf16[2048,3584]{1,0:T(8,128)(2,1)} %gate_weight.1) | copy-start | bytes 44040196
  0.0 22.9 %copy-start.1 = (bf16[2048,3584]{1,0:T(8,128)(2,1)S(1)}, bf16[2048,3584]{1,0:T(8,128)(2,1)}, u32[]{:S(2)}) copy-start(bf16[2048,3584]{1,0:T(8,128)(2,1)} %up_weight.1) | copy-start | bytes 44040196
  2.3 3.2 %collective-permute-start = (f32[5,8,128]{2,1,0:T(8,128)S(1)}, f32[5,8,128]{2,1,0:T(8,128)S(1)}, u32[]{:S(2)}, u32[]{:S(2)}) collective-permute-start(f32[5,8,128]{2,1,0:T(8,128)S(1)} %get-tuple-element.12), channel_id=1, source_target_pairs={{0,1},{1,0},{2,3},{3,2},{4,5},{5,4},{6,7},{7,6},{8,9},{9,8},{10,11... | collective-permute-start | bytes 61448 | tf_op jit(solution)/shard_map/ppermute | solution.py:24
  2.8 4.4 %collective-permute-start.1 = (f32[5,8,128]{2,1,0:T(8,128)S(1)}, f32[5,8,128]{2,1,0:T(8,128)S(1)}, u32[]{:S(2)}, u32[]{:S(2)}) collective-permute-start(f32[5,8,128]{2,1,0:T(8,128)S(1)} %get-tuple-element.13), channel_id=1, source_target_pairs={{0,2},{1,3},{2,0},{3,1},{4,6},{5,7},{6,4},{7,5},{8,10},{9,11},{10,... | collective-permute-start | bytes 61448 | tf_op jit(solution)/shard_map/ppermute | solution.py:24
  5.4 3.2 %collective-permute-start.2 = (f32[5,8,128]{2,1,0:T(8,128)S(1)}, f32[5,8,128]{2,1,0:T(8,128)S(1)}, u32[]{:S(2)}, u32[]{:S(2)}) collective-permute-start(f32[5,8,128]{2,1,0:T(8,128)S(1)} %get-tuple-element.14), channel_id=1, source_target_pairs={{0,3},{1,2},{2,1},{3,0},{4,7},{5,6},{6,5},{7,4},{8,11},{9,10},{10,... | collective-permute-start | bytes 61448 | tf_op jit(solution)/shard_map/ppermute | solution.py:24
  8.8 5.5 %collective-permute-start.3 = (bf16[4,1024]{1,0:T(4,128)(2,1)S(1)}, bf16[4,1024]{1,0:T(4,128)(2,1)S(1)}, u32[]{:S(2)}, u32[]{:S(2)}) collective-permute-start(bf16[4,1024]{1,0:T(4,128)(2,1)S(1)} %combine.1.refs_0_), channel_id=1, source_target_pairs={{0,12},{4,8},{8,4},{12,0},{1,13},{5,9},{9,5},{13,1},{2,14},{6,10},... | collective-permute-start | bytes 24584 | tf_op jit(solution)/shard_map/ppermute | solution.py:24
  12.5 4.5 %collective-permute-start.4 = (bf16[4,1024]{1,0:T(4,128)(2,1)S(1)}, bf16[4,1024]{1,0:T(4,128)(2,1)S(1)}, u32[]{:S(2)}, u32[]{:S(2)}) collective-permute-start(bf16[4,1024]{1,0:T(4,128)(2,1)S(1)} %combine.1.refs_0_), channel_id=1, source_target_pairs={{0,8},{4,12},{8,0},{12,4},{1,9},{5,13},{9,1},{13,5},{2,10},{6,14},... | collective-permute-start | bytes 24584 | tf_op jit(solution)/shard_map/ppermute | solution.py:24
  12.5 4.5 %collective-permute-start.5 = (bf16[4,1024]{1,0:T(4,128)(2,1)S(1)}, bf16[4,1024]{1,0:T(4,128)(2,1)S(1)}, u32[]{:S(2)}, u32[]{:S(2)}) collective-permute-start(bf16[4,1024]{1,0:T(4,128)(2,1)S(1)} %combine.1.refs_0_), channel_id=1, source_target_pairs={{0,4},{4,0},{8,12},{12,8},{1,5},{5,1},{9,13},{13,9},{2,6},{6,2},{1... | collective-permute-start | bytes 24584 | tf_op jit(solution)/shard_map/ppermute | solution.py:24
  17.0 24.7 %slice-start = ((s8[14680064]{0:T(1024)(128)(4,1)}), s8[4194304]{0:T(1024)(128)(4,1)S(1)}, s32[]{:S(2)}) async-start(s8[14680064]{0:T(1024)(128)(4,1)} %bitcast), calls=%async_computation | async-start | bytes 8388608
  17.8 23.9 %slice-start.1 = ((s8[14680064]{0:T(1024)(128)(4,1)}), s8[4194304]{0:T(1024)(128)(4,1)S(1)}, s32[]{:S(2)}) async-start(s8[14680064]{0:T(1024)(128)(4,1)} %bitcast), calls=%async_computation.1 | async-start | bytes 8388608
  17.8 23.9 %slice-start.2 = ((s8[14680064]{0:T(1024)(128)(4,1)}), s8[4194304]{0:T(1024)(128)(4,1)S(1)}, s32[]{:S(2)}) async-start(s8[14680064]{0:T(1024)(128)(4,1)} %bitcast), calls=%async_computation.2 | async-start | bytes 8388608
  17.8 23.9 %slice-start.3 = ((s8[14680064]{0:T(1024)(128)(4,1)}), s8[2097152]{0:T(1024)(128)(4,1)S(1)}, s32[]{:S(2)}) async-start(s8[14680064]{0:T(1024)(128)(4,1)} %bitcast), calls=%async_computation.3 | async-start | bytes 4194304
  17.8 3.8 %collective-permute-start.6 = (bf16[16,2048]{1,0:T(8,128)(2,1)S(1)}, bf16[16,2048]{1,0:T(8,128)(2,1)S(1)}, u32[]{:S(2)}, u32[]{:S(2)}) collective-permute-start(bf16[16,2048]{1,0:T(8,128)(2,1)S(1)} %out_projection.1.refs_0_), channel_id=1, source_target_pairs={{0,3},{1,2},{2,1},{3,0},{4,7},{5,6},{6,5},{7,4},{8,11},{9,10},{10,... | collective-permute-start | bytes 196616 | tf_op jit(solution)/shard_map/ppermute | solution.py:24
  17.9 5.0 %collective-permute-start.7 = (bf16[16,2048]{1,0:T(8,128)(2,1)S(1)}, bf16[16,2048]{1,0:T(8,128)(2,1)S(1)}, u32[]{:S(2)}, u32[]{:S(2)}) collective-permute-start(bf16[16,2048]{1,0:T(8,128)(2,1)S(1)} %out_projection.1.refs_0_), channel_id=1, source_target_pairs={{0,2},{1,3},{2,0},{3,1},{4,6},{5,7},{6,4},{7,5},{8,10},{9,11},{10,... | collective-permute-start | bytes 196616 | tf_op jit(solution)/shard_map/ppermute | solution.py:24
  18.7 4.2 %collective-permute-start.8 = (bf16[16,2048]{1,0:T(8,128)(2,1)S(1)}, bf16[16,2048]{1,0:T(8,128)(2,1)S(1)}, u32[]{:S(2)}, u32[]{:S(2)}) collective-permute-start(bf16[16,2048]{1,0:T(8,128)(2,1)S(1)} %out_projection.1.refs_0_), channel_id=1, source_target_pairs={{0,1},{1,0},{2,3},{3,2},{4,5},{5,4},{6,7},{7,6},{8,9},{9,8},{10,11... | collective-permute-start | bytes 196616 | tf_op jit(solution)/shard_map/ppermute | solution.py:24
  25.2 5.4 %collective-permute-start.9 = (bf16[32,1920]{1,0:T(8,128)(2,1)S(1)}, bf16[32,1920]{1,0:T(8,128)(2,1)S(1)}, u32[]{:S(2)}, u32[]{:S(2)}) collective-permute-start(bf16[32,1920]{1,0:T(8,128)(2,1)S(1)} %get-tuple-element.16.first), channel_id=1, source_target_pairs={{0,4},{4,0},{8,12},{12,8},{1,5},{5,1},{9,13},{13,9},{2,6},{6,2},{1... | collective-permute-start | bytes 368648 | tf_op jit(solution)/shard_map/ppermute | solution.py:24
  30.7 10.9 %collective-permute-start.12 = (bf16[32,1920]{1,0:T(8,128)(2,1)S(1)}, bf16[32,1920]{1,0:T(8,128)(2,1)S(1)}, u32[]{:S(2)}, u32[]{:S(2)}) collective-permute-start(bf16[32,1920]{1,0:T(8,128)(2,1)S(1)} %gate_up_sum.1.first), channel_id=1, source_target_pairs={{0,8},{4,12},{8,0},{12,4},{1,9},{5,13},{9,1},{13,5},{2,10},{6,14},... | collective-permute-start | bytes 368648 | tf_op jit(solution)/shard_map/ppermute | solution.py:24
  32.8 10.2 %collective-permute-start.10 = (bf16[32,1920]{1,0:T(8,128)(2,1)S(1)}, bf16[32,1920]{1,0:T(8,128)(2,1)S(1)}, u32[]{:S(2)}, u32[]{:S(2)}) collective-permute-start(bf16[32,1920]{1,0:T(8,128)(2,1)S(1)} %gate_up_sum.1.first), channel_id=1, source_target_pairs={{0,16},{16,0},{1,17},{17,1},{2,18},{18,2},{3,19},{19,3},{4,20},{20... | collective-permute-start | bytes 368648 | tf_op jit(solution)/shard_map/ppermute | solution.py:24
  34.3 10.7 %collective-permute-start.11 = (bf16[32,1920]{1,0:T(8,128)(2,1)S(1)}, bf16[32,1920]{1,0:T(8,128)(2,1)S(1)}, u32[]{:S(2)}, u32[]{:S(2)}) collective-permute-start(bf16[32,1920]{1,0:T(8,128)(2,1)S(1)} %gate_up_sum.1.first), channel_id=1, source_target_pairs={{0,24},{4,28},{8,16},{12,20},{16,8},{20,12},{24,0},{28,4},{1,25},{... | collective-permute-start | bytes 368648 | tf_op jit(solution)/shard_map/ppermute | solution.py:24
  46.4 4.3 %collective-permute-start.13 = (bf16[16,2048]{1,0:T(8,128)(2,1)S(1)}, bf16[16,2048]{1,0:T(8,128)(2,1)S(1)}, u32[]{:S(2)}, u32[]{:S(2)}) collective-permute-start(bf16[16,2048]{1,0:T(8,128)(2,1)S(1)} %down_second.1.refs_0_), channel_id=1, source_target_pairs={{0,3},{1,2},{2,1},{3,0},{4,7},{5,6},{6,5},{7,4},{8,11},{9,10},{10,... | collective-permute-start | bytes 196616 | tf_op jit(solution)/shard_map/ppermute | solution.py:24
  47.2 5.0 %collective-permute-start.14 = (bf16[16,2048]{1,0:T(8,128)(2,1)S(1)}, bf16[16,2048]{1,0:T(8,128)(2,1)S(1)}, u32[]{:S(2)}, u32[]{:S(2)}) collective-permute-start(bf16[16,2048]{1,0:T(8,128)(2,1)S(1)} %down_second.1.refs_0_), channel_id=1, source_target_pairs={{0,2},{1,3},{2,0},{3,1},{4,6},{5,7},{6,4},{7,5},{8,10},{9,11},{10,... | collective-permute-start | bytes 196616 | tf_op jit(solution)/shard_map/ppermute | solution.py:24
  48.0 4.2 %collective-permute-start.15 = (bf16[16,2048]{1,0:T(8,128)(2,1)S(1)}, bf16[16,2048]{1,0:T(8,128)(2,1)S(1)}, u32[]{:S(2)}, u32[]{:S(2)}) collective-permute-start(bf16[16,2048]{1,0:T(8,128)(2,1)S(1)} %down_second.1.refs_0_), channel_id=1, source_target_pairs={{0,1},{1,0},{2,3},{3,2},{4,5},{5,4},{6,7},{7,6},{8,9},{9,8},{10,11... | collective-permute-start | bytes 196616 | tf_op jit(solution)/shard_map/ppermute | solution.py:24

commit v3 on v2

--- a/solution.py
+++ b/solution.py
@@ -25,11 +25,7 @@
 
 
 def spread(piece, axis):
-    return [piece] + [partner(piece, axis, k) for k in reversed(range(1, lax.axis_size(axis)))]
-
-
-def by_distance(pieces):
-    return pieces[:1] + pieces[:0:-1]
+    return [piece] + [partner(piece, axis, k) for k in range(1, lax.axis_size(axis))]
 
 
 def tree_sum(values):
@@ -208,7 +204,7 @@
 
 
 def out_kernel(groups, *refs):
-    parts, (weight, out, canon, attended) = by_distance(refs[:groups]), refs[groups:]
+    parts, (weight, out, canon, attended) = refs[:groups], refs[groups:]
     attended[...] = canonical(parts, canon, lax.axis_index("row"))
 
     def body(at, size):
@@ -228,24 +224,31 @@
 
 
 def lift_kernel(groups, split, residual, gains, gate_weight, up_weight, *refs):
-    parts, (mid_out, out, lifted) = by_distance(refs[:-3]), refs[-3:]
+    parts, (mid_out, keep, send, lifted, packed) = refs[:-5], refs[-5:]
     hidden = gate_weight.shape[1] // split
     start = lax.axis_index("side") * hidden if split > 1 else 0
+    half = packed.shape[1] // 2
     mid = tree_sum([p[...].astype(jnp.float32) for p in parts])
     mid = group_order(residual[...].astype(jnp.float32), groups) + mid
     mid_out[...] = mid
     sent = in_pieces(jnp.sum(mid * mid, axis=1, keepdims=True))
     lifted[...] = (mid * gains[...].astype(jnp.float32).reshape(1, mid.shape[1])).astype(jnp.bfloat16)
-    out[:, hidden:] = jnp.concatenate([sent, sent], axis=0).astype(out.dtype)
+    for i in range(2):
+        piece = sent[i * half : (i + 1) * half]
+        packed[i, :, hidden:] = jnp.concatenate([piece, piece], axis=0)
 
     def body(at, size):
         block = pl.ds(pl.multiple_of(start + at, 128), size)
         gate = dot(lifted[...], gate_weight[:, block])
         up = dot(lifted[...], up_weight[:, block])
-        both = jnp.concatenate([gate, up], axis=0)
-        out[:, pl.ds(at, size)] = both.astype(out.dtype)
+        for i in range(2):
+            rows = slice(i * half, (i + 1) * half)
+            packed[i, :, pl.ds(at, size)] = jnp.concatenate([gate[rows], up[rows]], axis=0)
 
     over_columns(hidden, body)
+    bit = lax.axis_index("row") & 1
+    keep[...] = packed[bit].astype(keep.dtype)
+    send[...] = packed[1 - bit].astype(send.dtype)
 
 
 def sum_kernel(first, second, out):
@@ -267,6 +270,13 @@
     out[...] = (gate / (1.0 + jnp.exp(-gate)) * up).astype(out.dtype)
 
 
+def gather_kernel(own, received, out, packed):
+    bit = lax.axis_index("row") & 1
+    packed[bit] = own[...].astype(jnp.float32)
+    packed[1 - bit] = received[...].astype(jnp.float32)
+    out[...] = jnp.concatenate([packed[0], packed[1]], axis=0).astype(out.dtype)
+
+
 def down_kernel(other, act, weight, *refs):
     out = refs[-1]
     hidden = act.shape[1]
@@ -284,7 +294,7 @@
 
 
 def final_kernel(groups, mid, *refs):
-    parts, out = by_distance(refs[:-1]), refs[-1]
+    parts, out = refs[:-1], refs[-1]
     total = mid[...] + tree_sum([p[...].astype(jnp.float32) for p in parts])
     here = out.shape[1] // groups
     for t in range(TOKENS):
@@ -351,52 +361,53 @@
         [pltpu.VMEM((groups, pad, features), f32), pltpu.VMEM((m, features), bf16)],
         name="out_projection",
     )(*gathered, in_vmem(out_weight))
-    mid, value = call(
+    mid, keep, send = call(
         functools.partial(lift_kernel, groups, split),
-        [shape((m, width_share), f32), shape((2 * m, hidden + HD), WIRE)],
+        [shape((m, width_share), f32)] + [shape((m, hidden + HD), WIRE)] * 2,
         [VMEM_SPEC] * (cols + 4),
-        [pltpu.VMEM((m, width_share), bf16)],
+        [pltpu.VMEM((m, width_share), bf16), pltpu.VMEM((2, m, hidden + HD), f32)],
         name="gate_up",
     )(
         in_vmem(residual), in_vmem(norm_gain), in_vmem(gate_weight), in_vmem(up_weight),
         *spread(partial, "col"),
     )
-    last = groups // 2
-    for level in range(groups.bit_length() - 2):
-        value = call(
+    received = partner(send, "row", 1)
+    for level in range(1, groups.bit_length() - 1):
+        keep = call(
             sum_kernel,
-            shape(value.shape, WIRE),
+            shape(keep.shape, WIRE),
             [VMEM_SPEC] * 2,
             name="gate_up_sum",
-        )(value, partner(value, "row", 1 << level))
-
-    def activation(first, second):
-        return call(
-            functools.partial(act_kernel, model),
+        )(keep, received)
+        received = partner(keep, "row", 1 << level)
+    act = call(
+        functools.partial(act_kernel, model),
+        shape((m // 2, hidden), bf16),
+        [VMEM_SPEC] * 2,
+        name="activation",
+    )(keep, received)
+    down_weight = in_vmem(down_weight)
+
+    def down_part(same, from_row, other, before, result):
+        rows = call(
+            gather_kernel,
             shape((m, hidden), bf16),
             [VMEM_SPEC] * 2,
-            name="activation",
-        )(first, second)
-
-    own = activation(value, partner(value, "row", last))
-    down_weight = in_vmem(down_weight)
-    first = call(
-        functools.partial(down_kernel, 0),
-        shape((m, width_share), f32 if split > 1 else WIRE),
-        [VMEM_SPEC] * 2,
-        name="down_first",
-    )(own, down_weight)
-    down = first
+            [pltpu.VMEM((2, m // 2, hidden), f32)],
+            name="gather_act",
+        )(same, from_row)
+        return call(
+            functools.partial(down_kernel, other),
+            shape((m, width_share), result),
+            [VMEM_SPEC] * (2 + len(before)),
+            name="down",
+        )(rows, down_weight, *before)
+
+    before = []
     if split > 1:
-        crossed = activation(
-            partner(value, "side", 1), partner(value, ("side", "row"), groups + last)
-        )
-        down = call(
-            functools.partial(down_kernel, 1),
-            shape((m, width_share), WIRE),
-            [VMEM_SPEC] * 3,
-            name="down_second",
-        )(crossed, down_weight, first)
+        far = partner(act, ("side", "row"), groups + 1)
+        before = [down_part(partner(act, "side", 1), far, 1, before, f32)]
+    down = down_part(act, partner(act, "row", 1), 0, before, WIRE)
     return call(
         functools.partial(final_kernel, groups),
         shape((TOKENS, total_rows, width_share), bf16),

time: 53 us -> 48.9 us (0.923)
  waiting for transfers between devices: 27.8 us -> 22.6 us
  starting transfers between devices: 16 us -> 17.1 us
    ppermute x16 -> x17, waiting for transfers between devices: 27.8 us -> 22.6 us  [partner(): lax.ppermute(value, axis, [(i, i ^ k) for i in range(lax.axis_size(axis))])]
    ppermute x16 -> x17, starting transfers between devices: 16 us -> 17.1 us  [partner(): lax.ppermute(value, axis, [(i, i ^ k) for i in range(lax.axis_size(axis))])]
    pallas_call x5 -> x6, Pallas kernels: 2.71 us -> 2.63 us  [the longest x2 2.37 us: down_part(): call(functools.partial(down_kernel, other), shape((m, width_share), resul...]
  transfers between devices with their start and end apart: 16 -> 17, of which waited for: 11 -> 12; matrix products, arithmetic and copies ran while one was open for 0% -> 0% of each run, Pallas kernels for 2% -> 2%
where the time goes in v3:
time: 48.9 us; the launch traced here: 48.8 us
  waiting for transfers between devices  22.6 us (46%)
  starting transfers between devices  17.1 us (35%)
  Pallas kernels  8.89 us (18%)
    ppermute x17, waiting for transfers between devices, partner(): lax.ppermute(value, axis, [(i, i ^ k) for i in range(lax.axis_size(axis))])  22.6 us
    ppermute x17, starting transfers between devices, partner(): lax.ppermute(value, axis, [(i, i ^ k) for i in range(lax.axis_size(axis))])  17.1 us
    pallas_call x2, Pallas kernels, down_part(): call(functools.partial(down_kernel, other), shape((m, width_share), resul...  2.37 us
    pallas_call x1, Pallas kernels, shards(): call(functools.partial(lift_kernel, groups, split), [shape((m, width_shar...  2.34 us
    pallas_call x1, Pallas kernels, shards(): call(functools.partial(attention_kernel, cols), [message] * cols, [ANY_SP...  2.25 us
  transfers between devices with their start and end apart: 17, of which 12 were waited for; matrix products, arithmetic and copies ran while one was open for 0% of the time, Pallas kernels for 2%

profile of v3, /device:TPU:0, one launch (start us, length us, event | category | flops | bytes accessed | tf_op | source)
XLA Modules:
  0.0 48.8 jit_solution(3140120731894553229)
XLA Ops:
  0.0 2.3 %attention.1 = (f32[5,8,128]{2,1,0:T(8,128)S(1)}, f32[5,8,128]{2,1,0:T(8,128)S(1)}, f32[5,8,128]{2,1,0:T(8,128)S(1)}, f32[5,8,128]{2,1,0:T(8,128)S(1)}) custom-call(s32[2]{0:T(128)} %lengths.1, bf16[2,2,4096]{2,1,0:T(2,128)(2,1)} %rest_0_.1, bf16[2,2,512]{2,1,0:T(2,128)(2,1)} %rest_1_.1, bf16[2,2,512]{2,1,0:T(2,128)(2,1)} %rest_2_.1, ...), custom_call_target="tpu_custom_call" | custom-call | flops 40000000000 | bytes 1024 | tf_op jit(solution)/shard_map/attention/pallas_call | solution.py:339
  2.3 0.5 %collective-permute-start = (f32[5,8,128]{2,1,0:T(8,128)S(1)}, f32[5,8,128]{2,1,0:T(8,128)S(1)}, u32[]{:S(2)}, u32[]{:S(2)}) collective-permute-start(f32[5,8,128]{2,1,0:T(8,128)S(1)} %get-tuple-element.13), channel_id=1, source_target_pairs={{0,1},{1,0},{2,3},{3,2},{4,5},{5,4},{6,7},{7,6},{8,9},{9,8},{10,11... | collective-permute-start | bytes 61448 | tf_op jit(solution)/shard_map/ppermute | solution.py:24
  2.8 2.6 %collective-permute-start.1 = (f32[5,8,128]{2,1,0:T(8,128)S(1)}, f32[5,8,128]{2,1,0:T(8,128)S(1)}, u32[]{:S(2)}, u32[]{:S(2)}) collective-permute-start(f32[5,8,128]{2,1,0:T(8,128)S(1)} %get-tuple-element.14), channel_id=1, source_target_pairs={{0,2},{1,3},{2,0},{3,1},{4,6},{5,7},{6,4},{7,5},{8,10},{9,11},{10,... | collective-permute-start | bytes 61448 | tf_op jit(solution)/shard_map/ppermute | solution.py:24
  5.4 0.1 collective-permute-start.2
  5.5 0.0 collective-permute-done.refs_1_
  5.5 1.7 %collective-permute-done.1.refs_2_ = f32[5,8,128]{2,1,0:T(8,128)S(1)} collective-permute-done((f32[5,8,128]{2,1,0:T(8,128)S(1)}, f32[5,8,128]{2,1,0:T(8,128)S(1)}, u32[]{:S(2)}, u32[]{:S(2)}) %collective-permute-start.1) | collective-permute-done | bytes 20512 | tf_op jit(solution)/shard_map/ppermute | solution.py:24
  7.2 1.4 %collective-permute-done.2.refs_3_ = f32[5,8,128]{2,1,0:T(8,128)S(1)} collective-permute-done((f32[5,8,128]{2,1,0:T(8,128)S(1)}, f32[5,8,128]{2,1,0:T(8,128)S(1)}, u32[]{:S(2)}, u32[]{:S(2)}) %collective-permute-start.2) | collective-permute-done | bytes 20512 | tf_op jit(solution)/shard_map/ppermute | solution.py:24
  8.6 0.2 combine.1.refs_0_
  8.8 3.7 %collective-permute-start.5 = (bf16[4,1024]{1,0:T(4,128)(2,1)S(1)}, bf16[4,1024]{1,0:T(4,128)(2,1)S(1)}, u32[]{:S(2)}, u32[]{:S(2)}) collective-permute-start(bf16[4,1024]{1,0:T(4,128)(2,1)S(1)} %combine.1.refs_0_), channel_id=1, source_target_pairs={{0,12},{4,8},{8,4},{12,0},{1,13},{5,9},{9,5},{13,1},{2,14},{6,10},... | collective-permute-start | bytes 24584 | tf_op jit(solution)/shard_map/ppermute | solution.py:24
  12.5 0.0 collective-permute-start.4
  12.5 0.8 %collective-permute-start.3 = (bf16[4,1024]{1,0:T(4,128)(2,1)S(1)}, bf16[4,1024]{1,0:T(4,128)(2,1)S(1)}, u32[]{:S(2)}, u32[]{:S(2)}) collective-permute-start(bf16[4,1024]{1,0:T(4,128)(2,1)S(1)} %combine.1.refs_0_), channel_id=1, source_target_pairs={{0,4},{4,0},{8,12},{12,8},{1,5},{5,1},{9,13},{13,9},{2,6},{6,2},{1... | collective-permute-start | bytes 24584 | tf_op jit(solution)/shard_map/ppermute | solution.py:24
  13.2 1.1 %collective-permute-done.5.refs_3_ = bf16[4,1024]{1,0:T(4,128)(2,1)S(1)} collective-permute-done((bf16[4,1024]{1,0:T(4,128)(2,1)S(1)}, bf16[4,1024]{1,0:T(4,128)(2,1)S(1)}, u32[]{:S(2)}, u32[]{:S(2)}) %collective-permute-start.5) | collective-permute-done | bytes 8224 | tf_op jit(solution)/shard_map/ppermute | solution.py:24
  14.3 2.7 %collective-permute-done.4.refs_2_ = bf16[4,1024]{1,0:T(4,128)(2,1)S(1)} collective-permute-done((bf16[4,1024]{1,0:T(4,128)(2,1)S(1)}, bf16[4,1024]{1,0:T(4,128)(2,1)S(1)}, u32[]{:S(2)}, u32[]{:S(2)}) %collective-permute-start.4) | collective-permute-done | bytes 8224 | tf_op jit(solution)/shard_map/ppermute | solution.py:24
  17.0 0.0 collective-permute-done.3.refs_1_
  17.0 0.0 copy-done.2
  17.0 0.8 %out_projection.1.refs_0_ = bf16[16,2048]{1,0:T(8,128)(2,1)S(1)} custom-call(bf16[4,1024]{1,0:T(4,128)(2,1)S(1)} %combine.1.refs_0_, bf16[4,1024]{1,0:T(4,128)(2,1)S(1)} %collective-permute-done.3.refs_1_, bf16[4,1024]{1,0:T(4,128)(2,1)S(1)} %collective-permute-done.4.refs_2_, bf16[4,1024]{1,0:T(4,128)(2,1)S(1)} %collective-permute-done.5.refs_3_, ...), custom_call_target="tpu_custom_call" | custom-call | tf_op jit(solution)/shard_map/out_projection/pallas_call | solution.py:357
  17.8 0.1 collective-permute-start.8
  17.9 0.8 %collective-permute-start.7 = (bf16[16,2048]{1,0:T(8,128)(2,1)S(1)}, bf16[16,2048]{1,0:T(8,128)(2,1)S(1)}, u32[]{:S(2)}, u32[]{:S(2)}) collective-permute-start(bf16[16,2048]{1,0:T(8,128)(2,1)S(1)} %out_projection.1.refs_0_), channel_id=1, source_target_pairs={{0,2},{1,3},{2,0},{3,1},{4,6},{5,7},{6,4},{7,5},{8,10},{9,11},{10,... | collective-permute-start | bytes 196616 | tf_op jit(solution)/shard_map/ppermute | solution.py:24
  18.7 1.1 %collective-permute-start.6 = (bf16[16,2048]{1,0:T(8,128)(2,1)S(1)}, bf16[16,2048]{1,0:T(8,128)(2,1)S(1)}, u32[]{:S(2)}, u32[]{:S(2)}) collective-permute-start(bf16[16,2048]{1,0:T(8,128)(2,1)S(1)} %out_projection.1.refs_0_), channel_id=1, source_target_pairs={{0,1},{1,0},{2,3},{3,2},{4,5},{5,4},{6,7},{7,6},{8,9},{9,8},{10,11... | collective-permute-start | bytes 196616 | tf_op jit(solution)/shard_map/ppermute | solution.py:24
  19.8 1.9 %collective-permute-done.8.refs_3_ = bf16[16,2048]{1,0:T(8,128)(2,1)S(1)} collective-permute-done((bf16[16,2048]{1,0:T(8,128)(2,1)S(1)}, bf16[16,2048]{1,0:T(8,128)(2,1)S(1)}, u32[]{:S(2)}, u32[]{:S(2)}) %collective-permute-start.8) | collective-permute-done | bytes 65568 | tf_op jit(solution)/shard_map/ppermute | solution.py:24
  21.7 1.2 %collective-permute-done.7.refs_2_ = bf16[16,2048]{1,0:T(8,128)(2,1)S(1)} collective-permute-done((bf16[16,2048]{1,0:T(8,128)(2,1)S(1)}, bf16[16,2048]{1,0:T(8,128)(2,1)S(1)}, u32[]{:S(2)}, u32[]{:S(2)}) %collective-permute-start.7) | collective-permute-done | bytes 65568 | tf_op jit(solution)/shard_map/ppermute | solution.py:24
  22.9 0.0 collective-permute-done.6.refs_1_
  22.9 0.0 copy-done.1
  22.9 0.0 copy-done
  22.9 0.0 copy-done.4
  22.9 0.0 copy-done.3
  22.9 2.3 %gate_up.1 = (f32[16,2048]{1,0:T(8,128)S(1)}, bf16[16,1920]{1,0:T(8,128)(2,1)S(1)}, bf16[16,1920]{1,0:T(8,128)(2,1)S(1)}) custom-call(bf16[2,8,2048]{2,1,0:T(8,128)(2,1)S(1)} %copy-done.3, bf16[2048]{0:T(1024)(128)(2,1)S(1)} %copy-done.4, bf16[2048,3584]{1,0:T(8,128)(2,1)S(1)} %copy-done, bf16[2048,3584]{1,0:T(8,128)(2,1)S(1)} %copy-done.1, ...), custom_call_target="tpu_custom_call" | custom-call | tf_op jit(solution)/shard_map/gate_up/pallas_call | solution.py:364
  25.3 0.1 collective-permute-start.9
  25.4 4.2 %collective-permute-done.9.second = bf16[16,1920]{1,0:T(8,128)(2,1)S(1)} collective-permute-done((bf16[16,1920]{1,0:T(8,128)(2,1)S(1)}, bf16[16,1920]{1,0:T(8,128)(2,1)S(1)}, u32[]{:S(2)}, u32[]{:S(2)}) %collective-permute-start.9) | collective-permute-done | bytes 61472 | tf_op jit(solution)/shard_map/ppermute | solution.py:24
  29.6 0.1 gate_up_sum.1.first
  29.7 2.0 %collective-permute-start.10 = (bf16[16,1920]{1,0:T(8,128)(2,1)S(1)}, bf16[16,1920]{1,0:T(8,128)(2,1)S(1)}, u32[]{:S(2)}, u32[]{:S(2)}) collective-permute-start(bf16[16,1920]{1,0:T(8,128)(2,1)S(1)} %gate_up_sum.1.first), channel_id=1, source_target_pairs={{0,8},{4,12},{8,0},{12,4},{1,9},{5,13},{9,1},{13,5},{2,10},{6,14},... | collective-permute-start | bytes 184328 | tf_op jit(solution)/shard_map/ppermute | solution.py:24
  31.7 3.3 %collective-permute-done.10.second = bf16[16,1920]{1,0:T(8,128)(2,1)S(1)} collective-permute-done((bf16[16,1920]{1,0:T(8,128)(2,1)S(1)}, bf16[16,1920]{1,0:T(8,128)(2,1)S(1)}, u32[]{:S(2)}, u32[]{:S(2)}) %collective-permute-start.10) | collective-permute-done | bytes 61472 | tf_op jit(solution)/shard_map/ppermute | solution.py:24
  35.0 0.1 activation.1.own
  35.1 0.9 %collective-permute-start.13 = (bf16[8,1792]{1,0:T(8,128)(2,1)S(1)}, bf16[8,1792]{1,0:T(8,128)(2,1)S(1)}, u32[]{:S(2)}, u32[]{:S(2)}) collective-permute-start(bf16[8,1792]{1,0:T(8,128)(2,1)S(1)} %activation.1.own), channel_id=1, source_target_pairs={{0,20},{4,16},{8,28},{12,24},{16,4},{20,0},{24,12},{28,8},{1,21},{... | collective-permute-start | bytes 86024 | tf_op jit(solution)/shard_map/ppermute | solution.py:24
  36.0 0.7 %collective-permute-start.12 = (bf16[8,1792]{1,0:T(8,128)(2,1)S(1)}, bf16[8,1792]{1,0:T(8,128)(2,1)S(1)}, u32[]{:S(2)}, u32[]{:S(2)}) collective-permute-start(bf16[8,1792]{1,0:T(8,128)(2,1)S(1)} %activation.1.own), channel_id=1, source_target_pairs={{0,16},{16,0},{1,17},{17,1},{2,18},{18,2},{3,19},{19,3},{4,20},{20... | collective-permute-start | bytes 86024 | tf_op jit(solution)/shard_map/ppermute | solution.py:24
  36.7 1.9 %collective-permute-start.11 = (bf16[8,1792]{1,0:T(8,128)(2,1)S(1)}, bf16[8,1792]{1,0:T(8,128)(2,1)S(1)}, u32[]{:S(2)}, u32[]{:S(2)}) collective-permute-start(bf16[8,1792]{1,0:T(8,128)(2,1)S(1)} %activation.1.own), channel_id=1, source_target_pairs={{0,4},{4,0},{8,12},{12,8},{1,5},{5,1},{9,13},{13,9},{2,6},{6,2},{1... | collective-permute-start | bytes 86024 | tf_op jit(solution)/shard_map/ppermute | solution.py:24
  38.6 1.4 %collective-permute-done.13.received = bf16[8,1792]{1,0:T(8,128)(2,1)S(1)} collective-permute-done((bf16[8,1792]{1,0:T(8,128)(2,1)S(1)}, bf16[8,1792]{1,0:T(8,128)(2,1)S(1)}, u32[]{:S(2)}, u32[]{:S(2)}) %collective-permute-start.13) | collective-permute-done | bytes 28704 | tf_op jit(solution)/shard_map/ppermute | solution.py:24
  40.0 0.1 collective-permute-done.12.own
  40.3 1.2 %down.2.refs_0_ = f32[16,2048]{1,0:T(8,128)S(1)} custom-call(bf16[16,1792]{1,0:T(8,128)(2,1)S(1)} %gather_act.3.act, bf16[3584,2048]{1,0:T(8,128)(2,1)S(1)} %bitcast.1), custom_call_target="tpu_custom_call" | custom-call | tf_op jit(solution)/shard_map/down/pallas_call | solution.py:399
  41.4 0.0 collective-permute-done.11.received
  41.5 1.2 %down.3.refs_0_ = bf16[16,2048]{1,0:T(8,128)(2,1)S(1)} custom-call(bf16[16,1792]{1,0:T(8,128)(2,1)S(1)} %gather_act.2.act, bf16[3584,2048]{1,0:T(8,128)(2,1)S(1)} %bitcast.1, f32[16,2048]{1,0:T(8,128)S(1)} %down.2.refs_0_), custom_call_target="tpu_custom_call" | custom-call | tf_op jit(solution)/shard_map/down/pallas_call | solution.py:399
  42.7 0.0 collective-permute-start.16
  42.7 1.3 %collective-permute-start.15 = (bf16[16,2048]{1,0:T(8,128)(2,1)S(1)}, bf16[16,2048]{1,0:T(8,128)(2,1)S(1)}, u32[]{:S(2)}, u32[]{:S(2)}) collective-permute-start(bf16[16,2048]{1,0:T(8,128)(2,1)S(1)} %down.3.refs_0_), channel_id=1, source_target_pairs={{0,2},{1,3},{2,0},{3,1},{4,6},{5,7},{6,4},{7,5},{8,10},{9,11},{10,... | collective-permute-start | bytes 196616 | tf_op jit(solution)/shard_map/ppermute | solution.py:24
  44.0 0.6 %collective-permute-start.14 = (bf16[16,2048]{1,0:T(8,128)(2,1)S(1)}, bf16[16,2048]{1,0:T(8,128)(2,1)S(1)}, u32[]{:S(2)}, u32[]{:S(2)}) collective-permute-start(bf16[16,2048]{1,0:T(8,128)(2,1)S(1)} %down.3.refs_0_), channel_id=1, source_target_pairs={{0,1},{1,0},{2,3},{3,2},{4,5},{5,4},{6,7},{7,6},{8,9},{9,8},{10,11... | collective-permute-start | bytes 196616 | tf_op jit(solution)/shard_map/ppermute | solution.py:24
  44.6 2.5 %collective-permute-done.16.refs_3_ = bf16[16,2048]{1,0:T(8,128)(2,1)S(1)} collective-permute-done((bf16[16,2048]{1,0:T(8,128)(2,1)S(1)}, bf16[16,2048]{1,0:T(8,128)(2,1)S(1)}, u32[]{:S(2)}, u32[]{:S(2)}) %collective-permute-start.16) | collective-permute-done | bytes 65568 | tf_op jit(solution)/shard_map/ppermute | solution.py:24
  47.1 1.0 %collective-permute-done.15.refs_2_ = bf16[16,2048]{1,0:T(8,128)(2,1)S(1)} collective-permute-done((bf16[16,2048]{1,0:T(8,128)(2,1)S(1)}, bf16[16,2048]{1,0:T(8,128)(2,1)S(1)}, u32[]{:S(2)}, u32[]{:S(2)}) %collective-permute-start.15) | collective-permute-done | bytes 65568 | tf_op jit(solution)/shard_map/ppermute | solution.py:24
  48.1 0.0 collective-permute-done.14.refs_1_
  48.1 0.7 %final.1 = bf16[2,8,2048]{2,1,0:T(8,128)(2,1)} custom-call(f32[16,2048]{1,0:T(8,128)S(1)} %get-tuple-element.16.mid, bf16[16,2048]{1,0:T(8,128)(2,1)S(1)} %down.3.refs_0_, bf16[16,2048]{1,0:T(8,128)(2,1)S(1)} %collective-permute-done.14.refs_1_, bf16[16,2048]{1,0:T(8,128)(2,1)S(1)} %collective-permute-done.15.refs_2_, ...), custom_call_target="tpu_custom_call" | custom-call | tf_op jit(solution)/shard_map/final/pallas_call | solution.py:411
  (16 shorter events, 0.1 us)
Async XLA Ops:
  0.0 17.0 %copy-start.2 = (bf16[1024,2048]{1,0:T(8,128)(2,1)S(1)}, bf16[1024,2048]{1,0:T(8,128)(2,1)}, u32[]{:S(2)}) copy-start(bf16[1024,2048]{1,0:T(8,128)(2,1)} %refs_4_.1) | copy-start | bytes 12582916
  0.0 22.9 %copy-start.1 = (bf16[2048,3584]{1,0:T(8,128)(2,1)S(1)}, bf16[2048,3584]{1,0:T(8,128)(2,1)}, u32[]{:S(2)}) copy-start(bf16[2048,3584]{1,0:T(8,128)(2,1)} %up_weight.1) | copy-start | bytes 44040196
  0.0 22.9 %copy-start = (bf16[2048,3584]{1,0:T(8,128)(2,1)S(1)}, bf16[2048,3584]{1,0:T(8,128)(2,1)}, u32[]{:S(2)}) copy-start(bf16[2048,3584]{1,0:T(8,128)(2,1)} %gate_weight.1) | copy-start | bytes 44040196
  0.0 22.9 %copy-start.4 = (bf16[2048]{0:T(1024)(128)(2,1)S(1)}, bf16[2048]{0:T(1024)(128)(2,1)}, u32[]{:S(2)}) copy-start(bf16[2048]{0:T(1024)(128)(2,1)} %gains.1) | copy-start | bytes 12292
  0.0 22.9 %copy-start.3 = (bf16[2,8,2048]{2,1,0:T(8,128)(2,1)S(1)}, bf16[2,8,2048]{2,1,0:T(8,128)(2,1)}, u32[]{:S(2)}) copy-start(bf16[2,8,2048]{2,1,0:T(8,128)(2,1)} %residual.1) | copy-start | bytes 196612
  2.3 3.2 %collective-permute-start = (f32[5,8,128]{2,1,0:T(8,128)S(1)}, f32[5,8,128]{2,1,0:T(8,128)S(1)}, u32[]{:S(2)}, u32[]{:S(2)}) collective-permute-start(f32[5,8,128]{2,1,0:T(8,128)S(1)} %get-tuple-element.13), channel_id=1, source_target_pairs={{0,1},{1,0},{2,3},{3,2},{4,5},{5,4},{6,7},{7,6},{8,9},{9,8},{10,11... | collective-permute-start | bytes 61448 | tf_op jit(solution)/shard_map/ppermute | solution.py:24
  2.8 4.4 %collective-permute-start.1 = (f32[5,8,128]{2,1,0:T(8,128)S(1)}, f32[5,8,128]{2,1,0:T(8,128)S(1)}, u32[]{:S(2)}, u32[]{:S(2)}) collective-permute-start(f32[5,8,128]{2,1,0:T(8,128)S(1)} %get-tuple-element.14), channel_id=1, source_target_pairs={{0,2},{1,3},{2,0},{3,1},{4,6},{5,7},{6,4},{7,5},{8,10},{9,11},{10,... | collective-permute-start | bytes 61448 | tf_op jit(solution)/shard_map/ppermute | solution.py:24
  5.4 3.2 %collective-permute-start.2 = (f32[5,8,128]{2,1,0:T(8,128)S(1)}, f32[5,8,128]{2,1,0:T(8,128)S(1)}, u32[]{:S(2)}, u32[]{:S(2)}) collective-permute-start(f32[5,8,128]{2,1,0:T(8,128)S(1)} %get-tuple-element.15), channel_id=1, source_target_pairs={{0,3},{1,2},{2,1},{3,0},{4,7},{5,6},{6,5},{7,4},{8,11},{9,10},{10,... | collective-permute-start | bytes 61448 | tf_op jit(solution)/shard_map/ppermute | solution.py:24
  8.8 5.5 %collective-permute-start.5 = (bf16[4,1024]{1,0:T(4,128)(2,1)S(1)}, bf16[4,1024]{1,0:T(4,128)(2,1)S(1)}, u32[]{:S(2)}, u32[]{:S(2)}) collective-permute-start(bf16[4,1024]{1,0:T(4,128)(2,1)S(1)} %combine.1.refs_0_), channel_id=1, source_target_pairs={{0,12},{4,8},{8,4},{12,0},{1,13},{5,9},{9,5},{13,1},{2,14},{6,10},... | collective-permute-start | bytes 24584 | tf_op jit(solution)/shard_map/ppermute | solution.py:24
  12.5 4.5 %collective-permute-start.4 = (bf16[4,1024]{1,0:T(4,128)(2,1)S(1)}, bf16[4,1024]{1,0:T(4,128)(2,1)S(1)}, u32[]{:S(2)}, u32[]{:S(2)}) collective-permute-start(bf16[4,1024]{1,0:T(4,128)(2,1)S(1)} %combine.1.refs_0_), channel_id=1, source_target_pairs={{0,8},{4,12},{8,0},{12,4},{1,9},{5,13},{9,1},{13,5},{2,10},{6,14},... | collective-permute-start | bytes 24584 | tf_op jit(solution)/shard_map/ppermute | solution.py:24
  12.5 4.5 %collective-permute-start.3 = (bf16[4,1024]{1,0:T(4,128)(2,1)S(1)}, bf16[4,1024]{1,0:T(4,128)(2,1)S(1)}, u32[]{:S(2)}, u32[]{:S(2)}) collective-permute-start(bf16[4,1024]{1,0:T(4,128)(2,1)S(1)} %combine.1.refs_0_), channel_id=1, source_target_pairs={{0,4},{4,0},{8,12},{12,8},{1,5},{5,1},{9,13},{13,9},{2,6},{6,2},{1... | collective-permute-start | bytes 24584 | tf_op jit(solution)/shard_map/ppermute | solution.py:24
  17.0 23.2 %slice-start = ((s8[14680064]{0:T(1024)(128)(4,1)}), s8[4194304]{0:T(1024)(128)(4,1)S(1)}, s32[]{:S(2)}) async-start(s8[14680064]{0:T(1024)(128)(4,1)} %bitcast), calls=%async_computation | async-start | bytes 8388608
  17.8 22.4 %slice-start.1 = ((s8[14680064]{0:T(1024)(128)(4,1)}), s8[4194304]{0:T(1024)(128)(4,1)S(1)}, s32[]{:S(2)}) async-start(s8[14680064]{0:T(1024)(128)(4,1)} %bitcast), calls=%async_computation.1 | async-start | bytes 8388608
  17.8 22.4 %slice-start.2 = ((s8[14680064]{0:T(1024)(128)(4,1)}), s8[4194304]{0:T(1024)(128)(4,1)S(1)}, s32[]{:S(2)}) async-start(s8[14680064]{0:T(1024)(128)(4,1)} %bitcast), calls=%async_computation.2 | async-start | bytes 8388608
  17.8 22.4 %slice-start.3 = ((s8[14680064]{0:T(1024)(128)(4,1)}), s8[2097152]{0:T(1024)(128)(4,1)S(1)}, s32[]{:S(2)}) async-start(s8[14680064]{0:T(1024)(128)(4,1)} %bitcast), calls=%async_computation.3 | async-start | bytes 4194304
  17.8 3.8 %collective-permute-start.8 = (bf16[16,2048]{1,0:T(8,128)(2,1)S(1)}, bf16[16,2048]{1,0:T(8,128)(2,1)S(1)}, u32[]{:S(2)}, u32[]{:S(2)}) collective-permute-start(bf16[16,2048]{1,0:T(8,128)(2,1)S(1)} %out_projection.1.refs_0_), channel_id=1, source_target_pairs={{0,3},{1,2},{2,1},{3,0},{4,7},{5,6},{6,5},{7,4},{8,11},{9,10},{10,... | collective-permute-start | bytes 196616 | tf_op jit(solution)/shard_map/ppermute | solution.py:24
  17.9 5.0 %collective-permute-start.7 = (bf16[16,2048]{1,0:T(8,128)(2,1)S(1)}, bf16[16,2048]{1,0:T(8,128)(2,1)S(1)}, u32[]{:S(2)}, u32[]{:S(2)}) collective-permute-start(bf16[16,2048]{1,0:T(8,128)(2,1)S(1)} %out_projection.1.refs_0_), channel_id=1, source_target_pairs={{0,2},{1,3},{2,0},{3,1},{4,6},{5,7},{6,4},{7,5},{8,10},{9,11},{10,... | collective-permute-start | bytes 196616 | tf_op jit(solution)/shard_map/ppermute | solution.py:24
  18.7 4.2 %collective-permute-start.6 = (bf16[16,2048]{1,0:T(8,128)(2,1)S(1)}, bf16[16,2048]{1,0:T(8,128)(2,1)S(1)}, u32[]{:S(2)}, u32[]{:S(2)}) collective-permute-start(bf16[16,2048]{1,0:T(8,128)(2,1)S(1)} %out_projection.1.refs_0_), channel_id=1, source_target_pairs={{0,1},{1,0},{2,3},{3,2},{4,5},{5,4},{6,7},{7,6},{8,9},{9,8},{10,11... | collective-permute-start | bytes 196616 | tf_op jit(solution)/shard_map/ppermute | solution.py:24
  25.3 4.3 %collective-permute-start.9 = (bf16[16,1920]{1,0:T(8,128)(2,1)S(1)}, bf16[16,1920]{1,0:T(8,128)(2,1)S(1)}, u32[]{:S(2)}, u32[]{:S(2)}) collective-permute-start(bf16[16,1920]{1,0:T(8,128)(2,1)S(1)} %get-tuple-element.18), channel_id=1, source_target_pairs={{0,4},{4,0},{8,12},{12,8},{1,5},{5,1},{9,13},{13,9},{2,6},{6,2},{1... | collective-permute-start | bytes 184328 | tf_op jit(solution)/shard_map/ppermute | solution.py:24
  29.7 5.3 %collective-permute-start.10 = (bf16[16,1920]{1,0:T(8,128)(2,1)S(1)}, bf16[16,1920]{1,0:T(8,128)(2,1)S(1)}, u32[]{:S(2)}, u32[]{:S(2)}) collective-permute-start(bf16[16,1920]{1,0:T(8,128)(2,1)S(1)} %gate_up_sum.1.first), channel_id=1, source_target_pairs={{0,8},{4,12},{8,0},{12,4},{1,9},{5,13},{9,1},{13,5},{2,10},{6,14},... | collective-permute-start | bytes 184328 | tf_op jit(solution)/shard_map/ppermute | solution.py:24
  35.1 4.9 %collective-permute-start.13 = (bf16[8,1792]{1,0:T(8,128)(2,1)S(1)}, bf16[8,1792]{1,0:T(8,128)(2,1)S(1)}, u32[]{:S(2)}, u32[]{:S(2)}) collective-permute-start(bf16[8,1792]{1,0:T(8,128)(2,1)S(1)} %activation.1.own), channel_id=1, source_target_pairs={{0,20},{4,16},{8,28},{12,24},{16,4},{20,0},{24,12},{28,8},{1,21},{... | collective-permute-start | bytes 86024 | tf_op jit(solution)/shard_map/ppermute | solution.py:24
  36.0 4.2 %collective-permute-start.12 = (bf16[8,1792]{1,0:T(8,128)(2,1)S(1)}, bf16[8,1792]{1,0:T(8,128)(2,1)S(1)}, u32[]{:S(2)}, u32[]{:S(2)}) collective-permute-start(bf16[8,1792]{1,0:T(8,128)(2,1)S(1)} %activation.1.own), channel_id=1, source_target_pairs={{0,16},{16,0},{1,17},{17,1},{2,18},{18,2},{3,19},{19,3},{4,20},{20... | collective-permute-start | bytes 86024 | tf_op jit(solution)/shard_map/ppermute | solution.py:24
  36.7 4.7 %collective-permute-start.11 = (bf16[8,1792]{1,0:T(8,128)(2,1)S(1)}, bf16[8,1792]{1,0:T(8,128)(2,1)S(1)}, u32[]{:S(2)}, u32[]{:S(2)}) collective-permute-start(bf16[8,1792]{1,0:T(8,128)(2,1)S(1)} %activation.1.own), channel_id=1, source_target_pairs={{0,4},{4,0},{8,12},{12,8},{1,5},{5,1},{9,13},{13,9},{2,6},{6,2},{1... | collective-permute-start | bytes 86024 | tf_op jit(solution)/shard_map/ppermute | solution.py:24
  42.7 4.4 %collective-permute-start.16 = (bf16[16,2048]{1,0:T(8,128)(2,1)S(1)}, bf16[16,2048]{1,0:T(8,128)(2,1)S(1)}, u32[]{:S(2)}, u32[]{:S(2)}) collective-permute-start(bf16[16,2048]{1,0:T(8,128)(2,1)S(1)} %down.3.refs_0_), channel_id=1, source_target_pairs={{0,3},{1,2},{2,1},{3,0},{4,7},{5,6},{6,5},{7,4},{8,11},{9,10},{10,... | collective-permute-start | bytes 196616 | tf_op jit(solution)/shard_map/ppermute | solution.py:24
  42.7 5.4 %collective-permute-start.15 = (bf16[16,2048]{1,0:T(8,128)(2,1)S(1)}, bf16[16,2048]{1,0:T(8,128)(2,1)S(1)}, u32[]{:S(2)}, u32[]{:S(2)}) collective-permute-start(bf16[16,2048]{1,0:T(8,128)(2,1)S(1)} %down.3.refs_0_), channel_id=1, source_target_pairs={{0,2},{1,3},{2,0},{3,1},{4,6},{5,7},{6,4},{7,5},{8,10},{9,11},{10,... | collective-permute-start | bytes 196616 | tf_op jit(solution)/shard_map/ppermute | solution.py:24
  44.0 4.1 %collective-permute-start.14 = (bf16[16,2048]{1,0:T(8,128)(2,1)S(1)}, bf16[16,2048]{1,0:T(8,128)(2,1)S(1)}, u32[]{:S(2)}, u32[]{:S(2)}) collective-permute-start(bf16[16,2048]{1,0:T(8,128)(2,1)S(1)} %down.3.refs_0_), channel_id=1, source_target_pairs={{0,1},{1,0},{2,3},{3,2},{4,5},{5,4},{6,7},{7,6},{8,9},{9,8},{10,11... | collective-permute-start | bytes 196616 | tf_op jit(solution)/shard_map/ppermute | solution.py:24

commit v4 on v3

--- a/solution.py
+++ b/solution.py
@@ -251,18 +251,12 @@
     send[...] = packed[1 - bit].astype(send.dtype)
 
 
-def sum_kernel(first, second, out):
-    hidden = out.shape[1] - HD
-    total = first[...].astype(jnp.float32) + second[...].astype(jnp.float32)
-    out[:, :hidden] = total[:, :hidden].astype(out.dtype)
-    squares = jnp.sum(total[:, hidden:], axis=1, keepdims=True)
-    out[:, hidden:] = in_pieces(squares).astype(out.dtype)
-
-
-def act_kernel(model, first, second, out):
-    hidden = first.shape[1] - HD
-    cells = first.shape[0] // 2
-    total = first[...].astype(jnp.float32) + second[...].astype(jnp.float32)
+def act_kernel(model, *refs):
+    parts, out = refs[:-1], refs[-1]
+    hidden = parts[0].shape[1] - HD
+    cells = parts[0].shape[0] // 2
+    values = [p[...].astype(jnp.float32) for p in parts]
+    total = tree_sum(values[0::2]) + tree_sum(values[1::2])
     squares = jnp.sum(total[:cells, hidden:], axis=1, keepdims=True)
     inv = lax.rsqrt(squares / model + 1e-05)
     gate = total[:cells, :hidden] * inv
@@ -371,21 +365,13 @@
         in_vmem(residual), in_vmem(norm_gain), in_vmem(gate_weight), in_vmem(up_weight),
         *spread(partial, "col"),
     )
-    received = partner(send, "row", 1)
-    for level in range(1, groups.bit_length() - 1):
-        keep = call(
-            sum_kernel,
-            shape(keep.shape, WIRE),
-            [VMEM_SPEC] * 2,
-            name="gate_up_sum",
-        )(keep, received)
-        received = partner(keep, "row", 1 << level)
+    sums = [keep] + [partner((keep, send)[k % 2], "row", k) for k in range(1, groups)]
     act = call(
         functools.partial(act_kernel, model),
         shape((m // 2, hidden), bf16),
-        [VMEM_SPEC] * 2,
+        [VMEM_SPEC] * groups,
         name="activation",
-    )(keep, received)
+    )(*sums)
     down_weight = in_vmem(down_weight)
 
     def down_part(same, from_row, other, before, result):
@@ -403,11 +389,13 @@
             name="down",
         )(rows, down_weight, *before)
 
-    before = []
+    near = partner(act, "row", 1)
     if split > 1:
+        first = down_part(act, near, 0, [], f32)
         far = partner(act, ("side", "row"), groups + 1)
-        before = [down_part(partner(act, "side", 1), far, 1, before, f32)]
-    down = down_part(act, partner(act, "row", 1), 0, before, WIRE)
+        down = down_part(partner(act, "side", 1), far, 1, [first], WIRE)
+    else:
+        down = down_part(act, near, 0, [], WIRE)
     return call(
         functools.partial(final_kernel, groups),
         shape((TOKENS, total_rows, width_share), bf16),

time: 48.9 us -> 48 us (0.982)
  waiting for transfers between devices: 22.6 us -> 20.3 us
  starting transfers between devices: 17.1 us -> 18.6 us
    ppermute x17 -> x18, waiting for transfers between devices: 22.6 us -> 20.3 us  [partner(): lax.ppermute(value, axis, [(i, i ^ k) for i in range(lax.axis_size(axis))])]
    ppermute x17 -> x18, starting transfers between devices: 17.1 us -> 18.6 us  [partner(): lax.ppermute(value, axis, [(i, i ^ k) for i in range(lax.axis_size(axis))])]
  transfers between devices with their start and end apart: 17 -> 18, of which waited for: 12 -> 13; matrix products, arithmetic and copies ran while one was open for 0% -> 0% of each run, Pallas kernels for 2% -> 3%
where the time goes in v4:
time: 48 us; the launch traced here: 47.9 us
  waiting for transfers between devices  20.3 us (42%)
  starting transfers between devices  18.6 us (39%)
  Pallas kernels  8.82 us (18%)
    ppermute x18, waiting for transfers between devices, partner(): lax.ppermute(value, axis, [(i, i ^ k) for i in range(lax.axis_size(axis))])  20.3 us
    ppermute x18, starting transfers between devices, partner(): lax.ppermute(value, axis, [(i, i ^ k) for i in range(lax.axis_size(axis))])  18.6 us
    pallas_call x2, Pallas kernels, down_part(): call(functools.partial(down_kernel, other), shape((m, width_share), resul...  2.37 us
    pallas_call x1, Pallas kernels, shards(): call(functools.partial(lift_kernel, groups, split), [shape((m, width_shar...  2.34 us
    pallas_call x1, Pallas kernels, shards(): call(functools.partial(attention_kernel, cols), [message] * cols, [ANY_SP...  2.25 us
  transfers between devices with their start and end apart: 18, of which 13 were waited for; matrix products, arithmetic and copies ran while one was open for 0% of the time, Pallas kernels for 3%

profile of v4, /device:TPU:0, one launch (start us, length us, event | category | flops | bytes accessed | tf_op | source)
XLA Modules:
  0.0 47.9 jit_solution(18232839612518200369)
XLA Ops:
  0.0 2.3 %attention.1 = (f32[5,8,128]{2,1,0:T(8,128)S(1)}, f32[5,8,128]{2,1,0:T(8,128)S(1)}, f32[5,8,128]{2,1,0:T(8,128)S(1)}, f32[5,8,128]{2,1,0:T(8,128)S(1)}) custom-call(s32[2]{0:T(128)} %lengths.1, bf16[2,2,4096]{2,1,0:T(2,128)(2,1)} %rest_0_.1, bf16[2,2,512]{2,1,0:T(2,128)(2,1)} %rest_1_.1, bf16[2,2,512]{2,1,0:T(2,128)(2,1)} %rest_2_.1, ...), custom_call_target="tpu_custom_call" | custom-call | flops 40000000000 | bytes 1024 | tf_op jit(solution)/shard_map/attention/pallas_call | solution.py:333
  2.3 0.5 %collective-permute-start = (f32[5,8,128]{2,1,0:T(8,128)S(1)}, f32[5,8,128]{2,1,0:T(8,128)S(1)}, u32[]{:S(2)}, u32[]{:S(2)}) collective-permute-start(f32[5,8,128]{2,1,0:T(8,128)S(1)} %get-tuple-element.13), channel_id=1, source_target_pairs={{0,1},{1,0},{2,3},{3,2},{4,5},{5,4},{6,7},{7,6},{8,9},{9,8},{10,11... | collective-permute-start | bytes 61448 | tf_op jit(solution)/shard_map/ppermute | solution.py:24
  2.8 2.6 %collective-permute-start.1 = (f32[5,8,128]{2,1,0:T(8,128)S(1)}, f32[5,8,128]{2,1,0:T(8,128)S(1)}, u32[]{:S(2)}, u32[]{:S(2)}) collective-permute-start(f32[5,8,128]{2,1,0:T(8,128)S(1)} %get-tuple-element.14), channel_id=1, source_target_pairs={{0,2},{1,3},{2,0},{3,1},{4,6},{5,7},{6,4},{7,5},{8,10},{9,11},{10,... | collective-permute-start | bytes 61448 | tf_op jit(solution)/shard_map/ppermute | solution.py:24
  5.4 0.1 collective-permute-start.2
  5.5 0.0 collective-permute-done.refs_1_
  5.5 1.7 %collective-permute-done.1.refs_2_ = f32[5,8,128]{2,1,0:T(8,128)S(1)} collective-permute-done((f32[5,8,128]{2,1,0:T(8,128)S(1)}, f32[5,8,128]{2,1,0:T(8,128)S(1)}, u32[]{:S(2)}, u32[]{:S(2)}) %collective-permute-start.1) | collective-permute-done | bytes 20512 | tf_op jit(solution)/shard_map/ppermute | solution.py:24
  7.2 1.4 %collective-permute-done.2.refs_3_ = f32[5,8,128]{2,1,0:T(8,128)S(1)} collective-permute-done((f32[5,8,128]{2,1,0:T(8,128)S(1)}, f32[5,8,128]{2,1,0:T(8,128)S(1)}, u32[]{:S(2)}, u32[]{:S(2)}) %collective-permute-start.2) | collective-permute-done | bytes 20512 | tf_op jit(solution)/shard_map/ppermute | solution.py:24
  8.6 0.2 combine.1.refs_0_
  8.8 3.7 %collective-permute-start.5 = (bf16[4,1024]{1,0:T(4,128)(2,1)S(1)}, bf16[4,1024]{1,0:T(4,128)(2,1)S(1)}, u32[]{:S(2)}, u32[]{:S(2)}) collective-permute-start(bf16[4,1024]{1,0:T(4,128)(2,1)S(1)} %combine.1.refs_0_), channel_id=1, source_target_pairs={{0,12},{4,8},{8,4},{12,0},{1,13},{5,9},{9,5},{13,1},{2,14},{6,10},... | collective-permute-start | bytes 24584 | tf_op jit(solution)/shard_map/ppermute | solution.py:24
  12.5 0.0 collective-permute-start.4
  12.5 0.8 %collective-permute-start.3 = (bf16[4,1024]{1,0:T(4,128)(2,1)S(1)}, bf16[4,1024]{1,0:T(4,128)(2,1)S(1)}, u32[]{:S(2)}, u32[]{:S(2)}) collective-permute-start(bf16[4,1024]{1,0:T(4,128)(2,1)S(1)} %combine.1.refs_0_), channel_id=1, source_target_pairs={{0,4},{4,0},{8,12},{12,8},{1,5},{5,1},{9,13},{13,9},{2,6},{6,2},{1... | collective-permute-start | bytes 24584 | tf_op jit(solution)/shard_map/ppermute | solution.py:24
  13.2 1.1 %collective-permute-done.5.refs_3_ = bf16[4,1024]{1,0:T(4,128)(2,1)S(1)} collective-permute-done((bf16[4,1024]{1,0:T(4,128)(2,1)S(1)}, bf16[4,1024]{1,0:T(4,128)(2,1)S(1)}, u32[]{:S(2)}, u32[]{:S(2)}) %collective-permute-start.5) | collective-permute-done | bytes 8224 | tf_op jit(solution)/shard_map/ppermute | solution.py:24
  14.3 2.7 %collective-permute-done.4.refs_2_ = bf16[4,1024]{1,0:T(4,128)(2,1)S(1)} collective-permute-done((bf16[4,1024]{1,0:T(4,128)(2,1)S(1)}, bf16[4,1024]{1,0:T(4,128)(2,1)S(1)}, u32[]{:S(2)}, u32[]{:S(2)}) %collective-permute-start.4) | collective-permute-done | bytes 8224 | tf_op jit(solution)/shard_map/ppermute | solution.py:24
  17.0 0.0 collective-permute-done.3.refs_1_
  17.0 0.0 copy-done.2
  17.0 0.8 %out_projection.1.refs_0_ = bf16[16,2048]{1,0:T(8,128)(2,1)S(1)} custom-call(bf16[4,1024]{1,0:T(4,128)(2,1)S(1)} %combine.1.refs_0_, bf16[4,1024]{1,0:T(4,128)(2,1)S(1)} %collective-permute-done.3.refs_1_, bf16[4,1024]{1,0:T(4,128)(2,1)S(1)} %collective-permute-done.4.refs_2_, bf16[4,1024]{1,0:T(4,128)(2,1)S(1)} %collective-permute-done.5.refs_3_, ...), custom_call_target="tpu_custom_call" | custom-call | tf_op jit(solution)/shard_map/out_projection/pallas_call | solution.py:351
  17.8 0.1 collective-permute-start.8
  17.9 0.8 %collective-permute-start.7 = (bf16[16,2048]{1,0:T(8,128)(2,1)S(1)}, bf16[16,2048]{1,0:T(8,128)(2,1)S(1)}, u32[]{:S(2)}, u32[]{:S(2)}) collective-permute-start(bf16[16,2048]{1,0:T(8,128)(2,1)S(1)} %out_projection.1.refs_0_), channel_id=1, source_target_pairs={{0,2},{1,3},{2,0},{3,1},{4,6},{5,7},{6,4},{7,5},{8,10},{9,11},{10,... | collective-permute-start | bytes 196616 | tf_op jit(solution)/shard_map/ppermute | solution.py:24
  18.7 1.1 %collective-permute-start.6 = (bf16[16,2048]{1,0:T(8,128)(2,1)S(1)}, bf16[16,2048]{1,0:T(8,128)(2,1)S(1)}, u32[]{:S(2)}, u32[]{:S(2)}) collective-permute-start(bf16[16,2048]{1,0:T(8,128)(2,1)S(1)} %out_projection.1.refs_0_), channel_id=1, source_target_pairs={{0,1},{1,0},{2,3},{3,2},{4,5},{5,4},{6,7},{7,6},{8,9},{9,8},{10,11... | collective-permute-start | bytes 196616 | tf_op jit(solution)/shard_map/ppermute | solution.py:24
  19.8 1.9 %collective-permute-done.8.refs_3_ = bf16[16,2048]{1,0:T(8,128)(2,1)S(1)} collective-permute-done((bf16[16,2048]{1,0:T(8,128)(2,1)S(1)}, bf16[16,2048]{1,0:T(8,128)(2,1)S(1)}, u32[]{:S(2)}, u32[]{:S(2)}) %collective-permute-start.8) | collective-permute-done | bytes 65568 | tf_op jit(solution)/shard_map/ppermute | solution.py:24
  21.7 1.2 %collective-permute-done.7.refs_2_ = bf16[16,2048]{1,0:T(8,128)(2,1)S(1)} collective-permute-done((bf16[16,2048]{1,0:T(8,128)(2,1)S(1)}, bf16[16,2048]{1,0:T(8,128)(2,1)S(1)}, u32[]{:S(2)}, u32[]{:S(2)}) %collective-permute-start.7) | collective-permute-done | bytes 65568 | tf_op jit(solution)/shard_map/ppermute | solution.py:24
  22.9 0.0 collective-permute-done.6.refs_1_
  22.9 0.0 copy-done.1
  22.9 0.0 copy-done
  22.9 0.0 copy-done.4
  22.9 2.3 %gate_up.1 = (f32[16,2048]{1,0:T(8,128)S(1)}, bf16[16,1920]{1,0:T(8,128)(2,1)S(1)}, bf16[16,1920]{1,0:T(8,128)(2,1)S(1)}) custom-call(bf16[2,8,2048]{2,1,0:T(8,128)(2,1)S(1)} %copy-done.3, bf16[2048]{0:T(1024)(128)(2,1)S(1)} %copy-done.4, bf16[2048,3584]{1,0:T(8,128)(2,1)S(1)} %copy-done, bf16[2048,3584]{1,0:T(8,128)(2,1)S(1)} %copy-done.1, ...), custom_call_target="tpu_custom_call" | custom-call | tf_op jit(solution)/shard_map/gate_up/pallas_call | solution.py:358
  25.3 2.1 %collective-permute-start.10 = (bf16[16,1920]{1,0:T(8,128)(2,1)S(1)}, bf16[16,1920]{1,0:T(8,128)(2,1)S(1)}, u32[]{:S(2)}, u32[]{:S(2)}) collective-permute-start(bf16[16,1920]{1,0:T(8,128)(2,1)S(1)} %get-tuple-element.17.refs_0_), channel_id=1, source_target_pairs={{0,8},{4,12},{8,0},{12,4},{1,9},{5,13},{9,1},{13,5},{2,10},{6,14},... | collective-permute-start | bytes 184328 | tf_op jit(solution)/shard_map/ppermute | solution.py:24
  27.4 0.2 collective-permute-start.11
  27.6 1.3 %collective-permute-start.9 = (bf16[16,1920]{1,0:T(8,128)(2,1)S(1)}, bf16[16,1920]{1,0:T(8,128)(2,1)S(1)}, u32[]{:S(2)}, u32[]{:S(2)}) collective-permute-start(bf16[16,1920]{1,0:T(8,128)(2,1)S(1)} %get-tuple-element.18), channel_id=1, source_target_pairs={{0,4},{4,0},{8,12},{12,8},{1,5},{5,1},{9,13},{13,9},{2,6},{6,2},{1... | collective-permute-start | bytes 184328 | tf_op jit(solution)/shard_map/ppermute | solution.py:24
  28.8 2.4 %collective-permute-done.10.refs_2_ = bf16[16,1920]{1,0:T(8,128)(2,1)S(1)} collective-permute-done((bf16[16,1920]{1,0:T(8,128)(2,1)S(1)}, bf16[16,1920]{1,0:T(8,128)(2,1)S(1)}, u32[]{:S(2)}, u32[]{:S(2)}) %collective-permute-start.10) | collective-permute-done | bytes 61472 | tf_op jit(solution)/shard_map/ppermute | solution.py:24
  31.2 2.4 %collective-permute-done.11.refs_3_ = bf16[16,1920]{1,0:T(8,128)(2,1)S(1)} collective-permute-done((bf16[16,1920]{1,0:T(8,128)(2,1)S(1)}, bf16[16,1920]{1,0:T(8,128)(2,1)S(1)}, u32[]{:S(2)}, u32[]{:S(2)}) %collective-permute-start.11) | collective-permute-done | bytes 61472 | tf_op jit(solution)/shard_map/ppermute | solution.py:24
  33.6 0.0 collective-permute-done.9.refs_1_
  33.6 0.1 activation.1.own
  33.7 0.6 %collective-permute-start.14 = (bf16[8,1792]{1,0:T(8,128)(2,1)S(1)}, bf16[8,1792]{1,0:T(8,128)(2,1)S(1)}, u32[]{:S(2)}, u32[]{:S(2)}) collective-permute-start(bf16[8,1792]{1,0:T(8,128)(2,1)S(1)} %activation.1.own), channel_id=1, source_target_pairs={{0,4},{4,0},{8,12},{12,8},{1,5},{5,1},{9,13},{13,9},{2,6},{6,2},{1... | collective-permute-start | bytes 86024 | tf_op jit(solution)/shard_map/ppermute | solution.py:24
  34.3 2.5 %collective-permute-start.13 = (bf16[8,1792]{1,0:T(8,128)(2,1)S(1)}, bf16[8,1792]{1,0:T(8,128)(2,1)S(1)}, u32[]{:S(2)}, u32[]{:S(2)}) collective-permute-start(bf16[8,1792]{1,0:T(8,128)(2,1)S(1)} %activation.1.own), channel_id=1, source_target_pairs={{0,20},{4,16},{8,28},{12,24},{16,4},{20,0},{24,12},{28,8},{1,21},{... | collective-permute-start | bytes 86024 | tf_op jit(solution)/shard_map/ppermute | solution.py:24
  36.7 0.5 %collective-permute-start.12 = (bf16[8,1792]{1,0:T(8,128)(2,1)S(1)}, bf16[8,1792]{1,0:T(8,128)(2,1)S(1)}, u32[]{:S(2)}, u32[]{:S(2)}) collective-permute-start(bf16[8,1792]{1,0:T(8,128)(2,1)S(1)} %activation.1.own), channel_id=1, source_target_pairs={{0,16},{16,0},{1,17},{17,1},{2,18},{18,2},{3,19},{19,3},{4,20},{20... | collective-permute-start | bytes 86024 | tf_op jit(solution)/shard_map/ppermute | solution.py:24
  37.3 0.4 collective-permute-done.14.received
  37.7 1.2 %down.2.refs_0_ = f32[16,2048]{1,0:T(8,128)S(1)} custom-call(bf16[16,1792]{1,0:T(8,128)(2,1)S(1)} %gather_act.3.act, bf16[3584,2048]{1,0:T(8,128)(2,1)S(1)} %bitcast.1), custom_call_target="tpu_custom_call" | custom-call | tf_op jit(solution)/shard_map/down/pallas_call | solution.py:385
  38.9 0.1 collective-permute-done.13.received
  39.1 1.6 %collective-permute-done.12.own = bf16[8,1792]{1,0:T(8,128)(2,1)S(1)} collective-permute-done((bf16[8,1792]{1,0:T(8,128)(2,1)S(1)}, bf16[8,1792]{1,0:T(8,128)(2,1)S(1)}, u32[]{:S(2)}, u32[]{:S(2)}) %collective-permute-start.12) | collective-permute-done | bytes 28704 | tf_op jit(solution)/shard_map/ppermute | solution.py:24
  40.6 1.2 %down.3.refs_0_ = bf16[16,2048]{1,0:T(8,128)(2,1)S(1)} custom-call(bf16[16,1792]{1,0:T(8,128)(2,1)S(1)} %gather_act.2.act, bf16[3584,2048]{1,0:T(8,128)(2,1)S(1)} %bitcast.1, f32[16,2048]{1,0:T(8,128)S(1)} %down.2.refs_0_), custom_call_target="tpu_custom_call" | custom-call | tf_op jit(solution)/shard_map/down/pallas_call | solution.py:385
  41.8 0.0 collective-permute-start.17
  41.8 1.3 %collective-permute-start.16 = (bf16[16,2048]{1,0:T(8,128)(2,1)S(1)}, bf16[16,2048]{1,0:T(8,128)(2,1)S(1)}, u32[]{:S(2)}, u32[]{:S(2)}) collective-permute-start(bf16[16,2048]{1,0:T(8,128)(2,1)S(1)} %down.3.refs_0_), channel_id=1, source_target_pairs={{0,2},{1,3},{2,0},{3,1},{4,6},{5,7},{6,4},{7,5},{8,10},{9,11},{10,... | collective-permute-start | bytes 196616 | tf_op jit(solution)/shard_map/ppermute | solution.py:24
  43.1 0.6 %collective-permute-start.15 = (bf16[16,2048]{1,0:T(8,128)(2,1)S(1)}, bf16[16,2048]{1,0:T(8,128)(2,1)S(1)}, u32[]{:S(2)}, u32[]{:S(2)}) collective-permute-start(bf16[16,2048]{1,0:T(8,128)(2,1)S(1)} %down.3.refs_0_), channel_id=1, source_target_pairs={{0,1},{1,0},{2,3},{3,2},{4,5},{5,4},{6,7},{7,6},{8,9},{9,8},{10,11... | collective-permute-start | bytes 196616 | tf_op jit(solution)/shard_map/ppermute | solution.py:24
  43.7 2.5 %collective-permute-done.17.refs_3_ = bf16[16,2048]{1,0:T(8,128)(2,1)S(1)} collective-permute-done((bf16[16,2048]{1,0:T(8,128)(2,1)S(1)}, bf16[16,2048]{1,0:T(8,128)(2,1)S(1)}, u32[]{:S(2)}, u32[]{:S(2)}) %collective-permute-start.17) | collective-permute-done | bytes 65568 | tf_op jit(solution)/shard_map/ppermute | solution.py:24
  46.2 1.0 %collective-permute-done.16.refs_2_ = bf16[16,2048]{1,0:T(8,128)(2,1)S(1)} collective-permute-done((bf16[16,2048]{1,0:T(8,128)(2,1)S(1)}, bf16[16,2048]{1,0:T(8,128)(2,1)S(1)}, u32[]{:S(2)}, u32[]{:S(2)}) %collective-permute-start.16) | collective-permute-done | bytes 65568 | tf_op jit(solution)/shard_map/ppermute | solution.py:24
  47.2 0.0 collective-permute-done.15.refs_1_
  47.2 0.7 %final.1 = bf16[2,8,2048]{2,1,0:T(8,128)(2,1)} custom-call(f32[16,2048]{1,0:T(8,128)S(1)} %get-tuple-element.16.mid, bf16[16,2048]{1,0:T(8,128)(2,1)S(1)} %down.3.refs_0_, bf16[16,2048]{1,0:T(8,128)(2,1)S(1)} %collective-permute-done.15.refs_1_, bf16[16,2048]{1,0:T(8,128)(2,1)S(1)} %collective-permute-done.16.refs_2_, ...), custom_call_target="tpu_custom_call" | custom-call | tf_op jit(solution)/shard_map/final/pallas_call | solution.py:399
  (17 shorter events, 0.1 us)
Async XLA Ops:
  0.0 17.0 %copy-start.2 = (bf16[1024,2048]{1,0:T(8,128)(2,1)S(1)}, bf16[1024,2048]{1,0:T(8,128)(2,1)}, u32[]{:S(2)}) copy-start(bf16[1024,2048]{1,0:T(8,128)(2,1)} %refs_4_.1) | copy-start | bytes 12582916
  0.0 22.9 %copy-start.1 = (bf16[2048,3584]{1,0:T(8,128)(2,1)S(1)}, bf16[2048,3584]{1,0:T(8,128)(2,1)}, u32[]{:S(2)}) copy-start(bf16[2048,3584]{1,0:T(8,128)(2,1)} %up_weight.1) | copy-start | bytes 44040196
  0.0 22.9 %copy-start = (bf16[2048,3584]{1,0:T(8,128)(2,1)S(1)}, bf16[2048,3584]{1,0:T(8,128)(2,1)}, u32[]{:S(2)}) copy-start(bf16[2048,3584]{1,0:T(8,128)(2,1)} %gate_weight.1) | copy-start | bytes 44040196
  0.0 22.9 %copy-start.4 = (bf16[2048]{0:T(1024)(128)(2,1)S(1)}, bf16[2048]{0:T(1024)(128)(2,1)}, u32[]{:S(2)}) copy-start(bf16[2048]{0:T(1024)(128)(2,1)} %gains.1) | copy-start | bytes 12292
  0.0 22.9 %copy-start.3 = (bf16[2,8,2048]{2,1,0:T(8,128)(2,1)S(1)}, bf16[2,8,2048]{2,1,0:T(8,128)(2,1)}, u32[]{:S(2)}) copy-start(bf16[2,8,2048]{2,1,0:T(8,128)(2,1)} %residual.1) | copy-start | bytes 196612
  2.3 3.2 %collective-permute-start = (f32[5,8,128]{2,1,0:T(8,128)S(1)}, f32[5,8,128]{2,1,0:T(8,128)S(1)}, u32[]{:S(2)}, u32[]{:S(2)}) collective-permute-start(f32[5,8,128]{2,1,0:T(8,128)S(1)} %get-tuple-element.13), channel_id=1, source_target_pairs={{0,1},{1,0},{2,3},{3,2},{4,5},{5,4},{6,7},{7,6},{8,9},{9,8},{10,11... | collective-permute-start | bytes 61448 | tf_op jit(solution)/shard_map/ppermute | solution.py:24
  2.8 4.4 %collective-permute-start.1 = (f32[5,8,128]{2,1,0:T(8,128)S(1)}, f32[5,8,128]{2,1,0:T(8,128)S(1)}, u32[]{:S(2)}, u32[]{:S(2)}) collective-permute-start(f32[5,8,128]{2,1,0:T(8,128)S(1)} %get-tuple-element.14), channel_id=1, source_target_pairs={{0,2},{1,3},{2,0},{3,1},{4,6},{5,7},{6,4},{7,5},{8,10},{9,11},{10,... | collective-permute-start | bytes 61448 | tf_op jit(solution)/shard_map/ppermute | solution.py:24
  5.4 3.2 %collective-permute-start.2 = (f32[5,8,128]{2,1,0:T(8,128)S(1)}, f32[5,8,128]{2,1,0:T(8,128)S(1)}, u32[]{:S(2)}, u32[]{:S(2)}) collective-permute-start(f32[5,8,128]{2,1,0:T(8,128)S(1)} %get-tuple-element.15), channel_id=1, source_target_pairs={{0,3},{1,2},{2,1},{3,0},{4,7},{5,6},{6,5},{7,4},{8,11},{9,10},{10,... | collective-permute-start | bytes 61448 | tf_op jit(solution)/shard_map/ppermute | solution.py:24
  8.8 5.5 %collective-permute-start.5 = (bf16[4,1024]{1,0:T(4,128)(2,1)S(1)}, bf16[4,1024]{1,0:T(4,128)(2,1)S(1)}, u32[]{:S(2)}, u32[]{:S(2)}) collective-permute-start(bf16[4,1024]{1,0:T(4,128)(2,1)S(1)} %combine.1.refs_0_), channel_id=1, source_target_pairs={{0,12},{4,8},{8,4},{12,0},{1,13},{5,9},{9,5},{13,1},{2,14},{6,10},... | collective-permute-start | bytes 24584 | tf_op jit(solution)/shard_map/ppermute | solution.py:24
  12.5 4.5 %collective-permute-start.4 = (bf16[4,1024]{1,0:T(4,128)(2,1)S(1)}, bf16[4,1024]{1,0:T(4,128)(2,1)S(1)}, u32[]{:S(2)}, u32[]{:S(2)}) collective-permute-start(bf16[4,1024]{1,0:T(4,128)(2,1)S(1)} %combine.1.refs_0_), channel_id=1, source_target_pairs={{0,8},{4,12},{8,0},{12,4},{1,9},{5,13},{9,1},{13,5},{2,10},{6,14},... | collective-permute-start | bytes 24584 | tf_op jit(solution)/shard_map/ppermute | solution.py:24
  12.5 4.5 %collective-permute-start.3 = (bf16[4,1024]{1,0:T(4,128)(2,1)S(1)}, bf16[4,1024]{1,0:T(4,128)(2,1)S(1)}, u32[]{:S(2)}, u32[]{:S(2)}) collective-permute-start(bf16[4,1024]{1,0:T(4,128)(2,1)S(1)} %combine.1.refs_0_), channel_id=1, source_target_pairs={{0,4},{4,0},{8,12},{12,8},{1,5},{5,1},{9,13},{13,9},{2,6},{6,2},{1... | collective-permute-start | bytes 24584 | tf_op jit(solution)/shard_map/ppermute | solution.py:24
  17.0 20.7 %slice-start = ((s8[14680064]{0:T(1024)(128)(4,1)}), s8[4194304]{0:T(1024)(128)(4,1)S(1)}, s32[]{:S(2)}) async-start(s8[14680064]{0:T(1024)(128)(4,1)} %bitcast), calls=%async_computation | async-start | bytes 8388608
  17.8 19.9 %slice-start.1 = ((s8[14680064]{0:T(1024)(128)(4,1)}), s8[4194304]{0:T(1024)(128)(4,1)S(1)}, s32[]{:S(2)}) async-start(s8[14680064]{0:T(1024)(128)(4,1)} %bitcast), calls=%async_computation.1 | async-start | bytes 8388608
  17.8 19.9 %slice-start.2 = ((s8[14680064]{0:T(1024)(128)(4,1)}), s8[4194304]{0:T(1024)(128)(4,1)S(1)}, s32[]{:S(2)}) async-start(s8[14680064]{0:T(1024)(128)(4,1)} %bitcast), calls=%async_computation.2 | async-start | bytes 8388608
  17.8 19.9 %slice-start.3 = ((s8[14680064]{0:T(1024)(128)(4,1)}), s8[2097152]{0:T(1024)(128)(4,1)S(1)}, s32[]{:S(2)}) async-start(s8[14680064]{0:T(1024)(128)(4,1)} %bitcast), calls=%async_computation.3 | async-start | bytes 4194304
  17.8 3.8 %collective-permute-start.8 = (bf16[16,2048]{1,0:T(8,128)(2,1)S(1)}, bf16[16,2048]{1,0:T(8,128)(2,1)S(1)}, u32[]{:S(2)}, u32[]{:S(2)}) collective-permute-start(bf16[16,2048]{1,0:T(8,128)(2,1)S(1)} %out_projection.1.refs_0_), channel_id=1, source_target_pairs={{0,3},{1,2},{2,1},{3,0},{4,7},{5,6},{6,5},{7,4},{8,11},{9,10},{10,... | collective-permute-start | bytes 196616 | tf_op jit(solution)/shard_map/ppermute | solution.py:24
  17.9 5.0 %collective-permute-start.7 = (bf16[16,2048]{1,0:T(8,128)(2,1)S(1)}, bf16[16,2048]{1,0:T(8,128)(2,1)S(1)}, u32[]{:S(2)}, u32[]{:S(2)}) collective-permute-start(bf16[16,2048]{1,0:T(8,128)(2,1)S(1)} %out_projection.1.refs_0_), channel_id=1, source_target_pairs={{0,2},{1,3},{2,0},{3,1},{4,6},{5,7},{6,4},{7,5},{8,10},{9,11},{10,... | collective-permute-start | bytes 196616 | tf_op jit(solution)/shard_map/ppermute | solution.py:24
  18.7 4.2 %collective-permute-start.6 = (bf16[16,2048]{1,0:T(8,128)(2,1)S(1)}, bf16[16,2048]{1,0:T(8,128)(2,1)S(1)}, u32[]{:S(2)}, u32[]{:S(2)}) collective-permute-start(bf16[16,2048]{1,0:T(8,128)(2,1)S(1)} %out_projection.1.refs_0_), channel_id=1, source_target_pairs={{0,1},{1,0},{2,3},{3,2},{4,5},{5,4},{6,7},{7,6},{8,9},{9,8},{10,11... | collective-permute-start | bytes 196616 | tf_op jit(solution)/shard_map/ppermute | solution.py:24
  25.3 5.9 %collective-permute-start.10 = (bf16[16,1920]{1,0:T(8,128)(2,1)S(1)}, bf16[16,1920]{1,0:T(8,128)(2,1)S(1)}, u32[]{:S(2)}, u32[]{:S(2)}) collective-permute-start(bf16[16,1920]{1,0:T(8,128)(2,1)S(1)} %get-tuple-element.17.refs_0_), channel_id=1, source_target_pairs={{0,8},{4,12},{8,0},{12,4},{1,9},{5,13},{9,1},{13,5},{2,10},{6,14},... | collective-permute-start | bytes 184328 | tf_op jit(solution)/shard_map/ppermute | solution.py:24
  27.4 6.2 %collective-permute-start.11 = (bf16[16,1920]{1,0:T(8,128)(2,1)S(1)}, bf16[16,1920]{1,0:T(8,128)(2,1)S(1)}, u32[]{:S(2)}, u32[]{:S(2)}) collective-permute-start(bf16[16,1920]{1,0:T(8,128)(2,1)S(1)} %get-tuple-element.18), channel_id=1, source_target_pairs={{0,12},{4,8},{8,4},{12,0},{1,13},{5,9},{9,5},{13,1},{2,14},{6,10},... | collective-permute-start | bytes 184328 | tf_op jit(solution)/shard_map/ppermute | solution.py:24
  27.6 6.0 %collective-permute-start.9 = (bf16[16,1920]{1,0:T(8,128)(2,1)S(1)}, bf16[16,1920]{1,0:T(8,128)(2,1)S(1)}, u32[]{:S(2)}, u32[]{:S(2)}) collective-permute-start(bf16[16,1920]{1,0:T(8,128)(2,1)S(1)} %get-tuple-element.18), channel_id=1, source_target_pairs={{0,4},{4,0},{8,12},{12,8},{1,5},{5,1},{9,13},{13,9},{2,6},{6,2},{1... | collective-permute-start | bytes 184328 | tf_op jit(solution)/shard_map/ppermute | solution.py:24
  33.7 3.9 %collective-permute-start.14 = (bf16[8,1792]{1,0:T(8,128)(2,1)S(1)}, bf16[8,1792]{1,0:T(8,128)(2,1)S(1)}, u32[]{:S(2)}, u32[]{:S(2)}) collective-permute-start(bf16[8,1792]{1,0:T(8,128)(2,1)S(1)} %activation.1.own), channel_id=1, source_target_pairs={{0,4},{4,0},{8,12},{12,8},{1,5},{5,1},{9,13},{13,9},{2,6},{6,2},{1... | collective-permute-start | bytes 86024 | tf_op jit(solution)/shard_map/ppermute | solution.py:24
  34.3 4.8 %collective-permute-start.13 = (bf16[8,1792]{1,0:T(8,128)(2,1)S(1)}, bf16[8,1792]{1,0:T(8,128)(2,1)S(1)}, u32[]{:S(2)}, u32[]{:S(2)}) collective-permute-start(bf16[8,1792]{1,0:T(8,128)(2,1)S(1)} %activation.1.own), channel_id=1, source_target_pairs={{0,20},{4,16},{8,28},{12,24},{16,4},{20,0},{24,12},{28,8},{1,21},{... | collective-permute-start | bytes 86024 | tf_op jit(solution)/shard_map/ppermute | solution.py:24
  36.7 3.9 %collective-permute-start.12 = (bf16[8,1792]{1,0:T(8,128)(2,1)S(1)}, bf16[8,1792]{1,0:T(8,128)(2,1)S(1)}, u32[]{:S(2)}, u32[]{:S(2)}) collective-permute-start(bf16[8,1792]{1,0:T(8,128)(2,1)S(1)} %activation.1.own), channel_id=1, source_target_pairs={{0,16},{16,0},{1,17},{17,1},{2,18},{18,2},{3,19},{19,3},{4,20},{20... | collective-permute-start | bytes 86024 | tf_op jit(solution)/shard_map/ppermute | solution.py:24
  41.8 4.4 %collective-permute-start.17 = (bf16[16,2048]{1,0:T(8,128)(2,1)S(1)}, bf16[16,2048]{1,0:T(8,128)(2,1)S(1)}, u32[]{:S(2)}, u32[]{:S(2)}) collective-permute-start(bf16[16,2048]{1,0:T(8,128)(2,1)S(1)} %down.3.refs_0_), channel_id=1, source_target_pairs={{0,3},{1,2},{2,1},{3,0},{4,7},{5,6},{6,5},{7,4},{8,11},{9,10},{10,... | collective-permute-start | bytes 196616 | tf_op jit(solution)/shard_map/ppermute | solution.py:24
  41.8 5.4 %collective-permute-start.16 = (bf16[16,2048]{1,0:T(8,128)(2,1)S(1)}, bf16[16,2048]{1,0:T(8,128)(2,1)S(1)}, u32[]{:S(2)}, u32[]{:S(2)}) collective-permute-start(bf16[16,2048]{1,0:T(8,128)(2,1)S(1)} %down.3.refs_0_), channel_id=1, source_target_pairs={{0,2},{1,3},{2,0},{3,1},{4,6},{5,7},{6,4},{7,5},{8,10},{9,11},{10,... | collective-permute-start | bytes 196616 | tf_op jit(solution)/shard_map/ppermute | solution.py:24
  43.1 4.1 %collective-permute-start.15 = (bf16[16,2048]{1,0:T(8,128)(2,1)S(1)}, bf16[16,2048]{1,0:T(8,128)(2,1)S(1)}, u32[]{:S(2)}, u32[]{:S(2)}) collective-permute-start(bf16[16,2048]{1,0:T(8,128)(2,1)S(1)} %down.3.refs_0_), channel_id=1, source_target_pairs={{0,1},{1,0},{2,3},{3,2},{4,5},{5,4},{6,7},{7,6},{8,9},{9,8},{10,11... | collective-permute-start | bytes 196616 | tf_op jit(solution)/shard_map/ppermute | solution.py:24

commit v5 on v4

--- a/solution.py
+++ b/solution.py
@@ -66,27 +66,33 @@
     return pltpu.with_memory_space_constraint(value, pltpu.VMEM)
 
 
-def attention_kernel(cols, lengths, *rest):
-    sources, outs = rest[:5], rest[5 : 5 + cols]
-    held, (sized_ref, packed, sems) = rest[5 + cols : 10 + cols], rest[10 + cols :]
-    sized = pltpu.make_async_copy(lengths, sized_ref, sems.at[5])
-    sized.start()
-    lengths = sized_ref
+def attention_kernel(cols, far, lengths, *rest):
+    half = cols // 2
+    sources, outs = rest[:5], rest[5 : 5 + half]
+    held, (sized, packed, sems) = rest[5 + half : 10 + half], rest[10 + half :]
+    column = lax.axis_index("col")
+    heads = KV_HEADS // 2
+    part = jnp.bitwise_xor(column // half, far)
+
+    def lanes(source):
+        width = source.shape[2] // 2
+        return source.at[:, :, pl.ds(pl.multiple_of(part * width, 128), width)]
+
     copies = [
-        pltpu.make_async_copy(source, target, sems.at[i])
+        pltpu.make_async_copy(lanes(source), target, sems.at[i])
         for i, (source, target) in enumerate(zip(sources, held))
     ]
+    copies.append(pltpu.make_async_copy(lengths, sized, sems.at[5]))
     for copy in copies:
         copy.start()
     query, new_keys, new_values, keys, values = held
-    column = lax.axis_index("col")
     rows, span, _ = keys.shape
     hb = HEADS // cols
     inv_root = 1.0 / math.sqrt(HD)
     n = TOKENS * GROUP
-    pairs = [(b, g) for b in range(rows) for g in range(KV_HEADS)]
-    for copy in [sized] + copies[:4]:
-        copy.wait()
+    pairs = [(b, g) for b in range(rows) for g in range(heads)]
+    for i in (0, 1, 2, 5, 3):
+        copies[i].wait()
     q32 = query[...].astype(jnp.float32)
     nk, nv = new_keys[...].astype(jnp.float32), new_values[...].astype(jnp.float32)
     zeros = jnp.zeros((8 - TOKENS, HD), jnp.float32)
@@ -107,7 +113,7 @@
         ).astype(jnp.bfloat16)
         s = dot_t(q, keys[b, :, g * HD : (g + 1) * HD]) * inv_root
         position = column * span + lax.broadcasted_iota(jnp.int32, (n, span), 1)
-        scores.append(jnp.where(position < lengths[b], s, very_low))
+        scores.append(jnp.where(position < sized[b], s, very_low))
         f = dot_t(q, fresh(nk, b, g).astype(jnp.bfloat16)) * inv_root
         token = lax.broadcasted_iota(jnp.int32, (n, 8), 0) // GROUP
         slot = lax.broadcasted_iota(jnp.int32, (n, 8), 1)
@@ -128,7 +134,7 @@
         return jnp.concatenate([high, low], axis=0)
 
     lane = lax.broadcasted_iota(jnp.int32, (GROUP, HD), 1)
-    stats = [jnp.zeros((GROUP, HD), jnp.float32) for _ in range(KV_HEADS)]
+    stats = [jnp.zeros((GROUP, HD), jnp.float32) for _ in range(heads)]
     copies[4].wait()
     for i, (b, g) in enumerate(pairs):
         here = slice(i * n, (i + 1) * n)
@@ -147,15 +153,15 @@
             else:
                 for j in range(GROUP // hb):
                     packed[g * (GROUP // hb) + j, tb] = block[j * hb : (j + 1) * hb]
-    for g in range(KV_HEADS):
+    for g in range(heads):
         if hb >= GROUP:
             at = g * GROUP
             packed[at // hb, TOKENS * rows, at % hb : at % hb + GROUP] = stats[g]
         else:
             for j in range(GROUP // hb):
                 packed[g * (GROUP // hb) + j, TOKENS * rows] = stats[g][j * hb : (j + 1) * hb]
-    for k in range(cols):
-        outs[k][...] = packed[jnp.bitwise_xor(column, k)]
+    for k in range(half):
+        outs[k][...] = packed[jnp.bitwise_xor(column % half, k)]
 
 
 def combine_kernel(cols, *refs):
@@ -330,17 +336,24 @@
 
     sources = [query, new_keys, new_values, key_cache, value_cache]
     message = shape((cells + 1, hb, HD), f32)
-    parts = call(
-        functools.partial(attention_kernel, cols),
-        [message] * cols,
-        [ANY_SPEC] * 6,
-        [pltpu.VMEM(a.shape, a.dtype) for a in sources]
-        + [pltpu.SMEM(lengths.shape, lengths.dtype)]
-        + [pltpu.VMEM((cols, cells + 1, hb, HD), f32), pltpu.SemaphoreType.DMA((6,))],
-        flops=40 * 10**9,
-        name="attention",
-    )(*[in_hbm(a) for a in [lengths, *sources]])
-    parts = [parts[0]] + [partner(parts[k], "col", k) for k in range(1, cols)]
+    sources = [query, new_keys, new_values, key_cache, value_cache]
+
+    def messages(far):
+        return call(
+            functools.partial(attention_kernel, cols, far),
+            [message] * (cols // 2),
+            [ANY_SPEC] * 6,
+            [pltpu.VMEM((*a.shape[:2], a.shape[2] // 2), a.dtype) for a in sources]
+            + [pltpu.SMEM(lengths.shape, lengths.dtype)]
+            + [pltpu.VMEM((cols // 2, *message.shape), f32), pltpu.SemaphoreType.DMA((6,))],
+            flops=40 * 10**9 if far else None,
+            name="attention_far" if far else "attention_near",
+        )(*[in_hbm(a) for a in [lengths, *sources]])
+
+    parts = messages(1)
+    parts = [partner(parts[k], "col", cols // 2 + k) for k in range(cols // 2)]
+    near = messages(0)
+    parts = [near[0]] + [partner(near[k], "col", k) for k in range(1, cols // 2)] + parts
     attended = call(
         functools.partial(combine_kernel, cols),
         shape((cells, features), bf16),

time: 48 us -> 48.8 us (1.017)
  Pallas kernels: 8.82 us -> 11 us
  waiting for transfers between devices: 20.3 us -> 18.7 us
    pallas_call x1 -> x2, Pallas kernels: 2.25 us -> 4.44 us  [messages(): call(functools.partial(attention_kernel, cols, far), [message] * (cols //...]
    ppermute x18, waiting for transfers between devices: 20.3 us -> 18.7 us  [partner(): lax.ppermute(value, axis, [(i, i ^ k) for i in range(lax.axis_size(axis))])]
  transfers between devices with their start and end apart: 18 -> 18, of which waited for: 13 -> 13; matrix products, arithmetic and copies ran while one was open for 0% -> 0% of each run, Pallas kernels for 3% -> 8%
where the time goes in v5:
time: 48.8 us; the launch traced here: 48.6 us
  starting transfers between devices  18.8 us (39%)
  waiting for transfers between devices  18.7 us (38%)
  Pallas kernels  11 us (23%)
    ppermute x18, starting transfers between devices, partner(): lax.ppermute(value, axis, [(i, i ^ k) for i in range(lax.axis_size(axis))])  18.8 us
    ppermute x18, waiting for transfers between devices, partner(): lax.ppermute(value, axis, [(i, i ^ k) for i in range(lax.axis_size(axis))])  18.7 us
    pallas_call x2, Pallas kernels, messages(): call(functools.partial(attention_kernel, cols, far), [message] * (cols //...  4.44 us
    pallas_call x2, Pallas kernels, down_part(): call(functools.partial(down_kernel, other), shape((m, width_share), resul...  2.37 us
    pallas_call x1, Pallas kernels, shards(): call(functools.partial(lift_kernel, groups, split), [shape((m, width_shar...  2.34 us
  transfers between devices with their start and end apart: 18, of which 13 were waited for; matrix products, arithmetic and copies ran while one was open for 0% of the time, Pallas kernels for 8%

profile of v5, /device:TPU:0, one launch (start us, length us, event | category | flops | bytes accessed | tf_op | source)
XLA Modules:
  0.0 48.6 jit_solution(16945531563111906732)
XLA Ops:
  0.0 1.9 %attention_far.1 = (f32[5,8,128]{2,1,0:T(8,128)S(1)}, f32[5,8,128]{2,1,0:T(8,128)S(1)}) custom-call(s32[2]{0:T(128)} %lengths.3, bf16[2,2,4096]{2,1,0:T(2,128)(2,1)} %rest_0_.3, bf16[2,2,512]{2,1,0:T(2,128)(2,1)} %rest_1_.3, bf16[2,2,512]{2,1,0:T(2,128)(2,1)} %rest_2_.3, bf16[2,384,512]{2,1,0:T(8,128)(2,1)} %rest_3_.3, bf16[2,384,512]{2,1,0:T(8,128)(2,1)} %rest_4_.3), custom_call_target="tpu_custom_call" | custom-call | flops 40000000000 | bytes 1024 | tf_op jit(solution)/shard_map/attention_far/pallas_call | solution.py:342
  1.9 3.0 %collective-permute-start.1 = (f32[5,8,128]{2,1,0:T(8,128)S(1)}, f32[5,8,128]{2,1,0:T(8,128)S(1)}, u32[]{:S(2)}, u32[]{:S(2)}) collective-permute-start(f32[5,8,128]{2,1,0:T(8,128)S(1)} %get-tuple-element.14), channel_id=1, source_target_pairs={{0,2},{1,3},{2,0},{3,1},{4,6},{5,7},{6,4},{7,5},{8,10},{9,11},{10,... | collective-permute-start | bytes 61448 | tf_op jit(solution)/shard_map/ppermute | solution.py:24
  5.0 0.0 collective-permute-start.2
  5.0 2.5 %attention_near.1 = (f32[5,8,128]{2,1,0:T(8,128)S(1)}, f32[5,8,128]{2,1,0:T(8,128)S(1)}) custom-call(s32[2]{0:T(128)} %lengths.3, bf16[2,2,4096]{2,1,0:T(2,128)(2,1)} %rest_0_.3, bf16[2,2,512]{2,1,0:T(2,128)(2,1)} %rest_1_.3, bf16[2,2,512]{2,1,0:T(2,128)(2,1)} %rest_2_.3, bf16[2,384,512]{2,1,0:T(8,128)(2,1)} %rest_3_.3, bf16[2,384,512]{2,1,0:T(8,128)(2,1)} %rest_4_.3), custom_call_target="tpu_custom_call" | custom-call | tf_op jit(solution)/shard_map/attention_near/pallas_call | solution.py:342
  7.5 0.3 collective-permute-start
  7.8 0.0 collective-permute-done.1.refs_2_
  7.8 0.4 collective-permute-done.2.refs_3_
  8.2 0.6 %collective-permute-done.refs_1_ = f32[5,8,128]{2,1,0:T(8,128)S(1)} collective-permute-done((f32[5,8,128]{2,1,0:T(8,128)S(1)}, f32[5,8,128]{2,1,0:T(8,128)S(1)}, u32[]{:S(2)}, u32[]{:S(2)}) %collective-permute-start) | collective-permute-done | bytes 20512 | tf_op jit(solution)/shard_map/ppermute | solution.py:24
  8.8 0.2 combine.1.refs_0_
  8.9 3.9 %collective-permute-start.5 = (bf16[4,1024]{1,0:T(4,128)(2,1)S(1)}, bf16[4,1024]{1,0:T(4,128)(2,1)S(1)}, u32[]{:S(2)}, u32[]{:S(2)}) collective-permute-start(bf16[4,1024]{1,0:T(4,128)(2,1)S(1)} %combine.1.refs_0_), channel_id=1, source_target_pairs={{0,12},{4,8},{8,4},{12,0},{1,13},{5,9},{9,5},{13,1},{2,14},{6,10},... | collective-permute-start | bytes 24584 | tf_op jit(solution)/shard_map/ppermute | solution.py:24
  12.9 0.0 collective-permute-start.4
  12.9 0.6 %collective-permute-start.3 = (bf16[4,1024]{1,0:T(4,128)(2,1)S(1)}, bf16[4,1024]{1,0:T(4,128)(2,1)S(1)}, u32[]{:S(2)}, u32[]{:S(2)}) collective-permute-start(bf16[4,1024]{1,0:T(4,128)(2,1)S(1)} %combine.1.refs_0_), channel_id=1, source_target_pairs={{0,4},{4,0},{8,12},{12,8},{1,5},{5,1},{9,13},{13,9},{2,6},{6,2},{1... | collective-permute-start | bytes 24584 | tf_op jit(solution)/shard_map/ppermute | solution.py:24
  13.5 1.0 %collective-permute-done.5.refs_3_ = bf16[4,1024]{1,0:T(4,128)(2,1)S(1)} collective-permute-done((bf16[4,1024]{1,0:T(4,128)(2,1)S(1)}, bf16[4,1024]{1,0:T(4,128)(2,1)S(1)}, u32[]{:S(2)}, u32[]{:S(2)}) %collective-permute-start.5) | collective-permute-done | bytes 8224 | tf_op jit(solution)/shard_map/ppermute | solution.py:24
  14.5 2.9 %collective-permute-done.4.refs_2_ = bf16[4,1024]{1,0:T(4,128)(2,1)S(1)} collective-permute-done((bf16[4,1024]{1,0:T(4,128)(2,1)S(1)}, bf16[4,1024]{1,0:T(4,128)(2,1)S(1)}, u32[]{:S(2)}, u32[]{:S(2)}) %collective-permute-start.4) | collective-permute-done | bytes 8224 | tf_op jit(solution)/shard_map/ppermute | solution.py:24
  17.4 0.0 collective-permute-done.3.refs_1_
  17.4 0.0 copy-done.2
  17.4 0.8 %out_projection.1.refs_0_ = bf16[16,2048]{1,0:T(8,128)(2,1)S(1)} custom-call(bf16[4,1024]{1,0:T(4,128)(2,1)S(1)} %combine.1.refs_0_, bf16[4,1024]{1,0:T(4,128)(2,1)S(1)} %collective-permute-done.3.refs_1_, bf16[4,1024]{1,0:T(4,128)(2,1)S(1)} %collective-permute-done.4.refs_2_, bf16[4,1024]{1,0:T(4,128)(2,1)S(1)} %collective-permute-done.5.refs_3_, ...), custom_call_target="tpu_custom_call" | custom-call | tf_op jit(solution)/shard_map/out_projection/pallas_call | solution.py:364
  18.3 0.1 collective-permute-start.8
  18.4 1.6 %collective-permute-start.7 = (bf16[16,2048]{1,0:T(8,128)(2,1)S(1)}, bf16[16,2048]{1,0:T(8,128)(2,1)S(1)}, u32[]{:S(2)}, u32[]{:S(2)}) collective-permute-start(bf16[16,2048]{1,0:T(8,128)(2,1)S(1)} %out_projection.1.refs_0_), channel_id=1, source_target_pairs={{0,2},{1,3},{2,0},{3,1},{4,6},{5,7},{6,4},{7,5},{8,10},{9,11},{10,... | collective-permute-start | bytes 196616 | tf_op jit(solution)/shard_map/ppermute | solution.py:24
  19.9 0.3 collective-permute-start.6
  20.2 2.5 %collective-permute-done.8.refs_3_ = bf16[16,2048]{1,0:T(8,128)(2,1)S(1)} collective-permute-done((bf16[16,2048]{1,0:T(8,128)(2,1)S(1)}, bf16[16,2048]{1,0:T(8,128)(2,1)S(1)}, u32[]{:S(2)}, u32[]{:S(2)}) %collective-permute-start.8) | collective-permute-done | bytes 65568 | tf_op jit(solution)/shard_map/ppermute | solution.py:24
  22.6 1.5 %collective-permute-done.7.refs_2_ = bf16[16,2048]{1,0:T(8,128)(2,1)S(1)} collective-permute-done((bf16[16,2048]{1,0:T(8,128)(2,1)S(1)}, bf16[16,2048]{1,0:T(8,128)(2,1)S(1)}, u32[]{:S(2)}, u32[]{:S(2)}) %collective-permute-start.7) | collective-permute-done | bytes 65568 | tf_op jit(solution)/shard_map/ppermute | solution.py:24
  24.1 0.0 collective-permute-done.6.refs_1_
  24.1 0.0 copy-done.4
  24.1 0.0 copy-done.3
  24.2 2.3 %gate_up.1 = (f32[16,2048]{1,0:T(8,128)S(1)}, bf16[16,1920]{1,0:T(8,128)(2,1)S(1)}, bf16[16,1920]{1,0:T(8,128)(2,1)S(1)}) custom-call(bf16[2,8,2048]{2,1,0:T(8,128)(2,1)S(1)} %copy-done.3, bf16[2048]{0:T(1024)(128)(2,1)S(1)} %copy-done.4, bf16[2048,3584]{1,0:T(8,128)(2,1)S(1)} %copy-done, bf16[2048,3584]{1,0:T(8,128)(2,1)S(1)} %copy-done.1, ...), custom_call_target="tpu_custom_call" | custom-call | tf_op jit(solution)/shard_map/gate_up/pallas_call | solution.py:371
  26.5 2.1 %collective-permute-start.10 = (bf16[16,1920]{1,0:T(8,128)(2,1)S(1)}, bf16[16,1920]{1,0:T(8,128)(2,1)S(1)}, u32[]{:S(2)}, u32[]{:S(2)}) collective-permute-start(bf16[16,1920]{1,0:T(8,128)(2,1)S(1)} %get-tuple-element.17.refs_0_), channel_id=1, source_target_pairs={{0,8},{4,12},{8,0},{12,4},{1,9},{5,13},{9,1},{13,5},{2,10},{6,14},... | collective-permute-start | bytes 184328 | tf_op jit(solution)/shard_map/ppermute | solution.py:24
  28.6 0.1 collective-permute-start.11
  28.7 1.4 %collective-permute-start.9 = (bf16[16,1920]{1,0:T(8,128)(2,1)S(1)}, bf16[16,1920]{1,0:T(8,128)(2,1)S(1)}, u32[]{:S(2)}, u32[]{:S(2)}) collective-permute-start(bf16[16,1920]{1,0:T(8,128)(2,1)S(1)} %get-tuple-element.18), channel_id=1, source_target_pairs={{0,4},{4,0},{8,12},{12,8},{1,5},{5,1},{9,13},{13,9},{2,6},{6,2},{1... | collective-permute-start | bytes 184328 | tf_op jit(solution)/shard_map/ppermute | solution.py:24
  30.1 2.3 %collective-permute-done.10.refs_2_ = bf16[16,1920]{1,0:T(8,128)(2,1)S(1)} collective-permute-done((bf16[16,1920]{1,0:T(8,128)(2,1)S(1)}, bf16[16,1920]{1,0:T(8,128)(2,1)S(1)}, u32[]{:S(2)}, u32[]{:S(2)}) %collective-permute-start.10) | collective-permute-done | bytes 61472 | tf_op jit(solution)/shard_map/ppermute | solution.py:24
  32.3 2.4 %collective-permute-done.11.refs_3_ = bf16[16,1920]{1,0:T(8,128)(2,1)S(1)} collective-permute-done((bf16[16,1920]{1,0:T(8,128)(2,1)S(1)}, bf16[16,1920]{1,0:T(8,128)(2,1)S(1)}, u32[]{:S(2)}, u32[]{:S(2)}) %collective-permute-start.11) | collective-permute-done | bytes 61472 | tf_op jit(solution)/shard_map/ppermute | solution.py:24
  34.7 0.0 collective-permute-done.9.refs_1_
  34.7 0.1 activation.1.own
  34.9 0.6 %collective-permute-start.14 = (bf16[8,1792]{1,0:T(8,128)(2,1)S(1)}, bf16[8,1792]{1,0:T(8,128)(2,1)S(1)}, u32[]{:S(2)}, u32[]{:S(2)}) collective-permute-start(bf16[8,1792]{1,0:T(8,128)(2,1)S(1)} %activation.1.own), channel_id=1, source_target_pairs={{0,4},{4,0},{8,12},{12,8},{1,5},{5,1},{9,13},{13,9},{2,6},{6,2},{1... | collective-permute-start | bytes 86024 | tf_op jit(solution)/shard_map/ppermute | solution.py:24
  35.4 2.5 %collective-permute-start.13 = (bf16[8,1792]{1,0:T(8,128)(2,1)S(1)}, bf16[8,1792]{1,0:T(8,128)(2,1)S(1)}, u32[]{:S(2)}, u32[]{:S(2)}) collective-permute-start(bf16[8,1792]{1,0:T(8,128)(2,1)S(1)} %activation.1.own), channel_id=1, source_target_pairs={{0,20},{4,16},{8,28},{12,24},{16,4},{20,0},{24,12},{28,8},{1,21},{... | collective-permute-start | bytes 86024 | tf_op jit(solution)/shard_map/ppermute | solution.py:24
  37.9 0.5 %collective-permute-start.12 = (bf16[8,1792]{1,0:T(8,128)(2,1)S(1)}, bf16[8,1792]{1,0:T(8,128)(2,1)S(1)}, u32[]{:S(2)}, u32[]{:S(2)}) collective-permute-start(bf16[8,1792]{1,0:T(8,128)(2,1)S(1)} %activation.1.own), channel_id=1, source_target_pairs={{0,16},{16,0},{1,17},{17,1},{2,18},{18,2},{3,19},{19,3},{4,20},{20... | collective-permute-start | bytes 86024 | tf_op jit(solution)/shard_map/ppermute | solution.py:24
  38.4 0.4 collective-permute-done.14.received
  38.9 1.2 %down.2.refs_0_ = f32[16,2048]{1,0:T(8,128)S(1)} custom-call(bf16[16,1792]{1,0:T(8,128)(2,1)S(1)} %gather_act.3.act, bf16[3584,2048]{1,0:T(8,128)(2,1)S(1)} %bitcast.1), custom_call_target="tpu_custom_call" | custom-call | tf_op jit(solution)/shard_map/down/pallas_call | solution.py:398
  40.1 0.1 collective-permute-done.13.received
  40.2 1.6 %collective-permute-done.12.own = bf16[8,1792]{1,0:T(8,128)(2,1)S(1)} collective-permute-done((bf16[8,1792]{1,0:T(8,128)(2,1)S(1)}, bf16[8,1792]{1,0:T(8,128)(2,1)S(1)}, u32[]{:S(2)}, u32[]{:S(2)}) %collective-permute-start.12) | collective-permute-done | bytes 28704 | tf_op jit(solution)/shard_map/ppermute | solution.py:24
  41.8 1.2 %down.3.refs_0_ = bf16[16,2048]{1,0:T(8,128)(2,1)S(1)} custom-call(bf16[16,1792]{1,0:T(8,128)(2,1)S(1)} %gather_act.2.act, bf16[3584,2048]{1,0:T(8,128)(2,1)S(1)} %bitcast.1, f32[16,2048]{1,0:T(8,128)S(1)} %down.2.refs_0_), custom_call_target="tpu_custom_call" | custom-call | tf_op jit(solution)/shard_map/down/pallas_call | solution.py:398
  43.0 0.0 collective-permute-start.17
  43.0 0.8 %collective-permute-start.16 = (bf16[16,2048]{1,0:T(8,128)(2,1)S(1)}, bf16[16,2048]{1,0:T(8,128)(2,1)S(1)}, u32[]{:S(2)}, u32[]{:S(2)}) collective-permute-start(bf16[16,2048]{1,0:T(8,128)(2,1)S(1)} %down.3.refs_0_), channel_id=1, source_target_pairs={{0,2},{1,3},{2,0},{3,1},{4,6},{5,7},{6,4},{7,5},{8,10},{9,11},{10,... | collective-permute-start | bytes 196616 | tf_op jit(solution)/shard_map/ppermute | solution.py:24
  43.8 1.0 %collective-permute-start.15 = (bf16[16,2048]{1,0:T(8,128)(2,1)S(1)}, bf16[16,2048]{1,0:T(8,128)(2,1)S(1)}, u32[]{:S(2)}, u32[]{:S(2)}) collective-permute-start(bf16[16,2048]{1,0:T(8,128)(2,1)S(1)} %down.3.refs_0_), channel_id=1, source_target_pairs={{0,1},{1,0},{2,3},{3,2},{4,5},{5,4},{6,7},{7,6},{8,9},{9,8},{10,11... | collective-permute-start | bytes 196616 | tf_op jit(solution)/shard_map/ppermute | solution.py:24
  44.8 2.1 %collective-permute-done.17.refs_3_ = bf16[16,2048]{1,0:T(8,128)(2,1)S(1)} collective-permute-done((bf16[16,2048]{1,0:T(8,128)(2,1)S(1)}, bf16[16,2048]{1,0:T(8,128)(2,1)S(1)}, u32[]{:S(2)}, u32[]{:S(2)}) %collective-permute-start.17) | collective-permute-done | bytes 65568 | tf_op jit(solution)/shard_map/ppermute | solution.py:24
  46.9 1.0 %collective-permute-done.16.refs_2_ = bf16[16,2048]{1,0:T(8,128)(2,1)S(1)} collective-permute-done((bf16[16,2048]{1,0:T(8,128)(2,1)S(1)}, bf16[16,2048]{1,0:T(8,128)(2,1)S(1)}, u32[]{:S(2)}, u32[]{:S(2)}) %collective-permute-start.16) | collective-permute-done | bytes 65568 | tf_op jit(solution)/shard_map/ppermute | solution.py:24
  47.9 0.0 collective-permute-done.15.refs_1_
  47.9 0.7 %final.1 = bf16[2,8,2048]{2,1,0:T(8,128)(2,1)} custom-call(f32[16,2048]{1,0:T(8,128)S(1)} %get-tuple-element.16.mid, bf16[16,2048]{1,0:T(8,128)(2,1)S(1)} %down.3.refs_0_, bf16[16,2048]{1,0:T(8,128)(2,1)S(1)} %collective-permute-done.15.refs_1_, bf16[16,2048]{1,0:T(8,128)(2,1)S(1)} %collective-permute-done.16.refs_2_, ...), custom_call_target="tpu_custom_call" | custom-call | tf_op jit(solution)/shard_map/final/pallas_call | solution.py:412
  (18 shorter events, 0.1 us)
Async XLA Ops:
  0.0 17.4 %copy-start.2 = (bf16[1024,2048]{1,0:T(8,128)(2,1)S(1)}, bf16[1024,2048]{1,0:T(8,128)(2,1)}, u32[]{:S(2)}) copy-start(bf16[1024,2048]{1,0:T(8,128)(2,1)} %refs_4_.1) | copy-start | bytes 12582916
  0.0 24.1 %copy-start.4 = (bf16[2048]{0:T(1024)(128)(2,1)S(1)}, bf16[2048]{0:T(1024)(128)(2,1)}, u32[]{:S(2)}) copy-start(bf16[2048]{0:T(1024)(128)(2,1)} %gains.1) | copy-start | bytes 12292
  0.0 24.1 %copy-start.3 = (bf16[2,8,2048]{2,1,0:T(8,128)(2,1)S(1)}, bf16[2,8,2048]{2,1,0:T(8,128)(2,1)}, u32[]{:S(2)}) copy-start(bf16[2,8,2048]{2,1,0:T(8,128)(2,1)} %residual.1) | copy-start | bytes 196612
  0.0 24.1 %copy-start = (bf16[2048,3584]{1,0:T(8,128)(2,1)S(1)}, bf16[2048,3584]{1,0:T(8,128)(2,1)}, u32[]{:S(2)}) copy-start(bf16[2048,3584]{1,0:T(8,128)(2,1)} %gate_weight.1) | copy-start | bytes 44040196
  0.0 24.1 %copy-start.1 = (bf16[2048,3584]{1,0:T(8,128)(2,1)S(1)}, bf16[2048,3584]{1,0:T(8,128)(2,1)}, u32[]{:S(2)}) copy-start(bf16[2048,3584]{1,0:T(8,128)(2,1)} %up_weight.1) | copy-start | bytes 44040196
  1.9 5.9 %collective-permute-start.1 = (f32[5,8,128]{2,1,0:T(8,128)S(1)}, f32[5,8,128]{2,1,0:T(8,128)S(1)}, u32[]{:S(2)}, u32[]{:S(2)}) collective-permute-start(f32[5,8,128]{2,1,0:T(8,128)S(1)} %get-tuple-element.14), channel_id=1, source_target_pairs={{0,2},{1,3},{2,0},{3,1},{4,6},{5,7},{6,4},{7,5},{8,10},{9,11},{10,... | collective-permute-start | bytes 61448 | tf_op jit(solution)/shard_map/ppermute | solution.py:24
  5.0 3.2 %collective-permute-start.2 = (f32[5,8,128]{2,1,0:T(8,128)S(1)}, f32[5,8,128]{2,1,0:T(8,128)S(1)}, u32[]{:S(2)}, u32[]{:S(2)}) collective-permute-start(f32[5,8,128]{2,1,0:T(8,128)S(1)} %get-tuple-element.15), channel_id=1, source_target_pairs={{0,3},{1,2},{2,1},{3,0},{4,7},{5,6},{6,5},{7,4},{8,11},{9,10},{10,... | collective-permute-start | bytes 61448 | tf_op jit(solution)/shard_map/ppermute | solution.py:24
  7.5 1.3 %collective-permute-start = (f32[5,8,128]{2,1,0:T(8,128)S(1)}, f32[5,8,128]{2,1,0:T(8,128)S(1)}, u32[]{:S(2)}, u32[]{:S(2)}) collective-permute-start(f32[5,8,128]{2,1,0:T(8,128)S(1)} %get-tuple-element.13), channel_id=1, source_target_pairs={{0,1},{1,0},{2,3},{3,2},{4,5},{5,4},{6,7},{7,6},{8,9},{9,8},{10,11... | collective-permute-start | bytes 61448 | tf_op jit(solution)/shard_map/ppermute | solution.py:24
  8.9 5.6 %collective-permute-start.5 = (bf16[4,1024]{1,0:T(4,128)(2,1)S(1)}, bf16[4,1024]{1,0:T(4,128)(2,1)S(1)}, u32[]{:S(2)}, u32[]{:S(2)}) collective-permute-start(bf16[4,1024]{1,0:T(4,128)(2,1)S(1)} %combine.1.refs_0_), channel_id=1, source_target_pairs={{0,12},{4,8},{8,4},{12,0},{1,13},{5,9},{9,5},{13,1},{2,14},{6,10},... | collective-permute-start | bytes 24584 | tf_op jit(solution)/shard_map/ppermute | solution.py:24
  12.9 4.5 %collective-permute-start.4 = (bf16[4,1024]{1,0:T(4,128)(2,1)S(1)}, bf16[4,1024]{1,0:T(4,128)(2,1)S(1)}, u32[]{:S(2)}, u32[]{:S(2)}) collective-permute-start(bf16[4,1024]{1,0:T(4,128)(2,1)S(1)} %combine.1.refs_0_), channel_id=1, source_target_pairs={{0,8},{4,12},{8,0},{12,4},{1,9},{5,13},{9,1},{13,5},{2,10},{6,14},... | collective-permute-start | bytes 24584 | tf_op jit(solution)/shard_map/ppermute | solution.py:24
  12.9 4.5 %collective-permute-start.3 = (bf16[4,1024]{1,0:T(4,128)(2,1)S(1)}, bf16[4,1024]{1,0:T(4,128)(2,1)S(1)}, u32[]{:S(2)}, u32[]{:S(2)}) collective-permute-start(bf16[4,1024]{1,0:T(4,128)(2,1)S(1)} %combine.1.refs_0_), channel_id=1, source_target_pairs={{0,4},{4,0},{8,12},{12,8},{1,5},{5,1},{9,13},{13,9},{2,6},{6,2},{1... | collective-permute-start | bytes 24584 | tf_op jit(solution)/shard_map/ppermute | solution.py:24
  17.4 21.4 %slice-start = ((s8[14680064]{0:T(1024)(128)(4,1)}), s8[4194304]{0:T(1024)(128)(4,1)S(1)}, s32[]{:S(2)}) async-start(s8[14680064]{0:T(1024)(128)(4,1)} %bitcast), calls=%async_computation | async-start | bytes 8388608
  18.2 20.6 %slice-start.1 = ((s8[14680064]{0:T(1024)(128)(4,1)}), s8[4194304]{0:T(1024)(128)(4,1)S(1)}, s32[]{:S(2)}) async-start(s8[14680064]{0:T(1024)(128)(4,1)} %bitcast), calls=%async_computation.1 | async-start | bytes 8388608
  18.3 20.6 %slice-start.2 = ((s8[14680064]{0:T(1024)(128)(4,1)}), s8[4194304]{0:T(1024)(128)(4,1)S(1)}, s32[]{:S(2)}) async-start(s8[14680064]{0:T(1024)(128)(4,1)} %bitcast), calls=%async_computation.2 | async-start | bytes 8388608
  18.3 20.6 %slice-start.3 = ((s8[14680064]{0:T(1024)(128)(4,1)}), s8[2097152]{0:T(1024)(128)(4,1)S(1)}, s32[]{:S(2)}) async-start(s8[14680064]{0:T(1024)(128)(4,1)} %bitcast), calls=%async_computation.3 | async-start | bytes 4194304
  18.3 4.4 %collective-permute-start.8 = (bf16[16,2048]{1,0:T(8,128)(2,1)S(1)}, bf16[16,2048]{1,0:T(8,128)(2,1)S(1)}, u32[]{:S(2)}, u32[]{:S(2)}) collective-permute-start(bf16[16,2048]{1,0:T(8,128)(2,1)S(1)} %out_projection.1.refs_0_), channel_id=1, source_target_pairs={{0,3},{1,2},{2,1},{3,0},{4,7},{5,6},{6,5},{7,4},{8,11},{9,10},{10,... | collective-permute-start | bytes 196616 | tf_op jit(solution)/shard_map/ppermute | solution.py:24
  18.4 5.8 %collective-permute-start.7 = (bf16[16,2048]{1,0:T(8,128)(2,1)S(1)}, bf16[16,2048]{1,0:T(8,128)(2,1)S(1)}, u32[]{:S(2)}, u32[]{:S(2)}) collective-permute-start(bf16[16,2048]{1,0:T(8,128)(2,1)S(1)} %out_projection.1.refs_0_), channel_id=1, source_target_pairs={{0,2},{1,3},{2,0},{3,1},{4,6},{5,7},{6,4},{7,5},{8,10},{9,11},{10,... | collective-permute-start | bytes 196616 | tf_op jit(solution)/shard_map/ppermute | solution.py:24
  19.9 4.2 %collective-permute-start.6 = (bf16[16,2048]{1,0:T(8,128)(2,1)S(1)}, bf16[16,2048]{1,0:T(8,128)(2,1)S(1)}, u32[]{:S(2)}, u32[]{:S(2)}) collective-permute-start(bf16[16,2048]{1,0:T(8,128)(2,1)S(1)} %out_projection.1.refs_0_), channel_id=1, source_target_pairs={{0,1},{1,0},{2,3},{3,2},{4,5},{5,4},{6,7},{7,6},{8,9},{9,8},{10,11... | collective-permute-start | bytes 196616 | tf_op jit(solution)/shard_map/ppermute | solution.py:24
  26.5 5.8 %collective-permute-start.10 = (bf16[16,1920]{1,0:T(8,128)(2,1)S(1)}, bf16[16,1920]{1,0:T(8,128)(2,1)S(1)}, u32[]{:S(2)}, u32[]{:S(2)}) collective-permute-start(bf16[16,1920]{1,0:T(8,128)(2,1)S(1)} %get-tuple-element.17.refs_0_), channel_id=1, source_target_pairs={{0,8},{4,12},{8,0},{12,4},{1,9},{5,13},{9,1},{13,5},{2,10},{6,14},... | collective-permute-start | bytes 184328 | tf_op jit(solution)/shard_map/ppermute | solution.py:24
  28.6 6.1 %collective-permute-start.11 = (bf16[16,1920]{1,0:T(8,128)(2,1)S(1)}, bf16[16,1920]{1,0:T(8,128)(2,1)S(1)}, u32[]{:S(2)}, u32[]{:S(2)}) collective-permute-start(bf16[16,1920]{1,0:T(8,128)(2,1)S(1)} %get-tuple-element.18), channel_id=1, source_target_pairs={{0,12},{4,8},{8,4},{12,0},{1,13},{5,9},{9,5},{13,1},{2,14},{6,10},... | collective-permute-start | bytes 184328 | tf_op jit(solution)/shard_map/ppermute | solution.py:24
  28.7 6.1 %collective-permute-start.9 = (bf16[16,1920]{1,0:T(8,128)(2,1)S(1)}, bf16[16,1920]{1,0:T(8,128)(2,1)S(1)}, u32[]{:S(2)}, u32[]{:S(2)}) collective-permute-start(bf16[16,1920]{1,0:T(8,128)(2,1)S(1)} %get-tuple-element.18), channel_id=1, source_target_pairs={{0,4},{4,0},{8,12},{12,8},{1,5},{5,1},{9,13},{13,9},{2,6},{6,2},{1... | collective-permute-start | bytes 184328 | tf_op jit(solution)/shard_map/ppermute | solution.py:24
  34.9 3.9 %collective-permute-start.14 = (bf16[8,1792]{1,0:T(8,128)(2,1)S(1)}, bf16[8,1792]{1,0:T(8,128)(2,1)S(1)}, u32[]{:S(2)}, u32[]{:S(2)}) collective-permute-start(bf16[8,1792]{1,0:T(8,128)(2,1)S(1)} %activation.1.own), channel_id=1, source_target_pairs={{0,4},{4,0},{8,12},{12,8},{1,5},{5,1},{9,13},{13,9},{2,6},{6,2},{1... | collective-permute-start | bytes 86024 | tf_op jit(solution)/shard_map/ppermute | solution.py:24
  35.4 4.8 %collective-permute-start.13 = (bf16[8,1792]{1,0:T(8,128)(2,1)S(1)}, bf16[8,1792]{1,0:T(8,128)(2,1)S(1)}, u32[]{:S(2)}, u32[]{:S(2)}) collective-permute-start(bf16[8,1792]{1,0:T(8,128)(2,1)S(1)} %activation.1.own), channel_id=1, source_target_pairs={{0,20},{4,16},{8,28},{12,24},{16,4},{20,0},{24,12},{28,8},{1,21},{... | collective-permute-start | bytes 86024 | tf_op jit(solution)/shard_map/ppermute | solution.py:24
  37.9 3.9 %collective-permute-start.12 = (bf16[8,1792]{1,0:T(8,128)(2,1)S(1)}, bf16[8,1792]{1,0:T(8,128)(2,1)S(1)}, u32[]{:S(2)}, u32[]{:S(2)}) collective-permute-start(bf16[8,1792]{1,0:T(8,128)(2,1)S(1)} %activation.1.own), channel_id=1, source_target_pairs={{0,16},{16,0},{1,17},{17,1},{2,18},{18,2},{3,19},{19,3},{4,20},{20... | collective-permute-start | bytes 86024 | tf_op jit(solution)/shard_map/ppermute | solution.py:24
  43.0 3.9 %collective-permute-start.17 = (bf16[16,2048]{1,0:T(8,128)(2,1)S(1)}, bf16[16,2048]{1,0:T(8,128)(2,1)S(1)}, u32[]{:S(2)}, u32[]{:S(2)}) collective-permute-start(bf16[16,2048]{1,0:T(8,128)(2,1)S(1)} %down.3.refs_0_), channel_id=1, source_target_pairs={{0,3},{1,2},{2,1},{3,0},{4,7},{5,6},{6,5},{7,4},{8,11},{9,10},{10,... | collective-permute-start | bytes 196616 | tf_op jit(solution)/shard_map/ppermute | solution.py:24
  43.0 5.0 %collective-permute-start.16 = (bf16[16,2048]{1,0:T(8,128)(2,1)S(1)}, bf16[16,2048]{1,0:T(8,128)(2,1)S(1)}, u32[]{:S(2)}, u32[]{:S(2)}) collective-permute-start(bf16[16,2048]{1,0:T(8,128)(2,1)S(1)} %down.3.refs_0_), channel_id=1, source_target_pairs={{0,2},{1,3},{2,0},{3,1},{4,6},{5,7},{6,4},{7,5},{8,10},{9,11},{10,... | collective-permute-start | bytes 196616 | tf_op jit(solution)/shard_map/ppermute | solution.py:24
  43.8 4.1 %collective-permute-start.15 = (bf16[16,2048]{1,0:T(8,128)(2,1)S(1)}, bf16[16,2048]{1,0:T(8,128)(2,1)S(1)}, u32[]{:S(2)}, u32[]{:S(2)}) collective-permute-start(bf16[16,2048]{1,0:T(8,128)(2,1)S(1)} %down.3.refs_0_), channel_id=1, source_target_pairs={{0,1},{1,0},{2,3},{3,2},{4,5},{5,4},{6,7},{7,6},{8,9},{9,8},{10,11... | collective-permute-start | bytes 196616 | tf_op jit(solution)/shard_map/ppermute | solution.py:24

commit v6 on v5

--- a/solution.py
+++ b/solution.py
@@ -346,7 +346,6 @@
             [pltpu.VMEM((*a.shape[:2], a.shape[2] // 2), a.dtype) for a in sources]
             + [pltpu.SMEM(lengths.shape, lengths.dtype)]
             + [pltpu.VMEM((cols // 2, *message.shape), f32), pltpu.SemaphoreType.DMA((6,))],
-            flops=40 * 10**9 if far else None,
             name="attention_far" if far else "attention_near",
         )(*[in_hbm(a) for a in [lengths, *sources]])
 
@@ -358,6 +357,7 @@
         functools.partial(combine_kernel, cols),
         shape((cells, features), bf16),
         [VMEM_SPEC] * cols,
+        flops=40 * 10**9,
         name="combine",
     )(*parts)
     gathered = spread(attended, "row")

time: 48.8 us -> 48.1 us (0.986)
  Pallas kernels: 11 us -> 10.2 us
    pallas_call x2, Pallas kernels: 4.44 us -> 3.61 us  [messages(): call(functools.partial(attention_kernel, cols, far), [message] * (cols //...]
  transfers between devices with their start and end apart: 18 -> 18, of which waited for: 13 -> 12; matrix products, arithmetic and copies ran while one was open for 0% -> 0% of each run, Pallas kernels for 8% -> 6%
where the time goes in v6:
time: 48.1 us; the launch traced here: 47.9 us
  starting transfers between devices  18.7 us (39%)
  waiting for transfers between devices  18.7 us (39%)
  Pallas kernels  10.2 us (21%)
    ppermute x18, waiting for transfers between devices, partner(): lax.ppermute(value, axis, [(i, i ^ k) for i in range(lax.axis_size(axis))])  18.7 us
    ppermute x18, starting transfers between devices, partner(): lax.ppermute(value, axis, [(i, i ^ k) for i in range(lax.axis_size(axis))])  18.7 us
    pallas_call x2, Pallas kernels, messages(): call(functools.partial(attention_kernel, cols, far), [message] * (cols //...  3.61 us
    pallas_call x2, Pallas kernels, down_part(): call(functools.partial(down_kernel, other), shape((m, width_share), resul...  2.37 us
    pallas_call x1, Pallas kernels, shards(): call(functools.partial(lift_kernel, groups, split), [shape((m, width_shar...  2.34 us
  transfers between devices with their start and end apart: 18, of which 12 were waited for; matrix products, arithmetic and copies ran while one was open for 0% of the time, Pallas kernels for 6%

profile of v6, /device:TPU:0, one launch (start us, length us, event | category | flops | bytes accessed | tf_op | source)
XLA Modules:
  0.0 47.9 jit_solution(15935405340417865010)
XLA Ops:
  0.0 1.7 %attention_far.1 = (f32[5,8,128]{2,1,0:T(8,128)S(1)}, f32[5,8,128]{2,1,0:T(8,128)S(1)}) custom-call(s32[2]{0:T(128)} %lengths.3, bf16[2,2,4096]{2,1,0:T(2,128)(2,1)} %rest_0_.3, bf16[2,2,512]{2,1,0:T(2,128)(2,1)} %rest_1_.3, bf16[2,2,512]{2,1,0:T(2,128)(2,1)} %rest_2_.3, bf16[2,384,512]{2,1,0:T(8,128)(2,1)} %rest_3_.3, bf16[2,384,512]{2,1,0:T(8,128)(2,1)} %rest_4_.3), custom_call_target="tpu_custom_call" | custom-call | tf_op jit(solution)/shard_map/attention_far/pallas_call | solution.py:342
  1.7 3.0 %collective-permute-start.1 = (f32[5,8,128]{2,1,0:T(8,128)S(1)}, f32[5,8,128]{2,1,0:T(8,128)S(1)}, u32[]{:S(2)}, u32[]{:S(2)}) collective-permute-start(f32[5,8,128]{2,1,0:T(8,128)S(1)} %get-tuple-element.14), channel_id=1, source_target_pairs={{0,2},{1,3},{2,0},{3,1},{4,6},{5,7},{6,4},{7,5},{8,10},{9,11},{10,... | collective-permute-start | bytes 61448 | tf_op jit(solution)/shard_map/ppermute | solution.py:24
  4.8 0.0 collective-permute-start.2
  4.8 1.9 %attention_near.1 = (f32[5,8,128]{2,1,0:T(8,128)S(1)}, f32[5,8,128]{2,1,0:T(8,128)S(1)}) custom-call(s32[2]{0:T(128)} %lengths.3, bf16[2,2,4096]{2,1,0:T(2,128)(2,1)} %rest_0_.3, bf16[2,2,512]{2,1,0:T(2,128)(2,1)} %rest_1_.3, bf16[2,2,512]{2,1,0:T(2,128)(2,1)} %rest_2_.3, bf16[2,384,512]{2,1,0:T(8,128)(2,1)} %rest_3_.3, bf16[2,384,512]{2,1,0:T(8,128)(2,1)} %rest_4_.3), custom_call_target="tpu_custom_call" | custom-call | tf_op jit(solution)/shard_map/attention_near/pallas_call | solution.py:342
  6.7 0.3 collective-permute-start
  6.9 0.0 collective-permute-done.1.refs_2_
  6.9 1.0 %collective-permute-done.2.refs_3_ = f32[5,8,128]{2,1,0:T(8,128)S(1)} collective-permute-done((f32[5,8,128]{2,1,0:T(8,128)S(1)}, f32[5,8,128]{2,1,0:T(8,128)S(1)}, u32[]{:S(2)}, u32[]{:S(2)}) %collective-permute-start.2) | collective-permute-done | bytes 20512 | tf_op jit(solution)/shard_map/ppermute | solution.py:24
  8.0 0.0 collective-permute-done.refs_1_
  8.0 0.0 slice-start.7
  8.0 0.0 slice-start.9
  8.0 0.0 slice-start.10
  8.0 0.0 slice-start.11
  8.0 0.0 copy-start.1
  8.1 0.0 copy-start.2
  8.1 0.2 combine.1.refs_0_
  8.2 3.9 %collective-permute-start.5 = (bf16[4,1024]{1,0:T(4,128)(2,1)S(1)}, bf16[4,1024]{1,0:T(4,128)(2,1)S(1)}, u32[]{:S(2)}, u32[]{:S(2)}) collective-permute-start(bf16[4,1024]{1,0:T(4,128)(2,1)S(1)} %combine.1.refs_0_), channel_id=1, source_target_pairs={{0,12},{4,8},{8,4},{12,0},{1,13},{5,9},{9,5},{13,1},{2,14},{6,10},... | collective-permute-start | bytes 24584 | tf_op jit(solution)/shard_map/ppermute | solution.py:24
  12.1 0.0 collective-permute-start.4
  12.1 0.6 %collective-permute-start.3 = (bf16[4,1024]{1,0:T(4,128)(2,1)S(1)}, bf16[4,1024]{1,0:T(4,128)(2,1)S(1)}, u32[]{:S(2)}, u32[]{:S(2)}) collective-permute-start(bf16[4,1024]{1,0:T(4,128)(2,1)S(1)} %combine.1.refs_0_), channel_id=1, source_target_pairs={{0,4},{4,0},{8,12},{12,8},{1,5},{5,1},{9,13},{13,9},{2,6},{6,2},{1... | collective-permute-start | bytes 24584 | tf_op jit(solution)/shard_map/ppermute | solution.py:24
  12.8 1.0 %collective-permute-done.5.refs_3_ = bf16[4,1024]{1,0:T(4,128)(2,1)S(1)} collective-permute-done((bf16[4,1024]{1,0:T(4,128)(2,1)S(1)}, bf16[4,1024]{1,0:T(4,128)(2,1)S(1)}, u32[]{:S(2)}, u32[]{:S(2)}) %collective-permute-start.5) | collective-permute-done | bytes 8224 | tf_op jit(solution)/shard_map/ppermute | solution.py:24
  13.8 2.9 %collective-permute-done.4.refs_2_ = bf16[4,1024]{1,0:T(4,128)(2,1)S(1)} collective-permute-done((bf16[4,1024]{1,0:T(4,128)(2,1)S(1)}, bf16[4,1024]{1,0:T(4,128)(2,1)S(1)}, u32[]{:S(2)}, u32[]{:S(2)}) %collective-permute-start.4) | collective-permute-done | bytes 8224 | tf_op jit(solution)/shard_map/ppermute | solution.py:24
  16.7 0.0 collective-permute-done.3.refs_1_
  16.7 0.8 %out_projection.1.refs_0_ = bf16[16,2048]{1,0:T(8,128)(2,1)S(1)} custom-call(bf16[4,1024]{1,0:T(4,128)(2,1)S(1)} %combine.1.refs_0_, bf16[4,1024]{1,0:T(4,128)(2,1)S(1)} %collective-permute-done.3.refs_1_, bf16[4,1024]{1,0:T(4,128)(2,1)S(1)} %collective-permute-done.4.refs_2_, bf16[4,1024]{1,0:T(4,128)(2,1)S(1)} %collective-permute-done.5.refs_3_, ...), custom_call_target="tpu_custom_call" | custom-call | tf_op jit(solution)/shard_map/out_projection/pallas_call | solution.py:364
  17.5 0.1 collective-permute-start.8
  17.6 1.5 %collective-permute-start.7 = (bf16[16,2048]{1,0:T(8,128)(2,1)S(1)}, bf16[16,2048]{1,0:T(8,128)(2,1)S(1)}, u32[]{:S(2)}, u32[]{:S(2)}) collective-permute-start(bf16[16,2048]{1,0:T(8,128)(2,1)S(1)} %out_projection.1.refs_0_), channel_id=1, source_target_pairs={{0,2},{1,3},{2,0},{3,1},{4,6},{5,7},{6,4},{7,5},{8,10},{9,11},{10,... | collective-permute-start | bytes 196616 | tf_op jit(solution)/shard_map/ppermute | solution.py:24
  19.2 0.3 collective-permute-start.6
  19.4 2.5 %collective-permute-done.8.refs_3_ = bf16[16,2048]{1,0:T(8,128)(2,1)S(1)} collective-permute-done((bf16[16,2048]{1,0:T(8,128)(2,1)S(1)}, bf16[16,2048]{1,0:T(8,128)(2,1)S(1)}, u32[]{:S(2)}, u32[]{:S(2)}) %collective-permute-start.8) | collective-permute-done | bytes 65568 | tf_op jit(solution)/shard_map/ppermute | solution.py:24
  21.9 1.5 %collective-permute-done.7.refs_2_ = bf16[16,2048]{1,0:T(8,128)(2,1)S(1)} collective-permute-done((bf16[16,2048]{1,0:T(8,128)(2,1)S(1)}, bf16[16,2048]{1,0:T(8,128)(2,1)S(1)}, u32[]{:S(2)}, u32[]{:S(2)}) %collective-permute-start.7) | collective-permute-done | bytes 65568 | tf_op jit(solution)/shard_map/ppermute | solution.py:24
  23.5 2.3 %gate_up.1 = (f32[16,2048]{1,0:T(8,128)S(1)}, bf16[16,1920]{1,0:T(8,128)(2,1)S(1)}, bf16[16,1920]{1,0:T(8,128)(2,1)S(1)}) custom-call(bf16[2,8,2048]{2,1,0:T(8,128)(2,1)S(1)} %copy-done.1, bf16[2048]{0:T(1024)(128)(2,1)S(1)} %copy-done.2, bf16[2048,3584]{1,0:T(8,128)(2,1)S(1)} %bitcast.3, bf16[2048,3584]{1,0:T(8,128)(2,1)S(1)} %bitcast.5, ...), custom_call_target="tpu_custom_call" | custom-call | tf_op jit(solution)/shard_map/gate_up/pallas_call | solution.py:371
  25.8 2.1 %collective-permute-start.10 = (bf16[16,1920]{1,0:T(8,128)(2,1)S(1)}, bf16[16,1920]{1,0:T(8,128)(2,1)S(1)}, u32[]{:S(2)}, u32[]{:S(2)}) collective-permute-start(bf16[16,1920]{1,0:T(8,128)(2,1)S(1)} %get-tuple-element.17.refs_0_), channel_id=1, source_target_pairs={{0,8},{4,12},{8,0},{12,4},{1,9},{5,13},{9,1},{13,5},{2,10},{6,14},... | collective-permute-start | bytes 184328 | tf_op jit(solution)/shard_map/ppermute | solution.py:24
  27.9 0.1 collective-permute-start.11
  28.0 1.4 %collective-permute-start.9 = (bf16[16,1920]{1,0:T(8,128)(2,1)S(1)}, bf16[16,1920]{1,0:T(8,128)(2,1)S(1)}, u32[]{:S(2)}, u32[]{:S(2)}) collective-permute-start(bf16[16,1920]{1,0:T(8,128)(2,1)S(1)} %get-tuple-element.18), channel_id=1, source_target_pairs={{0,4},{4,0},{8,12},{12,8},{1,5},{5,1},{9,13},{13,9},{2,6},{6,2},{1... | collective-permute-start | bytes 184328 | tf_op jit(solution)/shard_map/ppermute | solution.py:24
  29.4 2.3 %collective-permute-done.10.refs_2_ = bf16[16,1920]{1,0:T(8,128)(2,1)S(1)} collective-permute-done((bf16[16,1920]{1,0:T(8,128)(2,1)S(1)}, bf16[16,1920]{1,0:T(8,128)(2,1)S(1)}, u32[]{:S(2)}, u32[]{:S(2)}) %collective-permute-start.10) | collective-permute-done | bytes 61472 | tf_op jit(solution)/shard_map/ppermute | solution.py:24
  31.6 2.4 %collective-permute-done.11.refs_3_ = bf16[16,1920]{1,0:T(8,128)(2,1)S(1)} collective-permute-done((bf16[16,1920]{1,0:T(8,128)(2,1)S(1)}, bf16[16,1920]{1,0:T(8,128)(2,1)S(1)}, u32[]{:S(2)}, u32[]{:S(2)}) %collective-permute-start.11) | collective-permute-done | bytes 61472 | tf_op jit(solution)/shard_map/ppermute | solution.py:24
  34.0 0.1 activation.1.own
  34.2 0.6 %collective-permute-start.14 = (bf16[8,1792]{1,0:T(8,128)(2,1)S(1)}, bf16[8,1792]{1,0:T(8,128)(2,1)S(1)}, u32[]{:S(2)}, u32[]{:S(2)}) collective-permute-start(bf16[8,1792]{1,0:T(8,128)(2,1)S(1)} %activation.1.own), channel_id=1, source_target_pairs={{0,4},{4,0},{8,12},{12,8},{1,5},{5,1},{9,13},{13,9},{2,6},{6,2},{1... | collective-permute-start | bytes 86024 | tf_op jit(solution)/shard_map/ppermute | solution.py:24
  34.7 2.5 %collective-permute-start.13 = (bf16[8,1792]{1,0:T(8,128)(2,1)S(1)}, bf16[8,1792]{1,0:T(8,128)(2,1)S(1)}, u32[]{:S(2)}, u32[]{:S(2)}) collective-permute-start(bf16[8,1792]{1,0:T(8,128)(2,1)S(1)} %activation.1.own), channel_id=1, source_target_pairs={{0,20},{4,16},{8,28},{12,24},{16,4},{20,0},{24,12},{28,8},{1,21},{... | collective-permute-start | bytes 86024 | tf_op jit(solution)/shard_map/ppermute | solution.py:24
  37.2 0.5 %collective-permute-start.12 = (bf16[8,1792]{1,0:T(8,128)(2,1)S(1)}, bf16[8,1792]{1,0:T(8,128)(2,1)S(1)}, u32[]{:S(2)}, u32[]{:S(2)}) collective-permute-start(bf16[8,1792]{1,0:T(8,128)(2,1)S(1)} %activation.1.own), channel_id=1, source_target_pairs={{0,16},{16,0},{1,17},{17,1},{2,18},{18,2},{3,19},{19,3},{4,20},{20... | collective-permute-start | bytes 86024 | tf_op jit(solution)/shard_map/ppermute | solution.py:24
  37.7 0.4 collective-permute-done.14.received
  38.2 1.2 %down.2.refs_0_ = f32[16,2048]{1,0:T(8,128)S(1)} custom-call(bf16[16,1792]{1,0:T(8,128)(2,1)S(1)} %gather_act.3.act, bf16[3584,2048]{1,0:T(8,128)(2,1)S(1)} %bitcast.1), custom_call_target="tpu_custom_call" | custom-call | tf_op jit(solution)/shard_map/down/pallas_call | solution.py:398
  39.4 0.1 collective-permute-done.13.received
  39.5 1.6 %collective-permute-done.12.own = bf16[8,1792]{1,0:T(8,128)(2,1)S(1)} collective-permute-done((bf16[8,1792]{1,0:T(8,128)(2,1)S(1)}, bf16[8,1792]{1,0:T(8,128)(2,1)S(1)}, u32[]{:S(2)}, u32[]{:S(2)}) %collective-permute-start.12) | collective-permute-done | bytes 28704 | tf_op jit(solution)/shard_map/ppermute | solution.py:24
  41.1 1.2 %down.3.refs_0_ = bf16[16,2048]{1,0:T(8,128)(2,1)S(1)} custom-call(bf16[16,1792]{1,0:T(8,128)(2,1)S(1)} %gather_act.2.act, bf16[3584,2048]{1,0:T(8,128)(2,1)S(1)} %bitcast.1, f32[16,2048]{1,0:T(8,128)S(1)} %down.2.refs_0_), custom_call_target="tpu_custom_call" | custom-call | tf_op jit(solution)/shard_map/down/pallas_call | solution.py:398
  42.3 0.8 %collective-permute-start.16 = (bf16[16,2048]{1,0:T(8,128)(2,1)S(1)}, bf16[16,2048]{1,0:T(8,128)(2,1)S(1)}, u32[]{:S(2)}, u32[]{:S(2)}) collective-permute-start(bf16[16,2048]{1,0:T(8,128)(2,1)S(1)} %down.3.refs_0_), channel_id=1, source_target_pairs={{0,2},{1,3},{2,0},{3,1},{4,6},{5,7},{6,4},{7,5},{8,10},{9,11},{10,... | collective-permute-start | bytes 196616 | tf_op jit(solution)/shard_map/ppermute | solution.py:24
  43.1 1.0 %collective-permute-start.15 = (bf16[16,2048]{1,0:T(8,128)(2,1)S(1)}, bf16[16,2048]{1,0:T(8,128)(2,1)S(1)}, u32[]{:S(2)}, u32[]{:S(2)}) collective-permute-start(bf16[16,2048]{1,0:T(8,128)(2,1)S(1)} %down.3.refs_0_), channel_id=1, source_target_pairs={{0,1},{1,0},{2,3},{3,2},{4,5},{5,4},{6,7},{7,6},{8,9},{9,8},{10,11... | collective-permute-start | bytes 196616 | tf_op jit(solution)/shard_map/ppermute | solution.py:24
  44.1 2.1 %collective-permute-done.17.refs_3_ = bf16[16,2048]{1,0:T(8,128)(2,1)S(1)} collective-permute-done((bf16[16,2048]{1,0:T(8,128)(2,1)S(1)}, bf16[16,2048]{1,0:T(8,128)(2,1)S(1)}, u32[]{:S(2)}, u32[]{:S(2)}) %collective-permute-start.17) | collective-permute-done | bytes 65568 | tf_op jit(solution)/shard_map/ppermute | solution.py:24
  46.2 1.0 %collective-permute-done.16.refs_2_ = bf16[16,2048]{1,0:T(8,128)(2,1)S(1)} collective-permute-done((bf16[16,2048]{1,0:T(8,128)(2,1)S(1)}, bf16[16,2048]{1,0:T(8,128)(2,1)S(1)}, u32[]{:S(2)}, u32[]{:S(2)}) %collective-permute-start.16) | collective-permute-done | bytes 65568 | tf_op jit(solution)/shard_map/ppermute | solution.py:24
  47.2 0.0 collective-permute-done.15.refs_1_
  47.2 0.7 %final.1 = bf16[2,8,2048]{2,1,0:T(8,128)(2,1)} custom-call(f32[16,2048]{1,0:T(8,128)S(1)} %get-tuple-element.16.mid, bf16[16,2048]{1,0:T(8,128)(2,1)S(1)} %down.3.refs_0_, bf16[16,2048]{1,0:T(8,128)(2,1)S(1)} %collective-permute-done.15.refs_1_, bf16[16,2048]{1,0:T(8,128)(2,1)S(1)} %collective-permute-done.16.refs_2_, ...), custom_call_target="tpu_custom_call" | custom-call | tf_op jit(solution)/shard_map/final/pallas_call | solution.py:412
  (32 shorter events, 0.1 us)
Async XLA Ops:
  1.7 5.2 %collective-permute-start.1 = (f32[5,8,128]{2,1,0:T(8,128)S(1)}, f32[5,8,128]{2,1,0:T(8,128)S(1)}, u32[]{:S(2)}, u32[]{:S(2)}) collective-permute-start(f32[5,8,128]{2,1,0:T(8,128)S(1)} %get-tuple-element.14), channel_id=1, source_target_pairs={{0,2},{1,3},{2,0},{3,1},{4,6},{5,7},{6,4},{7,5},{8,10},{9,11},{10,... | collective-permute-start | bytes 61448 | tf_op jit(solution)/shard_map/ppermute | solution.py:24
  4.8 3.2 %collective-permute-start.2 = (f32[5,8,128]{2,1,0:T(8,128)S(1)}, f32[5,8,128]{2,1,0:T(8,128)S(1)}, u32[]{:S(2)}, u32[]{:S(2)}) collective-permute-start(f32[5,8,128]{2,1,0:T(8,128)S(1)} %get-tuple-element.15), channel_id=1, source_target_pairs={{0,3},{1,2},{2,1},{3,0},{4,7},{5,6},{6,5},{7,4},{8,11},{9,10},{10,... | collective-permute-start | bytes 61448 | tf_op jit(solution)/shard_map/ppermute | solution.py:24
  4.8 18.6 %slice-start.4 = ((s8[14680064]{0:T(1024)(128)(4,1)}), s8[4194304]{0:T(1024)(128)(4,1)S(1)}, s32[]{:S(2)}) async-start(s8[14680064]{0:T(1024)(128)(4,1)} %bitcast.2), calls=%async_computation.4 | async-start | bytes 8388608
  4.8 18.6 %slice-start.8 = ((s8[14680064]{0:T(1024)(128)(4,1)}), s8[4194304]{0:T(1024)(128)(4,1)S(1)}, s32[]{:S(2)}) async-start(s8[14680064]{0:T(1024)(128)(4,1)} %bitcast.4), calls=%async_computation.8 | async-start | bytes 8388608
  6.7 1.3 %collective-permute-start = (f32[5,8,128]{2,1,0:T(8,128)S(1)}, f32[5,8,128]{2,1,0:T(8,128)S(1)}, u32[]{:S(2)}, u32[]{:S(2)}) collective-permute-start(f32[5,8,128]{2,1,0:T(8,128)S(1)} %get-tuple-element.13), channel_id=1, source_target_pairs={{0,1},{1,0},{2,3},{3,2},{4,5},{5,4},{6,7},{7,6},{8,9},{9,8},{10,11... | collective-permute-start | bytes 61448 | tf_op jit(solution)/shard_map/ppermute | solution.py:24
  8.0 8.7 %copy-start = (bf16[1024,2048]{1,0:T(8,128)(2,1)S(1)}, bf16[1024,2048]{1,0:T(8,128)(2,1)}, u32[]{:S(2)}) copy-start(bf16[1024,2048]{1,0:T(8,128)(2,1)} %refs_4_.1) | copy-start | bytes 12582916
  8.0 15.4 %slice-start.5 = ((s8[14680064]{0:T(1024)(128)(4,1)}), s8[4194304]{0:T(1024)(128)(4,1)S(1)}, s32[]{:S(2)}) async-start(s8[14680064]{0:T(1024)(128)(4,1)} %bitcast.2), calls=%async_computation.5 | async-start | bytes 8388608
  8.0 15.4 %slice-start.6 = ((s8[14680064]{0:T(1024)(128)(4,1)}), s8[4194304]{0:T(1024)(128)(4,1)S(1)}, s32[]{:S(2)}) async-start(s8[14680064]{0:T(1024)(128)(4,1)} %bitcast.2), calls=%async_computation.6 | async-start | bytes 8388608
  8.0 15.4 %slice-start.7 = ((s8[14680064]{0:T(1024)(128)(4,1)}), s8[2097152]{0:T(1024)(128)(4,1)S(1)}, s32[]{:S(2)}) async-start(s8[14680064]{0:T(1024)(128)(4,1)} %bitcast.2), calls=%async_computation.7 | async-start | bytes 4194304
  8.0 15.4 %slice-start.9 = ((s8[14680064]{0:T(1024)(128)(4,1)}), s8[4194304]{0:T(1024)(128)(4,1)S(1)}, s32[]{:S(2)}) async-start(s8[14680064]{0:T(1024)(128)(4,1)} %bitcast.4), calls=%async_computation.9 | async-start | bytes 8388608
  8.0 15.4 %slice-start.10 = ((s8[14680064]{0:T(1024)(128)(4,1)}), s8[4194304]{0:T(1024)(128)(4,1)S(1)}, s32[]{:S(2)}) async-start(s8[14680064]{0:T(1024)(128)(4,1)} %bitcast.4), calls=%async_computation.10 | async-start | bytes 8388608
  8.0 15.4 %slice-start.11 = ((s8[14680064]{0:T(1024)(128)(4,1)}), s8[2097152]{0:T(1024)(128)(4,1)S(1)}, s32[]{:S(2)}) async-start(s8[14680064]{0:T(1024)(128)(4,1)} %bitcast.4), calls=%async_computation.11 | async-start | bytes 4194304
  8.0 15.4 %copy-start.1 = (bf16[2,8,2048]{2,1,0:T(8,128)(2,1)S(1)}, bf16[2,8,2048]{2,1,0:T(8,128)(2,1)}, u32[]{:S(2)}) copy-start(bf16[2,8,2048]{2,1,0:T(8,128)(2,1)} %residual.1) | copy-start | bytes 196612
  8.1 15.4 %copy-start.2 = (bf16[2048]{0:T(1024)(128)(2,1)S(1)}, bf16[2048]{0:T(1024)(128)(2,1)}, u32[]{:S(2)}) copy-start(bf16[2048]{0:T(1024)(128)(2,1)} %gains.1) | copy-start | bytes 12292
  8.2 5.5 %collective-permute-start.5 = (bf16[4,1024]{1,0:T(4,128)(2,1)S(1)}, bf16[4,1024]{1,0:T(4,128)(2,1)S(1)}, u32[]{:S(2)}, u32[]{:S(2)}) collective-permute-start(bf16[4,1024]{1,0:T(4,128)(2,1)S(1)} %combine.1.refs_0_), channel_id=1, source_target_pairs={{0,12},{4,8},{8,4},{12,0},{1,13},{5,9},{9,5},{13,1},{2,14},{6,10},... | collective-permute-start | bytes 24584 | tf_op jit(solution)/shard_map/ppermute | solution.py:24
  12.1 4.5 %collective-permute-start.4 = (bf16[4,1024]{1,0:T(4,128)(2,1)S(1)}, bf16[4,1024]{1,0:T(4,128)(2,1)S(1)}, u32[]{:S(2)}, u32[]{:S(2)}) collective-permute-start(bf16[4,1024]{1,0:T(4,128)(2,1)S(1)} %combine.1.refs_0_), channel_id=1, source_target_pairs={{0,8},{4,12},{8,0},{12,4},{1,9},{5,13},{9,1},{13,5},{2,10},{6,14},... | collective-permute-start | bytes 24584 | tf_op jit(solution)/shard_map/ppermute | solution.py:24
  12.1 4.5 %collective-permute-start.3 = (bf16[4,1024]{1,0:T(4,128)(2,1)S(1)}, bf16[4,1024]{1,0:T(4,128)(2,1)S(1)}, u32[]{:S(2)}, u32[]{:S(2)}) collective-permute-start(bf16[4,1024]{1,0:T(4,128)(2,1)S(1)} %combine.1.refs_0_), channel_id=1, source_target_pairs={{0,4},{4,0},{8,12},{12,8},{1,5},{5,1},{9,13},{13,9},{2,6},{6,2},{1... | collective-permute-start | bytes 24584 | tf_op jit(solution)/shard_map/ppermute | solution.py:24
  16.7 21.5 %slice-start = ((s8[14680064]{0:T(1024)(128)(4,1)}), s8[4194304]{0:T(1024)(128)(4,1)S(1)}, s32[]{:S(2)}) async-start(s8[14680064]{0:T(1024)(128)(4,1)} %bitcast), calls=%async_computation | async-start | bytes 8388608
  17.5 20.7 %slice-start.1 = ((s8[14680064]{0:T(1024)(128)(4,1)}), s8[4194304]{0:T(1024)(128)(4,1)S(1)}, s32[]{:S(2)}) async-start(s8[14680064]{0:T(1024)(128)(4,1)} %bitcast), calls=%async_computation.1 | async-start | bytes 8388608
  17.5 20.7 %slice-start.2 = ((s8[14680064]{0:T(1024)(128)(4,1)}), s8[4194304]{0:T(1024)(128)(4,1)S(1)}, s32[]{:S(2)}) async-start(s8[14680064]{0:T(1024)(128)(4,1)} %bitcast), calls=%async_computation.2 | async-start | bytes 8388608
  17.5 20.7 %slice-start.3 = ((s8[14680064]{0:T(1024)(128)(4,1)}), s8[2097152]{0:T(1024)(128)(4,1)S(1)}, s32[]{:S(2)}) async-start(s8[14680064]{0:T(1024)(128)(4,1)} %bitcast), calls=%async_computation.3 | async-start | bytes 4194304
  17.5 4.4 %collective-permute-start.8 = (bf16[16,2048]{1,0:T(8,128)(2,1)S(1)}, bf16[16,2048]{1,0:T(8,128)(2,1)S(1)}, u32[]{:S(2)}, u32[]{:S(2)}) collective-permute-start(bf16[16,2048]{1,0:T(8,128)(2,1)S(1)} %out_projection.1.refs_0_), channel_id=1, source_target_pairs={{0,3},{1,2},{2,1},{3,0},{4,7},{5,6},{6,5},{7,4},{8,11},{9,10},{10,... | collective-permute-start | bytes 196616 | tf_op jit(solution)/shard_map/ppermute | solution.py:24
  17.6 5.7 %collective-permute-start.7 = (bf16[16,2048]{1,0:T(8,128)(2,1)S(1)}, bf16[16,2048]{1,0:T(8,128)(2,1)S(1)}, u32[]{:S(2)}, u32[]{:S(2)}) collective-permute-start(bf16[16,2048]{1,0:T(8,128)(2,1)S(1)} %out_projection.1.refs_0_), channel_id=1, source_target_pairs={{0,2},{1,3},{2,0},{3,1},{4,6},{5,7},{6,4},{7,5},{8,10},{9,11},{10,... | collective-permute-start | bytes 196616 | tf_op jit(solution)/shard_map/ppermute | solution.py:24
  19.2 4.2 %collective-permute-start.6 = (bf16[16,2048]{1,0:T(8,128)(2,1)S(1)}, bf16[16,2048]{1,0:T(8,128)(2,1)S(1)}, u32[]{:S(2)}, u32[]{:S(2)}) collective-permute-start(bf16[16,2048]{1,0:T(8,128)(2,1)S(1)} %out_projection.1.refs_0_), channel_id=1, source_target_pairs={{0,1},{1,0},{2,3},{3,2},{4,5},{5,4},{6,7},{7,6},{8,9},{9,8},{10,11... | collective-permute-start | bytes 196616 | tf_op jit(solution)/shard_map/ppermute | solution.py:24
  25.8 5.8 %collective-permute-start.10 = (bf16[16,1920]{1,0:T(8,128)(2,1)S(1)}, bf16[16,1920]{1,0:T(8,128)(2,1)S(1)}, u32[]{:S(2)}, u32[]{:S(2)}) collective-permute-start(bf16[16,1920]{1,0:T(8,128)(2,1)S(1)} %get-tuple-element.17.refs_0_), channel_id=1, source_target_pairs={{0,8},{4,12},{8,0},{12,4},{1,9},{5,13},{9,1},{13,5},{2,10},{6,14},... | collective-permute-start | bytes 184328 | tf_op jit(solution)/shard_map/ppermute | solution.py:24
  27.9 6.1 %collective-permute-start.11 = (bf16[16,1920]{1,0:T(8,128)(2,1)S(1)}, bf16[16,1920]{1,0:T(8,128)(2,1)S(1)}, u32[]{:S(2)}, u32[]{:S(2)}) collective-permute-start(bf16[16,1920]{1,0:T(8,128)(2,1)S(1)} %get-tuple-element.18), channel_id=1, source_target_pairs={{0,12},{4,8},{8,4},{12,0},{1,13},{5,9},{9,5},{13,1},{2,14},{6,10},... | collective-permute-start | bytes 184328 | tf_op jit(solution)/shard_map/ppermute | solution.py:24
  28.0 6.1 %collective-permute-start.9 = (bf16[16,1920]{1,0:T(8,128)(2,1)S(1)}, bf16[16,1920]{1,0:T(8,128)(2,1)S(1)}, u32[]{:S(2)}, u32[]{:S(2)}) collective-permute-start(bf16[16,1920]{1,0:T(8,128)(2,1)S(1)} %get-tuple-element.18), channel_id=1, source_target_pairs={{0,4},{4,0},{8,12},{12,8},{1,5},{5,1},{9,13},{13,9},{2,6},{6,2},{1... | collective-permute-start | bytes 184328 | tf_op jit(solution)/shard_map/ppermute | solution.py:24
  34.2 3.9 %collective-permute-start.14 = (bf16[8,1792]{1,0:T(8,128)(2,1)S(1)}, bf16[8,1792]{1,0:T(8,128)(2,1)S(1)}, u32[]{:S(2)}, u32[]{:S(2)}) collective-permute-start(bf16[8,1792]{1,0:T(8,128)(2,1)S(1)} %activation.1.own), channel_id=1, source_target_pairs={{0,4},{4,0},{8,12},{12,8},{1,5},{5,1},{9,13},{13,9},{2,6},{6,2},{1... | collective-permute-start | bytes 86024 | tf_op jit(solution)/shard_map/ppermute | solution.py:24
  34.7 4.8 %collective-permute-start.13 = (bf16[8,1792]{1,0:T(8,128)(2,1)S(1)}, bf16[8,1792]{1,0:T(8,128)(2,1)S(1)}, u32[]{:S(2)}, u32[]{:S(2)}) collective-permute-start(bf16[8,1792]{1,0:T(8,128)(2,1)S(1)} %activation.1.own), channel_id=1, source_target_pairs={{0,20},{4,16},{8,28},{12,24},{16,4},{20,0},{24,12},{28,8},{1,21},{... | collective-permute-start | bytes 86024 | tf_op jit(solution)/shard_map/ppermute | solution.py:24
  37.2 3.9 %collective-permute-start.12 = (bf16[8,1792]{1,0:T(8,128)(2,1)S(1)}, bf16[8,1792]{1,0:T(8,128)(2,1)S(1)}, u32[]{:S(2)}, u32[]{:S(2)}) collective-permute-start(bf16[8,1792]{1,0:T(8,128)(2,1)S(1)} %activation.1.own), channel_id=1, source_target_pairs={{0,16},{16,0},{1,17},{17,1},{2,18},{18,2},{3,19},{19,3},{4,20},{20... | collective-permute-start | bytes 86024 | tf_op jit(solution)/shard_map/ppermute | solution.py:24
  42.3 3.9 %collective-permute-start.17 = (bf16[16,2048]{1,0:T(8,128)(2,1)S(1)}, bf16[16,2048]{1,0:T(8,128)(2,1)S(1)}, u32[]{:S(2)}, u32[]{:S(2)}) collective-permute-start(bf16[16,2048]{1,0:T(8,128)(2,1)S(1)} %down.3.refs_0_), channel_id=1, source_target_pairs={{0,3},{1,2},{2,1},{3,0},{4,7},{5,6},{6,5},{7,4},{8,11},{9,10},{10,... | collective-permute-start | bytes 196616 | tf_op jit(solution)/shard_map/ppermute | solution.py:24
  42.3 5.0 %collective-permute-start.16 = (bf16[16,2048]{1,0:T(8,128)(2,1)S(1)}, bf16[16,2048]{1,0:T(8,128)(2,1)S(1)}, u32[]{:S(2)}, u32[]{:S(2)}) collective-permute-start(bf16[16,2048]{1,0:T(8,128)(2,1)S(1)} %down.3.refs_0_), channel_id=1, source_target_pairs={{0,2},{1,3},{2,0},{3,1},{4,6},{5,7},{6,4},{7,5},{8,10},{9,11},{10,... | collective-permute-start | bytes 196616 | tf_op jit(solution)/shard_map/ppermute | solution.py:24
  43.1 4.1 %collective-permute-start.15 = (bf16[16,2048]{1,0:T(8,128)(2,1)S(1)}, bf16[16,2048]{1,0:T(8,128)(2,1)S(1)}, u32[]{:S(2)}, u32[]{:S(2)}) collective-permute-start(bf16[16,2048]{1,0:T(8,128)(2,1)S(1)} %down.3.refs_0_), channel_id=1, source_target_pairs={{0,1},{1,0},{2,3},{3,2},{4,5},{5,4},{6,7},{7,6},{8,9},{9,8},{10,11... | collective-permute-start | bytes 196616 | tf_op jit(solution)/shard_map/ppermute | solution.py:24

commit v7 on v6

--- a/solution.py
+++ b/solution.py
@@ -40,6 +40,12 @@
 
 def dot_t(a, b):
     return lax.dot_general(a, b, (((1,), (1,)), ((), ())), preferred_element_type=jnp.float32)
+
+
+def pieces(value):
+    first = value.astype(WIRE).astype(jnp.float32)
+    second = (value - first).astype(WIRE).astype(jnp.float32)
+    return first, second, value - first - second
 
 
 def call(kernel, out_shape, in_specs, scratch=(), limit=4, name=None, flops=None):
@@ -90,6 +96,7 @@
     hb = HEADS // cols
     inv_root = 1.0 / math.sqrt(HD)
     n = TOKENS * GROUP
+    cells = TOKENS * rows
     pairs = [(b, g) for b in range(rows) for g in range(heads)]
     for i in (0, 1, 2, 5, 3):
         copies[i].wait()
@@ -144,15 +151,18 @@
         for t in range(TOKENS):
             tb = t * rows + b
             part = slice(i * n + t * GROUP, i * n + (t + 1) * GROUP)
-            stats[g] = jnp.where(lane == 2 * tb, peak[part], stats[g])
-            stats[g] = jnp.where(lane == 2 * tb + 1, total[part], stats[g])
-            block = s[t * GROUP : (t + 1) * GROUP]
+            for i_piece, pair in enumerate(zip(pieces(peak[part]), pieces(total[part]))):
+                at = 2 * (cells * i_piece + tb)
+                stats[g] = jnp.where(lane == at, pair[0], stats[g])
+                stats[g] = jnp.where(lane == at + 1, pair[1], stats[g])
+            block = s[t * GROUP : (t + 1) * GROUP].astype(WIRE)
             if hb >= GROUP:
                 at = g * GROUP
                 packed[at // hb, tb, at % hb : at % hb + GROUP] = block
             else:
                 for j in range(GROUP // hb):
                     packed[g * (GROUP // hb) + j, tb] = block[j * hb : (j + 1) * hb]
+    stats = [block.astype(WIRE) for block in stats]
     for g in range(heads):
         if hb >= GROUP:
             at = g * GROUP
@@ -168,7 +178,9 @@
     parts, out = refs[:cols], refs[cols]
     cells = parts[0].shape[0] - 1
     hb = parts[0].shape[1]
-    stats = [p[cells] for p in parts]
+    stats = [p[cells].astype(jnp.float32) for p in parts]
+    n = 2 * cells
+    stats = [s[:, :n] + s[:, n : 2 * n] + s[:, 2 * n : 3 * n] for s in stats]
     attended = []
     for tb in range(cells):
         peaks = [s[:, 2 * tb : 2 * tb + 1] for s in stats]
@@ -176,7 +188,7 @@
         top = functools.reduce(jnp.maximum, peaks)
         scales = [jnp.exp(p - top) for p in peaks]
         total = tree_sum([t * s for t, s in zip(totals, scales)])
-        summed = tree_sum([p[tb] * s for p, s in zip(parts, scales)])
+        summed = tree_sum([p[tb].astype(jnp.float32) * s for p, s in zip(parts, scales)])
         attended.append(summed / total)
     rows = [
         jnp.concatenate([attended[tb][h : h + 1] for tb in range(cells)], axis=0) for h in range(hb)
@@ -220,17 +232,20 @@
 
 
 def in_pieces(squares):
-    first = squares.astype(WIRE).astype(jnp.float32)
-    second = (squares - first).astype(WIRE).astype(jnp.float32)
-    third = squares - first - second
     lane = lax.broadcasted_iota(jnp.int32, (squares.shape[0], HD), 1)
-    return jnp.where(
-        lane == 0, first, jnp.where(lane == 1, second, jnp.where(lane == 2, third, 0.0))
-    )
-
-
-def lift_kernel(groups, split, residual, gains, gate_weight, up_weight, *refs):
-    parts, (mid_out, keep, send, lifted, packed) = refs[:-5], refs[-5:]
+    result = jnp.zeros(lane.shape, jnp.float32)
+    for i, piece in enumerate(pieces(squares)):
+        result = jnp.where(lane == i, piece, result)
+    return result
+
+
+def add_kernel(first, second, out):
+    out[...] = (first[...].astype(jnp.float32) + second[...].astype(jnp.float32)).astype(out.dtype)
+
+
+def lift_kernel(groups, cols, split, residual, gains, gate_weight, up_weight, *refs):
+    parts, mid_out, (lifted, packed) = refs[:cols], refs[cols], refs[-2:]
+    outs = refs[cols + 1 : -2]
     hidden = gate_weight.shape[1] // split
     start = lax.axis_index("side") * hidden if split > 1 else 0
     half = packed.shape[1] // 2
@@ -253,12 +268,13 @@
 
     over_columns(hidden, body)
     bit = lax.axis_index("row") & 1
-    keep[...] = packed[bit].astype(keep.dtype)
-    send[...] = packed[1 - bit].astype(send.dtype)
+    mine, theirs = (packed[i].astype(outs[0].dtype) for i in (bit, 1 - bit))
+    for k, out in enumerate(outs):
+        out[...] = theirs if k % 2 else mine
 
 
 def act_kernel(model, *refs):
-    parts, out = refs[:-1], refs[-1]
+    parts, out = refs[:1] + refs[-2:0:-1], refs[-1]
     hidden = parts[0].shape[1] - HD
     cells = parts[0].shape[0] // 2
     values = [p[...].astype(jnp.float32) for p in parts]
@@ -335,7 +351,7 @@
     pad = -(-cells // 8) * 8
 
     sources = [query, new_keys, new_values, key_cache, value_cache]
-    message = shape((cells + 1, hb, HD), f32)
+    message = shape((cells + 1, hb, HD), WIRE)
     sources = [query, new_keys, new_values, key_cache, value_cache]
 
     def messages(far):
@@ -345,7 +361,7 @@
             [ANY_SPEC] * 6,
             [pltpu.VMEM((*a.shape[:2], a.shape[2] // 2), a.dtype) for a in sources]
             + [pltpu.SMEM(lengths.shape, lengths.dtype)]
-            + [pltpu.VMEM((cols // 2, *message.shape), f32), pltpu.SemaphoreType.DMA((6,))],
+            + [pltpu.VMEM((cols // 2, *message.shape), WIRE), pltpu.SemaphoreType.DMA((6,))],
             name="attention_far" if far else "attention_near",
         )(*[in_hbm(a) for a in [lengths, *sources]])
 
@@ -368,9 +384,9 @@
         [pltpu.VMEM((groups, pad, features), f32), pltpu.VMEM((m, features), bf16)],
         name="out_projection",
     )(*gathered, in_vmem(out_weight))
-    mid, keep, send = call(
-        functools.partial(lift_kernel, groups, split),
-        [shape((m, width_share), f32)] + [shape((m, hidden + HD), WIRE)] * 2,
+    mid, *sums = call(
+        functools.partial(lift_kernel, groups, cols, split),
+        [shape((m, width_share), f32)] + [shape((m, hidden + HD), WIRE)] * groups,
         [VMEM_SPEC] * (cols + 4),
         [pltpu.VMEM((m, width_share), bf16), pltpu.VMEM((2, m, hidden + HD), f32)],
         name="gate_up",
@@ -378,13 +394,13 @@
         in_vmem(residual), in_vmem(norm_gain), in_vmem(gate_weight), in_vmem(up_weight),
         *spread(partial, "col"),
     )
-    sums = [keep] + [partner((keep, send)[k % 2], "row", k) for k in range(1, groups)]
+    sums = sums[:1] + [partner(sums[k], "row", k) for k in range(1, groups)]
     act = call(
         functools.partial(act_kernel, model),
         shape((m // 2, hidden), bf16),
         [VMEM_SPEC] * groups,
         name="activation",
-    )(*sums)
+    )(sums[0], *sums[:0:-1])
     down_weight = in_vmem(down_weight)
 
     def down_part(same, from_row, other, before, result):
@@ -409,12 +425,18 @@
         down = down_part(partner(act, "side", 1), far, 1, [first], WIRE)
     else:
         down = down_part(act, near, 0, [], WIRE)
+    step = 1
+    while step < cols // 2:
+        down = call(add_kernel, shape(down.shape, WIRE), [VMEM_SPEC] * 2, name="add")(
+            down, partner(down, "col", 2 * step - 1)
+        )
+        step *= 2
     return call(
         functools.partial(final_kernel, groups),
         shape((TOKENS, total_rows, width_share), bf16),
-        [VMEM_SPEC] * (cols + 1),
+        [VMEM_SPEC] * 3,
         name="final",
-    )(mid, *spread(down, "col"))
+    )(mid, down, partner(down, "col", 2 * step - 1))
 
 
 def solution(mesh):

time: 48.1 us -> 48.8 us (1.015)
  waiting for transfers between devices: 18.7 us -> 19.7 us
    ppermute x18 -> x17, waiting for transfers between devices: 18.7 us -> 19.7 us  [partner(): lax.ppermute(value, axis, [(i, i ^ k) for i in range(lax.axis_size(axis))])]
    ppermute x18 -> x17, starting transfers between devices: 18.7 us -> 18.4 us  [partner(): lax.ppermute(value, axis, [(i, i ^ k) for i in range(lax.axis_size(axis))])]
    pallas_call x1 -> x2, Pallas kernels: 2.34 us -> 2.36 us  [the longest x1 2.34 us: shards(): call(functools.partial(lift_kernel, groups, cols, split), [shape((m, widt...]
  transfers between devices with their start and end apart: 18 -> 17, of which waited for: 12 -> 11; matrix products, arithmetic and copies ran while one was open for 0% -> 0% of each run, Pallas kernels for 6% -> 6%
where the time goes in v7:
time: 48.8 us; the launch traced here: 48.7 us
  waiting for transfers between devices  19.7 us (40%)
  starting transfers between devices  18.4 us (38%)
  Pallas kernels  10.3 us (21%)
    ppermute x17, waiting for transfers between devices, partner(): lax.ppermute(value, axis, [(i, i ^ k) for i in range(lax.axis_size(axis))])  19.7 us
    ppermute x17, starting transfers between devices, partner(): lax.ppermute(value, axis, [(i, i ^ k) for i in range(lax.axis_size(axis))])  18.4 us
    pallas_call x2, Pallas kernels, messages(): call(functools.partial(attention_kernel, cols, far), [message] * (cols //...  3.62 us
    pallas_call x2, Pallas kernels, down_part(): call(functools.partial(down_kernel, other), shape((m, width_share), resul...  2.37 us
    pallas_call x1, Pallas kernels, shards(): call(functools.partial(lift_kernel, groups, cols, split), [shape((m, widt...  2.34 us
  transfers between devices with their start and end apart: 17, of which 11 were waited for; matrix products, arithmetic and copies ran while one was open for 0% of the time, Pallas kernels for 6%

profile of v7, /device:TPU:0, one launch (start us, length us, event | category | flops | bytes accessed | tf_op | source)
XLA Modules:
  0.0 48.7 jit_solution(7729356189450038420)
XLA Ops:
  0.0 1.7 %attention_far.1 = (bf16[5,8,128]{2,1,0:T(8,128)(2,1)S(1)}, bf16[5,8,128]{2,1,0:T(8,128)(2,1)S(1)}) custom-call(s32[2]{0:T(128)} %lengths.3, bf16[2,2,4096]{2,1,0:T(2,128)(2,1)} %rest_0_.3, bf16[2,2,512]{2,1,0:T(2,128)(2,1)} %rest_1_.3, bf16[2,2,512]{2,1,0:T(2,128)(2,1)} %rest_2_.3, bf16[2,384,512]{2,1,0:T(8,128)(2,1)} %rest_3_.3, bf16[2,384,512]{2,1,0:T(8,128)(2,1)} %rest_4_.3), custom_call_target="tpu_custom_call" | custom-call | tf_op jit(solution)/shard_map/attention_far/pallas_call | solution.py:358
  1.7 3.0 %collective-permute-start.1 = (bf16[5,8,128]{2,1,0:T(8,128)(2,1)S(1)}, bf16[5,8,128]{2,1,0:T(8,128)(2,1)S(1)}, u32[]{:S(2)}, u32[]{:S(2)}) collective-permute-start(bf16[5,8,128]{2,1,0:T(8,128)(2,1)S(1)} %get-tuple-element.16), channel_id=1, source_target_pairs={{0,2},{1,3},{2,0},{3,1},{4,6},{5,7},{6,4},{7,5},{8,10},{9,11},{10,... | collective-permute-start | bytes 30728 | tf_op jit(solution)/shard_map/ppermute | solution.py:24
  4.8 0.0 collective-permute-start.2
  4.8 1.9 %attention_near.1 = (bf16[5,8,128]{2,1,0:T(8,128)(2,1)S(1)}, bf16[5,8,128]{2,1,0:T(8,128)(2,1)S(1)}) custom-call(s32[2]{0:T(128)} %lengths.3, bf16[2,2,4096]{2,1,0:T(2,128)(2,1)} %rest_0_.3, bf16[2,2,512]{2,1,0:T(2,128)(2,1)} %rest_1_.3, bf16[2,2,512]{2,1,0:T(2,128)(2,1)} %rest_2_.3, bf16[2,384,512]{2,1,0:T(8,128)(2,1)} %rest_3_.3, bf16[2,384,512]{2,1,0:T(8,128)(2,1)} %rest_4_.3), custom_call_target="tpu_custom_call" | custom-call | tf_op jit(solution)/shard_map/attention_near/pallas_call | solution.py:358
  6.7 0.3 collective-permute-start
  6.9 0.0 collective-permute-done.1.refs_2_
  6.9 0.9 %collective-permute-done.2.refs_3_ = bf16[5,8,128]{2,1,0:T(8,128)(2,1)S(1)} collective-permute-done((bf16[5,8,128]{2,1,0:T(8,128)(2,1)S(1)}, bf16[5,8,128]{2,1,0:T(8,128)(2,1)S(1)}, u32[]{:S(2)}, u32[]{:S(2)}) %collective-permute-start.2) | collective-permute-done | bytes 10272 | tf_op jit(solution)/shard_map/ppermute | solution.py:24
  7.9 0.0 collective-permute-done.refs_1_
  7.9 0.0 slice-start.9
  7.9 0.0 slice-start.10
  7.9 0.0 slice-start.11
  8.0 0.0 copy-start.1
  8.0 0.0 copy-start.2
  8.0 0.2 combine.1.refs_0_
  8.2 3.9 %collective-permute-start.5 = (bf16[4,1024]{1,0:T(4,128)(2,1)S(1)}, bf16[4,1024]{1,0:T(4,128)(2,1)S(1)}, u32[]{:S(2)}, u32[]{:S(2)}) collective-permute-start(bf16[4,1024]{1,0:T(4,128)(2,1)S(1)} %combine.1.refs_0_), channel_id=1, source_target_pairs={{0,12},{4,8},{8,4},{12,0},{1,13},{5,9},{9,5},{13,1},{2,14},{6,10},... | collective-permute-start | bytes 24584 | tf_op jit(solution)/shard_map/ppermute | solution.py:24
  12.2 0.0 collective-permute-start.4
  12.2 0.6 %collective-permute-start.3 = (bf16[4,1024]{1,0:T(4,128)(2,1)S(1)}, bf16[4,1024]{1,0:T(4,128)(2,1)S(1)}, u32[]{:S(2)}, u32[]{:S(2)}) collective-permute-start(bf16[4,1024]{1,0:T(4,128)(2,1)S(1)} %combine.1.refs_0_), channel_id=1, source_target_pairs={{0,4},{4,0},{8,12},{12,8},{1,5},{5,1},{9,13},{13,9},{2,6},{6,2},{1... | collective-permute-start | bytes 24584 | tf_op jit(solution)/shard_map/ppermute | solution.py:24
  12.8 1.0 %collective-permute-done.5.refs_3_ = bf16[4,1024]{1,0:T(4,128)(2,1)S(1)} collective-permute-done((bf16[4,1024]{1,0:T(4,128)(2,1)S(1)}, bf16[4,1024]{1,0:T(4,128)(2,1)S(1)}, u32[]{:S(2)}, u32[]{:S(2)}) %collective-permute-start.5) | collective-permute-done | bytes 8224 | tf_op jit(solution)/shard_map/ppermute | solution.py:24
  13.8 2.9 %collective-permute-done.4.refs_2_ = bf16[4,1024]{1,0:T(4,128)(2,1)S(1)} collective-permute-done((bf16[4,1024]{1,0:T(4,128)(2,1)S(1)}, bf16[4,1024]{1,0:T(4,128)(2,1)S(1)}, u32[]{:S(2)}, u32[]{:S(2)}) %collective-permute-start.4) | collective-permute-done | bytes 8224 | tf_op jit(solution)/shard_map/ppermute | solution.py:24
  16.7 0.0 collective-permute-done.3.refs_1_
  16.7 0.8 %out_projection.1.refs_0_ = bf16[16,2048]{1,0:T(8,128)(2,1)S(1)} custom-call(bf16[4,1024]{1,0:T(4,128)(2,1)S(1)} %combine.1.refs_0_, bf16[4,1024]{1,0:T(4,128)(2,1)S(1)} %collective-permute-done.3.refs_1_, bf16[4,1024]{1,0:T(4,128)(2,1)S(1)} %collective-permute-done.4.refs_2_, bf16[4,1024]{1,0:T(4,128)(2,1)S(1)} %collective-permute-done.5.refs_3_, ...), custom_call_target="tpu_custom_call" | custom-call | tf_op jit(solution)/shard_map/out_projection/pallas_call | solution.py:380
  17.6 0.1 collective-permute-start.8
  17.7 1.5 %collective-permute-start.7 = (bf16[16,2048]{1,0:T(8,128)(2,1)S(1)}, bf16[16,2048]{1,0:T(8,128)(2,1)S(1)}, u32[]{:S(2)}, u32[]{:S(2)}) collective-permute-start(bf16[16,2048]{1,0:T(8,128)(2,1)S(1)} %out_projection.1.refs_0_), channel_id=1, source_target_pairs={{0,2},{1,3},{2,0},{3,1},{4,6},{5,7},{6,4},{7,5},{8,10},{9,11},{10,... | collective-permute-start | bytes 196616 | tf_op jit(solution)/shard_map/ppermute | solution.py:24
  19.2 0.3 collective-permute-start.6
  19.5 2.5 %collective-permute-done.8.refs_3_ = bf16[16,2048]{1,0:T(8,128)(2,1)S(1)} collective-permute-done((bf16[16,2048]{1,0:T(8,128)(2,1)S(1)}, bf16[16,2048]{1,0:T(8,128)(2,1)S(1)}, u32[]{:S(2)}, u32[]{:S(2)}) %collective-permute-start.8) | collective-permute-done | bytes 65568 | tf_op jit(solution)/shard_map/ppermute | solution.py:24
  21.9 1.5 %collective-permute-done.7.refs_2_ = bf16[16,2048]{1,0:T(8,128)(2,1)S(1)} collective-permute-done((bf16[16,2048]{1,0:T(8,128)(2,1)S(1)}, bf16[16,2048]{1,0:T(8,128)(2,1)S(1)}, u32[]{:S(2)}, u32[]{:S(2)}) %collective-permute-start.7) | collective-permute-done | bytes 65568 | tf_op jit(solution)/shard_map/ppermute | solution.py:24
  23.4 0.0 collective-permute-done.6.refs_1_
  23.5 2.3 %gate_up.1 = (f32[16,2048]{1,0:T(8,128)S(1)}, bf16[16,1920]{1,0:T(8,128)(2,1)S(1)}, bf16[16,1920]{1,0:T(8,128)(2,1)S(1)}, bf16[16,1920]{1,0:T(8,128)(2,1)S(1)}, bf16[16,1920]{1,0:T(8,128)(2,1)S(1)}) custom-call(bf16[2,8,2048]{2,1,0:T(8,128)(2,1)S(1)} %copy-done.1, bf16[2048]{0:T(1024)(128)(2,1)S(1)} %copy-done.2, bf16[2048,3584]{1,0:T(8,128)(2,1)S(1)} %bitcast.3, ...), custom_call_target="tpu_custom_call" | custom-call | tf_op jit(solution)/shard_map/gate_up/pallas_call | solution.py:387
  25.9 1.5 %collective-permute-start.9 = (bf16[16,1920]{1,0:T(8,128)(2,1)S(1)}, bf16[16,1920]{1,0:T(8,128)(2,1)S(1)}, u32[]{:S(2)}, u32[]{:S(2)}) collective-permute-start(bf16[16,1920]{1,0:T(8,128)(2,1)S(1)} %get-tuple-element.20), channel_id=1, source_target_pairs={{0,12},{4,8},{8,4},{12,0},{1,13},{5,9},{9,5},{13,1},{2,14},{6,10},... | collective-permute-start | bytes 184328 | tf_op jit(solution)/shard_map/ppermute | solution.py:24
  27.4 0.6 %collective-permute-start.10 = (bf16[16,1920]{1,0:T(8,128)(2,1)S(1)}, bf16[16,1920]{1,0:T(8,128)(2,1)S(1)}, u32[]{:S(2)}, u32[]{:S(2)}) collective-permute-start(bf16[16,1920]{1,0:T(8,128)(2,1)S(1)} %get-tuple-element.21), channel_id=1, source_target_pairs={{0,8},{4,12},{8,0},{12,4},{1,9},{5,13},{9,1},{13,5},{2,10},{6,14},... | collective-permute-start | bytes 184328 | tf_op jit(solution)/shard_map/ppermute | solution.py:24
  28.0 2.3 %collective-permute-start.11 = (bf16[16,1920]{1,0:T(8,128)(2,1)S(1)}, bf16[16,1920]{1,0:T(8,128)(2,1)S(1)}, u32[]{:S(2)}, u32[]{:S(2)}) collective-permute-start(bf16[16,1920]{1,0:T(8,128)(2,1)S(1)} %get-tuple-element.22), channel_id=1, source_target_pairs={{0,4},{4,0},{8,12},{12,8},{1,5},{5,1},{9,13},{13,9},{2,6},{6,2},{1... | collective-permute-start | bytes 184328 | tf_op jit(solution)/shard_map/ppermute | solution.py:24
  30.3 2.3 %collective-permute-done.9.refs_1_ = bf16[16,1920]{1,0:T(8,128)(2,1)S(1)} collective-permute-done((bf16[16,1920]{1,0:T(8,128)(2,1)S(1)}, bf16[16,1920]{1,0:T(8,128)(2,1)S(1)}, u32[]{:S(2)}, u32[]{:S(2)}) %collective-permute-start.9) | collective-permute-done | bytes 61472 | tf_op jit(solution)/shard_map/ppermute | solution.py:24
  32.6 1.7 %collective-permute-done.10.refs_2_ = bf16[16,1920]{1,0:T(8,128)(2,1)S(1)} collective-permute-done((bf16[16,1920]{1,0:T(8,128)(2,1)S(1)}, bf16[16,1920]{1,0:T(8,128)(2,1)S(1)}, u32[]{:S(2)}, u32[]{:S(2)}) %collective-permute-start.10) | collective-permute-done | bytes 61472 | tf_op jit(solution)/shard_map/ppermute | solution.py:24
  34.3 0.0 collective-permute-done.11.refs_3_
  34.3 0.1 activation.1.own
  34.5 0.3 collective-permute-start.14
  34.8 2.7 %collective-permute-start.13 = (bf16[8,1792]{1,0:T(8,128)(2,1)S(1)}, bf16[8,1792]{1,0:T(8,128)(2,1)S(1)}, u32[]{:S(2)}, u32[]{:S(2)}) collective-permute-start(bf16[8,1792]{1,0:T(8,128)(2,1)S(1)} %activation.1.own), channel_id=1, source_target_pairs={{0,20},{4,16},{8,28},{12,24},{16,4},{20,0},{24,12},{28,8},{1,21},{... | collective-permute-start | bytes 86024 | tf_op jit(solution)/shard_map/ppermute | solution.py:24
  37.5 0.5 %collective-permute-start.12 = (bf16[8,1792]{1,0:T(8,128)(2,1)S(1)}, bf16[8,1792]{1,0:T(8,128)(2,1)S(1)}, u32[]{:S(2)}, u32[]{:S(2)}) collective-permute-start(bf16[8,1792]{1,0:T(8,128)(2,1)S(1)} %activation.1.own), channel_id=1, source_target_pairs={{0,16},{16,0},{1,17},{17,1},{2,18},{18,2},{3,19},{19,3},{4,20},{20... | collective-permute-start | bytes 86024 | tf_op jit(solution)/shard_map/ppermute | solution.py:24
  38.0 0.7 %collective-permute-done.14.received = bf16[8,1792]{1,0:T(8,128)(2,1)S(1)} collective-permute-done((bf16[8,1792]{1,0:T(8,128)(2,1)S(1)}, bf16[8,1792]{1,0:T(8,128)(2,1)S(1)}, u32[]{:S(2)}, u32[]{:S(2)}) %collective-permute-start.14) | collective-permute-done | bytes 28704 | tf_op jit(solution)/shard_map/ppermute | solution.py:24
  38.8 1.2 %down.2.refs_0_ = f32[16,2048]{1,0:T(8,128)S(1)} custom-call(bf16[16,1792]{1,0:T(8,128)(2,1)S(1)} %gather_act.3.act, bf16[3584,2048]{1,0:T(8,128)(2,1)S(1)} %bitcast.1), custom_call_target="tpu_custom_call" | custom-call | tf_op jit(solution)/shard_map/down/pallas_call | solution.py:414
  39.9 0.0 collective-permute-done.13.received
  39.9 1.4 %collective-permute-done.12.own = bf16[8,1792]{1,0:T(8,128)(2,1)S(1)} collective-permute-done((bf16[8,1792]{1,0:T(8,128)(2,1)S(1)}, bf16[8,1792]{1,0:T(8,128)(2,1)S(1)}, u32[]{:S(2)}, u32[]{:S(2)}) %collective-permute-start.12) | collective-permute-done | bytes 28704 | tf_op jit(solution)/shard_map/ppermute | solution.py:24
  41.4 1.2 %down.3.first = bf16[16,2048]{1,0:T(8,128)(2,1)S(1)} custom-call(bf16[16,1792]{1,0:T(8,128)(2,1)S(1)} %gather_act.2.act, bf16[3584,2048]{1,0:T(8,128)(2,1)S(1)} %bitcast.1, f32[16,2048]{1,0:T(8,128)S(1)} %down.2.refs_0_), custom_call_target="tpu_custom_call" | custom-call | tf_op jit(solution)/shard_map/down/pallas_call | solution.py:414
  42.6 0.0 collective-permute-start.15
  42.6 1.3 %collective-permute-done.15.second = bf16[16,2048]{1,0:T(8,128)(2,1)S(1)} collective-permute-done((bf16[16,2048]{1,0:T(8,128)(2,1)S(1)}, bf16[16,2048]{1,0:T(8,128)(2,1)S(1)}, u32[]{:S(2)}, u32[]{:S(2)}) %collective-permute-start.15) | collective-permute-done | bytes 65568 | tf_op jit(solution)/shard_map/ppermute | solution.py:24
  43.9 0.6 %collective-permute-start.16 = (bf16[16,2048]{1,0:T(8,128)(2,1)S(1)}, bf16[16,2048]{1,0:T(8,128)(2,1)S(1)}, u32[]{:S(2)}, u32[]{:S(2)}) collective-permute-start(bf16[16,2048]{1,0:T(8,128)(2,1)S(1)} %add.1.refs_0_), channel_id=1, source_target_pairs={{0,3},{1,2},{2,1},{3,0},{4,7},{5,6},{6,5},{7,4},{8,11},{9,10},{10,... | collective-permute-start | bytes 196616 | tf_op jit(solution)/shard_map/ppermute | solution.py:24
  44.5 3.5 %collective-permute-done.16.refs_1_ = bf16[16,2048]{1,0:T(8,128)(2,1)S(1)} collective-permute-done((bf16[16,2048]{1,0:T(8,128)(2,1)S(1)}, bf16[16,2048]{1,0:T(8,128)(2,1)S(1)}, u32[]{:S(2)}, u32[]{:S(2)}) %collective-permute-start.16) | collective-permute-done | bytes 65568 | tf_op jit(solution)/shard_map/ppermute | solution.py:24
  48.0 0.7 %final.1 = bf16[2,8,2048]{2,1,0:T(8,128)(2,1)} custom-call(f32[16,2048]{1,0:T(8,128)S(1)} %get-tuple-element.18.mid, bf16[16,2048]{1,0:T(8,128)(2,1)S(1)} %add.1.refs_0_, bf16[16,2048]{1,0:T(8,128)(2,1)S(1)} %collective-permute-done.16.refs_1_), custom_call_target="tpu_custom_call" | custom-call | tf_op jit(solution)/shard_map/final/pallas_call | solution.py:434
  (31 shorter events, 0.1 us)
Async XLA Ops:
  1.7 5.2 %collective-permute-start.1 = (bf16[5,8,128]{2,1,0:T(8,128)(2,1)S(1)}, bf16[5,8,128]{2,1,0:T(8,128)(2,1)S(1)}, u32[]{:S(2)}, u32[]{:S(2)}) collective-permute-start(bf16[5,8,128]{2,1,0:T(8,128)(2,1)S(1)} %get-tuple-element.16), channel_id=1, source_target_pairs={{0,2},{1,3},{2,0},{3,1},{4,6},{5,7},{6,4},{7,5},{8,10},{9,11},{10,... | collective-permute-start | bytes 30728 | tf_op jit(solution)/shard_map/ppermute | solution.py:24
  4.8 3.1 %collective-permute-start.2 = (bf16[5,8,128]{2,1,0:T(8,128)(2,1)S(1)}, bf16[5,8,128]{2,1,0:T(8,128)(2,1)S(1)}, u32[]{:S(2)}, u32[]{:S(2)}) collective-permute-start(bf16[5,8,128]{2,1,0:T(8,128)(2,1)S(1)} %get-tuple-element.17), channel_id=1, source_target_pairs={{0,3},{1,2},{2,1},{3,0},{4,7},{5,6},{6,5},{7,4},{8,11},{9,10},{10,... | collective-permute-start | bytes 30728 | tf_op jit(solution)/shard_map/ppermute | solution.py:24
  4.8 18.6 %slice-start.4 = ((s8[14680064]{0:T(1024)(128)(4,1)}), s8[4194304]{0:T(1024)(128)(4,1)S(1)}, s32[]{:S(2)}) async-start(s8[14680064]{0:T(1024)(128)(4,1)} %bitcast.2), calls=%async_computation.4 | async-start | bytes 8388608
  4.8 18.6 %slice-start.8 = ((s8[14680064]{0:T(1024)(128)(4,1)}), s8[4194304]{0:T(1024)(128)(4,1)S(1)}, s32[]{:S(2)}) async-start(s8[14680064]{0:T(1024)(128)(4,1)} %bitcast.4), calls=%async_computation.8 | async-start | bytes 8388608
  6.7 1.2 %collective-permute-start = (bf16[5,8,128]{2,1,0:T(8,128)(2,1)S(1)}, bf16[5,8,128]{2,1,0:T(8,128)(2,1)S(1)}, u32[]{:S(2)}, u32[]{:S(2)}) collective-permute-start(bf16[5,8,128]{2,1,0:T(8,128)(2,1)S(1)} %get-tuple-element.15), channel_id=1, source_target_pairs={{0,1},{1,0},{2,3},{3,2},{4,5},{5,4},{6,7},{7,6},{8,9},{9,8},{10,11... | collective-permute-start | bytes 30728 | tf_op jit(solution)/shard_map/ppermute | solution.py:24
  7.9 8.8 %copy-start = (bf16[1024,2048]{1,0:T(8,128)(2,1)S(1)}, bf16[1024,2048]{1,0:T(8,128)(2,1)}, u32[]{:S(2)}) copy-start(bf16[1024,2048]{1,0:T(8,128)(2,1)} %refs_4_.1) | copy-start | bytes 12582916
  7.9 15.5 %slice-start.5 = ((s8[14680064]{0:T(1024)(128)(4,1)}), s8[4194304]{0:T(1024)(128)(4,1)S(1)}, s32[]{:S(2)}) async-start(s8[14680064]{0:T(1024)(128)(4,1)} %bitcast.2), calls=%async_computation.5 | async-start | bytes 8388608
  7.9 15.5 %slice-start.6 = ((s8[14680064]{0:T(1024)(128)(4,1)}), s8[4194304]{0:T(1024)(128)(4,1)S(1)}, s32[]{:S(2)}) async-start(s8[14680064]{0:T(1024)(128)(4,1)} %bitcast.2), calls=%async_computation.6 | async-start | bytes 8388608
  7.9 15.5 %slice-start.7 = ((s8[14680064]{0:T(1024)(128)(4,1)}), s8[2097152]{0:T(1024)(128)(4,1)S(1)}, s32[]{:S(2)}) async-start(s8[14680064]{0:T(1024)(128)(4,1)} %bitcast.2), calls=%async_computation.7 | async-start | bytes 4194304
  7.9 15.5 %slice-start.9 = ((s8[14680064]{0:T(1024)(128)(4,1)}), s8[4194304]{0:T(1024)(128)(4,1)S(1)}, s32[]{:S(2)}) async-start(s8[14680064]{0:T(1024)(128)(4,1)} %bitcast.4), calls=%async_computation.9 | async-start | bytes 8388608
  7.9 15.5 %slice-start.10 = ((s8[14680064]{0:T(1024)(128)(4,1)}), s8[4194304]{0:T(1024)(128)(4,1)S(1)}, s32[]{:S(2)}) async-start(s8[14680064]{0:T(1024)(128)(4,1)} %bitcast.4), calls=%async_computation.10 | async-start | bytes 8388608
  7.9 15.5 %slice-start.11 = ((s8[14680064]{0:T(1024)(128)(4,1)}), s8[2097152]{0:T(1024)(128)(4,1)S(1)}, s32[]{:S(2)}) async-start(s8[14680064]{0:T(1024)(128)(4,1)} %bitcast.4), calls=%async_computation.11 | async-start | bytes 4194304
  8.0 15.5 %copy-start.1 = (bf16[2,8,2048]{2,1,0:T(8,128)(2,1)S(1)}, bf16[2,8,2048]{2,1,0:T(8,128)(2,1)}, u32[]{:S(2)}) copy-start(bf16[2,8,2048]{2,1,0:T(8,128)(2,1)} %residual.1) | copy-start | bytes 196612
  8.0 15.5 %copy-start.2 = (bf16[2048]{0:T(1024)(128)(2,1)S(1)}, bf16[2048]{0:T(1024)(128)(2,1)}, u32[]{:S(2)}) copy-start(bf16[2048]{0:T(1024)(128)(2,1)} %gains.1) | copy-start | bytes 12292
  8.2 5.6 %collective-permute-start.5 = (bf16[4,1024]{1,0:T(4,128)(2,1)S(1)}, bf16[4,1024]{1,0:T(4,128)(2,1)S(1)}, u32[]{:S(2)}, u32[]{:S(2)}) collective-permute-start(bf16[4,1024]{1,0:T(4,128)(2,1)S(1)} %combine.1.refs_0_), channel_id=1, source_target_pairs={{0,12},{4,8},{8,4},{12,0},{1,13},{5,9},{9,5},{13,1},{2,14},{6,10},... | collective-permute-start | bytes 24584 | tf_op jit(solution)/shard_map/ppermute | solution.py:24
  12.2 4.5 %collective-permute-start.4 = (bf16[4,1024]{1,0:T(4,128)(2,1)S(1)}, bf16[4,1024]{1,0:T(4,128)(2,1)S(1)}, u32[]{:S(2)}, u32[]{:S(2)}) collective-permute-start(bf16[4,1024]{1,0:T(4,128)(2,1)S(1)} %combine.1.refs_0_), channel_id=1, source_target_pairs={{0,8},{4,12},{8,0},{12,4},{1,9},{5,13},{9,1},{13,5},{2,10},{6,14},... | collective-permute-start | bytes 24584 | tf_op jit(solution)/shard_map/ppermute | solution.py:24
  12.2 4.5 %collective-permute-start.3 = (bf16[4,1024]{1,0:T(4,128)(2,1)S(1)}, bf16[4,1024]{1,0:T(4,128)(2,1)S(1)}, u32[]{:S(2)}, u32[]{:S(2)}) collective-permute-start(bf16[4,1024]{1,0:T(4,128)(2,1)S(1)} %combine.1.refs_0_), channel_id=1, source_target_pairs={{0,4},{4,0},{8,12},{12,8},{1,5},{5,1},{9,13},{13,9},{2,6},{6,2},{1... | collective-permute-start | bytes 24584 | tf_op jit(solution)/shard_map/ppermute | solution.py:24
  16.7 22.0 %slice-start = ((s8[14680064]{0:T(1024)(128)(4,1)}), s8[4194304]{0:T(1024)(128)(4,1)S(1)}, s32[]{:S(2)}) async-start(s8[14680064]{0:T(1024)(128)(4,1)} %bitcast), calls=%async_computation | async-start | bytes 8388608
  17.5 21.2 %slice-start.1 = ((s8[14680064]{0:T(1024)(128)(4,1)}), s8[4194304]{0:T(1024)(128)(4,1)S(1)}, s32[]{:S(2)}) async-start(s8[14680064]{0:T(1024)(128)(4,1)} %bitcast), calls=%async_computation.1 | async-start | bytes 8388608
  17.5 21.2 %slice-start.2 = ((s8[14680064]{0:T(1024)(128)(4,1)}), s8[4194304]{0:T(1024)(128)(4,1)S(1)}, s32[]{:S(2)}) async-start(s8[14680064]{0:T(1024)(128)(4,1)} %bitcast), calls=%async_computation.2 | async-start | bytes 8388608
  17.5 21.2 %slice-start.3 = ((s8[14680064]{0:T(1024)(128)(4,1)}), s8[2097152]{0:T(1024)(128)(4,1)S(1)}, s32[]{:S(2)}) async-start(s8[14680064]{0:T(1024)(128)(4,1)} %bitcast), calls=%async_computation.3 | async-start | bytes 4194304
  17.6 4.4 %collective-permute-start.8 = (bf16[16,2048]{1,0:T(8,128)(2,1)S(1)}, bf16[16,2048]{1,0:T(8,128)(2,1)S(1)}, u32[]{:S(2)}, u32[]{:S(2)}) collective-permute-start(bf16[16,2048]{1,0:T(8,128)(2,1)S(1)} %out_projection.1.refs_0_), channel_id=1, source_target_pairs={{0,3},{1,2},{2,1},{3,0},{4,7},{5,6},{6,5},{7,4},{8,11},{9,10},{10,... | collective-permute-start | bytes 196616 | tf_op jit(solution)/shard_map/ppermute | solution.py:24
  17.7 5.7 %collective-permute-start.7 = (bf16[16,2048]{1,0:T(8,128)(2,1)S(1)}, bf16[16,2048]{1,0:T(8,128)(2,1)S(1)}, u32[]{:S(2)}, u32[]{:S(2)}) collective-permute-start(bf16[16,2048]{1,0:T(8,128)(2,1)S(1)} %out_projection.1.refs_0_), channel_id=1, source_target_pairs={{0,2},{1,3},{2,0},{3,1},{4,6},{5,7},{6,4},{7,5},{8,10},{9,11},{10,... | collective-permute-start | bytes 196616 | tf_op jit(solution)/shard_map/ppermute | solution.py:24
  19.2 4.2 %collective-permute-start.6 = (bf16[16,2048]{1,0:T(8,128)(2,1)S(1)}, bf16[16,2048]{1,0:T(8,128)(2,1)S(1)}, u32[]{:S(2)}, u32[]{:S(2)}) collective-permute-start(bf16[16,2048]{1,0:T(8,128)(2,1)S(1)} %out_projection.1.refs_0_), channel_id=1, source_target_pairs={{0,1},{1,0},{2,3},{3,2},{4,5},{5,4},{6,7},{7,6},{8,9},{9,8},{10,11... | collective-permute-start | bytes 196616 | tf_op jit(solution)/shard_map/ppermute | solution.py:24
  25.9 6.8 %collective-permute-start.9 = (bf16[16,1920]{1,0:T(8,128)(2,1)S(1)}, bf16[16,1920]{1,0:T(8,128)(2,1)S(1)}, u32[]{:S(2)}, u32[]{:S(2)}) collective-permute-start(bf16[16,1920]{1,0:T(8,128)(2,1)S(1)} %get-tuple-element.20), channel_id=1, source_target_pairs={{0,12},{4,8},{8,4},{12,0},{1,13},{5,9},{9,5},{13,1},{2,14},{6,10},... | collective-permute-start | bytes 184328 | tf_op jit(solution)/shard_map/ppermute | solution.py:24
  27.4 6.9 %collective-permute-start.10 = (bf16[16,1920]{1,0:T(8,128)(2,1)S(1)}, bf16[16,1920]{1,0:T(8,128)(2,1)S(1)}, u32[]{:S(2)}, u32[]{:S(2)}) collective-permute-start(bf16[16,1920]{1,0:T(8,128)(2,1)S(1)} %get-tuple-element.21), channel_id=1, source_target_pairs={{0,8},{4,12},{8,0},{12,4},{1,9},{5,13},{9,1},{13,5},{2,10},{6,14},... | collective-permute-start | bytes 184328 | tf_op jit(solution)/shard_map/ppermute | solution.py:24
  28.0 6.3 %collective-permute-start.11 = (bf16[16,1920]{1,0:T(8,128)(2,1)S(1)}, bf16[16,1920]{1,0:T(8,128)(2,1)S(1)}, u32[]{:S(2)}, u32[]{:S(2)}) collective-permute-start(bf16[16,1920]{1,0:T(8,128)(2,1)S(1)} %get-tuple-element.22), channel_id=1, source_target_pairs={{0,4},{4,0},{8,12},{12,8},{1,5},{5,1},{9,13},{13,9},{2,6},{6,2},{1... | collective-permute-start | bytes 184328 | tf_op jit(solution)/shard_map/ppermute | solution.py:24
  34.5 4.2 %collective-permute-start.14 = (bf16[8,1792]{1,0:T(8,128)(2,1)S(1)}, bf16[8,1792]{1,0:T(8,128)(2,1)S(1)}, u32[]{:S(2)}, u32[]{:S(2)}) collective-permute-start(bf16[8,1792]{1,0:T(8,128)(2,1)S(1)} %activation.1.own), channel_id=1, source_target_pairs={{0,4},{4,0},{8,12},{12,8},{1,5},{5,1},{9,13},{13,9},{2,6},{6,2},{1... | collective-permute-start | bytes 86024 | tf_op jit(solution)/shard_map/ppermute | solution.py:24
  34.8 5.2 %collective-permute-start.13 = (bf16[8,1792]{1,0:T(8,128)(2,1)S(1)}, bf16[8,1792]{1,0:T(8,128)(2,1)S(1)}, u32[]{:S(2)}, u32[]{:S(2)}) collective-permute-start(bf16[8,1792]{1,0:T(8,128)(2,1)S(1)} %activation.1.own), channel_id=1, source_target_pairs={{0,20},{4,16},{8,28},{12,24},{16,4},{20,0},{24,12},{28,8},{1,21},{... | collective-permute-start | bytes 86024 | tf_op jit(solution)/shard_map/ppermute | solution.py:24
  37.5 3.9 %collective-permute-start.12 = (bf16[8,1792]{1,0:T(8,128)(2,1)S(1)}, bf16[8,1792]{1,0:T(8,128)(2,1)S(1)}, u32[]{:S(2)}, u32[]{:S(2)}) collective-permute-start(bf16[8,1792]{1,0:T(8,128)(2,1)S(1)} %activation.1.own), channel_id=1, source_target_pairs={{0,16},{16,0},{1,17},{17,1},{2,18},{18,2},{3,19},{19,3},{4,20},{20... | collective-permute-start | bytes 86024 | tf_op jit(solution)/shard_map/ppermute | solution.py:24
  42.6 1.3 %collective-permute-start.15 = (bf16[16,2048]{1,0:T(8,128)(2,1)S(1)}, bf16[16,2048]{1,0:T(8,128)(2,1)S(1)}, u32[]{:S(2)}, u32[]{:S(2)}) collective-permute-start(bf16[16,2048]{1,0:T(8,128)(2,1)S(1)} %down.3.first), channel_id=1, source_target_pairs={{0,1},{1,0},{2,3},{3,2},{4,5},{5,4},{6,7},{7,6},{8,9},{9,8},{10,11... | collective-permute-start | bytes 196616 | tf_op jit(solution)/shard_map/ppermute | solution.py:24
  43.9 4.1 %collective-permute-start.16 = (bf16[16,2048]{1,0:T(8,128)(2,1)S(1)}, bf16[16,2048]{1,0:T(8,128)(2,1)S(1)}, u32[]{:S(2)}, u32[]{:S(2)}) collective-permute-start(bf16[16,2048]{1,0:T(8,128)(2,1)S(1)} %add.1.refs_0_), channel_id=1, source_target_pairs={{0,3},{1,2},{2,1},{3,0},{4,7},{5,6},{6,5},{7,4},{8,11},{9,10},{10,... | collective-permute-start | bytes 196616 | tf_op jit(solution)/shard_map/ppermute | solution.py:24

commit v8 on v6

--- a/solution.py
+++ b/solution.py
@@ -66,33 +66,50 @@
     return pltpu.with_memory_space_constraint(value, pltpu.VMEM)
 
 
-def attention_kernel(cols, far, lengths, *rest):
+def attention_far_kernel(cols, *refs):
     half = cols // 2
-    sources, outs = rest[:5], rest[5 : 5 + half]
-    held, (sized, packed, sems) = rest[5 + half : 10 + half], rest[10 + half :]
+    sources, (lengths, *outs), kept = refs[:5], refs[5 : 6 + half], refs[6 + half : 12 + half]
+    held, (sized, packed, sems) = refs[12 + half : 17 + half], refs[17 + half :]
+    mine = lax.axis_index("col") // half
+
+    def copies(part, targets, row):
+        result = []
+        for i, (source, target) in enumerate(zip(sources, targets)):
+            width = target.shape[2]
+            view = source.at[:, :, pl.ds(pl.multiple_of(part * width, 128), width)]
+            result.append(pltpu.make_async_copy(view, target, sems.at[row, i]))
+        return result
+
+    far, near = copies(1 - mine, held, 0), copies(mine, kept, 1)
+    far.append(pltpu.make_async_copy(lengths, sized, sems.at[0, 5]))
+    for copy in far + near:
+        copy.start()
+    for copy in far:
+        copy.wait()
+    rows = held[3].shape[0]
+    row = lax.broadcasted_iota(jnp.int32, (8, HD), 0)
+    limits = jnp.zeros((8, HD), jnp.int32)
+    for b in range(rows):
+        limits = jnp.where(row == b, sized[b], limits)
+    kept[5][...] = limits
+    attention(cols, limits, *held, outs, packed)
+    for copy in near:
+        copy.wait()
+
+
+def attention_near_kernel(cols, *refs):
+    attention(cols, refs[5][...], *refs[:5], refs[6:-1], refs[-1])
+
+
+def attention(cols, limits, query, new_keys, new_values, keys, values, outs, packed):
+    half = cols // 2
+    heads = KV_HEADS // 2
     column = lax.axis_index("col")
-    heads = KV_HEADS // 2
-    part = jnp.bitwise_xor(column // half, far)
-
-    def lanes(source):
-        width = source.shape[2] // 2
-        return source.at[:, :, pl.ds(pl.multiple_of(part * width, 128), width)]
-
-    copies = [
-        pltpu.make_async_copy(lanes(source), target, sems.at[i])
-        for i, (source, target) in enumerate(zip(sources, held))
-    ]
-    copies.append(pltpu.make_async_copy(lengths, sized, sems.at[5]))
-    for copy in copies:
-        copy.start()
-    query, new_keys, new_values, keys, values = held
     rows, span, _ = keys.shape
     hb = HEADS // cols
     inv_root = 1.0 / math.sqrt(HD)
     n = TOKENS * GROUP
     pairs = [(b, g) for b in range(rows) for g in range(heads)]
-    for i in (0, 1, 2, 5, 3):
-        copies[i].wait()
     q32 = query[...].astype(jnp.float32)
     nk, nv = new_keys[...].astype(jnp.float32), new_values[...].astype(jnp.float32)
     zeros = jnp.zeros((8 - TOKENS, HD), jnp.float32)
@@ -113,7 +130,7 @@
         ).astype(jnp.bfloat16)
         s = dot_t(q, keys[b, :, g * HD : (g + 1) * HD]) * inv_root
         position = column * span + lax.broadcasted_iota(jnp.int32, (n, span), 1)
-        scores.append(jnp.where(position < sized[b], s, very_low))
+        scores.append(jnp.where(position < limits[b : b + 1, :1], s, very_low))
         f = dot_t(q, fresh(nk, b, g).astype(jnp.bfloat16)) * inv_root
         token = lax.broadcasted_iota(jnp.int32, (n, 8), 0) // GROUP
         slot = lax.broadcasted_iota(jnp.int32, (n, 8), 1)
@@ -135,7 +152,6 @@
 
     lane = lax.broadcasted_iota(jnp.int32, (GROUP, HD), 1)
     stats = [jnp.zeros((GROUP, HD), jnp.float32) for _ in range(heads)]
-    copies[4].wait()
     for i, (b, g) in enumerate(pairs):
         here = slice(i * n, (i + 1) * n)
         s = dot(halves(weights[here]), values[b, :, g * HD : (g + 1) * HD])
@@ -338,21 +354,27 @@
     message = shape((cells + 1, hb, HD), f32)
     sources = [query, new_keys, new_values, key_cache, value_cache]
 
-    def messages(far):
-        return call(
-            functools.partial(attention_kernel, cols, far),
-            [message] * (cols // 2),
-            [ANY_SPEC] * 6,
-            [pltpu.VMEM((*a.shape[:2], a.shape[2] // 2), a.dtype) for a in sources]
-            + [pltpu.SMEM(lengths.shape, lengths.dtype)]
-            + [pltpu.VMEM((cols // 2, *message.shape), f32), pltpu.SemaphoreType.DMA((6,))],
-            name="attention_far" if far else "attention_near",
-        )(*[in_hbm(a) for a in [lengths, *sources]])
-
-    parts = messages(1)
-    parts = [partner(parts[k], "col", cols // 2 + k) for k in range(cols // 2)]
-    near = messages(0)
-    parts = [near[0]] + [partner(near[k], "col", k) for k in range(1, cols // 2)] + parts
+    inputs = [pltpu.VMEM((*a.shape[:2], a.shape[2] // 2), a.dtype) for a in sources]
+    packed = pltpu.VMEM((cols // 2, *message.shape), f32)
+    result = call(
+        functools.partial(attention_far_kernel, cols),
+        [message] * (cols // 2) + inputs + [pltpu.VMEM((8, HD), jnp.int32)],
+        [ANY_SPEC] * 6,
+        inputs
+        + [pltpu.SMEM(lengths.shape, lengths.dtype), packed, pltpu.SemaphoreType.DMA((2, 6))],
+        limit=8,
+        name="attention_far",
+    )(*[in_hbm(a) for a in [*sources, lengths]])
+    far, inputs = result[: cols // 2], result[cols // 2 :]
+    far = [partner(far[k], "col", cols // 2 + k) for k in range(cols // 2)]
+    near = call(
+        functools.partial(attention_near_kernel, cols),
+        [message] * (cols // 2),
+        [VMEM_SPEC] * 6,
+        [packed],
+        name="attention_near",
+    )(*[in_vmem(a) for a in inputs])
+    parts = far + [near[0]] + [partner(near[k], "col", k) for k in range(1, cols // 2)]
     attended = call(
         functools.partial(combine_kernel, cols),
         shape((cells, features), bf16),

time: 48.1 us -> 47.7 us (level)
  Pallas kernels: 10.2 us -> 8.98 us
  waiting for transfers between devices: 18.7 us -> 19.6 us
    pallas_call x2, Pallas kernels: 3.61 us -> 2.42 us  [the longest x1 1.93 us: shards(): call(functools.partial(attention_far_kernel, cols), [message] * (cols //...]
    ppermute x18, waiting for transfers between devices: 18.7 us -> 19.6 us  [partner(): lax.ppermute(value, axis, [(i, i ^ k) for i in range(lax.axis_size(axis))])]
  transfers between devices with their start and end apart: 18 -> 18, of which waited for: 12 -> 13; matrix products, arithmetic and copies ran while one was open for 0% -> 0% of each run, Pallas kernels for 6% -> 4%
where the time goes in v8:
time: 47.7 us; the launch traced here: 47.6 us
  waiting for transfers between devices  19.6 us (41%)
  starting transfers between devices  18.6 us (39%)
  Pallas kernels  8.98 us (19%)
    ppermute x18, waiting for transfers between devices, partner(): lax.ppermute(value, axis, [(i, i ^ k) for i in range(lax.axis_size(axis))])  19.6 us
    ppermute x18, starting transfers between devices, partner(): lax.ppermute(value, axis, [(i, i ^ k) for i in range(lax.axis_size(axis))])  18.6 us
    pallas_call x2, Pallas kernels, down_part(): call(functools.partial(down_kernel, other), shape((m, width_share), resul...  2.37 us
    pallas_call x1, Pallas kernels, shards(): call(functools.partial(lift_kernel, groups, split), [shape((m, width_shar...  2.34 us
    pallas_call x1, Pallas kernels, shards(): call(functools.partial(attention_far_kernel, cols), [message] * (cols //...  1.93 us
  transfers between devices with their start and end apart: 18, of which 13 were waited for; matrix products, arithmetic and copies ran while one was open for 0% of the time, Pallas kernels for 4%

profile of v8, /device:TPU:0, one launch (start us, length us, event | category | flops | bytes accessed | tf_op | source)
XLA Modules:
  0.0 47.6 jit_solution(947483708324041997)
XLA Ops:
  0.0 1.9 %attention_far.1 = (f32[5,8,128]{2,1,0:T(8,128)S(1)}, f32[5,8,128]{2,1,0:T(8,128)S(1)}, bf16[2,2,2048]{2,1,0:T(2,128)(2,1)S(1)}, bf16[2,2,256]{2,1,0:T(2,128)(2,...) custom-call(bf16[2,2,4096]{2,1,0:T(2,128)(2,1)} %refs_0_.1, ...), custom_call_target="tpu_custom_call" | custom-call | tf_op jit(solution)/shard_map/attention_far/pallas_call | solution.py:359
  1.9 3.0 %collective-permute-start = (f32[5,8,128]{2,1,0:T(8,128)S(1)}, f32[5,8,128]{2,1,0:T(8,128)S(1)}, u32[]{:S(2)}, u32[]{:S(2)}) collective-permute-start(f32[5,8,128]{2,1,0:T(8,128)S(1)} %get-tuple-element.18), channel_id=1, source_target_pairs={{0,2},{1,3},{2,0},{3,1},{4,6},{5,7},{6,4},{7,5},{8,10},{9,11},{10,... | collective-permute-start | bytes 61448 | tf_op jit(solution)/shard_map/ppermute | solution.py:24
  5.0 0.0 collective-permute-start.1
  5.0 0.5 %attention_near.1 = (f32[5,8,128]{2,1,0:T(8,128)S(1)}, f32[5,8,128]{2,1,0:T(8,128)S(1)}) custom-call(bf16[2,2,2048]{2,1,0:T(2,128)(2,1)S(1)} %get-tuple-element.20.refs_0_, bf16[2,2,256]{2,1,0:T(2,128)(2,1)S(1)} %get-tuple-element.21.refs_1_, bf16[2,2,256]{2,1,0:T(2,128)(2,1)S(1)} %get-tuple-element.22.refs_2_, ...), custom_call_target="tpu_custom_call" | custom-call | tf_op jit(solution)/shard_map/attention_near/pallas_call | solution.py:370
  5.5 0.3 collective-permute-start.2
  5.7 1.0 %collective-permute-done.refs_0_ = f32[5,8,128]{2,1,0:T(8,128)S(1)} collective-permute-done((f32[5,8,128]{2,1,0:T(8,128)S(1)}, f32[5,8,128]{2,1,0:T(8,128)S(1)}, u32[]{:S(2)}, u32[]{:S(2)}) %collective-permute-start) | collective-permute-done | bytes 20512 | tf_op jit(solution)/shard_map/ppermute | solution.py:24
  6.7 1.4 %collective-permute-done.1.refs_1_ = f32[5,8,128]{2,1,0:T(8,128)S(1)} collective-permute-done((f32[5,8,128]{2,1,0:T(8,128)S(1)}, f32[5,8,128]{2,1,0:T(8,128)S(1)}, u32[]{:S(2)}, u32[]{:S(2)}) %collective-permute-start.1) | collective-permute-done | bytes 20512 | tf_op jit(solution)/shard_map/ppermute | solution.py:24
  8.2 0.0 collective-permute-done.2.refs_3_
  8.2 0.0 slice-start.7
  8.2 0.0 slice-start.9
  8.2 0.0 slice-start.11
  8.2 0.0 copy-start.1
  8.3 0.0 copy-start.2
  8.3 0.2 combine.1.refs_0_
  8.4 3.7 %collective-permute-start.5 = (bf16[4,1024]{1,0:T(4,128)(2,1)S(1)}, bf16[4,1024]{1,0:T(4,128)(2,1)S(1)}, u32[]{:S(2)}, u32[]{:S(2)}) collective-permute-start(bf16[4,1024]{1,0:T(4,128)(2,1)S(1)} %combine.1.refs_0_), channel_id=1, source_target_pairs={{0,12},{4,8},{8,4},{12,0},{1,13},{5,9},{9,5},{13,1},{2,14},{6,10},... | collective-permute-start | bytes 24584 | tf_op jit(solution)/shard_map/ppermute | solution.py:24
  12.1 0.0 collective-permute-start.4
  12.1 0.8 %collective-permute-start.3 = (bf16[4,1024]{1,0:T(4,128)(2,1)S(1)}, bf16[4,1024]{1,0:T(4,128)(2,1)S(1)}, u32[]{:S(2)}, u32[]{:S(2)}) collective-permute-start(bf16[4,1024]{1,0:T(4,128)(2,1)S(1)} %combine.1.refs_0_), channel_id=1, source_target_pairs={{0,4},{4,0},{8,12},{12,8},{1,5},{5,1},{9,13},{13,9},{2,6},{6,2},{1... | collective-permute-start | bytes 24584 | tf_op jit(solution)/shard_map/ppermute | solution.py:24
  12.9 1.1 %collective-permute-done.5.refs_3_ = bf16[4,1024]{1,0:T(4,128)(2,1)S(1)} collective-permute-done((bf16[4,1024]{1,0:T(4,128)(2,1)S(1)}, bf16[4,1024]{1,0:T(4,128)(2,1)S(1)}, u32[]{:S(2)}, u32[]{:S(2)}) %collective-permute-start.5) | collective-permute-done | bytes 8224 | tf_op jit(solution)/shard_map/ppermute | solution.py:24
  14.0 2.6 %collective-permute-done.4.refs_2_ = bf16[4,1024]{1,0:T(4,128)(2,1)S(1)} collective-permute-done((bf16[4,1024]{1,0:T(4,128)(2,1)S(1)}, bf16[4,1024]{1,0:T(4,128)(2,1)S(1)}, u32[]{:S(2)}, u32[]{:S(2)}) %collective-permute-start.4) | collective-permute-done | bytes 8224 | tf_op jit(solution)/shard_map/ppermute | solution.py:24
  16.7 0.0 collective-permute-done.3.refs_1_
  16.7 0.8 %out_projection.1.refs_0_ = bf16[16,2048]{1,0:T(8,128)(2,1)S(1)} custom-call(bf16[4,1024]{1,0:T(4,128)(2,1)S(1)} %combine.1.refs_0_, bf16[4,1024]{1,0:T(4,128)(2,1)S(1)} %collective-permute-done.3.refs_1_, bf16[4,1024]{1,0:T(4,128)(2,1)S(1)} %collective-permute-done.4.refs_2_, bf16[4,1024]{1,0:T(4,128)(2,1)S(1)} %collective-permute-done.5.refs_3_, ...), custom_call_target="tpu_custom_call" | custom-call | tf_op jit(solution)/shard_map/out_projection/pallas_call | solution.py:386
  17.5 0.1 collective-permute-start.8
  17.6 0.8 %collective-permute-start.7 = (bf16[16,2048]{1,0:T(8,128)(2,1)S(1)}, bf16[16,2048]{1,0:T(8,128)(2,1)S(1)}, u32[]{:S(2)}, u32[]{:S(2)}) collective-permute-start(bf16[16,2048]{1,0:T(8,128)(2,1)S(1)} %out_projection.1.refs_0_), channel_id=1, source_target_pairs={{0,2},{1,3},{2,0},{3,1},{4,6},{5,7},{6,4},{7,5},{8,10},{9,11},{10,... | collective-permute-start | bytes 196616 | tf_op jit(solution)/shard_map/ppermute | solution.py:24
  18.4 1.0 %collective-permute-start.6 = (bf16[16,2048]{1,0:T(8,128)(2,1)S(1)}, bf16[16,2048]{1,0:T(8,128)(2,1)S(1)}, u32[]{:S(2)}, u32[]{:S(2)}) collective-permute-start(bf16[16,2048]{1,0:T(8,128)(2,1)S(1)} %out_projection.1.refs_0_), channel_id=1, source_target_pairs={{0,1},{1,0},{2,3},{3,2},{4,5},{5,4},{6,7},{7,6},{8,9},{9,8},{10,11... | collective-permute-start | bytes 196616 | tf_op jit(solution)/shard_map/ppermute | solution.py:24
  19.4 1.9 %collective-permute-done.8.refs_3_ = bf16[16,2048]{1,0:T(8,128)(2,1)S(1)} collective-permute-done((bf16[16,2048]{1,0:T(8,128)(2,1)S(1)}, bf16[16,2048]{1,0:T(8,128)(2,1)S(1)}, u32[]{:S(2)}, u32[]{:S(2)}) %collective-permute-start.8) | collective-permute-done | bytes 65568 | tf_op jit(solution)/shard_map/ppermute | solution.py:24
  21.4 1.2 %collective-permute-done.7.refs_2_ = bf16[16,2048]{1,0:T(8,128)(2,1)S(1)} collective-permute-done((bf16[16,2048]{1,0:T(8,128)(2,1)S(1)}, bf16[16,2048]{1,0:T(8,128)(2,1)S(1)}, u32[]{:S(2)}, u32[]{:S(2)}) %collective-permute-start.7) | collective-permute-done | bytes 65568 | tf_op jit(solution)/shard_map/ppermute | solution.py:24
  22.6 0.0 collective-permute-done.6.refs_1_
  22.7 2.3 %gate_up.1 = (f32[16,2048]{1,0:T(8,128)S(1)}, bf16[16,1920]{1,0:T(8,128)(2,1)S(1)}, bf16[16,1920]{1,0:T(8,128)(2,1)S(1)}) custom-call(bf16[2,8,2048]{2,1,0:T(8,128)(2,1)S(1)} %copy-done.1, bf16[2048]{0:T(1024)(128)(2,1)S(1)} %copy-done.2, bf16[2048,3584]{1,0:T(8,128)(2,1)S(1)} %bitcast.3, bf16[2048,3584]{1,0:T(8,128)(2,1)S(1)} %bitcast.5, ...), custom_call_target="tpu_custom_call" | custom-call | tf_op jit(solution)/shard_map/gate_up/pallas_call | solution.py:393
  25.0 2.1 %collective-permute-start.10 = (bf16[16,1920]{1,0:T(8,128)(2,1)S(1)}, bf16[16,1920]{1,0:T(8,128)(2,1)S(1)}, u32[]{:S(2)}, u32[]{:S(2)}) collective-permute-start(bf16[16,1920]{1,0:T(8,128)(2,1)S(1)} %get-tuple-element.29.refs_0_), channel_id=1, source_target_pairs={{0,8},{4,12},{8,0},{12,4},{1,9},{5,13},{9,1},{13,5},{2,10},{6,14},... | collective-permute-start | bytes 184328 | tf_op jit(solution)/shard_map/ppermute | solution.py:24
  27.1 0.2 collective-permute-start.11
  27.3 1.3 %collective-permute-start.9 = (bf16[16,1920]{1,0:T(8,128)(2,1)S(1)}, bf16[16,1920]{1,0:T(8,128)(2,1)S(1)}, u32[]{:S(2)}, u32[]{:S(2)}) collective-permute-start(bf16[16,1920]{1,0:T(8,128)(2,1)S(1)} %get-tuple-element.30), channel_id=1, source_target_pairs={{0,4},{4,0},{8,12},{12,8},{1,5},{5,1},{9,13},{13,9},{2,6},{6,2},{1... | collective-permute-start | bytes 184328 | tf_op jit(solution)/shard_map/ppermute | solution.py:24
  28.6 2.4 %collective-permute-done.10.refs_2_ = bf16[16,1920]{1,0:T(8,128)(2,1)S(1)} collective-permute-done((bf16[16,1920]{1,0:T(8,128)(2,1)S(1)}, bf16[16,1920]{1,0:T(8,128)(2,1)S(1)}, u32[]{:S(2)}, u32[]{:S(2)}) %collective-permute-start.10) | collective-permute-done | bytes 61472 | tf_op jit(solution)/shard_map/ppermute | solution.py:24
  30.9 2.4 %collective-permute-done.11.refs_3_ = bf16[16,1920]{1,0:T(8,128)(2,1)S(1)} collective-permute-done((bf16[16,1920]{1,0:T(8,128)(2,1)S(1)}, bf16[16,1920]{1,0:T(8,128)(2,1)S(1)}, u32[]{:S(2)}, u32[]{:S(2)}) %collective-permute-start.11) | collective-permute-done | bytes 61472 | tf_op jit(solution)/shard_map/ppermute | solution.py:24
  33.3 0.0 collective-permute-done.9.refs_1_
  33.3 0.1 activation.1.own
  33.5 0.6 %collective-permute-start.14 = (bf16[8,1792]{1,0:T(8,128)(2,1)S(1)}, bf16[8,1792]{1,0:T(8,128)(2,1)S(1)}, u32[]{:S(2)}, u32[]{:S(2)}) collective-permute-start(bf16[8,1792]{1,0:T(8,128)(2,1)S(1)} %activation.1.own), channel_id=1, source_target_pairs={{0,4},{4,0},{8,12},{12,8},{1,5},{5,1},{9,13},{13,9},{2,6},{6,2},{1... | collective-permute-start | bytes 86024 | tf_op jit(solution)/shard_map/ppermute | solution.py:24
  34.0 2.5 %collective-permute-start.13 = (bf16[8,1792]{1,0:T(8,128)(2,1)S(1)}, bf16[8,1792]{1,0:T(8,128)(2,1)S(1)}, u32[]{:S(2)}, u32[]{:S(2)}) collective-permute-start(bf16[8,1792]{1,0:T(8,128)(2,1)S(1)} %activation.1.own), channel_id=1, source_target_pairs={{0,20},{4,16},{8,28},{12,24},{16,4},{20,0},{24,12},{28,8},{1,21},{... | collective-permute-start | bytes 86024 | tf_op jit(solution)/shard_map/ppermute | solution.py:24
  36.5 0.5 %collective-permute-start.12 = (bf16[8,1792]{1,0:T(8,128)(2,1)S(1)}, bf16[8,1792]{1,0:T(8,128)(2,1)S(1)}, u32[]{:S(2)}, u32[]{:S(2)}) collective-permute-start(bf16[8,1792]{1,0:T(8,128)(2,1)S(1)} %activation.1.own), channel_id=1, source_target_pairs={{0,16},{16,0},{1,17},{17,1},{2,18},{18,2},{3,19},{19,3},{4,20},{20... | collective-permute-start | bytes 86024 | tf_op jit(solution)/shard_map/ppermute | solution.py:24
  37.0 0.4 collective-permute-done.14.received
  37.5 1.2 %down.2.refs_0_ = f32[16,2048]{1,0:T(8,128)S(1)} custom-call(bf16[16,1792]{1,0:T(8,128)(2,1)S(1)} %gather_act.3.act, bf16[3584,2048]{1,0:T(8,128)(2,1)S(1)} %bitcast.1), custom_call_target="tpu_custom_call" | custom-call | tf_op jit(solution)/shard_map/down/pallas_call | solution.py:420
  38.6 0.1 collective-permute-done.13.received
  38.8 1.6 %collective-permute-done.12.own = bf16[8,1792]{1,0:T(8,128)(2,1)S(1)} collective-permute-done((bf16[8,1792]{1,0:T(8,128)(2,1)S(1)}, bf16[8,1792]{1,0:T(8,128)(2,1)S(1)}, u32[]{:S(2)}, u32[]{:S(2)}) %collective-permute-start.12) | collective-permute-done | bytes 28704 | tf_op jit(solution)/shard_map/ppermute | solution.py:24
  40.4 1.2 %down.3.refs_0_ = bf16[16,2048]{1,0:T(8,128)(2,1)S(1)} custom-call(bf16[16,1792]{1,0:T(8,128)(2,1)S(1)} %gather_act.2.act, bf16[3584,2048]{1,0:T(8,128)(2,1)S(1)} %bitcast.1, f32[16,2048]{1,0:T(8,128)S(1)} %down.2.refs_0_), custom_call_target="tpu_custom_call" | custom-call | tf_op jit(solution)/shard_map/down/pallas_call | solution.py:420
  41.6 1.3 %collective-permute-start.16 = (bf16[16,2048]{1,0:T(8,128)(2,1)S(1)}, bf16[16,2048]{1,0:T(8,128)(2,1)S(1)}, u32[]{:S(2)}, u32[]{:S(2)}) collective-permute-start(bf16[16,2048]{1,0:T(8,128)(2,1)S(1)} %down.3.refs_0_), channel_id=1, source_target_pairs={{0,2},{1,3},{2,0},{3,1},{4,6},{5,7},{6,4},{7,5},{8,10},{9,11},{10,... | collective-permute-start | bytes 196616 | tf_op jit(solution)/shard_map/ppermute | solution.py:24
  42.8 0.6 %collective-permute-start.15 = (bf16[16,2048]{1,0:T(8,128)(2,1)S(1)}, bf16[16,2048]{1,0:T(8,128)(2,1)S(1)}, u32[]{:S(2)}, u32[]{:S(2)}) collective-permute-start(bf16[16,2048]{1,0:T(8,128)(2,1)S(1)} %down.3.refs_0_), channel_id=1, source_target_pairs={{0,1},{1,0},{2,3},{3,2},{4,5},{5,4},{6,7},{7,6},{8,9},{9,8},{10,11... | collective-permute-start | bytes 196616 | tf_op jit(solution)/shard_map/ppermute | solution.py:24
  43.4 2.5 %collective-permute-done.17.refs_3_ = bf16[16,2048]{1,0:T(8,128)(2,1)S(1)} collective-permute-done((bf16[16,2048]{1,0:T(8,128)(2,1)S(1)}, bf16[16,2048]{1,0:T(8,128)(2,1)S(1)}, u32[]{:S(2)}, u32[]{:S(2)}) %collective-permute-start.17) | collective-permute-done | bytes 65568 | tf_op jit(solution)/shard_map/ppermute | solution.py:24
  46.0 0.9 %collective-permute-done.16.refs_2_ = bf16[16,2048]{1,0:T(8,128)(2,1)S(1)} collective-permute-done((bf16[16,2048]{1,0:T(8,128)(2,1)S(1)}, bf16[16,2048]{1,0:T(8,128)(2,1)S(1)}, u32[]{:S(2)}, u32[]{:S(2)}) %collective-permute-start.16) | collective-permute-done | bytes 65568 | tf_op jit(solution)/shard_map/ppermute | solution.py:24
  46.9 0.7 %final.1 = bf16[2,8,2048]{2,1,0:T(8,128)(2,1)} custom-call(f32[16,2048]{1,0:T(8,128)S(1)} %get-tuple-element.28.mid, bf16[16,2048]{1,0:T(8,128)(2,1)S(1)} %down.3.refs_0_, bf16[16,2048]{1,0:T(8,128)(2,1)S(1)} %collective-permute-done.15.refs_1_, bf16[16,2048]{1,0:T(8,128)(2,1)S(1)} %collective-permute-done.16.refs_2_, ...), custom_call_target="tpu_custom_call" | custom-call | tf_op jit(solution)/shard_map/final/pallas_call | solution.py:434
  (32 shorter events, 0.1 us)
Async XLA Ops:
  0.0 22.6 %slice-start.4 = ((s8[14680064]{0:T(1024)(128)(4,1)}), s8[4194304]{0:T(1024)(128)(4,1)S(1)}, s32[]{:S(2)}) async-start(s8[14680064]{0:T(1024)(128)(4,1)} %bitcast.2), calls=%async_computation.4 | async-start | bytes 8388608
  0.0 22.6 %slice-start.8 = ((s8[14680064]{0:T(1024)(128)(4,1)}), s8[2097152]{0:T(1024)(128)(4,1)S(1)}, s32[]{:S(2)}) async-start(s8[14680064]{0:T(1024)(128)(4,1)} %bitcast.4), calls=%async_computation.8 | async-start | bytes 4194304
  1.9 4.8 %collective-permute-start = (f32[5,8,128]{2,1,0:T(8,128)S(1)}, f32[5,8,128]{2,1,0:T(8,128)S(1)}, u32[]{:S(2)}, u32[]{:S(2)}) collective-permute-start(f32[5,8,128]{2,1,0:T(8,128)S(1)} %get-tuple-element.18), channel_id=1, source_target_pairs={{0,2},{1,3},{2,0},{3,1},{4,6},{5,7},{6,4},{7,5},{8,10},{9,11},{10,... | collective-permute-start | bytes 61448 | tf_op jit(solution)/shard_map/ppermute | solution.py:24
  5.0 3.2 %collective-permute-start.1 = (f32[5,8,128]{2,1,0:T(8,128)S(1)}, f32[5,8,128]{2,1,0:T(8,128)S(1)}, u32[]{:S(2)}, u32[]{:S(2)}) collective-permute-start(f32[5,8,128]{2,1,0:T(8,128)S(1)} %get-tuple-element.19), channel_id=1, source_target_pairs={{0,3},{1,2},{2,1},{3,0},{4,7},{5,6},{6,5},{7,4},{8,11},{9,10},{10,... | collective-permute-start | bytes 61448 | tf_op jit(solution)/shard_map/ppermute | solution.py:24
  5.5 2.7 %collective-permute-start.2 = (f32[5,8,128]{2,1,0:T(8,128)S(1)}, f32[5,8,128]{2,1,0:T(8,128)S(1)}, u32[]{:S(2)}, u32[]{:S(2)}) collective-permute-start(f32[5,8,128]{2,1,0:T(8,128)S(1)} %get-tuple-element.27), channel_id=1, source_target_pairs={{0,1},{1,0},{2,3},{3,2},{4,5},{5,4},{6,7},{7,6},{8,9},{9,8},{10,11... | collective-permute-start | bytes 61448 | tf_op jit(solution)/shard_map/ppermute | solution.py:24
  8.2 8.5 %copy-start = (bf16[1024,2048]{1,0:T(8,128)(2,1)S(1)}, bf16[1024,2048]{1,0:T(8,128)(2,1)}, u32[]{:S(2)}) copy-start(bf16[1024,2048]{1,0:T(8,128)(2,1)} %refs_4_.3) | copy-start | bytes 12582916
  8.2 14.4 %slice-start.5 = ((s8[14680064]{0:T(1024)(128)(4,1)}), s8[4194304]{0:T(1024)(128)(4,1)S(1)}, s32[]{:S(2)}) async-start(s8[14680064]{0:T(1024)(128)(4,1)} %bitcast.2), calls=%async_computation.5 | async-start | bytes 8388608
  8.2 14.4 %slice-start.6 = ((s8[14680064]{0:T(1024)(128)(4,1)}), s8[4194304]{0:T(1024)(128)(4,1)S(1)}, s32[]{:S(2)}) async-start(s8[14680064]{0:T(1024)(128)(4,1)} %bitcast.2), calls=%async_computation.6 | async-start | bytes 8388608
  8.2 14.4 %slice-start.7 = ((s8[14680064]{0:T(1024)(128)(4,1)}), s8[2097152]{0:T(1024)(128)(4,1)S(1)}, s32[]{:S(2)}) async-start(s8[14680064]{0:T(1024)(128)(4,1)} %bitcast.2), calls=%async_computation.7 | async-start | bytes 4194304
  8.2 14.4 %slice-start.9 = ((s8[14680064]{0:T(1024)(128)(4,1)}), s8[4194304]{0:T(1024)(128)(4,1)S(1)}, s32[]{:S(2)}) async-start(s8[14680064]{0:T(1024)(128)(4,1)} %bitcast.4), calls=%async_computation.9 | async-start | bytes 8388608
  8.2 14.4 %slice-start.10 = ((s8[14680064]{0:T(1024)(128)(4,1)}), s8[4194304]{0:T(1024)(128)(4,1)S(1)}, s32[]{:S(2)}) async-start(s8[14680064]{0:T(1024)(128)(4,1)} %bitcast.4), calls=%async_computation.10 | async-start | bytes 8388608
  8.2 14.4 %slice-start.11 = ((s8[14680064]{0:T(1024)(128)(4,1)}), s8[4194304]{0:T(1024)(128)(4,1)S(1)}, s32[]{:S(2)}) async-start(s8[14680064]{0:T(1024)(128)(4,1)} %bitcast.4), calls=%async_computation.11 | async-start | bytes 8388608
  8.2 14.4 %copy-start.1 = (bf16[2,8,2048]{2,1,0:T(8,128)(2,1)S(1)}, bf16[2,8,2048]{2,1,0:T(8,128)(2,1)}, u32[]{:S(2)}) copy-start(bf16[2,8,2048]{2,1,0:T(8,128)(2,1)} %residual.1) | copy-start | bytes 196612
  8.3 14.4 %copy-start.2 = (bf16[2048]{0:T(1024)(128)(2,1)S(1)}, bf16[2048]{0:T(1024)(128)(2,1)}, u32[]{:S(2)}) copy-start(bf16[2048]{0:T(1024)(128)(2,1)} %gains.1) | copy-start | bytes 12292
  8.4 5.6 %collective-permute-start.5 = (bf16[4,1024]{1,0:T(4,128)(2,1)S(1)}, bf16[4,1024]{1,0:T(4,128)(2,1)S(1)}, u32[]{:S(2)}, u32[]{:S(2)}) collective-permute-start(bf16[4,1024]{1,0:T(4,128)(2,1)S(1)} %combine.1.refs_0_), channel_id=1, source_target_pairs={{0,12},{4,8},{8,4},{12,0},{1,13},{5,9},{9,5},{13,1},{2,14},{6,10},... | collective-permute-start | bytes 24584 | tf_op jit(solution)/shard_map/ppermute | solution.py:24
  12.1 4.5 %collective-permute-start.4 = (bf16[4,1024]{1,0:T(4,128)(2,1)S(1)}, bf16[4,1024]{1,0:T(4,128)(2,1)S(1)}, u32[]{:S(2)}, u32[]{:S(2)}) collective-permute-start(bf16[4,1024]{1,0:T(4,128)(2,1)S(1)} %combine.1.refs_0_), channel_id=1, source_target_pairs={{0,8},{4,12},{8,0},{12,4},{1,9},{5,13},{9,1},{13,5},{2,10},{6,14},... | collective-permute-start | bytes 24584 | tf_op jit(solution)/shard_map/ppermute | solution.py:24
  12.1 4.5 %collective-permute-start.3 = (bf16[4,1024]{1,0:T(4,128)(2,1)S(1)}, bf16[4,1024]{1,0:T(4,128)(2,1)S(1)}, u32[]{:S(2)}, u32[]{:S(2)}) collective-permute-start(bf16[4,1024]{1,0:T(4,128)(2,1)S(1)} %combine.1.refs_0_), channel_id=1, source_target_pairs={{0,4},{4,0},{8,12},{12,8},{1,5},{5,1},{9,13},{13,9},{2,6},{6,2},{1... | collective-permute-start | bytes 24584 | tf_op jit(solution)/shard_map/ppermute | solution.py:24
  16.7 20.7 %slice-start = ((s8[14680064]{0:T(1024)(128)(4,1)}), s8[4194304]{0:T(1024)(128)(4,1)S(1)}, s32[]{:S(2)}) async-start(s8[14680064]{0:T(1024)(128)(4,1)} %bitcast), calls=%async_computation | async-start | bytes 8388608
  17.5 19.9 %slice-start.1 = ((s8[14680064]{0:T(1024)(128)(4,1)}), s8[4194304]{0:T(1024)(128)(4,1)S(1)}, s32[]{:S(2)}) async-start(s8[14680064]{0:T(1024)(128)(4,1)} %bitcast), calls=%async_computation.1 | async-start | bytes 8388608
  17.5 20.0 %slice-start.2 = ((s8[14680064]{0:T(1024)(128)(4,1)}), s8[4194304]{0:T(1024)(128)(4,1)S(1)}, s32[]{:S(2)}) async-start(s8[14680064]{0:T(1024)(128)(4,1)} %bitcast), calls=%async_computation.2 | async-start | bytes 8388608
  17.5 20.0 %slice-start.3 = ((s8[14680064]{0:T(1024)(128)(4,1)}), s8[2097152]{0:T(1024)(128)(4,1)S(1)}, s32[]{:S(2)}) async-start(s8[14680064]{0:T(1024)(128)(4,1)} %bitcast), calls=%async_computation.3 | async-start | bytes 4194304
  17.5 3.9 %collective-permute-start.8 = (bf16[16,2048]{1,0:T(8,128)(2,1)S(1)}, bf16[16,2048]{1,0:T(8,128)(2,1)S(1)}, u32[]{:S(2)}, u32[]{:S(2)}) collective-permute-start(bf16[16,2048]{1,0:T(8,128)(2,1)S(1)} %out_projection.1.refs_0_), channel_id=1, source_target_pairs={{0,3},{1,2},{2,1},{3,0},{4,7},{5,6},{6,5},{7,4},{8,11},{9,10},{10,... | collective-permute-start | bytes 196616 | tf_op jit(solution)/shard_map/ppermute | solution.py:24
  17.6 5.0 %collective-permute-start.7 = (bf16[16,2048]{1,0:T(8,128)(2,1)S(1)}, bf16[16,2048]{1,0:T(8,128)(2,1)S(1)}, u32[]{:S(2)}, u32[]{:S(2)}) collective-permute-start(bf16[16,2048]{1,0:T(8,128)(2,1)S(1)} %out_projection.1.refs_0_), channel_id=1, source_target_pairs={{0,2},{1,3},{2,0},{3,1},{4,6},{5,7},{6,4},{7,5},{8,10},{9,11},{10,... | collective-permute-start | bytes 196616 | tf_op jit(solution)/shard_map/ppermute | solution.py:24
  18.4 4.2 %collective-permute-start.6 = (bf16[16,2048]{1,0:T(8,128)(2,1)S(1)}, bf16[16,2048]{1,0:T(8,128)(2,1)S(1)}, u32[]{:S(2)}, u32[]{:S(2)}) collective-permute-start(bf16[16,2048]{1,0:T(8,128)(2,1)S(1)} %out_projection.1.refs_0_), channel_id=1, source_target_pairs={{0,1},{1,0},{2,3},{3,2},{4,5},{5,4},{6,7},{7,6},{8,9},{9,8},{10,11... | collective-permute-start | bytes 196616 | tf_op jit(solution)/shard_map/ppermute | solution.py:24
  25.0 5.9 %collective-permute-start.10 = (bf16[16,1920]{1,0:T(8,128)(2,1)S(1)}, bf16[16,1920]{1,0:T(8,128)(2,1)S(1)}, u32[]{:S(2)}, u32[]{:S(2)}) collective-permute-start(bf16[16,1920]{1,0:T(8,128)(2,1)S(1)} %get-tuple-element.29.refs_0_), channel_id=1, source_target_pairs={{0,8},{4,12},{8,0},{12,4},{1,9},{5,13},{9,1},{13,5},{2,10},{6,14},... | collective-permute-start | bytes 184328 | tf_op jit(solution)/shard_map/ppermute | solution.py:24
  27.1 6.2 %collective-permute-start.11 = (bf16[16,1920]{1,0:T(8,128)(2,1)S(1)}, bf16[16,1920]{1,0:T(8,128)(2,1)S(1)}, u32[]{:S(2)}, u32[]{:S(2)}) collective-permute-start(bf16[16,1920]{1,0:T(8,128)(2,1)S(1)} %get-tuple-element.30), channel_id=1, source_target_pairs={{0,12},{4,8},{8,4},{12,0},{1,13},{5,9},{9,5},{13,1},{2,14},{6,10},... | collective-permute-start | bytes 184328 | tf_op jit(solution)/shard_map/ppermute | solution.py:24
  27.3 6.0 %collective-permute-start.9 = (bf16[16,1920]{1,0:T(8,128)(2,1)S(1)}, bf16[16,1920]{1,0:T(8,128)(2,1)S(1)}, u32[]{:S(2)}, u32[]{:S(2)}) collective-permute-start(bf16[16,1920]{1,0:T(8,128)(2,1)S(1)} %get-tuple-element.30), channel_id=1, source_target_pairs={{0,4},{4,0},{8,12},{12,8},{1,5},{5,1},{9,13},{13,9},{2,6},{6,2},{1... | collective-permute-start | bytes 184328 | tf_op jit(solution)/shard_map/ppermute | solution.py:24
  33.5 3.9 %collective-permute-start.14 = (bf16[8,1792]{1,0:T(8,128)(2,1)S(1)}, bf16[8,1792]{1,0:T(8,128)(2,1)S(1)}, u32[]{:S(2)}, u32[]{:S(2)}) collective-permute-start(bf16[8,1792]{1,0:T(8,128)(2,1)S(1)} %activation.1.own), channel_id=1, source_target_pairs={{0,4},{4,0},{8,12},{12,8},{1,5},{5,1},{9,13},{13,9},{2,6},{6,2},{1... | collective-permute-start | bytes 86024 | tf_op jit(solution)/shard_map/ppermute | solution.py:24
  34.0 4.8 %collective-permute-start.13 = (bf16[8,1792]{1,0:T(8,128)(2,1)S(1)}, bf16[8,1792]{1,0:T(8,128)(2,1)S(1)}, u32[]{:S(2)}, u32[]{:S(2)}) collective-permute-start(bf16[8,1792]{1,0:T(8,128)(2,1)S(1)} %activation.1.own), channel_id=1, source_target_pairs={{0,20},{4,16},{8,28},{12,24},{16,4},{20,0},{24,12},{28,8},{1,21},{... | collective-permute-start | bytes 86024 | tf_op jit(solution)/shard_map/ppermute | solution.py:24
  36.5 3.9 %collective-permute-start.12 = (bf16[8,1792]{1,0:T(8,128)(2,1)S(1)}, bf16[8,1792]{1,0:T(8,128)(2,1)S(1)}, u32[]{:S(2)}, u32[]{:S(2)}) collective-permute-start(bf16[8,1792]{1,0:T(8,128)(2,1)S(1)} %activation.1.own), channel_id=1, source_target_pairs={{0,16},{16,0},{1,17},{17,1},{2,18},{18,2},{3,19},{19,3},{4,20},{20... | collective-permute-start | bytes 86024 | tf_op jit(solution)/shard_map/ppermute | solution.py:24
  41.5 4.4 %collective-permute-start.17 = (bf16[16,2048]{1,0:T(8,128)(2,1)S(1)}, bf16[16,2048]{1,0:T(8,128)(2,1)S(1)}, u32[]{:S(2)}, u32[]{:S(2)}) collective-permute-start(bf16[16,2048]{1,0:T(8,128)(2,1)S(1)} %down.3.refs_0_), channel_id=1, source_target_pairs={{0,3},{1,2},{2,1},{3,0},{4,7},{5,6},{6,5},{7,4},{8,11},{9,10},{10,... | collective-permute-start | bytes 196616 | tf_op jit(solution)/shard_map/ppermute | solution.py:24
  41.6 5.3 %collective-permute-start.16 = (bf16[16,2048]{1,0:T(8,128)(2,1)S(1)}, bf16[16,2048]{1,0:T(8,128)(2,1)S(1)}, u32[]{:S(2)}, u32[]{:S(2)}) collective-permute-start(bf16[16,2048]{1,0:T(8,128)(2,1)S(1)} %down.3.refs_0_), channel_id=1, source_target_pairs={{0,2},{1,3},{2,0},{3,1},{4,6},{5,7},{6,4},{7,5},{8,10},{9,11},{10,... | collective-permute-start | bytes 196616 | tf_op jit(solution)/shard_map/ppermute | solution.py:24
  42.8 4.1 %collective-permute-start.15 = (bf16[16,2048]{1,0:T(8,128)(2,1)S(1)}, bf16[16,2048]{1,0:T(8,128)(2,1)S(1)}, u32[]{:S(2)}, u32[]{:S(2)}) collective-permute-start(bf16[16,2048]{1,0:T(8,128)(2,1)S(1)} %down.3.refs_0_), channel_id=1, source_target_pairs={{0,1},{1,0},{2,3},{3,2},{4,5},{5,4},{6,7},{7,6},{8,9},{9,8},{10,11... | collective-permute-start | bytes 196616 | tf_op jit(solution)/shard_map/ppermute | solution.py:24

commit v9 on v8

--- a/solution.py
+++ b/solution.py
@@ -84,15 +84,15 @@
     far.append(pltpu.make_async_copy(lengths, sized, sems.at[0, 5]))
     for copy in far + near:
         copy.start()
-    for copy in far:
-        copy.wait()
+    for i in (0, 1, 2, 5, 3):
+        far[i].wait()
     rows = held[3].shape[0]
     row = lax.broadcasted_iota(jnp.int32, (8, HD), 0)
     limits = jnp.zeros((8, HD), jnp.int32)
     for b in range(rows):
         limits = jnp.where(row == b, sized[b], limits)
     kept[5][...] = limits
-    attention(cols, limits, *held, outs, packed)
+    attention(cols, limits, *held, outs, packed, far[4].wait)
     for copy in near:
         copy.wait()
 
@@ -101,7 +101,9 @@
     attention(cols, refs[5][...], *refs[:5], refs[6:-1], refs[-1])
 
 
-def attention(cols, limits, query, new_keys, new_values, keys, values, outs, packed):
+def attention(
+    cols, limits, query, new_keys, new_values, keys, values, outs, packed, values_there=lambda: None
+):
     half = cols // 2
     heads = KV_HEADS // 2
     column = lax.axis_index("col")
@@ -152,6 +154,7 @@
 
     lane = lax.broadcasted_iota(jnp.int32, (GROUP, HD), 1)
     stats = [jnp.zeros((GROUP, HD), jnp.float32) for _ in range(heads)]
+    values_there()
     for i, (b, g) in enumerate(pairs):
         here = slice(i * n, (i + 1) * n)
         s = dot(halves(weights[here]), values[b, :, g * HD : (g + 1) * HD])
@@ -225,8 +228,13 @@
     lax.fori_loop(0, width // size, step, 0)
 
 
+def gather_order(groups):
+    return [0, 1, 3, 2] if groups == 4 else list(range(groups))
+
+
 def out_kernel(groups, *refs):
-    parts, (weight, out, canon, attended) = refs[:groups], refs[groups:]
+    weight, out, canon, attended = refs[groups:]
+    parts = [refs[gather_order(groups).index(k)] for k in range(groups)]
     attended[...] = canonical(parts, canon, lax.axis_index("row"))
 
     def body(at, size):
@@ -246,7 +254,8 @@
 
 
 def lift_kernel(groups, split, residual, gains, gate_weight, up_weight, *refs):
-    parts, (mid_out, keep, send, lifted, packed) = refs[:-5], refs[-5:]
+    mid_out, keep, send, lifted, packed = refs[-5:]
+    parts = [refs[gather_order(len(refs) - 5).index(k)] for k in range(len(refs) - 5)]
     hidden = gate_weight.shape[1] // split
     start = lax.axis_index("side") * hidden if split > 1 else 0
     half = packed.shape[1] // 2
@@ -389,7 +398,8 @@
         [VMEM_SPEC] * (groups + 1),
         [pltpu.VMEM((groups, pad, features), f32), pltpu.VMEM((m, features), bf16)],
         name="out_projection",
-    )(*gathered, in_vmem(out_weight))
+    )(*[gathered[k] for k in gather_order(groups)], in_vmem(out_weight))
+    partials = spread(partial, "col")
     mid, keep, send = call(
         functools.partial(lift_kernel, groups, split),
         [shape((m, width_share), f32)] + [shape((m, hidden + HD), WIRE)] * 2,
@@ -398,7 +408,7 @@
         name="gate_up",
     )(
         in_vmem(residual), in_vmem(norm_gain), in_vmem(gate_weight), in_vmem(up_weight),
-        *spread(partial, "col"),
+        *[partials[k] for k in gather_order(cols)],
     )
     sums = [keep] + [partner((keep, send)[k % 2], "row", k) for k in range(1, groups)]
     act = call(

time: 47.7 us -> 47.7 us (level)
  transfers between devices with their start and end apart: 18 -> 18, of which waited for: 13 -> 14; matrix products, arithmetic and copies ran while one was open for 0% -> 0% of each run, Pallas kernels for 4% -> 4%
where the time goes in v9:
time: 47.7 us; the launch traced here: 47.5 us
  waiting for transfers between devices  19.5 us (41%)
  starting transfers between devices  18.7 us (39%)
  Pallas kernels  9 us (19%)
    ppermute x18, waiting for transfers between devices, partner(): lax.ppermute(value, axis, [(i, i ^ k) for i in range(lax.axis_size(axis))])  19.5 us
    ppermute x18, starting transfers between devices, partner(): lax.ppermute(value, axis, [(i, i ^ k) for i in range(lax.axis_size(axis))])  18.7 us
    pallas_call x2, Pallas kernels, down_part(): call(functools.partial(down_kernel, other), shape((m, width_share), resul...  2.37 us
    pallas_call x1, Pallas kernels, shards(): call(functools.partial(lift_kernel, groups, split), [shape((m, width_shar...  2.34 us
    pallas_call x1, Pallas kernels, shards(): call(functools.partial(attention_far_kernel, cols), [message] * (cols //...  1.94 us
  transfers between devices with their start and end apart: 18, of which 14 were waited for; matrix products, arithmetic and copies ran while one was open for 0% of the time, Pallas kernels for 4%

profile of v9, /device:TPU:0, one launch (start us, length us, event | category | flops | bytes accessed | tf_op | source)
XLA Modules:
  0.0 47.5 jit_solution(8135557435151270363)
XLA Ops:
  0.0 1.9 %attention_far.1 = (f32[5,8,128]{2,1,0:T(8,128)S(1)}, f32[5,8,128]{2,1,0:T(8,128)S(1)}, bf16[2,2,2048]{2,1,0:T(2,128)(2,1)S(1)}, bf16[2,2,256]{2,1,0:T(2,128)(2,...) custom-call(bf16[2,2,4096]{2,1,0:T(2,128)(2,1)} %refs_0_.1, ...), custom_call_target="tpu_custom_call" | custom-call | tf_op jit(solution)/shard_map/attention_far/pallas_call | solution.py:368
  2.0 3.0 %collective-permute-start = (f32[5,8,128]{2,1,0:T(8,128)S(1)}, f32[5,8,128]{2,1,0:T(8,128)S(1)}, u32[]{:S(2)}, u32[]{:S(2)}) collective-permute-start(f32[5,8,128]{2,1,0:T(8,128)S(1)} %get-tuple-element.18), channel_id=1, source_target_pairs={{0,2},{1,3},{2,0},{3,1},{4,6},{5,7},{6,4},{7,5},{8,10},{9,11},{10,... | collective-permute-start | bytes 61448 | tf_op jit(solution)/shard_map/ppermute | solution.py:24
  5.0 0.0 collective-permute-start.1
  5.0 0.5 %attention_near.1 = (f32[5,8,128]{2,1,0:T(8,128)S(1)}, f32[5,8,128]{2,1,0:T(8,128)S(1)}) custom-call(bf16[2,2,2048]{2,1,0:T(2,128)(2,1)S(1)} %get-tuple-element.20.refs_0_, bf16[2,2,256]{2,1,0:T(2,128)(2,1)S(1)} %get-tuple-element.21.refs_1_, bf16[2,2,256]{2,1,0:T(2,128)(2,1)S(1)} %get-tuple-element.22.refs_2_, ...), custom_call_target="tpu_custom_call" | custom-call | tf_op jit(solution)/shard_map/attention_near/pallas_call | solution.py:379
  5.5 0.3 collective-permute-start.2
  5.7 1.0 %collective-permute-done.refs_0_ = f32[5,8,128]{2,1,0:T(8,128)S(1)} collective-permute-done((f32[5,8,128]{2,1,0:T(8,128)S(1)}, f32[5,8,128]{2,1,0:T(8,128)S(1)}, u32[]{:S(2)}, u32[]{:S(2)}) %collective-permute-start) | collective-permute-done | bytes 20512 | tf_op jit(solution)/shard_map/ppermute | solution.py:24
  6.8 1.4 %collective-permute-done.1.refs_1_ = f32[5,8,128]{2,1,0:T(8,128)S(1)} collective-permute-done((f32[5,8,128]{2,1,0:T(8,128)S(1)}, f32[5,8,128]{2,1,0:T(8,128)S(1)}, u32[]{:S(2)}, u32[]{:S(2)}) %collective-permute-start.1) | collective-permute-done | bytes 20512 | tf_op jit(solution)/shard_map/ppermute | solution.py:24
  8.2 0.0 collective-permute-done.2.refs_3_
  8.2 0.0 slice-start.7
  8.2 0.0 slice-start.9
  8.2 0.0 slice-start.10
  8.2 0.0 slice-start.11
  8.3 0.0 copy-start.1
  8.3 0.0 copy-start.2
  8.3 0.2 combine.1.refs_0_
  8.5 2.7 %collective-permute-start.5 = (bf16[4,1024]{1,0:T(4,128)(2,1)S(1)}, bf16[4,1024]{1,0:T(4,128)(2,1)S(1)}, u32[]{:S(2)}, u32[]{:S(2)}) collective-permute-start(bf16[4,1024]{1,0:T(4,128)(2,1)S(1)} %combine.1.refs_0_), channel_id=1, source_target_pairs={{0,8},{4,12},{8,0},{12,4},{1,9},{5,13},{9,1},{13,5},{2,10},{6,14},... | collective-permute-start | bytes 24584 | tf_op jit(solution)/shard_map/ppermute | solution.py:24
  11.1 1.3 %collective-permute-start.4 = (bf16[4,1024]{1,0:T(4,128)(2,1)S(1)}, bf16[4,1024]{1,0:T(4,128)(2,1)S(1)}, u32[]{:S(2)}, u32[]{:S(2)}) collective-permute-start(bf16[4,1024]{1,0:T(4,128)(2,1)S(1)} %combine.1.refs_0_), channel_id=1, source_target_pairs={{0,12},{4,8},{8,4},{12,0},{1,13},{5,9},{9,5},{13,1},{2,14},{6,10},... | collective-permute-start | bytes 24584 | tf_op jit(solution)/shard_map/ppermute | solution.py:24
  12.5 0.2 collective-permute-start.3
  12.7 0.4 collective-permute-done.5.refs_3_
  13.1 3.5 %collective-permute-done.4.refs_2_ = bf16[4,1024]{1,0:T(4,128)(2,1)S(1)} collective-permute-done((bf16[4,1024]{1,0:T(4,128)(2,1)S(1)}, bf16[4,1024]{1,0:T(4,128)(2,1)S(1)}, u32[]{:S(2)}, u32[]{:S(2)}) %collective-permute-start.4) | collective-permute-done | bytes 8224 | tf_op jit(solution)/shard_map/ppermute | solution.py:24
  16.6 0.0 collective-permute-done.3.refs_1_
  16.6 0.8 %out_projection.1.refs_0_ = bf16[16,2048]{1,0:T(8,128)(2,1)S(1)} custom-call(bf16[4,1024]{1,0:T(4,128)(2,1)S(1)} %combine.1.refs_0_, bf16[4,1024]{1,0:T(4,128)(2,1)S(1)} %collective-permute-done.3.refs_1_, bf16[4,1024]{1,0:T(4,128)(2,1)S(1)} %collective-permute-done.4.refs_2_, bf16[4,1024]{1,0:T(4,128)(2,1)S(1)} %collective-permute-done.5.refs_3_, ...), custom_call_target="tpu_custom_call" | custom-call | tf_op jit(solution)/shard_map/out_projection/pallas_call | solution.py:395
  17.4 0.8 %collective-permute-start.8 = (bf16[16,2048]{1,0:T(8,128)(2,1)S(1)}, bf16[16,2048]{1,0:T(8,128)(2,1)S(1)}, u32[]{:S(2)}, u32[]{:S(2)}) collective-permute-start(bf16[16,2048]{1,0:T(8,128)(2,1)S(1)} %out_projection.1.refs_0_), channel_id=1, source_target_pairs={{0,2},{1,3},{2,0},{3,1},{4,6},{5,7},{6,4},{7,5},{8,10},{9,11},{10,... | collective-permute-start | bytes 196616 | tf_op jit(solution)/shard_map/ppermute | solution.py:24
  18.2 0.0 collective-permute-start.7
  18.2 1.4 %collective-permute-start.6 = (bf16[16,2048]{1,0:T(8,128)(2,1)S(1)}, bf16[16,2048]{1,0:T(8,128)(2,1)S(1)}, u32[]{:S(2)}, u32[]{:S(2)}) collective-permute-start(bf16[16,2048]{1,0:T(8,128)(2,1)S(1)} %out_projection.1.refs_0_), channel_id=1, source_target_pairs={{0,1},{1,0},{2,3},{3,2},{4,5},{5,4},{6,7},{7,6},{8,9},{9,8},{10,11... | collective-permute-start | bytes 196616 | tf_op jit(solution)/shard_map/ppermute | solution.py:24
  19.6 2.6 %collective-permute-done.8.refs_3_ = bf16[16,2048]{1,0:T(8,128)(2,1)S(1)} collective-permute-done((bf16[16,2048]{1,0:T(8,128)(2,1)S(1)}, bf16[16,2048]{1,0:T(8,128)(2,1)S(1)}, u32[]{:S(2)}, u32[]{:S(2)}) %collective-permute-start.8) | collective-permute-done | bytes 65568 | tf_op jit(solution)/shard_map/ppermute | solution.py:24
  22.3 0.3 collective-permute-done.7.refs_2_
  22.7 2.3 %gate_up.1 = (f32[16,2048]{1,0:T(8,128)S(1)}, bf16[16,1920]{1,0:T(8,128)(2,1)S(1)}, bf16[16,1920]{1,0:T(8,128)(2,1)S(1)}) custom-call(bf16[2,8,2048]{2,1,0:T(8,128)(2,1)S(1)} %copy-done.1, bf16[2048]{0:T(1024)(128)(2,1)S(1)} %copy-done.2, bf16[2048,3584]{1,0:T(8,128)(2,1)S(1)} %bitcast.3, bf16[2048,3584]{1,0:T(8,128)(2,1)S(1)} %bitcast.5, ...), custom_call_target="tpu_custom_call" | custom-call | tf_op jit(solution)/shard_map/gate_up/pallas_call | solution.py:403
  25.1 1.3 %collective-permute-start.10 = (bf16[16,1920]{1,0:T(8,128)(2,1)S(1)}, bf16[16,1920]{1,0:T(8,128)(2,1)S(1)}, u32[]{:S(2)}, u32[]{:S(2)}) collective-permute-start(bf16[16,1920]{1,0:T(8,128)(2,1)S(1)} %get-tuple-element.29.refs_0_), channel_id=1, source_target_pairs={{0,8},{4,12},{8,0},{12,4},{1,9},{5,13},{9,1},{13,5},{2,10},{6,14},... | collective-permute-start | bytes 184328 | tf_op jit(solution)/shard_map/ppermute | solution.py:24
  26.3 0.9 %collective-permute-start.11 = (bf16[16,1920]{1,0:T(8,128)(2,1)S(1)}, bf16[16,1920]{1,0:T(8,128)(2,1)S(1)}, u32[]{:S(2)}, u32[]{:S(2)}) collective-permute-start(bf16[16,1920]{1,0:T(8,128)(2,1)S(1)} %get-tuple-element.30), channel_id=1, source_target_pairs={{0,12},{4,8},{8,4},{12,0},{1,13},{5,9},{9,5},{13,1},{2,14},{6,10},... | collective-permute-start | bytes 184328 | tf_op jit(solution)/shard_map/ppermute | solution.py:24
  27.3 1.4 %collective-permute-start.9 = (bf16[16,1920]{1,0:T(8,128)(2,1)S(1)}, bf16[16,1920]{1,0:T(8,128)(2,1)S(1)}, u32[]{:S(2)}, u32[]{:S(2)}) collective-permute-start(bf16[16,1920]{1,0:T(8,128)(2,1)S(1)} %get-tuple-element.30), channel_id=1, source_target_pairs={{0,4},{4,0},{8,12},{12,8},{1,5},{5,1},{9,13},{13,9},{2,6},{6,2},{1... | collective-permute-start | bytes 184328 | tf_op jit(solution)/shard_map/ppermute | solution.py:24
  28.6 3.1 %collective-permute-done.10.refs_2_ = bf16[16,1920]{1,0:T(8,128)(2,1)S(1)} collective-permute-done((bf16[16,1920]{1,0:T(8,128)(2,1)S(1)}, bf16[16,1920]{1,0:T(8,128)(2,1)S(1)}, u32[]{:S(2)}, u32[]{:S(2)}) %collective-permute-start.10) | collective-permute-done | bytes 61472 | tf_op jit(solution)/shard_map/ppermute | solution.py:24
  31.7 1.1 %collective-permute-done.11.refs_3_ = bf16[16,1920]{1,0:T(8,128)(2,1)S(1)} collective-permute-done((bf16[16,1920]{1,0:T(8,128)(2,1)S(1)}, bf16[16,1920]{1,0:T(8,128)(2,1)S(1)}, u32[]{:S(2)}, u32[]{:S(2)}) %collective-permute-start.11) | collective-permute-done | bytes 61472 | tf_op jit(solution)/shard_map/ppermute | solution.py:24
  32.8 0.8 %collective-permute-done.9.refs_1_ = bf16[16,1920]{1,0:T(8,128)(2,1)S(1)} collective-permute-done((bf16[16,1920]{1,0:T(8,128)(2,1)S(1)}, bf16[16,1920]{1,0:T(8,128)(2,1)S(1)}, u32[]{:S(2)}, u32[]{:S(2)}) %collective-permute-start.9) | collective-permute-done | bytes 61472 | tf_op jit(solution)/shard_map/ppermute | solution.py:24
  33.6 0.1 activation.1.own
  33.8 0.6 %collective-permute-start.14 = (bf16[8,1792]{1,0:T(8,128)(2,1)S(1)}, bf16[8,1792]{1,0:T(8,128)(2,1)S(1)}, u32[]{:S(2)}, u32[]{:S(2)}) collective-permute-start(bf16[8,1792]{1,0:T(8,128)(2,1)S(1)} %activation.1.own), channel_id=1, source_target_pairs={{0,4},{4,0},{8,12},{12,8},{1,5},{5,1},{9,13},{13,9},{2,6},{6,2},{1... | collective-permute-start | bytes 86024 | tf_op jit(solution)/shard_map/ppermute | solution.py:24
  34.4 2.4 %collective-permute-start.13 = (bf16[8,1792]{1,0:T(8,128)(2,1)S(1)}, bf16[8,1792]{1,0:T(8,128)(2,1)S(1)}, u32[]{:S(2)}, u32[]{:S(2)}) collective-permute-start(bf16[8,1792]{1,0:T(8,128)(2,1)S(1)} %activation.1.own), channel_id=1, source_target_pairs={{0,20},{4,16},{8,28},{12,24},{16,4},{20,0},{24,12},{28,8},{1,21},{... | collective-permute-start | bytes 86024 | tf_op jit(solution)/shard_map/ppermute | solution.py:24
  36.8 0.5 %collective-permute-start.12 = (bf16[8,1792]{1,0:T(8,128)(2,1)S(1)}, bf16[8,1792]{1,0:T(8,128)(2,1)S(1)}, u32[]{:S(2)}, u32[]{:S(2)}) collective-permute-start(bf16[8,1792]{1,0:T(8,128)(2,1)S(1)} %activation.1.own), channel_id=1, source_target_pairs={{0,16},{16,0},{1,17},{17,1},{2,18},{18,2},{3,19},{19,3},{4,20},{20... | collective-permute-start | bytes 86024 | tf_op jit(solution)/shard_map/ppermute | solution.py:24
  37.3 0.4 collective-permute-done.14.received
  37.8 1.2 %down.2.refs_0_ = f32[16,2048]{1,0:T(8,128)S(1)} custom-call(bf16[16,1792]{1,0:T(8,128)(2,1)S(1)} %gather_act.3.act, bf16[3584,2048]{1,0:T(8,128)(2,1)S(1)} %bitcast.1), custom_call_target="tpu_custom_call" | custom-call | tf_op jit(solution)/shard_map/down/pallas_call | solution.py:430
  39.0 0.3 collective-permute-done.13.received
  39.3 1.4 %collective-permute-done.12.own = bf16[8,1792]{1,0:T(8,128)(2,1)S(1)} collective-permute-done((bf16[8,1792]{1,0:T(8,128)(2,1)S(1)}, bf16[8,1792]{1,0:T(8,128)(2,1)S(1)}, u32[]{:S(2)}, u32[]{:S(2)}) %collective-permute-start.12) | collective-permute-done | bytes 28704 | tf_op jit(solution)/shard_map/ppermute | solution.py:24
  40.7 1.2 %down.3.refs_0_ = bf16[16,2048]{1,0:T(8,128)(2,1)S(1)} custom-call(bf16[16,1792]{1,0:T(8,128)(2,1)S(1)} %gather_act.2.act, bf16[3584,2048]{1,0:T(8,128)(2,1)S(1)} %bitcast.1, f32[16,2048]{1,0:T(8,128)S(1)} %down.2.refs_0_), custom_call_target="tpu_custom_call" | custom-call | tf_op jit(solution)/shard_map/down/pallas_call | solution.py:430
  41.9 1.1 %collective-permute-start.16 = (bf16[16,2048]{1,0:T(8,128)(2,1)S(1)}, bf16[16,2048]{1,0:T(8,128)(2,1)S(1)}, u32[]{:S(2)}, u32[]{:S(2)}) collective-permute-start(bf16[16,2048]{1,0:T(8,128)(2,1)S(1)} %down.3.refs_0_), channel_id=1, source_target_pairs={{0,2},{1,3},{2,0},{3,1},{4,6},{5,7},{6,4},{7,5},{8,10},{9,11},{10,... | collective-permute-start | bytes 196616 | tf_op jit(solution)/shard_map/ppermute | solution.py:24
  42.9 0.8 %collective-permute-start.15 = (bf16[16,2048]{1,0:T(8,128)(2,1)S(1)}, bf16[16,2048]{1,0:T(8,128)(2,1)S(1)}, u32[]{:S(2)}, u32[]{:S(2)}) collective-permute-start(bf16[16,2048]{1,0:T(8,128)(2,1)S(1)} %down.3.refs_0_), channel_id=1, source_target_pairs={{0,1},{1,0},{2,3},{3,2},{4,5},{5,4},{6,7},{7,6},{8,9},{9,8},{10,11... | collective-permute-start | bytes 196616 | tf_op jit(solution)/shard_map/ppermute | solution.py:24
  43.7 2.5 %collective-permute-done.17.refs_3_ = bf16[16,2048]{1,0:T(8,128)(2,1)S(1)} collective-permute-done((bf16[16,2048]{1,0:T(8,128)(2,1)S(1)}, bf16[16,2048]{1,0:T(8,128)(2,1)S(1)}, u32[]{:S(2)}, u32[]{:S(2)}) %collective-permute-start.17) | collective-permute-done | bytes 65568 | tf_op jit(solution)/shard_map/ppermute | solution.py:24
  46.2 0.6 %collective-permute-done.16.refs_2_ = bf16[16,2048]{1,0:T(8,128)(2,1)S(1)} collective-permute-done((bf16[16,2048]{1,0:T(8,128)(2,1)S(1)}, bf16[16,2048]{1,0:T(8,128)(2,1)S(1)}, u32[]{:S(2)}, u32[]{:S(2)}) %collective-permute-start.16) | collective-permute-done | bytes 65568 | tf_op jit(solution)/shard_map/ppermute | solution.py:24
  46.8 0.7 %final.1 = bf16[2,8,2048]{2,1,0:T(8,128)(2,1)} custom-call(f32[16,2048]{1,0:T(8,128)S(1)} %get-tuple-element.28.mid, bf16[16,2048]{1,0:T(8,128)(2,1)S(1)} %down.3.refs_0_, bf16[16,2048]{1,0:T(8,128)(2,1)S(1)} %collective-permute-done.15.refs_1_, bf16[16,2048]{1,0:T(8,128)(2,1)S(1)} %collective-permute-done.16.refs_2_, ...), custom_call_target="tpu_custom_call" | custom-call | tf_op jit(solution)/shard_map/final/pallas_call | solution.py:444
  (32 shorter events, 0.1 us)
Async XLA Ops:
  0.0 22.6 %slice-start.4 = ((s8[14680064]{0:T(1024)(128)(4,1)}), s8[4194304]{0:T(1024)(128)(4,1)S(1)}, s32[]{:S(2)}) async-start(s8[14680064]{0:T(1024)(128)(4,1)} %bitcast.2), calls=%async_computation.4 | async-start | bytes 8388608
  0.0 22.6 %slice-start.8 = ((s8[14680064]{0:T(1024)(128)(4,1)}), s8[2097152]{0:T(1024)(128)(4,1)S(1)}, s32[]{:S(2)}) async-start(s8[14680064]{0:T(1024)(128)(4,1)} %bitcast.4), calls=%async_computation.8 | async-start | bytes 4194304
  2.0 4.8 %collective-permute-start = (f32[5,8,128]{2,1,0:T(8,128)S(1)}, f32[5,8,128]{2,1,0:T(8,128)S(1)}, u32[]{:S(2)}, u32[]{:S(2)}) collective-permute-start(f32[5,8,128]{2,1,0:T(8,128)S(1)} %get-tuple-element.18), channel_id=1, source_target_pairs={{0,2},{1,3},{2,0},{3,1},{4,6},{5,7},{6,4},{7,5},{8,10},{9,11},{10,... | collective-permute-start | bytes 61448 | tf_op jit(solution)/shard_map/ppermute | solution.py:24
  5.0 3.2 %collective-permute-start.1 = (f32[5,8,128]{2,1,0:T(8,128)S(1)}, f32[5,8,128]{2,1,0:T(8,128)S(1)}, u32[]{:S(2)}, u32[]{:S(2)}) collective-permute-start(f32[5,8,128]{2,1,0:T(8,128)S(1)} %get-tuple-element.19), channel_id=1, source_target_pairs={{0,3},{1,2},{2,1},{3,0},{4,7},{5,6},{6,5},{7,4},{8,11},{9,10},{10,... | collective-permute-start | bytes 61448 | tf_op jit(solution)/shard_map/ppermute | solution.py:24
  5.5 2.7 %collective-permute-start.2 = (f32[5,8,128]{2,1,0:T(8,128)S(1)}, f32[5,8,128]{2,1,0:T(8,128)S(1)}, u32[]{:S(2)}, u32[]{:S(2)}) collective-permute-start(f32[5,8,128]{2,1,0:T(8,128)S(1)} %get-tuple-element.27), channel_id=1, source_target_pairs={{0,1},{1,0},{2,3},{3,2},{4,5},{5,4},{6,7},{7,6},{8,9},{9,8},{10,11... | collective-permute-start | bytes 61448 | tf_op jit(solution)/shard_map/ppermute | solution.py:24
  8.2 8.4 %copy-start = (bf16[1024,2048]{1,0:T(8,128)(2,1)S(1)}, bf16[1024,2048]{1,0:T(8,128)(2,1)}, u32[]{:S(2)}) copy-start(bf16[1024,2048]{1,0:T(8,128)(2,1)} %refs_4_.3) | copy-start | bytes 12582916
  8.2 14.4 %slice-start.5 = ((s8[14680064]{0:T(1024)(128)(4,1)}), s8[4194304]{0:T(1024)(128)(4,1)S(1)}, s32[]{:S(2)}) async-start(s8[14680064]{0:T(1024)(128)(4,1)} %bitcast.2), calls=%async_computation.5 | async-start | bytes 8388608
  8.2 14.4 %slice-start.6 = ((s8[14680064]{0:T(1024)(128)(4,1)}), s8[4194304]{0:T(1024)(128)(4,1)S(1)}, s32[]{:S(2)}) async-start(s8[14680064]{0:T(1024)(128)(4,1)} %bitcast.2), calls=%async_computation.6 | async-start | bytes 8388608
  8.2 14.4 %slice-start.7 = ((s8[14680064]{0:T(1024)(128)(4,1)}), s8[2097152]{0:T(1024)(128)(4,1)S(1)}, s32[]{:S(2)}) async-start(s8[14680064]{0:T(1024)(128)(4,1)} %bitcast.2), calls=%async_computation.7 | async-start | bytes 4194304
  8.2 14.4 %slice-start.9 = ((s8[14680064]{0:T(1024)(128)(4,1)}), s8[4194304]{0:T(1024)(128)(4,1)S(1)}, s32[]{:S(2)}) async-start(s8[14680064]{0:T(1024)(128)(4,1)} %bitcast.4), calls=%async_computation.9 | async-start | bytes 8388608
  8.2 14.4 %slice-start.10 = ((s8[14680064]{0:T(1024)(128)(4,1)}), s8[4194304]{0:T(1024)(128)(4,1)S(1)}, s32[]{:S(2)}) async-start(s8[14680064]{0:T(1024)(128)(4,1)} %bitcast.4), calls=%async_computation.10 | async-start | bytes 8388608
  8.2 14.4 %slice-start.11 = ((s8[14680064]{0:T(1024)(128)(4,1)}), s8[4194304]{0:T(1024)(128)(4,1)S(1)}, s32[]{:S(2)}) async-start(s8[14680064]{0:T(1024)(128)(4,1)} %bitcast.4), calls=%async_computation.11 | async-start | bytes 8388608
  8.3 14.4 %copy-start.1 = (bf16[2,8,2048]{2,1,0:T(8,128)(2,1)S(1)}, bf16[2,8,2048]{2,1,0:T(8,128)(2,1)}, u32[]{:S(2)}) copy-start(bf16[2,8,2048]{2,1,0:T(8,128)(2,1)} %residual.1) | copy-start | bytes 196612
  8.3 14.4 %copy-start.2 = (bf16[2048]{0:T(1024)(128)(2,1)S(1)}, bf16[2048]{0:T(1024)(128)(2,1)}, u32[]{:S(2)}) copy-start(bf16[2048]{0:T(1024)(128)(2,1)} %gains.1) | copy-start | bytes 12292
  8.5 4.6 %collective-permute-start.5 = (bf16[4,1024]{1,0:T(4,128)(2,1)S(1)}, bf16[4,1024]{1,0:T(4,128)(2,1)S(1)}, u32[]{:S(2)}, u32[]{:S(2)}) collective-permute-start(bf16[4,1024]{1,0:T(4,128)(2,1)S(1)} %combine.1.refs_0_), channel_id=1, source_target_pairs={{0,8},{4,12},{8,0},{12,4},{1,9},{5,13},{9,1},{13,5},{2,10},{6,14},... | collective-permute-start | bytes 24584 | tf_op jit(solution)/shard_map/ppermute | solution.py:24
  11.1 5.4 %collective-permute-start.4 = (bf16[4,1024]{1,0:T(4,128)(2,1)S(1)}, bf16[4,1024]{1,0:T(4,128)(2,1)S(1)}, u32[]{:S(2)}, u32[]{:S(2)}) collective-permute-start(bf16[4,1024]{1,0:T(4,128)(2,1)S(1)} %combine.1.refs_0_), channel_id=1, source_target_pairs={{0,12},{4,8},{8,4},{12,0},{1,13},{5,9},{9,5},{13,1},{2,14},{6,10},... | collective-permute-start | bytes 24584 | tf_op jit(solution)/shard_map/ppermute | solution.py:24
  12.5 4.1 %collective-permute-start.3 = (bf16[4,1024]{1,0:T(4,128)(2,1)S(1)}, bf16[4,1024]{1,0:T(4,128)(2,1)S(1)}, u32[]{:S(2)}, u32[]{:S(2)}) collective-permute-start(bf16[4,1024]{1,0:T(4,128)(2,1)S(1)} %combine.1.refs_0_), channel_id=1, source_target_pairs={{0,4},{4,0},{8,12},{12,8},{1,5},{5,1},{9,13},{13,9},{2,6},{6,2},{1... | collective-permute-start | bytes 24584 | tf_op jit(solution)/shard_map/ppermute | solution.py:24
  16.6 21.2 %slice-start = ((s8[14680064]{0:T(1024)(128)(4,1)}), s8[4194304]{0:T(1024)(128)(4,1)S(1)}, s32[]{:S(2)}) async-start(s8[14680064]{0:T(1024)(128)(4,1)} %bitcast), calls=%async_computation | async-start | bytes 8388608
  17.4 20.4 %slice-start.1 = ((s8[14680064]{0:T(1024)(128)(4,1)}), s8[4194304]{0:T(1024)(128)(4,1)S(1)}, s32[]{:S(2)}) async-start(s8[14680064]{0:T(1024)(128)(4,1)} %bitcast), calls=%async_computation.1 | async-start | bytes 8388608
  17.4 20.4 %slice-start.2 = ((s8[14680064]{0:T(1024)(128)(4,1)}), s8[4194304]{0:T(1024)(128)(4,1)S(1)}, s32[]{:S(2)}) async-start(s8[14680064]{0:T(1024)(128)(4,1)} %bitcast), calls=%async_computation.2 | async-start | bytes 8388608
  17.4 20.4 %slice-start.3 = ((s8[14680064]{0:T(1024)(128)(4,1)}), s8[2097152]{0:T(1024)(128)(4,1)S(1)}, s32[]{:S(2)}) async-start(s8[14680064]{0:T(1024)(128)(4,1)} %bitcast), calls=%async_computation.3 | async-start | bytes 4194304
  17.4 4.9 %collective-permute-start.8 = (bf16[16,2048]{1,0:T(8,128)(2,1)S(1)}, bf16[16,2048]{1,0:T(8,128)(2,1)S(1)}, u32[]{:S(2)}, u32[]{:S(2)}) collective-permute-start(bf16[16,2048]{1,0:T(8,128)(2,1)S(1)} %out_projection.1.refs_0_), channel_id=1, source_target_pairs={{0,2},{1,3},{2,0},{3,1},{4,6},{5,7},{6,4},{7,5},{8,10},{9,11},{10,... | collective-permute-start | bytes 196616 | tf_op jit(solution)/shard_map/ppermute | solution.py:24
  18.2 4.4 %collective-permute-start.7 = (bf16[16,2048]{1,0:T(8,128)(2,1)S(1)}, bf16[16,2048]{1,0:T(8,128)(2,1)S(1)}, u32[]{:S(2)}, u32[]{:S(2)}) collective-permute-start(bf16[16,2048]{1,0:T(8,128)(2,1)S(1)} %out_projection.1.refs_0_), channel_id=1, source_target_pairs={{0,3},{1,2},{2,1},{3,0},{4,7},{5,6},{6,5},{7,4},{8,11},{9,10},{10,... | collective-permute-start | bytes 196616 | tf_op jit(solution)/shard_map/ppermute | solution.py:24
  18.2 4.4 %collective-permute-start.6 = (bf16[16,2048]{1,0:T(8,128)(2,1)S(1)}, bf16[16,2048]{1,0:T(8,128)(2,1)S(1)}, u32[]{:S(2)}, u32[]{:S(2)}) collective-permute-start(bf16[16,2048]{1,0:T(8,128)(2,1)S(1)} %out_projection.1.refs_0_), channel_id=1, source_target_pairs={{0,1},{1,0},{2,3},{3,2},{4,5},{5,4},{6,7},{7,6},{8,9},{9,8},{10,11... | collective-permute-start | bytes 196616 | tf_op jit(solution)/shard_map/ppermute | solution.py:24
  25.1 6.7 %collective-permute-start.10 = (bf16[16,1920]{1,0:T(8,128)(2,1)S(1)}, bf16[16,1920]{1,0:T(8,128)(2,1)S(1)}, u32[]{:S(2)}, u32[]{:S(2)}) collective-permute-start(bf16[16,1920]{1,0:T(8,128)(2,1)S(1)} %get-tuple-element.29.refs_0_), channel_id=1, source_target_pairs={{0,8},{4,12},{8,0},{12,4},{1,9},{5,13},{9,1},{13,5},{2,10},{6,14},... | collective-permute-start | bytes 184328 | tf_op jit(solution)/shard_map/ppermute | solution.py:24
  26.3 6.5 %collective-permute-start.11 = (bf16[16,1920]{1,0:T(8,128)(2,1)S(1)}, bf16[16,1920]{1,0:T(8,128)(2,1)S(1)}, u32[]{:S(2)}, u32[]{:S(2)}) collective-permute-start(bf16[16,1920]{1,0:T(8,128)(2,1)S(1)} %get-tuple-element.30), channel_id=1, source_target_pairs={{0,12},{4,8},{8,4},{12,0},{1,13},{5,9},{9,5},{13,1},{2,14},{6,10},... | collective-permute-start | bytes 184328 | tf_op jit(solution)/shard_map/ppermute | solution.py:24
  27.3 6.3 %collective-permute-start.9 = (bf16[16,1920]{1,0:T(8,128)(2,1)S(1)}, bf16[16,1920]{1,0:T(8,128)(2,1)S(1)}, u32[]{:S(2)}, u32[]{:S(2)}) collective-permute-start(bf16[16,1920]{1,0:T(8,128)(2,1)S(1)} %get-tuple-element.30), channel_id=1, source_target_pairs={{0,4},{4,0},{8,12},{12,8},{1,5},{5,1},{9,13},{13,9},{2,6},{6,2},{1... | collective-permute-start | bytes 184328 | tf_op jit(solution)/shard_map/ppermute | solution.py:24
  33.8 3.9 %collective-permute-start.14 = (bf16[8,1792]{1,0:T(8,128)(2,1)S(1)}, bf16[8,1792]{1,0:T(8,128)(2,1)S(1)}, u32[]{:S(2)}, u32[]{:S(2)}) collective-permute-start(bf16[8,1792]{1,0:T(8,128)(2,1)S(1)} %activation.1.own), channel_id=1, source_target_pairs={{0,4},{4,0},{8,12},{12,8},{1,5},{5,1},{9,13},{13,9},{2,6},{6,2},{1... | collective-permute-start | bytes 86024 | tf_op jit(solution)/shard_map/ppermute | solution.py:24
  34.4 4.9 %collective-permute-start.13 = (bf16[8,1792]{1,0:T(8,128)(2,1)S(1)}, bf16[8,1792]{1,0:T(8,128)(2,1)S(1)}, u32[]{:S(2)}, u32[]{:S(2)}) collective-permute-start(bf16[8,1792]{1,0:T(8,128)(2,1)S(1)} %activation.1.own), channel_id=1, source_target_pairs={{0,20},{4,16},{8,28},{12,24},{16,4},{20,0},{24,12},{28,8},{1,21},{... | collective-permute-start | bytes 86024 | tf_op jit(solution)/shard_map/ppermute | solution.py:24
  36.8 3.9 %collective-permute-start.12 = (bf16[8,1792]{1,0:T(8,128)(2,1)S(1)}, bf16[8,1792]{1,0:T(8,128)(2,1)S(1)}, u32[]{:S(2)}, u32[]{:S(2)}) collective-permute-start(bf16[8,1792]{1,0:T(8,128)(2,1)S(1)} %activation.1.own), channel_id=1, source_target_pairs={{0,16},{16,0},{1,17},{17,1},{2,18},{18,2},{3,19},{19,3},{4,20},{20... | collective-permute-start | bytes 86024 | tf_op jit(solution)/shard_map/ppermute | solution.py:24
  41.9 4.3 %collective-permute-start.17 = (bf16[16,2048]{1,0:T(8,128)(2,1)S(1)}, bf16[16,2048]{1,0:T(8,128)(2,1)S(1)}, u32[]{:S(2)}, u32[]{:S(2)}) collective-permute-start(bf16[16,2048]{1,0:T(8,128)(2,1)S(1)} %down.3.refs_0_), channel_id=1, source_target_pairs={{0,3},{1,2},{2,1},{3,0},{4,7},{5,6},{6,5},{7,4},{8,11},{9,10},{10,... | collective-permute-start | bytes 196616 | tf_op jit(solution)/shard_map/ppermute | solution.py:24
  41.9 5.0 %collective-permute-start.16 = (bf16[16,2048]{1,0:T(8,128)(2,1)S(1)}, bf16[16,2048]{1,0:T(8,128)(2,1)S(1)}, u32[]{:S(2)}, u32[]{:S(2)}) collective-permute-start(bf16[16,2048]{1,0:T(8,128)(2,1)S(1)} %down.3.refs_0_), channel_id=1, source_target_pairs={{0,2},{1,3},{2,0},{3,1},{4,6},{5,7},{6,4},{7,5},{8,10},{9,11},{10,... | collective-permute-start | bytes 196616 | tf_op jit(solution)/shard_map/ppermute | solution.py:24
  42.9 3.9 %collective-permute-start.15 = (bf16[16,2048]{1,0:T(8,128)(2,1)S(1)}, bf16[16,2048]{1,0:T(8,128)(2,1)S(1)}, u32[]{:S(2)}, u32[]{:S(2)}) collective-permute-start(bf16[16,2048]{1,0:T(8,128)(2,1)S(1)} %down.3.refs_0_), channel_id=1, source_target_pairs={{0,1},{1,0},{2,3},{3,2},{4,5},{5,4},{6,7},{7,6},{8,9},{9,8},{10,11... | collective-permute-start | bytes 196616 | tf_op jit(solution)/shard_map/ppermute | solution.py:24

commit v10 on v9

--- a/solution.py
+++ b/solution.py
@@ -232,6 +232,10 @@
     return [0, 1, 3, 2] if groups == 4 else list(range(groups))
 
 
+def sum_order(groups):
+    return [0, 3, 1, 2] if groups == 4 else list(range(groups))
+
+
 def out_kernel(groups, *refs):
     weight, out, canon, attended = refs[groups:]
     parts = [refs[gather_order(groups).index(k)] for k in range(groups)]
@@ -253,9 +257,9 @@
     )
 
 
-def lift_kernel(groups, split, residual, gains, gate_weight, up_weight, *refs):
-    mid_out, keep, send, lifted, packed = refs[-5:]
-    parts = [refs[gather_order(len(refs) - 5).index(k)] for k in range(len(refs) - 5)]
+def lift_kernel(groups, cols, split, residual, gains, gate_weight, up_weight, *refs):
+    parts, mid_out, (lifted, packed) = refs[:cols], refs[cols], refs[-2:]
+    outs = refs[cols + 1 : -2]
     hidden = gate_weight.shape[1] // split
     start = lax.axis_index("side") * hidden if split > 1 else 0
     half = packed.shape[1] // 2
@@ -278,12 +282,14 @@
 
     over_columns(hidden, body)
     bit = lax.axis_index("row") & 1
-    keep[...] = packed[bit].astype(keep.dtype)
-    send[...] = packed[1 - bit].astype(send.dtype)
+    mine, theirs = (packed[i].astype(outs[0].dtype) for i in (bit, 1 - bit))
+    for k, out in enumerate(outs):
+        out[...] = theirs if k % 2 else mine
 
 
 def act_kernel(model, *refs):
-    parts, out = refs[:-1], refs[-1]
+    out = refs[-1]
+    parts = [refs[sum_order(len(refs) - 1).index(k)] for k in range(len(refs) - 1)]
     hidden = parts[0].shape[1] - HD
     cells = parts[0].shape[0] // 2
     values = [p[...].astype(jnp.float32) for p in parts]
@@ -400,23 +406,23 @@
         name="out_projection",
     )(*[gathered[k] for k in gather_order(groups)], in_vmem(out_weight))
     partials = spread(partial, "col")
-    mid, keep, send = call(
-        functools.partial(lift_kernel, groups, split),
-        [shape((m, width_share), f32)] + [shape((m, hidden + HD), WIRE)] * 2,
+    mid, *sums = call(
+        functools.partial(lift_kernel, groups, cols, split),
+        [shape((m, width_share), f32)] + [shape((m, hidden + HD), WIRE)] * groups,
         [VMEM_SPEC] * (cols + 4),
         [pltpu.VMEM((m, width_share), bf16), pltpu.VMEM((2, m, hidden + HD), f32)],
         name="gate_up",
     )(
         in_vmem(residual), in_vmem(norm_gain), in_vmem(gate_weight), in_vmem(up_weight),
-        *[partials[k] for k in gather_order(cols)],
-    )
-    sums = [keep] + [partner((keep, send)[k % 2], "row", k) for k in range(1, groups)]
+        *partials,
+    )
+    sums = sums[:1] + [partner(sums[k], "row", k) for k in range(1, groups)]
     act = call(
         functools.partial(act_kernel, model),
         shape((m // 2, hidden), bf16),
         [VMEM_SPEC] * groups,
         name="activation",
-    )(*sums)
+    )(*[sums[k] for k in sum_order(groups)])
     down_weight = in_vmem(down_weight)
 
     def down_part(same, from_row, other, before, result):

time: 47.7 us -> 48.1 us (level)
  starting transfers between devices: 18.7 us -> 19.3 us
    ppermute x18, starting transfers between devices: 18.7 us -> 19.3 us  [partner(): lax.ppermute(value, axis, [(i, i ^ k) for i in range(lax.axis_size(axis))])]
where the time goes in v10:
time: 48.1 us; the launch traced here: 47.9 us
  starting transfers between devices  19.3 us (40%)
  waiting for transfers between devices  19.3 us (40%)
  Pallas kernels  9 us (19%)
    ppermute x18, starting transfers between devices, partner(): lax.ppermute(value, axis, [(i, i ^ k) for i in range(lax.axis_size(axis))])  19.3 us
    ppermute x18, waiting for transfers between devices, partner(): lax.ppermute(value, axis, [(i, i ^ k) for i in range(lax.axis_size(axis))])  19.3 us
    pallas_call x2, Pallas kernels, down_part(): call(functools.partial(down_kernel, other), shape((m, width_share), resul...  2.37 us
    pallas_call x1, Pallas kernels, shards(): call(functools.partial(lift_kernel, groups, cols, split), [shape((m, widt...  2.34 us
    pallas_call x1, Pallas kernels, shards(): call(functools.partial(attention_far_kernel, cols), [message] * (cols //...  1.94 us
  transfers between devices with their start and end apart: 18, of which 14 were waited for; matrix products, arithmetic and copies ran while one was open for 0% of the time, Pallas kernels for 4%

profile of v10, /device:TPU:0, one launch (start us, length us, event | category | flops | bytes accessed | tf_op | source)
XLA Modules:
  0.0 47.9 jit_solution(6608827953912194953)
XLA Ops:
  0.0 1.9 %attention_far.1 = (f32[5,8,128]{2,1,0:T(8,128)S(1)}, f32[5,8,128]{2,1,0:T(8,128)S(1)}, bf16[2,2,2048]{2,1,0:T(2,128)(2,1)S(1)}, bf16[2,2,256]{2,1,0:T(2,128)(2,...) custom-call(bf16[2,2,4096]{2,1,0:T(2,128)(2,1)} %refs_0_.1, ...), custom_call_target="tpu_custom_call" | custom-call | tf_op jit(solution)/shard_map/attention_far/pallas_call | solution.py:374
  2.0 3.0 %collective-permute-start = (f32[5,8,128]{2,1,0:T(8,128)S(1)}, f32[5,8,128]{2,1,0:T(8,128)S(1)}, u32[]{:S(2)}, u32[]{:S(2)}) collective-permute-start(f32[5,8,128]{2,1,0:T(8,128)S(1)} %get-tuple-element.20), channel_id=1, source_target_pairs={{0,2},{1,3},{2,0},{3,1},{4,6},{5,7},{6,4},{7,5},{8,10},{9,11},{10,... | collective-permute-start | bytes 61448 | tf_op jit(solution)/shard_map/ppermute | solution.py:24
  5.0 0.0 collective-permute-start.1
  5.0 0.5 %attention_near.1 = (f32[5,8,128]{2,1,0:T(8,128)S(1)}, f32[5,8,128]{2,1,0:T(8,128)S(1)}) custom-call(bf16[2,2,2048]{2,1,0:T(2,128)(2,1)S(1)} %get-tuple-element.22.refs_0_, bf16[2,2,256]{2,1,0:T(2,128)(2,1)S(1)} %get-tuple-element.23.refs_1_, bf16[2,2,256]{2,1,0:T(2,128)(2,1)S(1)} %get-tuple-element.24.refs_2_, ...), custom_call_target="tpu_custom_call" | custom-call | tf_op jit(solution)/shard_map/attention_near/pallas_call | solution.py:385
  5.5 0.3 collective-permute-start.2
  5.7 1.0 %collective-permute-done.refs_0_ = f32[5,8,128]{2,1,0:T(8,128)S(1)} collective-permute-done((f32[5,8,128]{2,1,0:T(8,128)S(1)}, f32[5,8,128]{2,1,0:T(8,128)S(1)}, u32[]{:S(2)}, u32[]{:S(2)}) %collective-permute-start) | collective-permute-done | bytes 20512 | tf_op jit(solution)/shard_map/ppermute | solution.py:24
  6.8 1.4 %collective-permute-done.1.refs_1_ = f32[5,8,128]{2,1,0:T(8,128)S(1)} collective-permute-done((f32[5,8,128]{2,1,0:T(8,128)S(1)}, f32[5,8,128]{2,1,0:T(8,128)S(1)}, u32[]{:S(2)}, u32[]{:S(2)}) %collective-permute-start.1) | collective-permute-done | bytes 20512 | tf_op jit(solution)/shard_map/ppermute | solution.py:24
  8.2 0.0 collective-permute-done.2.refs_3_
  8.2 0.0 slice-start.9
  8.2 0.0 slice-start.10
  8.3 0.0 copy-start.1
  8.3 0.0 copy-start.2
  8.3 0.2 combine.1.refs_0_
  8.5 2.7 %collective-permute-start.5 = (bf16[4,1024]{1,0:T(4,128)(2,1)S(1)}, bf16[4,1024]{1,0:T(4,128)(2,1)S(1)}, u32[]{:S(2)}, u32[]{:S(2)}) collective-permute-start(bf16[4,1024]{1,0:T(4,128)(2,1)S(1)} %combine.1.refs_0_), channel_id=1, source_target_pairs={{0,8},{4,12},{8,0},{12,4},{1,9},{5,13},{9,1},{13,5},{2,10},{6,14},... | collective-permute-start | bytes 24584 | tf_op jit(solution)/shard_map/ppermute | solution.py:24
  11.1 1.3 %collective-permute-start.4 = (bf16[4,1024]{1,0:T(4,128)(2,1)S(1)}, bf16[4,1024]{1,0:T(4,128)(2,1)S(1)}, u32[]{:S(2)}, u32[]{:S(2)}) collective-permute-start(bf16[4,1024]{1,0:T(4,128)(2,1)S(1)} %combine.1.refs_0_), channel_id=1, source_target_pairs={{0,12},{4,8},{8,4},{12,0},{1,13},{5,9},{9,5},{13,1},{2,14},{6,10},... | collective-permute-start | bytes 24584 | tf_op jit(solution)/shard_map/ppermute | solution.py:24
  12.5 0.2 collective-permute-start.3
  12.7 0.4 collective-permute-done.5.refs_3_
  13.1 3.5 %collective-permute-done.4.refs_2_ = bf16[4,1024]{1,0:T(4,128)(2,1)S(1)} collective-permute-done((bf16[4,1024]{1,0:T(4,128)(2,1)S(1)}, bf16[4,1024]{1,0:T(4,128)(2,1)S(1)}, u32[]{:S(2)}, u32[]{:S(2)}) %collective-permute-start.4) | collective-permute-done | bytes 8224 | tf_op jit(solution)/shard_map/ppermute | solution.py:24
  16.6 0.8 %out_projection.1.refs_0_ = bf16[16,2048]{1,0:T(8,128)(2,1)S(1)} custom-call(bf16[4,1024]{1,0:T(4,128)(2,1)S(1)} %combine.1.refs_0_, bf16[4,1024]{1,0:T(4,128)(2,1)S(1)} %collective-permute-done.3.refs_1_, bf16[4,1024]{1,0:T(4,128)(2,1)S(1)} %collective-permute-done.4.refs_2_, bf16[4,1024]{1,0:T(4,128)(2,1)S(1)} %collective-permute-done.5.refs_3_, ...), custom_call_target="tpu_custom_call" | custom-call | tf_op jit(solution)/shard_map/out_projection/pallas_call | solution.py:401
  17.4 0.1 collective-permute-start.8
  17.5 0.8 %collective-permute-start.7 = (bf16[16,2048]{1,0:T(8,128)(2,1)S(1)}, bf16[16,2048]{1,0:T(8,128)(2,1)S(1)}, u32[]{:S(2)}, u32[]{:S(2)}) collective-permute-start(bf16[16,2048]{1,0:T(8,128)(2,1)S(1)} %out_projection.1.refs_0_), channel_id=1, source_target_pairs={{0,2},{1,3},{2,0},{3,1},{4,6},{5,7},{6,4},{7,5},{8,10},{9,11},{10,... | collective-permute-start | bytes 196616 | tf_op jit(solution)/shard_map/ppermute | solution.py:24
  18.3 1.0 %collective-permute-start.6 = (bf16[16,2048]{1,0:T(8,128)(2,1)S(1)}, bf16[16,2048]{1,0:T(8,128)(2,1)S(1)}, u32[]{:S(2)}, u32[]{:S(2)}) collective-permute-start(bf16[16,2048]{1,0:T(8,128)(2,1)S(1)} %out_projection.1.refs_0_), channel_id=1, source_target_pairs={{0,1},{1,0},{2,3},{3,2},{4,5},{5,4},{6,7},{7,6},{8,9},{9,8},{10,11... | collective-permute-start | bytes 196616 | tf_op jit(solution)/shard_map/ppermute | solution.py:24
  19.3 1.9 %collective-permute-done.8.refs_3_ = bf16[16,2048]{1,0:T(8,128)(2,1)S(1)} collective-permute-done((bf16[16,2048]{1,0:T(8,128)(2,1)S(1)}, bf16[16,2048]{1,0:T(8,128)(2,1)S(1)}, u32[]{:S(2)}, u32[]{:S(2)}) %collective-permute-start.8) | collective-permute-done | bytes 65568 | tf_op jit(solution)/shard_map/ppermute | solution.py:24
  21.3 1.2 %collective-permute-done.7.refs_2_ = bf16[16,2048]{1,0:T(8,128)(2,1)S(1)} collective-permute-done((bf16[16,2048]{1,0:T(8,128)(2,1)S(1)}, bf16[16,2048]{1,0:T(8,128)(2,1)S(1)}, u32[]{:S(2)}, u32[]{:S(2)}) %collective-permute-start.7) | collective-permute-done | bytes 65568 | tf_op jit(solution)/shard_map/ppermute | solution.py:24
  22.5 0.0 collective-permute-done.6.refs_1_
  22.6 2.3 %gate_up.1 = (f32[16,2048]{1,0:T(8,128)S(1)}, bf16[16,1920]{1,0:T(8,128)(2,1)S(1)}, bf16[16,1920]{1,0:T(8,128)(2,1)S(1)}, bf16[16,1920]{1,0:T(8,128)(2,1)S(1)}, bf16[16,1920]{1,0:T(8,128)(2,1)S(1)}) custom-call(bf16[2,8,2048]{2,1,0:T(8,128)(2,1)S(1)} %copy-done.1, bf16[2048]{0:T(1024)(128)(2,1)S(1)} %copy-done.2, bf16[2048,3584]{1,0:T(8,128)(2,1)S(1)} %bitcast.3, ...), custom_call_target="tpu_custom_call" | custom-call | tf_op jit(solution)/shard_map/gate_up/pallas_call | solution.py:409
  24.9 2.1 %collective-permute-start.9 = (bf16[16,1920]{1,0:T(8,128)(2,1)S(1)}, bf16[16,1920]{1,0:T(8,128)(2,1)S(1)}, u32[]{:S(2)}, u32[]{:S(2)}) collective-permute-start(bf16[16,1920]{1,0:T(8,128)(2,1)S(1)} %get-tuple-element.32), channel_id=1, source_target_pairs={{0,12},{4,8},{8,4},{12,0},{1,13},{5,9},{9,5},{13,1},{2,14},{6,10},... | collective-permute-start | bytes 184328 | tf_op jit(solution)/shard_map/ppermute | solution.py:24
  27.0 0.0 collective-permute-start.10
  27.0 2.4 %collective-permute-start.11 = (bf16[16,1920]{1,0:T(8,128)(2,1)S(1)}, bf16[16,1920]{1,0:T(8,128)(2,1)S(1)}, u32[]{:S(2)}, u32[]{:S(2)}) collective-permute-start(bf16[16,1920]{1,0:T(8,128)(2,1)S(1)} %get-tuple-element.34), channel_id=1, source_target_pairs={{0,8},{4,12},{8,0},{12,4},{1,9},{5,13},{9,1},{13,5},{2,10},{6,14},... | collective-permute-start | bytes 184328 | tf_op jit(solution)/shard_map/ppermute | solution.py:24
  29.4 2.1 %collective-permute-done.9.refs_1_ = bf16[16,1920]{1,0:T(8,128)(2,1)S(1)} collective-permute-done((bf16[16,1920]{1,0:T(8,128)(2,1)S(1)}, bf16[16,1920]{1,0:T(8,128)(2,1)S(1)}, u32[]{:S(2)}, u32[]{:S(2)}) %collective-permute-start.9) | collective-permute-done | bytes 61472 | tf_op jit(solution)/shard_map/ppermute | solution.py:24
  31.5 1.8 %collective-permute-done.10.refs_2_ = bf16[16,1920]{1,0:T(8,128)(2,1)S(1)} collective-permute-done((bf16[16,1920]{1,0:T(8,128)(2,1)S(1)}, bf16[16,1920]{1,0:T(8,128)(2,1)S(1)}, u32[]{:S(2)}, u32[]{:S(2)}) %collective-permute-start.10) | collective-permute-done | bytes 61472 | tf_op jit(solution)/shard_map/ppermute | solution.py:24
  33.3 0.3 collective-permute-done.11.refs_3_
  33.6 0.1 activation.1.own
  33.8 0.6 %collective-permute-start.14 = (bf16[8,1792]{1,0:T(8,128)(2,1)S(1)}, bf16[8,1792]{1,0:T(8,128)(2,1)S(1)}, u32[]{:S(2)}, u32[]{:S(2)}) collective-permute-start(bf16[8,1792]{1,0:T(8,128)(2,1)S(1)} %activation.1.own), channel_id=1, source_target_pairs={{0,4},{4,0},{8,12},{12,8},{1,5},{5,1},{9,13},{13,9},{2,6},{6,2},{1... | collective-permute-start | bytes 86024 | tf_op jit(solution)/shard_map/ppermute | solution.py:24
  34.4 2.4 %collective-permute-start.13 = (bf16[8,1792]{1,0:T(8,128)(2,1)S(1)}, bf16[8,1792]{1,0:T(8,128)(2,1)S(1)}, u32[]{:S(2)}, u32[]{:S(2)}) collective-permute-start(bf16[8,1792]{1,0:T(8,128)(2,1)S(1)} %activation.1.own), channel_id=1, source_target_pairs={{0,20},{4,16},{8,28},{12,24},{16,4},{20,0},{24,12},{28,8},{1,21},{... | collective-permute-start | bytes 86024 | tf_op jit(solution)/shard_map/ppermute | solution.py:24
  36.8 0.5 %collective-permute-start.12 = (bf16[8,1792]{1,0:T(8,128)(2,1)S(1)}, bf16[8,1792]{1,0:T(8,128)(2,1)S(1)}, u32[]{:S(2)}, u32[]{:S(2)}) collective-permute-start(bf16[8,1792]{1,0:T(8,128)(2,1)S(1)} %activation.1.own), channel_id=1, source_target_pairs={{0,16},{16,0},{1,17},{17,1},{2,18},{18,2},{3,19},{19,3},{4,20},{20... | collective-permute-start | bytes 86024 | tf_op jit(solution)/shard_map/ppermute | solution.py:24
  37.3 0.4 collective-permute-done.14.received
  37.8 1.2 %down.2.refs_0_ = f32[16,2048]{1,0:T(8,128)S(1)} custom-call(bf16[16,1792]{1,0:T(8,128)(2,1)S(1)} %gather_act.3.act, bf16[3584,2048]{1,0:T(8,128)(2,1)S(1)} %bitcast.1), custom_call_target="tpu_custom_call" | custom-call | tf_op jit(solution)/shard_map/down/pallas_call | solution.py:436
  39.0 0.2 collective-permute-done.13.received
  39.1 1.5 %collective-permute-done.12.own = bf16[8,1792]{1,0:T(8,128)(2,1)S(1)} collective-permute-done((bf16[8,1792]{1,0:T(8,128)(2,1)S(1)}, bf16[8,1792]{1,0:T(8,128)(2,1)S(1)}, u32[]{:S(2)}, u32[]{:S(2)}) %collective-permute-start.12) | collective-permute-done | bytes 28704 | tf_op jit(solution)/shard_map/ppermute | solution.py:24
  40.7 1.2 %down.3.refs_0_ = bf16[16,2048]{1,0:T(8,128)(2,1)S(1)} custom-call(bf16[16,1792]{1,0:T(8,128)(2,1)S(1)} %gather_act.2.act, bf16[3584,2048]{1,0:T(8,128)(2,1)S(1)} %bitcast.1, f32[16,2048]{1,0:T(8,128)S(1)} %down.2.refs_0_), custom_call_target="tpu_custom_call" | custom-call | tf_op jit(solution)/shard_map/down/pallas_call | solution.py:436
  41.9 0.0 collective-permute-start.17
  41.9 1.3 %collective-permute-start.16 = (bf16[16,2048]{1,0:T(8,128)(2,1)S(1)}, bf16[16,2048]{1,0:T(8,128)(2,1)S(1)}, u32[]{:S(2)}, u32[]{:S(2)}) collective-permute-start(bf16[16,2048]{1,0:T(8,128)(2,1)S(1)} %down.3.refs_0_), channel_id=1, source_target_pairs={{0,2},{1,3},{2,0},{3,1},{4,6},{5,7},{6,4},{7,5},{8,10},{9,11},{10,... | collective-permute-start | bytes 196616 | tf_op jit(solution)/shard_map/ppermute | solution.py:24
  43.1 0.6 %collective-permute-start.15 = (bf16[16,2048]{1,0:T(8,128)(2,1)S(1)}, bf16[16,2048]{1,0:T(8,128)(2,1)S(1)}, u32[]{:S(2)}, u32[]{:S(2)}) collective-permute-start(bf16[16,2048]{1,0:T(8,128)(2,1)S(1)} %down.3.refs_0_), channel_id=1, source_target_pairs={{0,1},{1,0},{2,3},{3,2},{4,5},{5,4},{6,7},{7,6},{8,9},{9,8},{10,11... | collective-permute-start | bytes 196616 | tf_op jit(solution)/shard_map/ppermute | solution.py:24
  43.7 2.5 %collective-permute-done.17.refs_3_ = bf16[16,2048]{1,0:T(8,128)(2,1)S(1)} collective-permute-done((bf16[16,2048]{1,0:T(8,128)(2,1)S(1)}, bf16[16,2048]{1,0:T(8,128)(2,1)S(1)}, u32[]{:S(2)}, u32[]{:S(2)}) %collective-permute-start.17) | collective-permute-done | bytes 65568 | tf_op jit(solution)/shard_map/ppermute | solution.py:24
  46.3 0.9 %collective-permute-done.16.refs_2_ = bf16[16,2048]{1,0:T(8,128)(2,1)S(1)} collective-permute-done((bf16[16,2048]{1,0:T(8,128)(2,1)S(1)}, bf16[16,2048]{1,0:T(8,128)(2,1)S(1)}, u32[]{:S(2)}, u32[]{:S(2)}) %collective-permute-start.16) | collective-permute-done | bytes 65568 | tf_op jit(solution)/shard_map/ppermute | solution.py:24
  47.2 0.0 collective-permute-done.15.refs_1_
  47.2 0.7 %final.1 = bf16[2,8,2048]{2,1,0:T(8,128)(2,1)} custom-call(f32[16,2048]{1,0:T(8,128)S(1)} %get-tuple-element.30.mid, bf16[16,2048]{1,0:T(8,128)(2,1)S(1)} %down.3.refs_0_, bf16[16,2048]{1,0:T(8,128)(2,1)S(1)} %collective-permute-done.15.refs_1_, bf16[16,2048]{1,0:T(8,128)(2,1)S(1)} %collective-permute-done.16.refs_2_, ...), custom_call_target="tpu_custom_call" | custom-call | tf_op jit(solution)/shard_map/final/pallas_call | solution.py:450
  (32 shorter events, 0.1 us)
Async XLA Ops:
  0.0 22.5 %slice-start.4 = ((s8[14680064]{0:T(1024)(128)(4,1)}), s8[4194304]{0:T(1024)(128)(4,1)S(1)}, s32[]{:S(2)}) async-start(s8[14680064]{0:T(1024)(128)(4,1)} %bitcast.2), calls=%async_computation.4 | async-start | bytes 8388608
  0.0 22.5 %slice-start.8 = ((s8[14680064]{0:T(1024)(128)(4,1)}), s8[2097152]{0:T(1024)(128)(4,1)S(1)}, s32[]{:S(2)}) async-start(s8[14680064]{0:T(1024)(128)(4,1)} %bitcast.4), calls=%async_computation.8 | async-start | bytes 4194304
  2.0 4.8 %collective-permute-start = (f32[5,8,128]{2,1,0:T(8,128)S(1)}, f32[5,8,128]{2,1,0:T(8,128)S(1)}, u32[]{:S(2)}, u32[]{:S(2)}) collective-permute-start(f32[5,8,128]{2,1,0:T(8,128)S(1)} %get-tuple-element.20), channel_id=1, source_target_pairs={{0,2},{1,3},{2,0},{3,1},{4,6},{5,7},{6,4},{7,5},{8,10},{9,11},{10,... | collective-permute-start | bytes 61448 | tf_op jit(solution)/shard_map/ppermute | solution.py:24
  5.0 3.2 %collective-permute-start.1 = (f32[5,8,128]{2,1,0:T(8,128)S(1)}, f32[5,8,128]{2,1,0:T(8,128)S(1)}, u32[]{:S(2)}, u32[]{:S(2)}) collective-permute-start(f32[5,8,128]{2,1,0:T(8,128)S(1)} %get-tuple-element.21), channel_id=1, source_target_pairs={{0,3},{1,2},{2,1},{3,0},{4,7},{5,6},{6,5},{7,4},{8,11},{9,10},{10,... | collective-permute-start | bytes 61448 | tf_op jit(solution)/shard_map/ppermute | solution.py:24
  5.5 2.7 %collective-permute-start.2 = (f32[5,8,128]{2,1,0:T(8,128)S(1)}, f32[5,8,128]{2,1,0:T(8,128)S(1)}, u32[]{:S(2)}, u32[]{:S(2)}) collective-permute-start(f32[5,8,128]{2,1,0:T(8,128)S(1)} %get-tuple-element.29), channel_id=1, source_target_pairs={{0,1},{1,0},{2,3},{3,2},{4,5},{5,4},{6,7},{7,6},{8,9},{9,8},{10,11... | collective-permute-start | bytes 61448 | tf_op jit(solution)/shard_map/ppermute | solution.py:24
  8.2 8.4 %copy-start = (bf16[1024,2048]{1,0:T(8,128)(2,1)S(1)}, bf16[1024,2048]{1,0:T(8,128)(2,1)}, u32[]{:S(2)}) copy-start(bf16[1024,2048]{1,0:T(8,128)(2,1)} %refs_4_.3) | copy-start | bytes 12582916
  8.2 14.3 %slice-start.5 = ((s8[14680064]{0:T(1024)(128)(4,1)}), s8[4194304]{0:T(1024)(128)(4,1)S(1)}, s32[]{:S(2)}) async-start(s8[14680064]{0:T(1024)(128)(4,1)} %bitcast.2), calls=%async_computation.5 | async-start | bytes 8388608
  8.2 14.3 %slice-start.6 = ((s8[14680064]{0:T(1024)(128)(4,1)}), s8[4194304]{0:T(1024)(128)(4,1)S(1)}, s32[]{:S(2)}) async-start(s8[14680064]{0:T(1024)(128)(4,1)} %bitcast.2), calls=%async_computation.6 | async-start | bytes 8388608
  8.2 14.3 %slice-start.7 = ((s8[14680064]{0:T(1024)(128)(4,1)}), s8[2097152]{0:T(1024)(128)(4,1)S(1)}, s32[]{:S(2)}) async-start(s8[14680064]{0:T(1024)(128)(4,1)} %bitcast.2), calls=%async_computation.7 | async-start | bytes 4194304
  8.2 14.3 %slice-start.9 = ((s8[14680064]{0:T(1024)(128)(4,1)}), s8[4194304]{0:T(1024)(128)(4,1)S(1)}, s32[]{:S(2)}) async-start(s8[14680064]{0:T(1024)(128)(4,1)} %bitcast.4), calls=%async_computation.9 | async-start | bytes 8388608
  8.2 14.3 %slice-start.10 = ((s8[14680064]{0:T(1024)(128)(4,1)}), s8[4194304]{0:T(1024)(128)(4,1)S(1)}, s32[]{:S(2)}) async-start(s8[14680064]{0:T(1024)(128)(4,1)} %bitcast.4), calls=%async_computation.10 | async-start | bytes 8388608
  8.2 14.3 %slice-start.11 = ((s8[14680064]{0:T(1024)(128)(4,1)}), s8[4194304]{0:T(1024)(128)(4,1)S(1)}, s32[]{:S(2)}) async-start(s8[14680064]{0:T(1024)(128)(4,1)} %bitcast.4), calls=%async_computation.11 | async-start | bytes 8388608
  8.3 14.3 %copy-start.1 = (bf16[2,8,2048]{2,1,0:T(8,128)(2,1)S(1)}, bf16[2,8,2048]{2,1,0:T(8,128)(2,1)}, u32[]{:S(2)}) copy-start(bf16[2,8,2048]{2,1,0:T(8,128)(2,1)} %residual.1) | copy-start | bytes 196612
  8.3 14.3 %copy-start.2 = (bf16[2048]{0:T(1024)(128)(2,1)S(1)}, bf16[2048]{0:T(1024)(128)(2,1)}, u32[]{:S(2)}) copy-start(bf16[2048]{0:T(1024)(128)(2,1)} %gains.1) | copy-start | bytes 12292
  8.5 4.6 %collective-permute-start.5 = (bf16[4,1024]{1,0:T(4,128)(2,1)S(1)}, bf16[4,1024]{1,0:T(4,128)(2,1)S(1)}, u32[]{:S(2)}, u32[]{:S(2)}) collective-permute-start(bf16[4,1024]{1,0:T(4,128)(2,1)S(1)} %combine.1.refs_0_), channel_id=1, source_target_pairs={{0,8},{4,12},{8,0},{12,4},{1,9},{5,13},{9,1},{13,5},{2,10},{6,14},... | collective-permute-start | bytes 24584 | tf_op jit(solution)/shard_map/ppermute | solution.py:24
  11.1 5.4 %collective-permute-start.4 = (bf16[4,1024]{1,0:T(4,128)(2,1)S(1)}, bf16[4,1024]{1,0:T(4,128)(2,1)S(1)}, u32[]{:S(2)}, u32[]{:S(2)}) collective-permute-start(bf16[4,1024]{1,0:T(4,128)(2,1)S(1)} %combine.1.refs_0_), channel_id=1, source_target_pairs={{0,12},{4,8},{8,4},{12,0},{1,13},{5,9},{9,5},{13,1},{2,14},{6,10},... | collective-permute-start | bytes 24584 | tf_op jit(solution)/shard_map/ppermute | solution.py:24
  12.5 4.1 %collective-permute-start.3 = (bf16[4,1024]{1,0:T(4,128)(2,1)S(1)}, bf16[4,1024]{1,0:T(4,128)(2,1)S(1)}, u32[]{:S(2)}, u32[]{:S(2)}) collective-permute-start(bf16[4,1024]{1,0:T(4,128)(2,1)S(1)} %combine.1.refs_0_), channel_id=1, source_target_pairs={{0,4},{4,0},{8,12},{12,8},{1,5},{5,1},{9,13},{13,9},{2,6},{6,2},{1... | collective-permute-start | bytes 24584 | tf_op jit(solution)/shard_map/ppermute | solution.py:24
  16.6 21.2 %slice-start = ((s8[14680064]{0:T(1024)(128)(4,1)}), s8[4194304]{0:T(1024)(128)(4,1)S(1)}, s32[]{:S(2)}) async-start(s8[14680064]{0:T(1024)(128)(4,1)} %bitcast), calls=%async_computation | async-start | bytes 8388608
  17.4 20.4 %slice-start.1 = ((s8[14680064]{0:T(1024)(128)(4,1)}), s8[4194304]{0:T(1024)(128)(4,1)S(1)}, s32[]{:S(2)}) async-start(s8[14680064]{0:T(1024)(128)(4,1)} %bitcast), calls=%async_computation.1 | async-start | bytes 8388608
  17.4 20.4 %slice-start.2 = ((s8[14680064]{0:T(1024)(128)(4,1)}), s8[4194304]{0:T(1024)(128)(4,1)S(1)}, s32[]{:S(2)}) async-start(s8[14680064]{0:T(1024)(128)(4,1)} %bitcast), calls=%async_computation.2 | async-start | bytes 8388608
  17.4 20.4 %slice-start.3 = ((s8[14680064]{0:T(1024)(128)(4,1)}), s8[2097152]{0:T(1024)(128)(4,1)S(1)}, s32[]{:S(2)}) async-start(s8[14680064]{0:T(1024)(128)(4,1)} %bitcast), calls=%async_computation.3 | async-start | bytes 4194304
  17.4 3.9 %collective-permute-start.8 = (bf16[16,2048]{1,0:T(8,128)(2,1)S(1)}, bf16[16,2048]{1,0:T(8,128)(2,1)S(1)}, u32[]{:S(2)}, u32[]{:S(2)}) collective-permute-start(bf16[16,2048]{1,0:T(8,128)(2,1)S(1)} %out_projection.1.refs_0_), channel_id=1, source_target_pairs={{0,3},{1,2},{2,1},{3,0},{4,7},{5,6},{6,5},{7,4},{8,11},{9,10},{10,... | collective-permute-start | bytes 196616 | tf_op jit(solution)/shard_map/ppermute | solution.py:24
  17.5 5.0 %collective-permute-start.7 = (bf16[16,2048]{1,0:T(8,128)(2,1)S(1)}, bf16[16,2048]{1,0:T(8,128)(2,1)S(1)}, u32[]{:S(2)}, u32[]{:S(2)}) collective-permute-start(bf16[16,2048]{1,0:T(8,128)(2,1)S(1)} %out_projection.1.refs_0_), channel_id=1, source_target_pairs={{0,2},{1,3},{2,0},{3,1},{4,6},{5,7},{6,4},{7,5},{8,10},{9,11},{10,... | collective-permute-start | bytes 196616 | tf_op jit(solution)/shard_map/ppermute | solution.py:24
  18.3 4.2 %collective-permute-start.6 = (bf16[16,2048]{1,0:T(8,128)(2,1)S(1)}, bf16[16,2048]{1,0:T(8,128)(2,1)S(1)}, u32[]{:S(2)}, u32[]{:S(2)}) collective-permute-start(bf16[16,2048]{1,0:T(8,128)(2,1)S(1)} %out_projection.1.refs_0_), channel_id=1, source_target_pairs={{0,1},{1,0},{2,3},{3,2},{4,5},{5,4},{6,7},{7,6},{8,9},{9,8},{10,11... | collective-permute-start | bytes 196616 | tf_op jit(solution)/shard_map/ppermute | solution.py:24
  24.9 6.6 %collective-permute-start.9 = (bf16[16,1920]{1,0:T(8,128)(2,1)S(1)}, bf16[16,1920]{1,0:T(8,128)(2,1)S(1)}, u32[]{:S(2)}, u32[]{:S(2)}) collective-permute-start(bf16[16,1920]{1,0:T(8,128)(2,1)S(1)} %get-tuple-element.32), channel_id=1, source_target_pairs={{0,12},{4,8},{8,4},{12,0},{1,13},{5,9},{9,5},{13,1},{2,14},{6,10},... | collective-permute-start | bytes 184328 | tf_op jit(solution)/shard_map/ppermute | solution.py:24
  27.0 6.3 %collective-permute-start.10 = (bf16[16,1920]{1,0:T(8,128)(2,1)S(1)}, bf16[16,1920]{1,0:T(8,128)(2,1)S(1)}, u32[]{:S(2)}, u32[]{:S(2)}) collective-permute-start(bf16[16,1920]{1,0:T(8,128)(2,1)S(1)} %get-tuple-element.33), channel_id=1, source_target_pairs={{0,4},{4,0},{8,12},{12,8},{1,5},{5,1},{9,13},{13,9},{2,6},{6,2},{1... | collective-permute-start | bytes 184328 | tf_op jit(solution)/shard_map/ppermute | solution.py:24
  27.0 6.6 %collective-permute-start.11 = (bf16[16,1920]{1,0:T(8,128)(2,1)S(1)}, bf16[16,1920]{1,0:T(8,128)(2,1)S(1)}, u32[]{:S(2)}, u32[]{:S(2)}) collective-permute-start(bf16[16,1920]{1,0:T(8,128)(2,1)S(1)} %get-tuple-element.34), channel_id=1, source_target_pairs={{0,8},{4,12},{8,0},{12,4},{1,9},{5,13},{9,1},{13,5},{2,10},{6,14},... | collective-permute-start | bytes 184328 | tf_op jit(solution)/shard_map/ppermute | solution.py:24
  33.8 3.9 %collective-permute-start.14 = (bf16[8,1792]{1,0:T(8,128)(2,1)S(1)}, bf16[8,1792]{1,0:T(8,128)(2,1)S(1)}, u32[]{:S(2)}, u32[]{:S(2)}) collective-permute-start(bf16[8,1792]{1,0:T(8,128)(2,1)S(1)} %activation.1.own), channel_id=1, source_target_pairs={{0,4},{4,0},{8,12},{12,8},{1,5},{5,1},{9,13},{13,9},{2,6},{6,2},{1... | collective-permute-start | bytes 86024 | tf_op jit(solution)/shard_map/ppermute | solution.py:24
  34.4 4.8 %collective-permute-start.13 = (bf16[8,1792]{1,0:T(8,128)(2,1)S(1)}, bf16[8,1792]{1,0:T(8,128)(2,1)S(1)}, u32[]{:S(2)}, u32[]{:S(2)}) collective-permute-start(bf16[8,1792]{1,0:T(8,128)(2,1)S(1)} %activation.1.own), channel_id=1, source_target_pairs={{0,20},{4,16},{8,28},{12,24},{16,4},{20,0},{24,12},{28,8},{1,21},{... | collective-permute-start | bytes 86024 | tf_op jit(solution)/shard_map/ppermute | solution.py:24
  36.8 3.9 %collective-permute-start.12 = (bf16[8,1792]{1,0:T(8,128)(2,1)S(1)}, bf16[8,1792]{1,0:T(8,128)(2,1)S(1)}, u32[]{:S(2)}, u32[]{:S(2)}) collective-permute-start(bf16[8,1792]{1,0:T(8,128)(2,1)S(1)} %activation.1.own), channel_id=1, source_target_pairs={{0,16},{16,0},{1,17},{17,1},{2,18},{18,2},{3,19},{19,3},{4,20},{20... | collective-permute-start | bytes 86024 | tf_op jit(solution)/shard_map/ppermute | solution.py:24
  41.9 4.4 %collective-permute-start.17 = (bf16[16,2048]{1,0:T(8,128)(2,1)S(1)}, bf16[16,2048]{1,0:T(8,128)(2,1)S(1)}, u32[]{:S(2)}, u32[]{:S(2)}) collective-permute-start(bf16[16,2048]{1,0:T(8,128)(2,1)S(1)} %down.3.refs_0_), channel_id=1, source_target_pairs={{0,3},{1,2},{2,1},{3,0},{4,7},{5,6},{6,5},{7,4},{8,11},{9,10},{10,... | collective-permute-start | bytes 196616 | tf_op jit(solution)/shard_map/ppermute | solution.py:24
  41.9 5.3 %collective-permute-start.16 = (bf16[16,2048]{1,0:T(8,128)(2,1)S(1)}, bf16[16,2048]{1,0:T(8,128)(2,1)S(1)}, u32[]{:S(2)}, u32[]{:S(2)}) collective-permute-start(bf16[16,2048]{1,0:T(8,128)(2,1)S(1)} %down.3.refs_0_), channel_id=1, source_target_pairs={{0,2},{1,3},{2,0},{3,1},{4,6},{5,7},{6,4},{7,5},{8,10},{9,11},{10,... | collective-permute-start | bytes 196616 | tf_op jit(solution)/shard_map/ppermute | solution.py:24
  43.1 4.1 %collective-permute-start.15 = (bf16[16,2048]{1,0:T(8,128)(2,1)S(1)}, bf16[16,2048]{1,0:T(8,128)(2,1)S(1)}, u32[]{:S(2)}, u32[]{:S(2)}) collective-permute-start(bf16[16,2048]{1,0:T(8,128)(2,1)S(1)} %down.3.refs_0_), channel_id=1, source_target_pairs={{0,1},{1,0},{2,3},{3,2},{4,5},{5,4},{6,7},{7,6},{8,9},{9,8},{10,11... | collective-permute-start | bytes 196616 | tf_op jit(solution)/shard_map/ppermute | solution.py:24

commit v11 on v8

--- a/solution.py
+++ b/solution.py
@@ -69,49 +69,49 @@
 def attention_far_kernel(cols, *refs):
     half = cols // 2
     sources, (lengths, *outs), kept = refs[:5], refs[5 : 6 + half], refs[6 + half : 12 + half]
-    held, (sized, packed, sems) = refs[12 + half : 17 + half], refs[17 + half :]
-    mine = lax.axis_index("col") // half
-
-    def copies(part, targets, row):
-        result = []
-        for i, (source, target) in enumerate(zip(sources, targets)):
-            width = target.shape[2]
-            view = source.at[:, :, pl.ds(pl.multiple_of(part * width, 128), width)]
-            result.append(pltpu.make_async_copy(view, target, sems.at[row, i]))
-        return result
-
-    far, near = copies(1 - mine, held, 0), copies(mine, kept, 1)
-    far.append(pltpu.make_async_copy(lengths, sized, sems.at[0, 5]))
-    for copy in far + near:
+    sized, packed, sems = refs[12 + half :]
+    copies = [
+        pltpu.make_async_copy(source, target, sems.at[i])
+        for i, (source, target) in enumerate(zip(sources, kept))
+    ]
+    copies.append(pltpu.make_async_copy(lengths, sized, sems.at[5]))
+    for copy in copies:
         copy.start()
-    for copy in far:
-        copy.wait()
-    rows = held[3].shape[0]
+    for i in (0, 1, 2, 5, 3):
+        copies[i].wait()
     row = lax.broadcasted_iota(jnp.int32, (8, HD), 0)
     limits = jnp.zeros((8, HD), jnp.int32)
-    for b in range(rows):
+    for b in range(kept[3].shape[0]):
         limits = jnp.where(row == b, sized[b], limits)
     kept[5][...] = limits
-    attention(cols, limits, *held, outs, packed)
-    for copy in near:
-        copy.wait()
+    attention(cols, 1, limits, *kept[:5], outs, packed, copies[4].wait)
 
 
 def attention_near_kernel(cols, *refs):
-    attention(cols, refs[5][...], *refs[:5], refs[6:-1], refs[-1])
-
-
-def attention(cols, limits, query, new_keys, new_values, keys, values, outs, packed):
+    attention(cols, 0, refs[5][...], *refs[:5], refs[6:-1], refs[-1], lambda: None)
+
+
+def attention(
+    cols, far, limits, query, new_keys, new_values, keys, values, outs, packed, values_there
+):
     half = cols // 2
     heads = KV_HEADS // 2
     column = lax.axis_index("col")
+    chosen = jnp.bitwise_xor(column // half, far)
+
+    def lanes(source):
+        width = source.shape[2] // 2
+        return source[:, :, pl.ds(pl.multiple_of(chosen * width, 128), width)].astype(jnp.float32)
+
+    def head(source, b, g):
+        return source[b, :, pl.ds(pl.multiple_of((chosen * heads + g) * HD, 128), HD)]
+
     rows, span, _ = keys.shape
     hb = HEADS // cols
     inv_root = 1.0 / math.sqrt(HD)
     n = TOKENS * GROUP
     pairs = [(b, g) for b in range(rows) for g in range(heads)]
-    q32 = query[...].astype(jnp.float32)
-    nk, nv = new_keys[...].astype(jnp.float32), new_values[...].astype(jnp.float32)
+    q32, nk, nv = lanes(query), lanes(new_keys), lanes(new_values)
     zeros = jnp.zeros((8 - TOKENS, HD), jnp.float32)
 
     def fresh(block, b, g):
@@ -128,7 +128,7 @@
             ],
             axis=0,
         ).astype(jnp.bfloat16)
-        s = dot_t(q, keys[b, :, g * HD : (g + 1) * HD]) * inv_root
+        s = dot_t(q, head(keys, b, g)) * inv_root
         position = column * span + lax.broadcasted_iota(jnp.int32, (n, span), 1)
         scores.append(jnp.where(position < limits[b : b + 1, :1], s, very_low))
         f = dot_t(q, fresh(nk, b, g).astype(jnp.bfloat16)) * inv_root
@@ -152,9 +152,10 @@
 
     lane = lax.broadcasted_iota(jnp.int32, (GROUP, HD), 1)
     stats = [jnp.zeros((GROUP, HD), jnp.float32) for _ in range(heads)]
+    values_there()
     for i, (b, g) in enumerate(pairs):
         here = slice(i * n, (i + 1) * n)
-        s = dot(halves(weights[here]), values[b, :, g * HD : (g + 1) * HD])
+        s = dot(halves(weights[here]), head(values, b, g))
         s = s + dot(halves(fresh_weights[here]), fresh(nv, b, g).astype(jnp.bfloat16))
         s = s[:n] + s[n:]
         for t in range(TOKENS):
@@ -216,7 +217,7 @@
 
 
 def over_columns(width, body):
-    size = width // 2 if width % 256 == 0 else width
+    size = width
 
     def step(j, carry):
         body(pl.multiple_of(j * size, 128), size)
@@ -225,14 +226,25 @@
     lax.fori_loop(0, width // size, step, 0)
 
 
+def across(count):
+    return [0, *range(count - 1, 0, -1)]
+
+
+def by_distance(refs):
+    order = across(len(refs))
+    return [refs[order.index(k)] for k in range(len(refs))]
+
+
 def out_kernel(groups, *refs):
-    parts, (weight, out, canon, attended) = refs[:groups], refs[groups:]
+    parts, (weight, *outs) = refs[:groups], refs[groups:-3]
+    canon, attended, packed = refs[-3:]
+    half = packed.shape[2]
     attended[...] = canonical(parts, canon, lax.axis_index("row"))
-
-    def body(at, size):
-        out[:, pl.ds(at, size)] = dot(attended[...], weight[:, pl.ds(at, size)]).astype(out.dtype)
-
-    over_columns(out.shape[1], body)
+    for i in range(2):
+        packed[i] = dot(attended[...], weight[:, i * half : (i + 1) * half])
+    bit = lax.axis_index("col") & 1
+    for k, out in enumerate(outs):
+        out[...] = packed[jnp.bitwise_xor(bit, k & 1)].astype(out.dtype)
 
 
 def in_pieces(squares):
@@ -245,29 +257,53 @@
     )
 
 
-def lift_kernel(groups, split, residual, gains, gate_weight, up_weight, *refs):
-    parts, (mid_out, keep, send, lifted, packed) = refs[:-5], refs[-5:]
-    hidden = gate_weight.shape[1] // split
-    start = lax.axis_index("side") * hidden if split > 1 else 0
-    half = packed.shape[1] // 2
-    mid = tree_sum([p[...].astype(jnp.float32) for p in parts])
-    mid = group_order(residual[...].astype(jnp.float32), groups) + mid
-    mid_out[...] = mid
-    sent = in_pieces(jnp.sum(mid * mid, axis=1, keepdims=True))
-    lifted[...] = (mid * gains[...].astype(jnp.float32).reshape(1, mid.shape[1])).astype(jnp.bfloat16)
+def lanes_of(bit, half):
+    return pl.ds(pl.multiple_of(bit * half, 128), half)
+
+
+def mid_kernel(groups, residual, gains, *refs):
+    parts, (mid, lifted) = by_distance(refs[:-2]), refs[-2:]
+    half = mid.shape[1]
+    here = lanes_of(lax.axis_index("col") & 1, half)
+    own = residual[:, :, here].astype(jnp.float32)
+    value = group_order(own, groups) + tree_sum([p[...].astype(jnp.float32) for p in parts])
+    mid[...] = value
+    lifted[...] = (value * gains[here].astype(jnp.float32).reshape(1, half)).astype(jnp.bfloat16)
+
+
+def products(lifted, bit, gate_weight, up_weight, out_hidden):
+    half = lifted.shape[1]
+    start = 0
+    if gate_weight.shape[1] > out_hidden:
+        start = pl.multiple_of(lax.axis_index("side") * out_hidden, 128)
+    rows, columns = lanes_of(bit, half), pl.ds(start, out_hidden)
+    return dot(lifted, gate_weight[rows, columns]), dot(lifted, up_weight[rows, columns])
+
+
+def lift_first_kernel(lifted, gate_weight, up_weight, gate, up):
+    bit = lax.axis_index("col") & 1
+    gate[...], up[...] = products(lifted[...], bit, gate_weight, up_weight, gate.shape[1])
+
+
+def lift_second_kernel(
+    own, received, gains, gate_weight, up_weight, gate_first, up_first, mid, keep, send, packed
+):
+    rows, hidden = gate_first.shape
+    half, bit = rows // 2, lax.axis_index("col") & 1
+    width = own.shape[1]
+    mid[:, lanes_of(bit, width)] = own[...]
+    mid[:, lanes_of(1 - bit, width)] = received[...]
+    value = received[...]
+    squares = own[...] * own[...] + value * value
+    sent = in_pieces(jnp.sum(squares, axis=1, keepdims=True))
+    gain = gains[lanes_of(1 - bit, width)].astype(jnp.float32).reshape(1, width)
+    lifted = (value * gain).astype(jnp.bfloat16)
+    gate, up = products(lifted, 1 - bit, gate_weight, up_weight, hidden)
+    gate, up = gate + gate_first[...], up + up_first[...]
     for i in range(2):
-        piece = sent[i * half : (i + 1) * half]
-        packed[i, :, hidden:] = jnp.concatenate([piece, piece], axis=0)
-
-    def body(at, size):
-        block = pl.ds(pl.multiple_of(start + at, 128), size)
-        gate = dot(lifted[...], gate_weight[:, block])
-        up = dot(lifted[...], up_weight[:, block])
-        for i in range(2):
-            rows = slice(i * half, (i + 1) * half)
-            packed[i, :, pl.ds(at, size)] = jnp.concatenate([gate[rows], up[rows]], axis=0)
-
-    over_columns(hidden, body)
+        part = slice(i * half, (i + 1) * half)
+        packed[i, :, hidden:] = jnp.concatenate([sent[part], sent[part]], axis=0)
+        packed[i, :, :hidden] = jnp.concatenate([gate[part], up[part]], axis=0)
     bit = lax.axis_index("row") & 1
     keep[...] = packed[bit].astype(keep.dtype)
     send[...] = packed[1 - bit].astype(send.dtype)
@@ -354,15 +390,13 @@
     message = shape((cells + 1, hb, HD), f32)
     sources = [query, new_keys, new_values, key_cache, value_cache]
 
-    inputs = [pltpu.VMEM((*a.shape[:2], a.shape[2] // 2), a.dtype) for a in sources]
+    inputs = [pltpu.VMEM(a.shape, a.dtype) for a in sources]
     packed = pltpu.VMEM((cols // 2, *message.shape), f32)
     result = call(
         functools.partial(attention_far_kernel, cols),
         [message] * (cols // 2) + inputs + [pltpu.VMEM((8, HD), jnp.int32)],
         [ANY_SPEC] * 6,
-        inputs
-        + [pltpu.SMEM(lengths.shape, lengths.dtype), packed, pltpu.SemaphoreType.DMA((2, 6))],
-        limit=8,
+        [pltpu.SMEM(lengths.shape, lengths.dtype), packed, pltpu.SemaphoreType.DMA((6,))],
         name="attention_far",
     )(*[in_hbm(a) for a in [*sources, lengths]])
     far, inputs = result[: cols // 2], result[cols // 2 :]
@@ -383,23 +417,42 @@
         name="combine",
     )(*parts)
     gathered = spread(attended, "row")
-    partial = call(
+    half = width_share // 2
+    partials = call(
         functools.partial(out_kernel, groups),
-        shape((m, width_share), WIRE),
+        [shape((m, half), WIRE)] * cols,
         [VMEM_SPEC] * (groups + 1),
-        [pltpu.VMEM((groups, pad, features), f32), pltpu.VMEM((m, features), bf16)],
+        [
+            pltpu.VMEM((groups, pad, features), f32),
+            pltpu.VMEM((m, features), bf16),
+            pltpu.VMEM((2, m, half), f32),
+        ],
         name="out_projection",
     )(*gathered, in_vmem(out_weight))
+    partials = [partials[0]] + [partner(partials[k], "col", k) for k in range(1, cols)]
+    norm_gain = in_vmem(norm_gain)
+    own, own_lifted = call(
+        functools.partial(mid_kernel, groups),
+        [shape((m, half), f32), shape((m, half), bf16)],
+        [VMEM_SPEC] * (cols + 2),
+        name="mid",
+    )(in_vmem(residual), norm_gain, *[partials[k] for k in across(cols)])
+    received = partner(own, "col", 1)
+    weights = [in_vmem(gate_weight), in_vmem(up_weight)]
+    first = call(
+        lift_first_kernel,
+        [shape((m, hidden), f32)] * 2,
+        [VMEM_SPEC] * 3,
+        name="gate_up_first",
+    )(own_lifted, *weights)
     mid, keep, send = call(
-        functools.partial(lift_kernel, groups, split),
+        lift_second_kernel,
         [shape((m, width_share), f32)] + [shape((m, hidden + HD), WIRE)] * 2,
-        [VMEM_SPEC] * (cols + 4),
-        [pltpu.VMEM((m, width_share), bf16), pltpu.VMEM((2, m, hidden + HD), f32)],
-        name="gate_up",
-    )(
-        in_vmem(residual), in_vmem(norm_gain), in_vmem(gate_weight), in_vmem(up_weight),
-        *spread(partial, "col"),
-    )
+        [VMEM_SPEC] * 7,
+        [pltpu.VMEM((2, m, hidden + HD), f32)],
+        limit=8,
+        name="gate_up_second",
+    )(own, received, norm_gain, *weights, *first)
     sums = [keep] + [partner((keep, send)[k % 2], "row", k) for k in range(1, groups)]
     act = call(
         functools.partial(act_kernel, model),

time: 47.7 us -> 51.2 us (1.073)
  local copies, waits for them, and re-layouts: 0.07 us -> 6.29 us
  waiting for transfers between devices: 19.6 us -> 17.4 us
  Pallas kernels: 8.98 us -> 8.43 us
    unnamed x30 -> x32, local copies, waits for them, and re-layouts: 0.07 us -> 6.29 us
    ppermute x18 -> x19, waiting for transfers between devices: 19.6 us -> 17.4 us  [partner(): lax.ppermute(value, axis, [(i, i ^ k) for i in range(lax.axis_size(axis))])]
    pallas_call x2 -> x4, Pallas kernels: 3.14 us -> 2.87 us  [the longest x1 1.08 us: shards(): call(lift_second_kernel, [shape((m, width_share), f32)] + [shape((m, hidd...]
    ppermute x18 -> x19, starting transfers between devices: 18.6 us -> 18.6 us  [partner(): lax.ppermute(value, axis, [(i, i ^ k) for i in range(lax.axis_size(axis))])]
  transfers between devices with their start and end apart: 18 -> 19, of which waited for: 13 -> 12; matrix products, arithmetic and copies ran while one was open for 0% -> 0% of each run, Pallas kernels for 4% -> 5%
where the time goes in v11:
time: 51.2 us; the launch traced here: 51 us
  starting transfers between devices  18.6 us (36%)
  waiting for transfers between devices  17.4 us (34%)
  Pallas kernels  8.43 us (16%)
  local copies, waits for them, and re-layouts  6.29 us (12%)
    ppermute x19, starting transfers between devices, partner(): lax.ppermute(value, axis, [(i, i ^ k) for i in range(lax.axis_size(axis))])  18.6 us
    ppermute x19, waiting for transfers between devices, partner(): lax.ppermute(value, axis, [(i, i ^ k) for i in range(lax.axis_size(axis))])  17.4 us
    unnamed x32, local copies, waits for them, and re-layouts  6.29 us
    pallas_call x2, Pallas kernels, down_part(): call(functools.partial(down_kernel, other), shape((m, width_share), resul...  2.11 us
    pallas_call x1, Pallas kernels, shards(): call(functools.partial(attention_far_kernel, cols), [message] * (cols //...  1.88 us
    pallas_call x1, Pallas kernels, shards(): call(lift_second_kernel, [shape((m, width_share), f32)] + [shape((m, hidd...  1.08 us
    pallas_call x1, Pallas kernels, shards(): call(lift_first_kernel, [shape((m, hidden), f32)] * 2, [VMEM_SPEC] * 3, n...  1.07 us
  transfers between devices with their start and end apart: 19, of which 12 were waited for; matrix products, arithmetic and copies ran while one was open for 0% of the time, Pallas kernels for 5%

profile of v11, /device:TPU:0, one launch (start us, length us, event | category | flops | bytes accessed | tf_op | source)
XLA Modules:
  0.0 51.0 jit_solution(17514510474802817974)
XLA Ops:
  0.0 1.9 %attention_far.1 = (f32[5,8,128]{2,1,0:T(8,128)S(1)}, f32[5,8,128]{2,1,0:T(8,128)S(1)}, bf16[2,2,4096]{2,1,0:T(2,128)(2,1)S(1)}, bf16[2,2,512]{2,1,0:T(2,128)(2,...) custom-call(bf16[2,2,4096]{2,1,0:T(2,128)(2,1)} %refs_0_.1, ...), custom_call_target="tpu_custom_call" | custom-call | tf_op jit(solution)/shard_map/attention_far/pallas_call | solution.py:395
  1.9 3.0 %collective-permute-start = (f32[5,8,128]{2,1,0:T(8,128)S(1)}, f32[5,8,128]{2,1,0:T(8,128)S(1)}, u32[]{:S(2)}, u32[]{:S(2)}) collective-permute-start(f32[5,8,128]{2,1,0:T(8,128)S(1)} %get-tuple-element.26), channel_id=1, source_target_pairs={{0,2},{1,3},{2,0},{3,1},{4,6},{5,7},{6,4},{7,5},{8,10},{9,11},{10,... | collective-permute-start | bytes 61448 | tf_op jit(solution)/shard_map/ppermute | solution.py:24
  4.9 0.0 collective-permute-start.1
  4.9 0.5 attention_near.1
  5.4 0.2 collective-permute-start.2
  5.7 1.0 %collective-permute-done.refs_0_ = f32[5,8,128]{2,1,0:T(8,128)S(1)} collective-permute-done((f32[5,8,128]{2,1,0:T(8,128)S(1)}, f32[5,8,128]{2,1,0:T(8,128)S(1)}, u32[]{:S(2)}, u32[]{:S(2)}) %collective-permute-start) | collective-permute-done | bytes 20512 | tf_op jit(solution)/shard_map/ppermute | solution.py:24
  6.7 1.4 %collective-permute-done.1.refs_1_ = f32[5,8,128]{2,1,0:T(8,128)S(1)} collective-permute-done((f32[5,8,128]{2,1,0:T(8,128)S(1)}, f32[5,8,128]{2,1,0:T(8,128)S(1)}, u32[]{:S(2)}, u32[]{:S(2)}) %collective-permute-start.1) | collective-permute-done | bytes 20512 | tf_op jit(solution)/shard_map/ppermute | solution.py:24
  8.1 0.0 slice-start.1
  8.2 0.0 slice-start.5
  8.2 0.0 slice-start.6
  8.2 0.2 combine.1.refs_0_
  8.4 3.7 %collective-permute-start.5 = (bf16[4,1024]{1,0:T(4,128)(2,1)S(1)}, bf16[4,1024]{1,0:T(4,128)(2,1)S(1)}, u32[]{:S(2)}, u32[]{:S(2)}) collective-permute-start(bf16[4,1024]{1,0:T(4,128)(2,1)S(1)} %combine.1.refs_0_), channel_id=1, source_target_pairs={{0,12},{4,8},{8,4},{12,0},{1,13},{5,9},{9,5},{13,1},{2,14},{6,10},... | collective-permute-start | bytes 24584 | tf_op jit(solution)/shard_map/ppermute | solution.py:24
  12.1 0.8 %collective-permute-start.3 = (bf16[4,1024]{1,0:T(4,128)(2,1)S(1)}, bf16[4,1024]{1,0:T(4,128)(2,1)S(1)}, u32[]{:S(2)}, u32[]{:S(2)}) collective-permute-start(bf16[4,1024]{1,0:T(4,128)(2,1)S(1)} %combine.1.refs_0_), channel_id=1, source_target_pairs={{0,4},{4,0},{8,12},{12,8},{1,5},{5,1},{9,13},{13,9},{2,6},{6,2},{1... | collective-permute-start | bytes 24584 | tf_op jit(solution)/shard_map/ppermute | solution.py:24
  12.8 1.1 %collective-permute-done.5.refs_3_ = bf16[4,1024]{1,0:T(4,128)(2,1)S(1)} collective-permute-done((bf16[4,1024]{1,0:T(4,128)(2,1)S(1)}, bf16[4,1024]{1,0:T(4,128)(2,1)S(1)}, u32[]{:S(2)}, u32[]{:S(2)}) %collective-permute-start.5) | collective-permute-done | bytes 8224 | tf_op jit(solution)/shard_map/ppermute | solution.py:24
  14.0 2.6 %collective-permute-done.4.refs_2_ = bf16[4,1024]{1,0:T(4,128)(2,1)S(1)} collective-permute-done((bf16[4,1024]{1,0:T(4,128)(2,1)S(1)}, bf16[4,1024]{1,0:T(4,128)(2,1)S(1)}, u32[]{:S(2)}, u32[]{:S(2)}) %collective-permute-start.4) | collective-permute-done | bytes 8224 | tf_op jit(solution)/shard_map/ppermute | solution.py:24
  16.6 0.0 collective-permute-done.3.refs_1_
  16.6 0.7 %out_projection.1 = (bf16[16,1024]{1,0:T(8,128)(2,1)S(1)}, bf16[16,1024]{1,0:T(8,128)(2,1)S(1)}, bf16[16,1024]{1,0:T(8,128)(2,1)S(1)}, bf16[16,1024]{1,0:T(8,128)(2,1)S(1)}) custom-call(bf16[4,1024]{1,0:T(4,128)(2,1)S(1)} %combine.1.refs_0_, bf16[4,1024]{1,0:T(4,128)(2,1)S(1)} %collective-permute-done.3.refs_1_, ...), custom_call_target="tpu_custom_call" | custom-call | tf_op jit(solution)/shard_map/out_projection/pallas_call | solution.py:421
  17.3 0.1 collective-permute-start.6
  17.4 0.8 %collective-permute-start.7 = (bf16[16,1024]{1,0:T(8,128)(2,1)S(1)}, bf16[16,1024]{1,0:T(8,128)(2,1)S(1)}, u32[]{:S(2)}, u32[]{:S(2)}) collective-permute-start(bf16[16,1024]{1,0:T(8,128)(2,1)S(1)} %get-tuple-element.38), channel_id=1, source_target_pairs={{0,2},{1,3},{2,0},{3,1},{4,6},{5,7},{6,4},{7,5},{8,10},{9,11},{10,... | collective-permute-start | bytes 98312 | tf_op jit(solution)/shard_map/ppermute | solution.py:24
  18.2 1.0 %collective-permute-start.8 = (bf16[16,1024]{1,0:T(8,128)(2,1)S(1)}, bf16[16,1024]{1,0:T(8,128)(2,1)S(1)}, u32[]{:S(2)}, u32[]{:S(2)}) collective-permute-start(bf16[16,1024]{1,0:T(8,128)(2,1)S(1)} %get-tuple-element.39), channel_id=1, source_target_pairs={{0,1},{1,0},{2,3},{3,2},{4,5},{5,4},{6,7},{7,6},{8,9},{9,8},{10,11... | collective-permute-start | bytes 98312 | tf_op jit(solution)/shard_map/ppermute | solution.py:24
  19.2 1.5 %collective-permute-done.6.refs_1_ = bf16[16,1024]{1,0:T(8,128)(2,1)S(1)} collective-permute-done((bf16[16,1024]{1,0:T(8,128)(2,1)S(1)}, bf16[16,1024]{1,0:T(8,128)(2,1)S(1)}, u32[]{:S(2)}, u32[]{:S(2)}) %collective-permute-start.6) | collective-permute-done | bytes 32800 | tf_op jit(solution)/shard_map/ppermute | solution.py:24
  20.7 0.8 %collective-permute-done.7.refs_2_ = bf16[16,1024]{1,0:T(8,128)(2,1)S(1)} collective-permute-done((bf16[16,1024]{1,0:T(8,128)(2,1)S(1)}, bf16[16,1024]{1,0:T(8,128)(2,1)S(1)}, u32[]{:S(2)}, u32[]{:S(2)}) %collective-permute-start.7) | collective-permute-done | bytes 32800 | tf_op jit(solution)/shard_map/ppermute | solution.py:24
  21.5 0.0 collective-permute-done.8.refs_3_
  21.6 0.1 collective-permute-start.9
  21.8 1.1 %gate_up_first.1 = (f32[16,1792]{1,0:T(8,128)S(1)}, f32[16,1792]{1,0:T(8,128)S(1)}) custom-call(bf16[16,1024]{1,0:T(8,128)(2,1)S(1)} %get-tuple-element.41.lifted, bf16[2048,3584]{1,0:T(8,128)(2,1)S(1)} %bitcast.1, bf16[2048,3584]{1,0:T(8,128)(2,1)S(1)} %bitcast.3), custom_call_target="tpu_custom_call" | custom-call | tf_op jit(solution)/shard_map/gate_up_first/pallas_call | solution.py:442
  22.8 0.1 collective-permute-done.9.received
  22.9 1.1 %gate_up_second.1 = (f32[16,2048]{1,0:T(8,128)S(1)}, bf16[16,1920]{1,0:T(8,128)(2,1)S(1)}, bf16[16,1920]{1,0:T(8,128)(2,1)S(1)}) custom-call(f32[16,1024]{1,0:T(8,128)S(1)} %get-tuple-element.40.own, f32[16,1024]{1,0:T(8,128)S(1)} %collective-permute-done.9.received, bf16[2048]{0:T(1024)(128)(2,1)S(1)} %copy-done.3, bf16[2048,3584]{1,0:T(8,128)(2,1)S(1)} %bitcast.1, ...), custom_call_target="tpu_custom_call" | custom-call | tf_op jit(solution)/shard_map/gate_up_second/pallas_call | solution.py:448
  24.0 2.0 %collective-permute-start.11 = (bf16[16,1920]{1,0:T(8,128)(2,1)S(1)}, bf16[16,1920]{1,0:T(8,128)(2,1)S(1)}, u32[]{:S(2)}, u32[]{:S(2)}) collective-permute-start(bf16[16,1920]{1,0:T(8,128)(2,1)S(1)} %get-tuple-element.45.refs_0_), channel_id=1, source_target_pairs={{0,8},{4,12},{8,0},{12,4},{1,9},{5,13},{9,1},{13,5},{2,10},{6,14},... | collective-permute-start | bytes 184328 | tf_op jit(solution)/shard_map/ppermute | solution.py:24
  26.0 0.1 collective-permute-start.12
  26.1 1.4 %collective-permute-start.10 = (bf16[16,1920]{1,0:T(8,128)(2,1)S(1)}, bf16[16,1920]{1,0:T(8,128)(2,1)S(1)}, u32[]{:S(2)}, u32[]{:S(2)}) collective-permute-start(bf16[16,1920]{1,0:T(8,128)(2,1)S(1)} %get-tuple-element.46), channel_id=1, source_target_pairs={{0,4},{4,0},{8,12},{12,8},{1,5},{5,1},{9,13},{13,9},{2,6},{6,2},{1... | collective-permute-start | bytes 184328 | tf_op jit(solution)/shard_map/ppermute | solution.py:24
  27.5 2.4 %collective-permute-done.11.refs_2_ = bf16[16,1920]{1,0:T(8,128)(2,1)S(1)} collective-permute-done((bf16[16,1920]{1,0:T(8,128)(2,1)S(1)}, bf16[16,1920]{1,0:T(8,128)(2,1)S(1)}, u32[]{:S(2)}, u32[]{:S(2)}) %collective-permute-start.11) | collective-permute-done | bytes 61472 | tf_op jit(solution)/shard_map/ppermute | solution.py:24
  29.9 2.7 %collective-permute-done.12.refs_3_ = bf16[16,1920]{1,0:T(8,128)(2,1)S(1)} collective-permute-done((bf16[16,1920]{1,0:T(8,128)(2,1)S(1)}, bf16[16,1920]{1,0:T(8,128)(2,1)S(1)}, u32[]{:S(2)}, u32[]{:S(2)}) %collective-permute-start.12) | collective-permute-done | bytes 61472 | tf_op jit(solution)/shard_map/ppermute | solution.py:24
  32.6 0.1 activation.1.own
  32.7 0.6 %collective-permute-start.15 = (bf16[8,1792]{1,0:T(8,128)(2,1)S(1)}, bf16[8,1792]{1,0:T(8,128)(2,1)S(1)}, u32[]{:S(2)}, u32[]{:S(2)}) collective-permute-start(bf16[8,1792]{1,0:T(8,128)(2,1)S(1)} %activation.1.own), channel_id=1, source_target_pairs={{0,4},{4,0},{8,12},{12,8},{1,5},{5,1},{9,13},{13,9},{2,6},{6,2},{1... | collective-permute-start | bytes 86024 | tf_op jit(solution)/shard_map/ppermute | solution.py:24
  33.3 2.5 %collective-permute-start.14 = (bf16[8,1792]{1,0:T(8,128)(2,1)S(1)}, bf16[8,1792]{1,0:T(8,128)(2,1)S(1)}, u32[]{:S(2)}, u32[]{:S(2)}) collective-permute-start(bf16[8,1792]{1,0:T(8,128)(2,1)S(1)} %activation.1.own), channel_id=1, source_target_pairs={{0,20},{4,16},{8,28},{12,24},{16,4},{20,0},{24,12},{28,8},{1,21},{... | collective-permute-start | bytes 86024 | tf_op jit(solution)/shard_map/ppermute | solution.py:24
  35.7 0.5 %collective-permute-start.13 = (bf16[8,1792]{1,0:T(8,128)(2,1)S(1)}, bf16[8,1792]{1,0:T(8,128)(2,1)S(1)}, u32[]{:S(2)}, u32[]{:S(2)}) collective-permute-start(bf16[8,1792]{1,0:T(8,128)(2,1)S(1)} %activation.1.own), channel_id=1, source_target_pairs={{0,16},{16,0},{1,17},{17,1},{2,18},{18,2},{3,19},{19,3},{4,20},{20... | collective-permute-start | bytes 86024 | tf_op jit(solution)/shard_map/ppermute | solution.py:24
  36.3 0.6 %collective-permute-done.15.received = bf16[8,1792]{1,0:T(8,128)(2,1)S(1)} collective-permute-done((bf16[8,1792]{1,0:T(8,128)(2,1)S(1)}, bf16[8,1792]{1,0:T(8,128)(2,1)S(1)}, u32[]{:S(2)}, u32[]{:S(2)}) %collective-permute-start.15) | collective-permute-done | bytes 28704 | tf_op jit(solution)/shard_map/ppermute | solution.py:24
  36.9 0.0 copy-start
  36.9 5.2 %copy-done = bf16[3584,2048]{1,0:T(8,128)(2,1)S(1)} copy-done((bf16[3584,2048]{1,0:T(8,128)(2,1)S(1)}, bf16[3584,2048]{1,0:T(8,128)(2,1)}, u32[]{:S(2)}) %copy-start) | copy-done | bytes 14680088
  42.1 1.1 %down.2.refs_0_ = f32[16,2048]{1,0:T(8,128)S(1)} custom-call(bf16[16,1792]{1,0:T(8,128)(2,1)S(1)} %gather_act.3.act, bf16[3584,2048]{1,0:T(8,128)(2,1)S(1)} %copy-done), custom_call_target="tpu_custom_call" | custom-call | tf_op jit(solution)/shard_map/down/pallas_call | solution.py:473
  43.2 1.1 %slice-done.11 = s8[4194304]{0:T(1024)(128)(4,1)S(1)} async-done(((s8[14680064]{0:T(1024)(128)(4,1)}), s8[4194304]{0:T(1024)(128)(4,1)S(1)}, s32[]{:S(2)}) %slice-start.11) | async-done | bytes 4194328
  44.3 1.1 %down.3.refs_0_ = bf16[16,2048]{1,0:T(8,128)(2,1)S(1)} custom-call(bf16[16,1792]{1,0:T(8,128)(2,1)S(1)} %gather_act.2.act, bf16[3584,2048]{1,0:T(8,128)(2,1)S(1)} %bitcast.5, f32[16,2048]{1,0:T(8,128)S(1)} %down.2.refs_0_), custom_call_target="tpu_custom_call" | custom-call | tf_op jit(solution)/shard_map/down/pallas_call | solution.py:473
  45.3 0.0 collective-permute-start.18
  45.3 0.7 %collective-permute-start.17 = (bf16[16,2048]{1,0:T(8,128)(2,1)S(1)}, bf16[16,2048]{1,0:T(8,128)(2,1)S(1)}, u32[]{:S(2)}, u32[]{:S(2)}) collective-permute-start(bf16[16,2048]{1,0:T(8,128)(2,1)S(1)} %down.3.refs_0_), channel_id=1, source_target_pairs={{0,2},{1,3},{2,0},{3,1},{4,6},{5,7},{6,4},{7,5},{8,10},{9,11},{10,... | collective-permute-start | bytes 196616 | tf_op jit(solution)/shard_map/ppermute | solution.py:24
  46.0 1.2 %collective-permute-start.16 = (bf16[16,2048]{1,0:T(8,128)(2,1)S(1)}, bf16[16,2048]{1,0:T(8,128)(2,1)S(1)}, u32[]{:S(2)}, u32[]{:S(2)}) collective-permute-start(bf16[16,2048]{1,0:T(8,128)(2,1)S(1)} %down.3.refs_0_), channel_id=1, source_target_pairs={{0,1},{1,0},{2,3},{3,2},{4,5},{5,4},{6,7},{7,6},{8,9},{9,8},{10,11... | collective-permute-start | bytes 196616 | tf_op jit(solution)/shard_map/ppermute | solution.py:24
  47.2 2.0 %collective-permute-done.18.refs_3_ = bf16[16,2048]{1,0:T(8,128)(2,1)S(1)} collective-permute-done((bf16[16,2048]{1,0:T(8,128)(2,1)S(1)}, bf16[16,2048]{1,0:T(8,128)(2,1)S(1)}, u32[]{:S(2)}, u32[]{:S(2)}) %collective-permute-start.18) | collective-permute-done | bytes 65568 | tf_op jit(solution)/shard_map/ppermute | solution.py:24
  49.2 1.1 %collective-permute-done.17.refs_2_ = bf16[16,2048]{1,0:T(8,128)(2,1)S(1)} collective-permute-done((bf16[16,2048]{1,0:T(8,128)(2,1)S(1)}, bf16[16,2048]{1,0:T(8,128)(2,1)S(1)}, u32[]{:S(2)}, u32[]{:S(2)}) %collective-permute-start.17) | collective-permute-done | bytes 65568 | tf_op jit(solution)/shard_map/ppermute | solution.py:24
  50.3 0.7 %final.1 = bf16[2,8,2048]{2,1,0:T(8,128)(2,1)} custom-call(f32[16,2048]{1,0:T(8,128)S(1)} %get-tuple-element.44.mid, bf16[16,2048]{1,0:T(8,128)(2,1)S(1)} %down.3.refs_0_, bf16[16,2048]{1,0:T(8,128)(2,1)S(1)} %collective-permute-done.16.refs_1_, bf16[16,2048]{1,0:T(8,128)(2,1)S(1)} %collective-permute-done.17.refs_2_, ...), custom_call_target="tpu_custom_call" | custom-call | tf_op jit(solution)/shard_map/final/pallas_call | solution.py:487
  (38 shorter events, 0.2 us)
Async XLA Ops:
  1.9 4.8 %collective-permute-start = (f32[5,8,128]{2,1,0:T(8,128)S(1)}, f32[5,8,128]{2,1,0:T(8,128)S(1)}, u32[]{:S(2)}, u32[]{:S(2)}) collective-permute-start(f32[5,8,128]{2,1,0:T(8,128)S(1)} %get-tuple-element.26), channel_id=1, source_target_pairs={{0,2},{1,3},{2,0},{3,1},{4,6},{5,7},{6,4},{7,5},{8,10},{9,11},{10,... | collective-permute-start | bytes 61448 | tf_op jit(solution)/shard_map/ppermute | solution.py:24
  4.9 3.2 %collective-permute-start.1 = (f32[5,8,128]{2,1,0:T(8,128)S(1)}, f32[5,8,128]{2,1,0:T(8,128)S(1)}, u32[]{:S(2)}, u32[]{:S(2)}) collective-permute-start(f32[5,8,128]{2,1,0:T(8,128)S(1)} %get-tuple-element.27), channel_id=1, source_target_pairs={{0,3},{1,2},{2,1},{3,0},{4,7},{5,6},{6,5},{7,4},{8,11},{9,10},{10,... | collective-permute-start | bytes 61448 | tf_op jit(solution)/shard_map/ppermute | solution.py:24
  4.9 16.7 %slice-start = ((s8[14680064]{0:T(1024)(128)(4,1)}), s8[4194304]{0:T(1024)(128)(4,1)S(1)}, s32[]{:S(2)}) async-start(s8[14680064]{0:T(1024)(128)(4,1)} %bitcast), calls=%async_computation | async-start | bytes 8388608
  4.9 16.8 %slice-start.4 = ((s8[14680064]{0:T(1024)(128)(4,1)}), s8[4194304]{0:T(1024)(128)(4,1)S(1)}, s32[]{:S(2)}) async-start(s8[14680064]{0:T(1024)(128)(4,1)} %bitcast.2), calls=%async_computation.4 | async-start | bytes 8388608
  5.4 2.7 %collective-permute-start.2 = (f32[5,8,128]{2,1,0:T(8,128)S(1)}, f32[5,8,128]{2,1,0:T(8,128)S(1)}, u32[]{:S(2)}, u32[]{:S(2)}) collective-permute-start(f32[5,8,128]{2,1,0:T(8,128)S(1)} %get-tuple-element.35), channel_id=1, source_target_pairs={{0,1},{1,0},{2,3},{3,2},{4,5},{5,4},{6,7},{7,6},{8,9},{9,8},{10,11... | collective-permute-start | bytes 61448 | tf_op jit(solution)/shard_map/ppermute | solution.py:24
  8.1 8.5 %copy-start.1 = (bf16[1024,2048]{1,0:T(8,128)(2,1)S(1)}, bf16[1024,2048]{1,0:T(8,128)(2,1)}, u32[]{:S(2)}) copy-start(bf16[1024,2048]{1,0:T(8,128)(2,1)} %refs_4_.3) | copy-start | bytes 12582916
  8.1 13.4 %copy-start.2 = (bf16[2,8,2048]{2,1,0:T(8,128)(2,1)S(1)}, bf16[2,8,2048]{2,1,0:T(8,128)(2,1)}, u32[]{:S(2)}) copy-start(bf16[2,8,2048]{2,1,0:T(8,128)(2,1)} %residual.1) | copy-start | bytes 196612
  8.1 13.4 %copy-start.3 = (bf16[2048]{0:T(1024)(128)(2,1)S(1)}, bf16[2048]{0:T(1024)(128)(2,1)}, u32[]{:S(2)}) copy-start(bf16[2048]{0:T(1024)(128)(2,1)} %gains.3) | copy-start | bytes 12292
  8.1 13.5 %slice-start.1 = ((s8[14680064]{0:T(1024)(128)(4,1)}), s8[4194304]{0:T(1024)(128)(4,1)S(1)}, s32[]{:S(2)}) async-start(s8[14680064]{0:T(1024)(128)(4,1)} %bitcast), calls=%async_computation.1 | async-start | bytes 8388608
  8.2 13.5 %slice-start.2 = ((s8[14680064]{0:T(1024)(128)(4,1)}), s8[4194304]{0:T(1024)(128)(4,1)S(1)}, s32[]{:S(2)}) async-start(s8[14680064]{0:T(1024)(128)(4,1)} %bitcast), calls=%async_computation.2 | async-start | bytes 8388608
  8.2 13.5 %slice-start.3 = ((s8[14680064]{0:T(1024)(128)(4,1)}), s8[2097152]{0:T(1024)(128)(4,1)S(1)}, s32[]{:S(2)}) async-start(s8[14680064]{0:T(1024)(128)(4,1)} %bitcast), calls=%async_computation.3 | async-start | bytes 4194304
  8.2 13.5 %slice-start.5 = ((s8[14680064]{0:T(1024)(128)(4,1)}), s8[4194304]{0:T(1024)(128)(4,1)S(1)}, s32[]{:S(2)}) async-start(s8[14680064]{0:T(1024)(128)(4,1)} %bitcast.2), calls=%async_computation.5 | async-start | bytes 8388608
  8.2 13.5 %slice-start.6 = ((s8[14680064]{0:T(1024)(128)(4,1)}), s8[4194304]{0:T(1024)(128)(4,1)S(1)}, s32[]{:S(2)}) async-start(s8[14680064]{0:T(1024)(128)(4,1)} %bitcast.2), calls=%async_computation.6 | async-start | bytes 8388608
  8.2 13.5 %slice-start.7 = ((s8[14680064]{0:T(1024)(128)(4,1)}), s8[2097152]{0:T(1024)(128)(4,1)S(1)}, s32[]{:S(2)}) async-start(s8[14680064]{0:T(1024)(128)(4,1)} %bitcast.2), calls=%async_computation.7 | async-start | bytes 4194304
  8.4 5.6 %collective-permute-start.5 = (bf16[4,1024]{1,0:T(4,128)(2,1)S(1)}, bf16[4,1024]{1,0:T(4,128)(2,1)S(1)}, u32[]{:S(2)}, u32[]{:S(2)}) collective-permute-start(bf16[4,1024]{1,0:T(4,128)(2,1)S(1)} %combine.1.refs_0_), channel_id=1, source_target_pairs={{0,12},{4,8},{8,4},{12,0},{1,13},{5,9},{9,5},{13,1},{2,14},{6,10},... | collective-permute-start | bytes 24584 | tf_op jit(solution)/shard_map/ppermute | solution.py:24
  12.1 4.5 %collective-permute-start.4 = (bf16[4,1024]{1,0:T(4,128)(2,1)S(1)}, bf16[4,1024]{1,0:T(4,128)(2,1)S(1)}, u32[]{:S(2)}, u32[]{:S(2)}) collective-permute-start(bf16[4,1024]{1,0:T(4,128)(2,1)S(1)} %combine.1.refs_0_), channel_id=1, source_target_pairs={{0,8},{4,12},{8,0},{12,4},{1,9},{5,13},{9,1},{13,5},{2,10},{6,14},... | collective-permute-start | bytes 24584 | tf_op jit(solution)/shard_map/ppermute | solution.py:24
  12.1 4.5 %collective-permute-start.3 = (bf16[4,1024]{1,0:T(4,128)(2,1)S(1)}, bf16[4,1024]{1,0:T(4,128)(2,1)S(1)}, u32[]{:S(2)}, u32[]{:S(2)}) collective-permute-start(bf16[4,1024]{1,0:T(4,128)(2,1)S(1)} %combine.1.refs_0_), channel_id=1, source_target_pairs={{0,4},{4,0},{8,12},{12,8},{1,5},{5,1},{9,13},{13,9},{2,6},{6,2},{1... | collective-permute-start | bytes 24584 | tf_op jit(solution)/shard_map/ppermute | solution.py:24
  17.3 3.4 %collective-permute-start.6 = (bf16[16,1024]{1,0:T(8,128)(2,1)S(1)}, bf16[16,1024]{1,0:T(8,128)(2,1)S(1)}, u32[]{:S(2)}, u32[]{:S(2)}) collective-permute-start(bf16[16,1024]{1,0:T(8,128)(2,1)S(1)} %get-tuple-element.37), channel_id=1, source_target_pairs={{0,3},{1,2},{2,1},{3,0},{4,7},{5,6},{6,5},{7,4},{8,11},{9,10},{10,... | collective-permute-start | bytes 98312 | tf_op jit(solution)/shard_map/ppermute | solution.py:24
  17.4 4.2 %collective-permute-start.7 = (bf16[16,1024]{1,0:T(8,128)(2,1)S(1)}, bf16[16,1024]{1,0:T(8,128)(2,1)S(1)}, u32[]{:S(2)}, u32[]{:S(2)}) collective-permute-start(bf16[16,1024]{1,0:T(8,128)(2,1)S(1)} %get-tuple-element.38), channel_id=1, source_target_pairs={{0,2},{1,3},{2,0},{3,1},{4,6},{5,7},{6,4},{7,5},{8,10},{9,11},{10,... | collective-permute-start | bytes 98312 | tf_op jit(solution)/shard_map/ppermute | solution.py:24
  18.2 3.3 %collective-permute-start.8 = (bf16[16,1024]{1,0:T(8,128)(2,1)S(1)}, bf16[16,1024]{1,0:T(8,128)(2,1)S(1)}, u32[]{:S(2)}, u32[]{:S(2)}) collective-permute-start(bf16[16,1024]{1,0:T(8,128)(2,1)S(1)} %get-tuple-element.39), channel_id=1, source_target_pairs={{0,1},{1,0},{2,3},{3,2},{4,5},{5,4},{6,7},{7,6},{8,9},{9,8},{10,11... | collective-permute-start | bytes 98312 | tf_op jit(solution)/shard_map/ppermute | solution.py:24
  21.6 1.3 %collective-permute-start.9 = (f32[16,1024]{1,0:T(8,128)S(1)}, f32[16,1024]{1,0:T(8,128)S(1)}, u32[]{:S(2)}, u32[]{:S(2)}) collective-permute-start(f32[16,1024]{1,0:T(8,128)S(1)} %get-tuple-element.40.own), channel_id=1, source_target_pairs={{0,1},{1,0},{2,3},{3,2},{4,5},{5,4},{6,7},{7,6},{8,9},{9,8},{10,11... | collective-permute-start | bytes 196616 | tf_op jit(solution)/shard_map/ppermute | solution.py:24
  22.9 20.3 %slice-start.8 = ((s8[14680064]{0:T(1024)(128)(4,1)}), s8[2097152]{0:T(1024)(128)(4,1)S(1)}, s32[]{:S(2)}) async-start(s8[14680064]{0:T(1024)(128)(4,1)} %bitcast.4), calls=%async_computation.8 | async-start | bytes 4194304
  22.9 20.3 %slice-start.9 = ((s8[14680064]{0:T(1024)(128)(4,1)}), s8[4194304]{0:T(1024)(128)(4,1)S(1)}, s32[]{:S(2)}) async-start(s8[14680064]{0:T(1024)(128)(4,1)} %bitcast.4), calls=%async_computation.9 | async-start | bytes 8388608
  22.9 20.3 %slice-start.10 = ((s8[14680064]{0:T(1024)(128)(4,1)}), s8[4194304]{0:T(1024)(128)(4,1)S(1)}, s32[]{:S(2)}) async-start(s8[14680064]{0:T(1024)(128)(4,1)} %bitcast.4), calls=%async_computation.10 | async-start | bytes 8388608
  24.0 5.9 %collective-permute-start.11 = (bf16[16,1920]{1,0:T(8,128)(2,1)S(1)}, bf16[16,1920]{1,0:T(8,128)(2,1)S(1)}, u32[]{:S(2)}, u32[]{:S(2)}) collective-permute-start(bf16[16,1920]{1,0:T(8,128)(2,1)S(1)} %get-tuple-element.45.refs_0_), channel_id=1, source_target_pairs={{0,8},{4,12},{8,0},{12,4},{1,9},{5,13},{9,1},{13,5},{2,10},{6,14},... | collective-permute-start | bytes 184328 | tf_op jit(solution)/shard_map/ppermute | solution.py:24
  26.0 6.5 %collective-permute-start.12 = (bf16[16,1920]{1,0:T(8,128)(2,1)S(1)}, bf16[16,1920]{1,0:T(8,128)(2,1)S(1)}, u32[]{:S(2)}, u32[]{:S(2)}) collective-permute-start(bf16[16,1920]{1,0:T(8,128)(2,1)S(1)} %get-tuple-element.46), channel_id=1, source_target_pairs={{0,12},{4,8},{8,4},{12,0},{1,13},{5,9},{9,5},{13,1},{2,14},{6,10},... | collective-permute-start | bytes 184328 | tf_op jit(solution)/shard_map/ppermute | solution.py:24
  26.1 6.4 %collective-permute-start.10 = (bf16[16,1920]{1,0:T(8,128)(2,1)S(1)}, bf16[16,1920]{1,0:T(8,128)(2,1)S(1)}, u32[]{:S(2)}, u32[]{:S(2)}) collective-permute-start(bf16[16,1920]{1,0:T(8,128)(2,1)S(1)} %get-tuple-element.46), channel_id=1, source_target_pairs={{0,4},{4,0},{8,12},{12,8},{1,5},{5,1},{9,13},{13,9},{2,6},{6,2},{1... | collective-permute-start | bytes 184328 | tf_op jit(solution)/shard_map/ppermute | solution.py:24
  32.7 4.2 %collective-permute-start.15 = (bf16[8,1792]{1,0:T(8,128)(2,1)S(1)}, bf16[8,1792]{1,0:T(8,128)(2,1)S(1)}, u32[]{:S(2)}, u32[]{:S(2)}) collective-permute-start(bf16[8,1792]{1,0:T(8,128)(2,1)S(1)} %activation.1.own), channel_id=1, source_target_pairs={{0,4},{4,0},{8,12},{12,8},{1,5},{5,1},{9,13},{13,9},{2,6},{6,2},{1... | collective-permute-start | bytes 86024 | tf_op jit(solution)/shard_map/ppermute | solution.py:24
  33.3 9.9 %collective-permute-start.14 = (bf16[8,1792]{1,0:T(8,128)(2,1)S(1)}, bf16[8,1792]{1,0:T(8,128)(2,1)S(1)}, u32[]{:S(2)}, u32[]{:S(2)}) collective-permute-start(bf16[8,1792]{1,0:T(8,128)(2,1)S(1)} %activation.1.own), channel_id=1, source_target_pairs={{0,20},{4,16},{8,28},{12,24},{16,4},{20,0},{24,12},{28,8},{1,21},{... | collective-permute-start | bytes 86024 | tf_op jit(solution)/shard_map/ppermute | solution.py:24
  35.7 7.4 %collective-permute-start.13 = (bf16[8,1792]{1,0:T(8,128)(2,1)S(1)}, bf16[8,1792]{1,0:T(8,128)(2,1)S(1)}, u32[]{:S(2)}, u32[]{:S(2)}) collective-permute-start(bf16[8,1792]{1,0:T(8,128)(2,1)S(1)} %activation.1.own), channel_id=1, source_target_pairs={{0,16},{16,0},{1,17},{17,1},{2,18},{18,2},{3,19},{19,3},{4,20},{20... | collective-permute-start | bytes 86024 | tf_op jit(solution)/shard_map/ppermute | solution.py:24
  36.9 5.2 %copy-start = (bf16[3584,2048]{1,0:T(8,128)(2,1)S(1)}, bf16[3584,2048]{1,0:T(8,128)(2,1)}, u32[]{:S(2)}) copy-start(bf16[3584,2048]{1,0:T(8,128)(2,1)} %weight.3) | copy-start | bytes 44040196
  42.1 2.2 %slice-start.11 = ((s8[14680064]{0:T(1024)(128)(4,1)}), s8[4194304]{0:T(1024)(128)(4,1)S(1)}, s32[]{:S(2)}) async-start(s8[14680064]{0:T(1024)(128)(4,1)} %bitcast.4), calls=%async_computation.11 | async-start | bytes 8388608
  45.3 3.8 %collective-permute-start.18 = (bf16[16,2048]{1,0:T(8,128)(2,1)S(1)}, bf16[16,2048]{1,0:T(8,128)(2,1)S(1)}, u32[]{:S(2)}, u32[]{:S(2)}) collective-permute-start(bf16[16,2048]{1,0:T(8,128)(2,1)S(1)} %down.3.refs_0_), channel_id=1, source_target_pairs={{0,3},{1,2},{2,1},{3,0},{4,7},{5,6},{6,5},{7,4},{8,11},{9,10},{10,... | collective-permute-start | bytes 196616 | tf_op jit(solution)/shard_map/ppermute | solution.py:24
  45.3 5.0 %collective-permute-start.17 = (bf16[16,2048]{1,0:T(8,128)(2,1)S(1)}, bf16[16,2048]{1,0:T(8,128)(2,1)S(1)}, u32[]{:S(2)}, u32[]{:S(2)}) collective-permute-start(bf16[16,2048]{1,0:T(8,128)(2,1)S(1)} %down.3.refs_0_), channel_id=1, source_target_pairs={{0,2},{1,3},{2,0},{3,1},{4,6},{5,7},{6,4},{7,5},{8,10},{9,11},{10,... | collective-permute-start | bytes 196616 | tf_op jit(solution)/shard_map/ppermute | solution.py:24
  46.0 4.3 %collective-permute-start.16 = (bf16[16,2048]{1,0:T(8,128)(2,1)S(1)}, bf16[16,2048]{1,0:T(8,128)(2,1)S(1)}, u32[]{:S(2)}, u32[]{:S(2)}) collective-permute-start(bf16[16,2048]{1,0:T(8,128)(2,1)S(1)} %down.3.refs_0_), channel_id=1, source_target_pairs={{0,1},{1,0},{2,3},{3,2},{4,5},{5,4},{6,7},{7,6},{8,9},{9,8},{10,11... | collective-permute-start | bytes 196616 | tf_op jit(solution)/shard_map/ppermute | solution.py:24

commit v12 on v11

--- a/solution.py
+++ b/solution.py
@@ -450,7 +450,7 @@
         [shape((m, width_share), f32)] + [shape((m, hidden + HD), WIRE)] * 2,
         [VMEM_SPEC] * 7,
         [pltpu.VMEM((2, m, hidden + HD), f32)],
-        limit=8,
+        flops=40 * 10**9,
         name="gate_up_second",
     )(own, received, norm_gain, *weights, *first)
     sums = [keep] + [partner((keep, send)[k % 2], "row", k) for k in range(1, groups)]

time: 51.2 us -> 46.5 us (0.908)
  local copies, waits for them, and re-layouts: 6.29 us -> 0.07 us
  waiting for transfers between devices: 17.4 us -> 18.9 us
    unnamed x32 -> x30, local copies, waits for them, and re-layouts: 6.29 us -> 0.07 us
    ppermute x19, waiting for transfers between devices: 17.4 us -> 18.9 us  [partner(): lax.ppermute(value, axis, [(i, i ^ k) for i in range(lax.axis_size(axis))])]
  transfers between devices with their start and end apart: 19 -> 19, of which waited for: 12 -> 14; matrix products, arithmetic and copies ran while one was open for 0% -> 0% of each run, Pallas kernels for 5% -> 6%
where the time goes in v12:
time: 46.5 us; the launch traced here: 46.4 us
  waiting for transfers between devices  18.9 us (41%)
  starting transfers between devices  18.6 us (40%)
  Pallas kernels  8.44 us (18%)
    ppermute x19, waiting for transfers between devices, partner(): lax.ppermute(value, axis, [(i, i ^ k) for i in range(lax.axis_size(axis))])  18.9 us
    ppermute x19, starting transfers between devices, partner(): lax.ppermute(value, axis, [(i, i ^ k) for i in range(lax.axis_size(axis))])  18.6 us
    pallas_call x2, Pallas kernels, down_part(): call(functools.partial(down_kernel, other), shape((m, width_share), resul...  2.13 us
    pallas_call x1, Pallas kernels, shards(): call(functools.partial(attention_far_kernel, cols), [message] * (cols //...  1.88 us
    pallas_call x1, Pallas kernels, shards(): call(lift_second_kernel, [shape((m, width_share), f32)] + [shape((m, hidd...  1.08 us
    pallas_call x1, Pallas kernels, shards(): call(lift_first_kernel, [shape((m, hidden), f32)] * 2, [VMEM_SPEC] * 3, n...  1.07 us
  transfers between devices with their start and end apart: 19, of which 14 were waited for; matrix products, arithmetic and copies ran while one was open for 0% of the time, Pallas kernels for 6%

profile of v12, /device:TPU:0, one launch (start us, length us, event | category | flops | bytes accessed | tf_op | source)
XLA Modules:
  0.0 46.4 jit_solution(4943736425146771493)
XLA Ops:
  0.0 1.9 %attention_far.1 = (f32[5,8,128]{2,1,0:T(8,128)S(1)}, f32[5,8,128]{2,1,0:T(8,128)S(1)}, bf16[2,2,4096]{2,1,0:T(2,128)(2,1)S(1)}, bf16[2,2,512]{2,1,0:T(2,128)(2,...) custom-call(bf16[2,2,4096]{2,1,0:T(2,128)(2,1)} %refs_0_.1, ...), custom_call_target="tpu_custom_call" | custom-call | tf_op jit(solution)/shard_map/attention_far/pallas_call | solution.py:395
  1.9 3.0 %collective-permute-start = (f32[5,8,128]{2,1,0:T(8,128)S(1)}, f32[5,8,128]{2,1,0:T(8,128)S(1)}, u32[]{:S(2)}, u32[]{:S(2)}) collective-permute-start(f32[5,8,128]{2,1,0:T(8,128)S(1)} %get-tuple-element.26), channel_id=1, source_target_pairs={{0,2},{1,3},{2,0},{3,1},{4,6},{5,7},{6,4},{7,5},{8,10},{9,11},{10,... | collective-permute-start | bytes 61448 | tf_op jit(solution)/shard_map/ppermute | solution.py:24
  4.9 0.5 %attention_near.1 = (f32[5,8,128]{2,1,0:T(8,128)S(1)}, f32[5,8,128]{2,1,0:T(8,128)S(1)}) custom-call(bf16[2,2,4096]{2,1,0:T(2,128)(2,1)S(1)} %get-tuple-element.28.refs_0_, bf16[2,2,512]{2,1,0:T(2,128)(2,1)S(1)} %get-tuple-element.29.refs_1_, bf16[2,2,512]{2,1,0:T(2,128)(2,1)S(1)} %get-tuple-element.30.refs_2_, ...), custom_call_target="tpu_custom_call" | custom-call | tf_op jit(solution)/shard_map/attention_near/pallas_call | solution.py:404
  5.4 0.2 collective-permute-start.2
  5.7 1.0 %collective-permute-done.refs_0_ = f32[5,8,128]{2,1,0:T(8,128)S(1)} collective-permute-done((f32[5,8,128]{2,1,0:T(8,128)S(1)}, f32[5,8,128]{2,1,0:T(8,128)S(1)}, u32[]{:S(2)}, u32[]{:S(2)}) %collective-permute-start) | collective-permute-done | bytes 20512 | tf_op jit(solution)/shard_map/ppermute | solution.py:24
  6.7 1.4 %collective-permute-done.1.refs_1_ = f32[5,8,128]{2,1,0:T(8,128)S(1)} collective-permute-done((f32[5,8,128]{2,1,0:T(8,128)S(1)}, f32[5,8,128]{2,1,0:T(8,128)S(1)}, u32[]{:S(2)}, u32[]{:S(2)}) %collective-permute-start.1) | collective-permute-done | bytes 20512 | tf_op jit(solution)/shard_map/ppermute | solution.py:24
  8.1 0.0 slice-start.5
  8.2 0.0 slice-start.6
  8.2 0.0 slice-start.7
  8.2 0.0 slice-start.9
  8.2 0.0 slice-start.11
  8.2 0.2 combine.1.refs_0_
  8.4 3.7 %collective-permute-start.5 = (bf16[4,1024]{1,0:T(4,128)(2,1)S(1)}, bf16[4,1024]{1,0:T(4,128)(2,1)S(1)}, u32[]{:S(2)}, u32[]{:S(2)}) collective-permute-start(bf16[4,1024]{1,0:T(4,128)(2,1)S(1)} %combine.1.refs_0_), channel_id=1, source_target_pairs={{0,12},{4,8},{8,4},{12,0},{1,13},{5,9},{9,5},{13,1},{2,14},{6,10},... | collective-permute-start | bytes 24584 | tf_op jit(solution)/shard_map/ppermute | solution.py:24
  12.1 0.0 collective-permute-start.4
  12.1 0.8 %collective-permute-start.3 = (bf16[4,1024]{1,0:T(4,128)(2,1)S(1)}, bf16[4,1024]{1,0:T(4,128)(2,1)S(1)}, u32[]{:S(2)}, u32[]{:S(2)}) collective-permute-start(bf16[4,1024]{1,0:T(4,128)(2,1)S(1)} %combine.1.refs_0_), channel_id=1, source_target_pairs={{0,4},{4,0},{8,12},{12,8},{1,5},{5,1},{9,13},{13,9},{2,6},{6,2},{1... | collective-permute-start | bytes 24584 | tf_op jit(solution)/shard_map/ppermute | solution.py:24
  12.8 1.1 %collective-permute-done.5.refs_3_ = bf16[4,1024]{1,0:T(4,128)(2,1)S(1)} collective-permute-done((bf16[4,1024]{1,0:T(4,128)(2,1)S(1)}, bf16[4,1024]{1,0:T(4,128)(2,1)S(1)}, u32[]{:S(2)}, u32[]{:S(2)}) %collective-permute-start.5) | collective-permute-done | bytes 8224 | tf_op jit(solution)/shard_map/ppermute | solution.py:24
  14.0 2.6 %collective-permute-done.4.refs_2_ = bf16[4,1024]{1,0:T(4,128)(2,1)S(1)} collective-permute-done((bf16[4,1024]{1,0:T(4,128)(2,1)S(1)}, bf16[4,1024]{1,0:T(4,128)(2,1)S(1)}, u32[]{:S(2)}, u32[]{:S(2)}) %collective-permute-start.4) | collective-permute-done | bytes 8224 | tf_op jit(solution)/shard_map/ppermute | solution.py:24
  16.6 0.7 %out_projection.1 = (bf16[16,1024]{1,0:T(8,128)(2,1)S(1)}, bf16[16,1024]{1,0:T(8,128)(2,1)S(1)}, bf16[16,1024]{1,0:T(8,128)(2,1)S(1)}, bf16[16,1024]{1,0:T(8,128)(2,1)S(1)}) custom-call(bf16[4,1024]{1,0:T(4,128)(2,1)S(1)} %combine.1.refs_0_, bf16[4,1024]{1,0:T(4,128)(2,1)S(1)} %collective-permute-done.3.refs_1_, ...), custom_call_target="tpu_custom_call" | custom-call | tf_op jit(solution)/shard_map/out_projection/pallas_call | solution.py:421
  17.3 0.1 collective-permute-start.6
  17.4 0.8 %collective-permute-start.7 = (bf16[16,1024]{1,0:T(8,128)(2,1)S(1)}, bf16[16,1024]{1,0:T(8,128)(2,1)S(1)}, u32[]{:S(2)}, u32[]{:S(2)}) collective-permute-start(bf16[16,1024]{1,0:T(8,128)(2,1)S(1)} %get-tuple-element.38), channel_id=1, source_target_pairs={{0,2},{1,3},{2,0},{3,1},{4,6},{5,7},{6,4},{7,5},{8,10},{9,11},{10,... | collective-permute-start | bytes 98312 | tf_op jit(solution)/shard_map/ppermute | solution.py:24
  18.2 1.0 %collective-permute-start.8 = (bf16[16,1024]{1,0:T(8,128)(2,1)S(1)}, bf16[16,1024]{1,0:T(8,128)(2,1)S(1)}, u32[]{:S(2)}, u32[]{:S(2)}) collective-permute-start(bf16[16,1024]{1,0:T(8,128)(2,1)S(1)} %get-tuple-element.39), channel_id=1, source_target_pairs={{0,1},{1,0},{2,3},{3,2},{4,5},{5,4},{6,7},{7,6},{8,9},{9,8},{10,11... | collective-permute-start | bytes 98312 | tf_op jit(solution)/shard_map/ppermute | solution.py:24
  19.2 1.5 %collective-permute-done.6.refs_1_ = bf16[16,1024]{1,0:T(8,128)(2,1)S(1)} collective-permute-done((bf16[16,1024]{1,0:T(8,128)(2,1)S(1)}, bf16[16,1024]{1,0:T(8,128)(2,1)S(1)}, u32[]{:S(2)}, u32[]{:S(2)}) %collective-permute-start.6) | collective-permute-done | bytes 32800 | tf_op jit(solution)/shard_map/ppermute | solution.py:24
  20.7 0.8 %collective-permute-done.7.refs_2_ = bf16[16,1024]{1,0:T(8,128)(2,1)S(1)} collective-permute-done((bf16[16,1024]{1,0:T(8,128)(2,1)S(1)}, bf16[16,1024]{1,0:T(8,128)(2,1)S(1)}, u32[]{:S(2)}, u32[]{:S(2)}) %collective-permute-start.7) | collective-permute-done | bytes 32800 | tf_op jit(solution)/shard_map/ppermute | solution.py:24
  21.6 0.1 collective-permute-start.9
  21.8 0.0 slice-start
  21.8 1.1 %gate_up_first.1 = (f32[16,1792]{1,0:T(8,128)S(1)}, f32[16,1792]{1,0:T(8,128)S(1)}) custom-call(bf16[16,1024]{1,0:T(8,128)(2,1)S(1)} %get-tuple-element.41.lifted, bf16[2048,3584]{1,0:T(8,128)(2,1)S(1)} %bitcast.3, bf16[2048,3584]{1,0:T(8,128)(2,1)S(1)} %bitcast.5), custom_call_target="tpu_custom_call" | custom-call | tf_op jit(solution)/shard_map/gate_up_first/pallas_call | solution.py:442
  22.8 0.1 collective-permute-done.9.received
  22.9 1.1 %gate_up_second.1 = (f32[16,2048]{1,0:T(8,128)S(1)}, bf16[16,1920]{1,0:T(8,128)(2,1)S(1)}, bf16[16,1920]{1,0:T(8,128)(2,1)S(1)}) custom-call(f32[16,1024]{1,0:T(8,128)S(1)} %get-tuple-element.40.own, f32[16,1024]{1,0:T(8,128)S(1)} %collective-permute-done.9.received, bf16[2048]{0:T(1024)(128)(2,1)S(1)} %copy-done.2, bf16[2048,3584]{1,0:T(8,128)(2,1)S(1)} %bitcast.3, ...), custom_call_target="tpu_custom_call" | custom-call | flops 40000000000 | bytes 1024 | tf_op jit(solution)/shard_map/gate_up_second/pallas_call | solution.py:448
  24.0 2.0 %collective-permute-start.11 = (bf16[16,1920]{1,0:T(8,128)(2,1)S(1)}, bf16[16,1920]{1,0:T(8,128)(2,1)S(1)}, u32[]{:S(2)}, u32[]{:S(2)}) collective-permute-start(bf16[16,1920]{1,0:T(8,128)(2,1)S(1)} %get-tuple-element.45.refs_0_), channel_id=1, source_target_pairs={{0,8},{4,12},{8,0},{12,4},{1,9},{5,13},{9,1},{13,5},{2,10},{6,14},... | collective-permute-start | bytes 184328 | tf_op jit(solution)/shard_map/ppermute | solution.py:24
  26.0 0.1 collective-permute-start.12
  26.1 1.4 %collective-permute-start.10 = (bf16[16,1920]{1,0:T(8,128)(2,1)S(1)}, bf16[16,1920]{1,0:T(8,128)(2,1)S(1)}, u32[]{:S(2)}, u32[]{:S(2)}) collective-permute-start(bf16[16,1920]{1,0:T(8,128)(2,1)S(1)} %get-tuple-element.46), channel_id=1, source_target_pairs={{0,4},{4,0},{8,12},{12,8},{1,5},{5,1},{9,13},{13,9},{2,6},{6,2},{1... | collective-permute-start | bytes 184328 | tf_op jit(solution)/shard_map/ppermute | solution.py:24
  27.5 2.4 %collective-permute-done.11.refs_2_ = bf16[16,1920]{1,0:T(8,128)(2,1)S(1)} collective-permute-done((bf16[16,1920]{1,0:T(8,128)(2,1)S(1)}, bf16[16,1920]{1,0:T(8,128)(2,1)S(1)}, u32[]{:S(2)}, u32[]{:S(2)}) %collective-permute-start.11) | collective-permute-done | bytes 61472 | tf_op jit(solution)/shard_map/ppermute | solution.py:24
  29.9 2.7 %collective-permute-done.12.refs_3_ = bf16[16,1920]{1,0:T(8,128)(2,1)S(1)} collective-permute-done((bf16[16,1920]{1,0:T(8,128)(2,1)S(1)}, bf16[16,1920]{1,0:T(8,128)(2,1)S(1)}, u32[]{:S(2)}, u32[]{:S(2)}) %collective-permute-start.12) | collective-permute-done | bytes 61472 | tf_op jit(solution)/shard_map/ppermute | solution.py:24
  32.6 0.0 collective-permute-done.10.refs_1_
  32.6 0.1 activation.1.own
  32.7 0.6 %collective-permute-start.15 = (bf16[8,1792]{1,0:T(8,128)(2,1)S(1)}, bf16[8,1792]{1,0:T(8,128)(2,1)S(1)}, u32[]{:S(2)}, u32[]{:S(2)}) collective-permute-start(bf16[8,1792]{1,0:T(8,128)(2,1)S(1)} %activation.1.own), channel_id=1, source_target_pairs={{0,4},{4,0},{8,12},{12,8},{1,5},{5,1},{9,13},{13,9},{2,6},{6,2},{1... | collective-permute-start | bytes 86024 | tf_op jit(solution)/shard_map/ppermute | solution.py:24
  33.3 2.5 %collective-permute-start.14 = (bf16[8,1792]{1,0:T(8,128)(2,1)S(1)}, bf16[8,1792]{1,0:T(8,128)(2,1)S(1)}, u32[]{:S(2)}, u32[]{:S(2)}) collective-permute-start(bf16[8,1792]{1,0:T(8,128)(2,1)S(1)} %activation.1.own), channel_id=1, source_target_pairs={{0,20},{4,16},{8,28},{12,24},{16,4},{20,0},{24,12},{28,8},{1,21},{... | collective-permute-start | bytes 86024 | tf_op jit(solution)/shard_map/ppermute | solution.py:24
  35.7 0.5 %collective-permute-start.13 = (bf16[8,1792]{1,0:T(8,128)(2,1)S(1)}, bf16[8,1792]{1,0:T(8,128)(2,1)S(1)}, u32[]{:S(2)}, u32[]{:S(2)}) collective-permute-start(bf16[8,1792]{1,0:T(8,128)(2,1)S(1)} %activation.1.own), channel_id=1, source_target_pairs={{0,16},{16,0},{1,17},{17,1},{2,18},{18,2},{3,19},{19,3},{4,20},{20... | collective-permute-start | bytes 86024 | tf_op jit(solution)/shard_map/ppermute | solution.py:24
  36.3 0.6 %collective-permute-done.15.received = bf16[8,1792]{1,0:T(8,128)(2,1)S(1)} collective-permute-done((bf16[8,1792]{1,0:T(8,128)(2,1)S(1)}, bf16[8,1792]{1,0:T(8,128)(2,1)S(1)}, u32[]{:S(2)}, u32[]{:S(2)}) %collective-permute-start.15) | collective-permute-done | bytes 28704 | tf_op jit(solution)/shard_map/ppermute | solution.py:24
  37.0 1.1 %down.2.refs_0_ = f32[16,2048]{1,0:T(8,128)S(1)} custom-call(bf16[16,1792]{1,0:T(8,128)(2,1)S(1)} %gather_act.3.act, bf16[3584,2048]{1,0:T(8,128)(2,1)S(1)} %bitcast.1), custom_call_target="tpu_custom_call" | custom-call | tf_op jit(solution)/shard_map/down/pallas_call | solution.py:473
  38.0 0.1 collective-permute-done.14.received
  38.1 1.5 %collective-permute-done.13.own = bf16[8,1792]{1,0:T(8,128)(2,1)S(1)} collective-permute-done((bf16[8,1792]{1,0:T(8,128)(2,1)S(1)}, bf16[8,1792]{1,0:T(8,128)(2,1)S(1)}, u32[]{:S(2)}, u32[]{:S(2)}) %collective-permute-start.13) | collective-permute-done | bytes 28704 | tf_op jit(solution)/shard_map/ppermute | solution.py:24
  39.6 1.1 %down.3.refs_0_ = bf16[16,2048]{1,0:T(8,128)(2,1)S(1)} custom-call(bf16[16,1792]{1,0:T(8,128)(2,1)S(1)} %gather_act.2.act, bf16[3584,2048]{1,0:T(8,128)(2,1)S(1)} %bitcast.1, f32[16,2048]{1,0:T(8,128)S(1)} %down.2.refs_0_), custom_call_target="tpu_custom_call" | custom-call | tf_op jit(solution)/shard_map/down/pallas_call | solution.py:473
  40.7 0.6 %collective-permute-start.17 = (bf16[16,2048]{1,0:T(8,128)(2,1)S(1)}, bf16[16,2048]{1,0:T(8,128)(2,1)S(1)}, u32[]{:S(2)}, u32[]{:S(2)}) collective-permute-start(bf16[16,2048]{1,0:T(8,128)(2,1)S(1)} %down.3.refs_0_), channel_id=1, source_target_pairs={{0,2},{1,3},{2,0},{3,1},{4,6},{5,7},{6,4},{7,5},{8,10},{9,11},{10,... | collective-permute-start | bytes 196616 | tf_op jit(solution)/shard_map/ppermute | solution.py:24
  41.4 1.2 %collective-permute-start.16 = (bf16[16,2048]{1,0:T(8,128)(2,1)S(1)}, bf16[16,2048]{1,0:T(8,128)(2,1)S(1)}, u32[]{:S(2)}, u32[]{:S(2)}) collective-permute-start(bf16[16,2048]{1,0:T(8,128)(2,1)S(1)} %down.3.refs_0_), channel_id=1, source_target_pairs={{0,1},{1,0},{2,3},{3,2},{4,5},{5,4},{6,7},{7,6},{8,9},{9,8},{10,11... | collective-permute-start | bytes 196616 | tf_op jit(solution)/shard_map/ppermute | solution.py:24
  42.6 2.0 %collective-permute-done.18.refs_3_ = bf16[16,2048]{1,0:T(8,128)(2,1)S(1)} collective-permute-done((bf16[16,2048]{1,0:T(8,128)(2,1)S(1)}, bf16[16,2048]{1,0:T(8,128)(2,1)S(1)}, u32[]{:S(2)}, u32[]{:S(2)}) %collective-permute-start.18) | collective-permute-done | bytes 65568 | tf_op jit(solution)/shard_map/ppermute | solution.py:24
  44.5 1.1 %collective-permute-done.17.refs_2_ = bf16[16,2048]{1,0:T(8,128)(2,1)S(1)} collective-permute-done((bf16[16,2048]{1,0:T(8,128)(2,1)S(1)}, bf16[16,2048]{1,0:T(8,128)(2,1)S(1)}, u32[]{:S(2)}, u32[]{:S(2)}) %collective-permute-start.17) | collective-permute-done | bytes 65568 | tf_op jit(solution)/shard_map/ppermute | solution.py:24
  45.7 0.7 %final.1 = bf16[2,8,2048]{2,1,0:T(8,128)(2,1)} custom-call(f32[16,2048]{1,0:T(8,128)S(1)} %get-tuple-element.44.mid, bf16[16,2048]{1,0:T(8,128)(2,1)S(1)} %down.3.refs_0_, bf16[16,2048]{1,0:T(8,128)(2,1)S(1)} %collective-permute-done.16.refs_1_, bf16[16,2048]{1,0:T(8,128)(2,1)S(1)} %collective-permute-done.17.refs_2_, ...), custom_call_target="tpu_custom_call" | custom-call | tf_op jit(solution)/shard_map/final/pallas_call | solution.py:487
  (36 shorter events, 0.1 us)
Async XLA Ops:
  1.9 4.8 %collective-permute-start = (f32[5,8,128]{2,1,0:T(8,128)S(1)}, f32[5,8,128]{2,1,0:T(8,128)S(1)}, u32[]{:S(2)}, u32[]{:S(2)}) collective-permute-start(f32[5,8,128]{2,1,0:T(8,128)S(1)} %get-tuple-element.26), channel_id=1, source_target_pairs={{0,2},{1,3},{2,0},{3,1},{4,6},{5,7},{6,4},{7,5},{8,10},{9,11},{10,... | collective-permute-start | bytes 61448 | tf_op jit(solution)/shard_map/ppermute | solution.py:24
  4.9 3.2 %collective-permute-start.1 = (f32[5,8,128]{2,1,0:T(8,128)S(1)}, f32[5,8,128]{2,1,0:T(8,128)S(1)}, u32[]{:S(2)}, u32[]{:S(2)}) collective-permute-start(f32[5,8,128]{2,1,0:T(8,128)S(1)} %get-tuple-element.27), channel_id=1, source_target_pairs={{0,3},{1,2},{2,1},{3,0},{4,7},{5,6},{6,5},{7,4},{8,11},{9,10},{10,... | collective-permute-start | bytes 61448 | tf_op jit(solution)/shard_map/ppermute | solution.py:24
  4.9 16.7 %slice-start.4 = ((s8[14680064]{0:T(1024)(128)(4,1)}), s8[4194304]{0:T(1024)(128)(4,1)S(1)}, s32[]{:S(2)}) async-start(s8[14680064]{0:T(1024)(128)(4,1)} %bitcast.2), calls=%async_computation.4 | async-start | bytes 8388608
  4.9 16.8 %slice-start.8 = ((s8[14680064]{0:T(1024)(128)(4,1)}), s8[4194304]{0:T(1024)(128)(4,1)S(1)}, s32[]{:S(2)}) async-start(s8[14680064]{0:T(1024)(128)(4,1)} %bitcast.4), calls=%async_computation.8 | async-start | bytes 8388608
  5.4 2.7 %collective-permute-start.2 = (f32[5,8,128]{2,1,0:T(8,128)S(1)}, f32[5,8,128]{2,1,0:T(8,128)S(1)}, u32[]{:S(2)}, u32[]{:S(2)}) collective-permute-start(f32[5,8,128]{2,1,0:T(8,128)S(1)} %get-tuple-element.35), channel_id=1, source_target_pairs={{0,1},{1,0},{2,3},{3,2},{4,5},{5,4},{6,7},{7,6},{8,9},{9,8},{10,11... | collective-permute-start | bytes 61448 | tf_op jit(solution)/shard_map/ppermute | solution.py:24
  8.1 8.5 %copy-start = (bf16[1024,2048]{1,0:T(8,128)(2,1)S(1)}, bf16[1024,2048]{1,0:T(8,128)(2,1)}, u32[]{:S(2)}) copy-start(bf16[1024,2048]{1,0:T(8,128)(2,1)} %refs_4_.3) | copy-start | bytes 12582916
  8.1 13.4 %copy-start.1 = (bf16[2,8,2048]{2,1,0:T(8,128)(2,1)S(1)}, bf16[2,8,2048]{2,1,0:T(8,128)(2,1)}, u32[]{:S(2)}) copy-start(bf16[2,8,2048]{2,1,0:T(8,128)(2,1)} %residual.1) | copy-start | bytes 196612
  8.1 13.4 %copy-start.2 = (bf16[2048]{0:T(1024)(128)(2,1)S(1)}, bf16[2048]{0:T(1024)(128)(2,1)}, u32[]{:S(2)}) copy-start(bf16[2048]{0:T(1024)(128)(2,1)} %gains.3) | copy-start | bytes 12292
  8.1 13.5 %slice-start.5 = ((s8[14680064]{0:T(1024)(128)(4,1)}), s8[4194304]{0:T(1024)(128)(4,1)S(1)}, s32[]{:S(2)}) async-start(s8[14680064]{0:T(1024)(128)(4,1)} %bitcast.2), calls=%async_computation.5 | async-start | bytes 8388608
  8.2 13.5 %slice-start.6 = ((s8[14680064]{0:T(1024)(128)(4,1)}), s8[4194304]{0:T(1024)(128)(4,1)S(1)}, s32[]{:S(2)}) async-start(s8[14680064]{0:T(1024)(128)(4,1)} %bitcast.2), calls=%async_computation.6 | async-start | bytes 8388608
  8.2 13.5 %slice-start.7 = ((s8[14680064]{0:T(1024)(128)(4,1)}), s8[2097152]{0:T(1024)(128)(4,1)S(1)}, s32[]{:S(2)}) async-start(s8[14680064]{0:T(1024)(128)(4,1)} %bitcast.2), calls=%async_computation.7 | async-start | bytes 4194304
  8.2 13.5 %slice-start.9 = ((s8[14680064]{0:T(1024)(128)(4,1)}), s8[4194304]{0:T(1024)(128)(4,1)S(1)}, s32[]{:S(2)}) async-start(s8[14680064]{0:T(1024)(128)(4,1)} %bitcast.4), calls=%async_computation.9 | async-start | bytes 8388608
  8.2 13.5 %slice-start.10 = ((s8[14680064]{0:T(1024)(128)(4,1)}), s8[4194304]{0:T(1024)(128)(4,1)S(1)}, s32[]{:S(2)}) async-start(s8[14680064]{0:T(1024)(128)(4,1)} %bitcast.4), calls=%async_computation.10 | async-start | bytes 8388608
  8.2 13.5 %slice-start.11 = ((s8[14680064]{0:T(1024)(128)(4,1)}), s8[2097152]{0:T(1024)(128)(4,1)S(1)}, s32[]{:S(2)}) async-start(s8[14680064]{0:T(1024)(128)(4,1)} %bitcast.4), calls=%async_computation.11 | async-start | bytes 4194304
  8.4 5.6 %collective-permute-start.5 = (bf16[4,1024]{1,0:T(4,128)(2,1)S(1)}, bf16[4,1024]{1,0:T(4,128)(2,1)S(1)}, u32[]{:S(2)}, u32[]{:S(2)}) collective-permute-start(bf16[4,1024]{1,0:T(4,128)(2,1)S(1)} %combine.1.refs_0_), channel_id=1, source_target_pairs={{0,12},{4,8},{8,4},{12,0},{1,13},{5,9},{9,5},{13,1},{2,14},{6,10},... | collective-permute-start | bytes 24584 | tf_op jit(solution)/shard_map/ppermute | solution.py:24
  12.1 4.5 %collective-permute-start.4 = (bf16[4,1024]{1,0:T(4,128)(2,1)S(1)}, bf16[4,1024]{1,0:T(4,128)(2,1)S(1)}, u32[]{:S(2)}, u32[]{:S(2)}) collective-permute-start(bf16[4,1024]{1,0:T(4,128)(2,1)S(1)} %combine.1.refs_0_), channel_id=1, source_target_pairs={{0,8},{4,12},{8,0},{12,4},{1,9},{5,13},{9,1},{13,5},{2,10},{6,14},... | collective-permute-start | bytes 24584 | tf_op jit(solution)/shard_map/ppermute | solution.py:24
  12.1 4.5 %collective-permute-start.3 = (bf16[4,1024]{1,0:T(4,128)(2,1)S(1)}, bf16[4,1024]{1,0:T(4,128)(2,1)S(1)}, u32[]{:S(2)}, u32[]{:S(2)}) collective-permute-start(bf16[4,1024]{1,0:T(4,128)(2,1)S(1)} %combine.1.refs_0_), channel_id=1, source_target_pairs={{0,4},{4,0},{8,12},{12,8},{1,5},{5,1},{9,13},{13,9},{2,6},{6,2},{1... | collective-permute-start | bytes 24584 | tf_op jit(solution)/shard_map/ppermute | solution.py:24
  17.3 3.4 %collective-permute-start.6 = (bf16[16,1024]{1,0:T(8,128)(2,1)S(1)}, bf16[16,1024]{1,0:T(8,128)(2,1)S(1)}, u32[]{:S(2)}, u32[]{:S(2)}) collective-permute-start(bf16[16,1024]{1,0:T(8,128)(2,1)S(1)} %get-tuple-element.37), channel_id=1, source_target_pairs={{0,3},{1,2},{2,1},{3,0},{4,7},{5,6},{6,5},{7,4},{8,11},{9,10},{10,... | collective-permute-start | bytes 98312 | tf_op jit(solution)/shard_map/ppermute | solution.py:24
  17.4 4.2 %collective-permute-start.7 = (bf16[16,1024]{1,0:T(8,128)(2,1)S(1)}, bf16[16,1024]{1,0:T(8,128)(2,1)S(1)}, u32[]{:S(2)}, u32[]{:S(2)}) collective-permute-start(bf16[16,1024]{1,0:T(8,128)(2,1)S(1)} %get-tuple-element.38), channel_id=1, source_target_pairs={{0,2},{1,3},{2,0},{3,1},{4,6},{5,7},{6,4},{7,5},{8,10},{9,11},{10,... | collective-permute-start | bytes 98312 | tf_op jit(solution)/shard_map/ppermute | solution.py:24
  18.2 3.3 %collective-permute-start.8 = (bf16[16,1024]{1,0:T(8,128)(2,1)S(1)}, bf16[16,1024]{1,0:T(8,128)(2,1)S(1)}, u32[]{:S(2)}, u32[]{:S(2)}) collective-permute-start(bf16[16,1024]{1,0:T(8,128)(2,1)S(1)} %get-tuple-element.39), channel_id=1, source_target_pairs={{0,1},{1,0},{2,3},{3,2},{4,5},{5,4},{6,7},{7,6},{8,9},{9,8},{10,11... | collective-permute-start | bytes 98312 | tf_op jit(solution)/shard_map/ppermute | solution.py:24
  21.6 1.3 %collective-permute-start.9 = (f32[16,1024]{1,0:T(8,128)S(1)}, f32[16,1024]{1,0:T(8,128)S(1)}, u32[]{:S(2)}, u32[]{:S(2)}) collective-permute-start(f32[16,1024]{1,0:T(8,128)S(1)} %get-tuple-element.40.own), channel_id=1, source_target_pairs={{0,1},{1,0},{2,3},{3,2},{4,5},{5,4},{6,7},{7,6},{8,9},{9,8},{10,11... | collective-permute-start | bytes 196616 | tf_op jit(solution)/shard_map/ppermute | solution.py:24
  21.8 15.1 %slice-start = ((s8[14680064]{0:T(1024)(128)(4,1)}), s8[4194304]{0:T(1024)(128)(4,1)S(1)}, s32[]{:S(2)}) async-start(s8[14680064]{0:T(1024)(128)(4,1)} %bitcast), calls=%async_computation | async-start | bytes 8388608
  22.9 14.0 %slice-start.1 = ((s8[14680064]{0:T(1024)(128)(4,1)}), s8[4194304]{0:T(1024)(128)(4,1)S(1)}, s32[]{:S(2)}) async-start(s8[14680064]{0:T(1024)(128)(4,1)} %bitcast), calls=%async_computation.1 | async-start | bytes 8388608
  22.9 14.0 %slice-start.2 = ((s8[14680064]{0:T(1024)(128)(4,1)}), s8[4194304]{0:T(1024)(128)(4,1)S(1)}, s32[]{:S(2)}) async-start(s8[14680064]{0:T(1024)(128)(4,1)} %bitcast), calls=%async_computation.2 | async-start | bytes 8388608
  22.9 14.0 %slice-start.3 = ((s8[14680064]{0:T(1024)(128)(4,1)}), s8[2097152]{0:T(1024)(128)(4,1)S(1)}, s32[]{:S(2)}) async-start(s8[14680064]{0:T(1024)(128)(4,1)} %bitcast), calls=%async_computation.3 | async-start | bytes 4194304
  24.0 5.9 %collective-permute-start.11 = (bf16[16,1920]{1,0:T(8,128)(2,1)S(1)}, bf16[16,1920]{1,0:T(8,128)(2,1)S(1)}, u32[]{:S(2)}, u32[]{:S(2)}) collective-permute-start(bf16[16,1920]{1,0:T(8,128)(2,1)S(1)} %get-tuple-element.45.refs_0_), channel_id=1, source_target_pairs={{0,8},{4,12},{8,0},{12,4},{1,9},{5,13},{9,1},{13,5},{2,10},{6,14},... | collective-permute-start | bytes 184328 | tf_op jit(solution)/shard_map/ppermute | solution.py:24
  26.0 6.5 %collective-permute-start.12 = (bf16[16,1920]{1,0:T(8,128)(2,1)S(1)}, bf16[16,1920]{1,0:T(8,128)(2,1)S(1)}, u32[]{:S(2)}, u32[]{:S(2)}) collective-permute-start(bf16[16,1920]{1,0:T(8,128)(2,1)S(1)} %get-tuple-element.46), channel_id=1, source_target_pairs={{0,12},{4,8},{8,4},{12,0},{1,13},{5,9},{9,5},{13,1},{2,14},{6,10},... | collective-permute-start | bytes 184328 | tf_op jit(solution)/shard_map/ppermute | solution.py:24
  26.1 6.4 %collective-permute-start.10 = (bf16[16,1920]{1,0:T(8,128)(2,1)S(1)}, bf16[16,1920]{1,0:T(8,128)(2,1)S(1)}, u32[]{:S(2)}, u32[]{:S(2)}) collective-permute-start(bf16[16,1920]{1,0:T(8,128)(2,1)S(1)} %get-tuple-element.46), channel_id=1, source_target_pairs={{0,4},{4,0},{8,12},{12,8},{1,5},{5,1},{9,13},{13,9},{2,6},{6,2},{1... | collective-permute-start | bytes 184328 | tf_op jit(solution)/shard_map/ppermute | solution.py:24
  32.7 4.2 %collective-permute-start.15 = (bf16[8,1792]{1,0:T(8,128)(2,1)S(1)}, bf16[8,1792]{1,0:T(8,128)(2,1)S(1)}, u32[]{:S(2)}, u32[]{:S(2)}) collective-permute-start(bf16[8,1792]{1,0:T(8,128)(2,1)S(1)} %activation.1.own), channel_id=1, source_target_pairs={{0,4},{4,0},{8,12},{12,8},{1,5},{5,1},{9,13},{13,9},{2,6},{6,2},{1... | collective-permute-start | bytes 86024 | tf_op jit(solution)/shard_map/ppermute | solution.py:24
  33.3 4.8 %collective-permute-start.14 = (bf16[8,1792]{1,0:T(8,128)(2,1)S(1)}, bf16[8,1792]{1,0:T(8,128)(2,1)S(1)}, u32[]{:S(2)}, u32[]{:S(2)}) collective-permute-start(bf16[8,1792]{1,0:T(8,128)(2,1)S(1)} %activation.1.own), channel_id=1, source_target_pairs={{0,20},{4,16},{8,28},{12,24},{16,4},{20,0},{24,12},{28,8},{1,21},{... | collective-permute-start | bytes 86024 | tf_op jit(solution)/shard_map/ppermute | solution.py:24
  35.7 3.9 %collective-permute-start.13 = (bf16[8,1792]{1,0:T(8,128)(2,1)S(1)}, bf16[8,1792]{1,0:T(8,128)(2,1)S(1)}, u32[]{:S(2)}, u32[]{:S(2)}) collective-permute-start(bf16[8,1792]{1,0:T(8,128)(2,1)S(1)} %activation.1.own), channel_id=1, source_target_pairs={{0,16},{16,0},{1,17},{17,1},{2,18},{18,2},{3,19},{19,3},{4,20},{20... | collective-permute-start | bytes 86024 | tf_op jit(solution)/shard_map/ppermute | solution.py:24
  40.7 3.8 %collective-permute-start.18 = (bf16[16,2048]{1,0:T(8,128)(2,1)S(1)}, bf16[16,2048]{1,0:T(8,128)(2,1)S(1)}, u32[]{:S(2)}, u32[]{:S(2)}) collective-permute-start(bf16[16,2048]{1,0:T(8,128)(2,1)S(1)} %down.3.refs_0_), channel_id=1, source_target_pairs={{0,3},{1,2},{2,1},{3,0},{4,7},{5,6},{6,5},{7,4},{8,11},{9,10},{10,... | collective-permute-start | bytes 196616 | tf_op jit(solution)/shard_map/ppermute | solution.py:24
  40.7 5.0 %collective-permute-start.17 = (bf16[16,2048]{1,0:T(8,128)(2,1)S(1)}, bf16[16,2048]{1,0:T(8,128)(2,1)S(1)}, u32[]{:S(2)}, u32[]{:S(2)}) collective-permute-start(bf16[16,2048]{1,0:T(8,128)(2,1)S(1)} %down.3.refs_0_), channel_id=1, source_target_pairs={{0,2},{1,3},{2,0},{3,1},{4,6},{5,7},{6,4},{7,5},{8,10},{9,11},{10,... | collective-permute-start | bytes 196616 | tf_op jit(solution)/shard_map/ppermute | solution.py:24
  41.4 4.3 %collective-permute-start.16 = (bf16[16,2048]{1,0:T(8,128)(2,1)S(1)}, bf16[16,2048]{1,0:T(8,128)(2,1)S(1)}, u32[]{:S(2)}, u32[]{:S(2)}) collective-permute-start(bf16[16,2048]{1,0:T(8,128)(2,1)S(1)} %down.3.refs_0_), channel_id=1, source_target_pairs={{0,1},{1,0},{2,3},{3,2},{4,5},{5,4},{6,7},{7,6},{8,9},{9,8},{10,11... | collective-permute-start | bytes 196616 | tf_op jit(solution)/shard_map/ppermute | solution.py:24

commit v13 on v12

--- a/solution.py
+++ b/solution.py
@@ -40,6 +40,12 @@
 
 def dot_t(a, b):
     return lax.dot_general(a, b, (((1,), (1,)), ((), ())), preferred_element_type=jnp.float32)
+
+
+def pieces(value):
+    first = value.astype(WIRE).astype(jnp.float32)
+    second = (value - first).astype(WIRE).astype(jnp.float32)
+    return first, second, value - first - second
 
 
 def call(kernel, out_shape, in_specs, scratch=(), limit=4, name=None, flops=None):
@@ -70,21 +76,30 @@
     half = cols // 2
     sources, (lengths, *outs), kept = refs[:5], refs[5 : 6 + half], refs[6 + half : 12 + half]
     sized, packed, sems = refs[12 + half :]
-    copies = [
-        pltpu.make_async_copy(source, target, sems.at[i])
-        for i, (source, target) in enumerate(zip(sources, kept))
-    ]
-    copies.append(pltpu.make_async_copy(lengths, sized, sems.at[5]))
-    for copy in copies:
+    keys, values, small = [], [], [pltpu.make_async_copy(lengths, sized, sems.at[0])]
+    for i, (source, target) in enumerate(zip(sources, kept)):
+        if i < 3:
+            small.append(pltpu.make_async_copy(source, target, sems.at[i + 1]))
+            continue
+        for b in range(source.shape[0]):
+            sem = sems.at[4 + (i - 3) * source.shape[0] + b]
+            copy = pltpu.make_async_copy(source.at[b], target.at[b], sem)
+            (keys, values)[i - 3].append(copy)
+    for copy in small[:2] + keys + small[2:] + values:
         copy.start()
-    for i in (0, 1, 2, 5, 3):
-        copies[i].wait()
+    for copy in small + keys:
+        copy.wait()
+
+    def values_there():
+        for copy in values:
+            copy.wait()
+
     row = lax.broadcasted_iota(jnp.int32, (8, HD), 0)
     limits = jnp.zeros((8, HD), jnp.int32)
     for b in range(kept[3].shape[0]):
         limits = jnp.where(row == b, sized[b], limits)
     kept[5][...] = limits
-    attention(cols, 1, limits, *kept[:5], outs, packed, copies[4].wait)
+    attention(cols, 1, limits, *kept[:5], outs, packed, values_there)
 
 
 def attention_near_kernel(cols, *refs):
@@ -161,15 +176,18 @@
         for t in range(TOKENS):
             tb = t * rows + b
             part = slice(i * n + t * GROUP, i * n + (t + 1) * GROUP)
-            stats[g] = jnp.where(lane == 2 * tb, peak[part], stats[g])
-            stats[g] = jnp.where(lane == 2 * tb + 1, total[part], stats[g])
-            block = s[t * GROUP : (t + 1) * GROUP]
+            for k, pair in enumerate(zip(pieces(peak[part]), pieces(total[part]))):
+                at = 2 * (TOKENS * rows * k + tb)
+                stats[g] = jnp.where(lane == at, pair[0], stats[g])
+                stats[g] = jnp.where(lane == at + 1, pair[1], stats[g])
+            block = s[t * GROUP : (t + 1) * GROUP].astype(WIRE)
             if hb >= GROUP:
                 at = g * GROUP
                 packed[at // hb, tb, at % hb : at % hb + GROUP] = block
             else:
                 for j in range(GROUP // hb):
                     packed[g * (GROUP // hb) + j, tb] = block[j * hb : (j + 1) * hb]
+    stats = [block.astype(WIRE) for block in stats]
     for g in range(heads):
         if hb >= GROUP:
             at = g * GROUP
@@ -185,7 +203,9 @@
     parts, out = refs[:cols], refs[cols]
     cells = parts[0].shape[0] - 1
     hb = parts[0].shape[1]
-    stats = [p[cells] for p in parts]
+    n = 2 * cells
+    stats = [p[cells].astype(jnp.float32) for p in parts]
+    stats = [s[:, :n] + s[:, n : 2 * n] + s[:, 2 * n : 3 * n] for s in stats]
     attended = []
     for tb in range(cells):
         peaks = [s[:, 2 * tb : 2 * tb + 1] for s in stats]
@@ -193,7 +213,7 @@
         top = functools.reduce(jnp.maximum, peaks)
         scales = [jnp.exp(p - top) for p in peaks]
         total = tree_sum([t * s for t, s in zip(totals, scales)])
-        summed = tree_sum([p[tb] * s for p, s in zip(parts, scales)])
+        summed = tree_sum([p[tb].astype(jnp.float32) * s for p, s in zip(parts, scales)])
         attended.append(summed / total)
     rows = [
         jnp.concatenate([attended[tb][h : h + 1] for tb in range(cells)], axis=0) for h in range(hb)
@@ -248,13 +268,11 @@
 
 
 def in_pieces(squares):
-    first = squares.astype(WIRE).astype(jnp.float32)
-    second = (squares - first).astype(WIRE).astype(jnp.float32)
-    third = squares - first - second
     lane = lax.broadcasted_iota(jnp.int32, (squares.shape[0], HD), 1)
-    return jnp.where(
-        lane == 0, first, jnp.where(lane == 1, second, jnp.where(lane == 2, third, 0.0))
-    )
+    result = jnp.zeros(lane.shape, jnp.float32)
+    for i, piece in enumerate(pieces(squares)):
+        result = jnp.where(lane == i, piece, result)
+    return result
 
 
 def lanes_of(bit, half):
@@ -387,16 +405,20 @@
     pad = -(-cells // 8) * 8
 
     sources = [query, new_keys, new_values, key_cache, value_cache]
-    message = shape((cells + 1, hb, HD), f32)
+    message = shape((cells + 1, hb, HD), WIRE)
     sources = [query, new_keys, new_values, key_cache, value_cache]
 
     inputs = [pltpu.VMEM(a.shape, a.dtype) for a in sources]
-    packed = pltpu.VMEM((cols // 2, *message.shape), f32)
+    packed = pltpu.VMEM((cols // 2, *message.shape), WIRE)
     result = call(
         functools.partial(attention_far_kernel, cols),
         [message] * (cols // 2) + inputs + [pltpu.VMEM((8, HD), jnp.int32)],
         [ANY_SPEC] * 6,
-        [pltpu.SMEM(lengths.shape, lengths.dtype), packed, pltpu.SemaphoreType.DMA((6,))],
+        [
+            pltpu.SMEM(lengths.shape, lengths.dtype),
+            packed,
+            pltpu.SemaphoreType.DMA((4 + 2 * rows_here,)),
+        ],
         name="attention_far",
     )(*[in_hbm(a) for a in [*sources, lengths]])
     far, inputs = result[: cols // 2], result[cols // 2 :]

time: 46.5 us -> 46.3 us (level)
  no operation moved by 1% of the time
where the time goes in v13:
time: 46.3 us; the launch traced here: 46.2 us
  waiting for transfers between devices  18.7 us (40%)
  starting transfers between devices  18.6 us (40%)
  Pallas kernels  8.49 us (18%)
    ppermute x19, waiting for transfers between devices, partner(): lax.ppermute(value, axis, [(i, i ^ k) for i in range(lax.axis_size(axis))])  18.7 us
    ppermute x19, starting transfers between devices, partner(): lax.ppermute(value, axis, [(i, i ^ k) for i in range(lax.axis_size(axis))])  18.6 us
    pallas_call x2, Pallas kernels, down_part(): call(functools.partial(down_kernel, other), shape((m, width_share), resul...  2.13 us
    pallas_call x1, Pallas kernels, shards(): call(functools.partial(attention_far_kernel, cols), [message] * (cols //...  1.85 us
    pallas_call x1, Pallas kernels, shards(): call(lift_second_kernel, [shape((m, width_share), f32)] + [shape((m, hidd...  1.08 us
    pallas_call x1, Pallas kernels, shards(): call(lift_first_kernel, [shape((m, hidden), f32)] * 2, [VMEM_SPEC] * 3, n...  1.07 us
  transfers between devices with their start and end apart: 19, of which 14 were waited for; matrix products, arithmetic and copies ran while one was open for 0% of the time, Pallas kernels for 6%

profile of v13, /device:TPU:0, one launch (start us, length us, event | category | flops | bytes accessed | tf_op | source)
XLA Modules:
  0.0 46.2 jit_solution(12696665557401215944)
XLA Ops:
  0.0 1.9 %attention_far.1 = (bf16[5,8,128]{2,1,0:T(8,128)(2,1)S(1)}, bf16[5,8,128]{2,1,0:T(8,128)(2,1)S(1)}, bf16[2,2,4096]{2,1,0:T(2,128)(2,1)S(1)}, bf16[2,2,512]{2,1,0...) custom-call(bf16[2,2,4096]{2,1,0:T(2,128)(2,1)} %refs_0_.1, ...), custom_call_target="tpu_custom_call" | custom-call | tf_op jit(solution)/shard_map/attention_far/pallas_call | solution.py:413
  1.9 3.0 %collective-permute-start = (bf16[5,8,128]{2,1,0:T(8,128)(2,1)S(1)}, bf16[5,8,128]{2,1,0:T(8,128)(2,1)S(1)}, u32[]{:S(2)}, u32[]{:S(2)}) collective-permute-start(bf16[5,8,128]{2,1,0:T(8,128)(2,1)S(1)} %get-tuple-element.26), channel_id=1, source_target_pairs={{0,2},{1,3},{2,0},{3,1},{4,6},{5,7},{6,4},{7,5},{8,10},{9,11},{10,... | collective-permute-start | bytes 30728 | tf_op jit(solution)/shard_map/ppermute | solution.py:24
  4.9 0.0 collective-permute-start.1
  4.9 0.5 %attention_near.1 = (bf16[5,8,128]{2,1,0:T(8,128)(2,1)S(1)}, bf16[5,8,128]{2,1,0:T(8,128)(2,1)S(1)}) custom-call(bf16[2,2,4096]{2,1,0:T(2,128)(2,1)S(1)} %get-tuple-element.28.refs_0_, bf16[2,2,512]{2,1,0:T(2,128)(2,1)S(1)} %get-tuple-element.29.refs_1_, bf16[2,2,512]{2,1,0:T(2,128)(2,1)S(1)} %get-tuple-element.30.refs_2_, ...), custom_call_target="tpu_custom_call" | custom-call | tf_op jit(solution)/shard_map/attention_near/pallas_call | solution.py:426
  5.4 0.2 collective-permute-start.2
  5.6 0.9 %collective-permute-done.refs_0_ = bf16[5,8,128]{2,1,0:T(8,128)(2,1)S(1)} collective-permute-done((bf16[5,8,128]{2,1,0:T(8,128)(2,1)S(1)}, bf16[5,8,128]{2,1,0:T(8,128)(2,1)S(1)}, u32[]{:S(2)}, u32[]{:S(2)}) %collective-permute-start) | collective-permute-done | bytes 10272 | tf_op jit(solution)/shard_map/ppermute | solution.py:24
  6.5 1.4 %collective-permute-done.1.refs_1_ = bf16[5,8,128]{2,1,0:T(8,128)(2,1)S(1)} collective-permute-done((bf16[5,8,128]{2,1,0:T(8,128)(2,1)S(1)}, bf16[5,8,128]{2,1,0:T(8,128)(2,1)S(1)}, u32[]{:S(2)}, u32[]{:S(2)}) %collective-permute-start.1) | collective-permute-done | bytes 10272 | tf_op jit(solution)/shard_map/ppermute | solution.py:24
  8.0 0.0 slice-start.5
  8.0 0.0 slice-start.7
  8.0 0.0 slice-start.9
  8.1 0.2 combine.1.refs_0_
  8.3 3.7 %collective-permute-start.5 = (bf16[4,1024]{1,0:T(4,128)(2,1)S(1)}, bf16[4,1024]{1,0:T(4,128)(2,1)S(1)}, u32[]{:S(2)}, u32[]{:S(2)}) collective-permute-start(bf16[4,1024]{1,0:T(4,128)(2,1)S(1)} %combine.1.refs_0_), channel_id=1, source_target_pairs={{0,12},{4,8},{8,4},{12,0},{1,13},{5,9},{9,5},{13,1},{2,14},{6,10},... | collective-permute-start | bytes 24584 | tf_op jit(solution)/shard_map/ppermute | solution.py:24
  12.0 0.8 %collective-permute-start.3 = (bf16[4,1024]{1,0:T(4,128)(2,1)S(1)}, bf16[4,1024]{1,0:T(4,128)(2,1)S(1)}, u32[]{:S(2)}, u32[]{:S(2)}) collective-permute-start(bf16[4,1024]{1,0:T(4,128)(2,1)S(1)} %combine.1.refs_0_), channel_id=1, source_target_pairs={{0,4},{4,0},{8,12},{12,8},{1,5},{5,1},{9,13},{13,9},{2,6},{6,2},{1... | collective-permute-start | bytes 24584 | tf_op jit(solution)/shard_map/ppermute | solution.py:24
  12.8 1.1 %collective-permute-done.5.refs_3_ = bf16[4,1024]{1,0:T(4,128)(2,1)S(1)} collective-permute-done((bf16[4,1024]{1,0:T(4,128)(2,1)S(1)}, bf16[4,1024]{1,0:T(4,128)(2,1)S(1)}, u32[]{:S(2)}, u32[]{:S(2)}) %collective-permute-start.5) | collective-permute-done | bytes 8224 | tf_op jit(solution)/shard_map/ppermute | solution.py:24
  13.9 2.6 %collective-permute-done.4.refs_2_ = bf16[4,1024]{1,0:T(4,128)(2,1)S(1)} collective-permute-done((bf16[4,1024]{1,0:T(4,128)(2,1)S(1)}, bf16[4,1024]{1,0:T(4,128)(2,1)S(1)}, u32[]{:S(2)}, u32[]{:S(2)}) %collective-permute-start.4) | collective-permute-done | bytes 8224 | tf_op jit(solution)/shard_map/ppermute | solution.py:24
  16.5 0.7 %out_projection.1 = (bf16[16,1024]{1,0:T(8,128)(2,1)S(1)}, bf16[16,1024]{1,0:T(8,128)(2,1)S(1)}, bf16[16,1024]{1,0:T(8,128)(2,1)S(1)}, bf16[16,1024]{1,0:T(8,128)(2,1)S(1)}) custom-call(bf16[4,1024]{1,0:T(4,128)(2,1)S(1)} %combine.1.refs_0_, bf16[4,1024]{1,0:T(4,128)(2,1)S(1)} %collective-permute-done.3.refs_1_, ...), custom_call_target="tpu_custom_call" | custom-call | tf_op jit(solution)/shard_map/out_projection/pallas_call | solution.py:443
  17.2 0.1 collective-permute-start.6
  17.3 0.7 %collective-permute-start.7 = (bf16[16,1024]{1,0:T(8,128)(2,1)S(1)}, bf16[16,1024]{1,0:T(8,128)(2,1)S(1)}, u32[]{:S(2)}, u32[]{:S(2)}) collective-permute-start(bf16[16,1024]{1,0:T(8,128)(2,1)S(1)} %get-tuple-element.38), channel_id=1, source_target_pairs={{0,2},{1,3},{2,0},{3,1},{4,6},{5,7},{6,4},{7,5},{8,10},{9,11},{10,... | collective-permute-start | bytes 98312 | tf_op jit(solution)/shard_map/ppermute | solution.py:24
  18.0 1.1 %collective-permute-start.8 = (bf16[16,1024]{1,0:T(8,128)(2,1)S(1)}, bf16[16,1024]{1,0:T(8,128)(2,1)S(1)}, u32[]{:S(2)}, u32[]{:S(2)}) collective-permute-start(bf16[16,1024]{1,0:T(8,128)(2,1)S(1)} %get-tuple-element.39), channel_id=1, source_target_pairs={{0,1},{1,0},{2,3},{3,2},{4,5},{5,4},{6,7},{7,6},{8,9},{9,8},{10,11... | collective-permute-start | bytes 98312 | tf_op jit(solution)/shard_map/ppermute | solution.py:24
  19.1 1.5 %collective-permute-done.6.refs_1_ = bf16[16,1024]{1,0:T(8,128)(2,1)S(1)} collective-permute-done((bf16[16,1024]{1,0:T(8,128)(2,1)S(1)}, bf16[16,1024]{1,0:T(8,128)(2,1)S(1)}, u32[]{:S(2)}, u32[]{:S(2)}) %collective-permute-start.6) | collective-permute-done | bytes 32800 | tf_op jit(solution)/shard_map/ppermute | solution.py:24
  20.6 0.7 %collective-permute-done.7.refs_2_ = bf16[16,1024]{1,0:T(8,128)(2,1)S(1)} collective-permute-done((bf16[16,1024]{1,0:T(8,128)(2,1)S(1)}, bf16[16,1024]{1,0:T(8,128)(2,1)S(1)}, u32[]{:S(2)}, u32[]{:S(2)}) %collective-permute-start.7) | collective-permute-done | bytes 32800 | tf_op jit(solution)/shard_map/ppermute | solution.py:24
  21.4 0.1 collective-permute-start.9
  21.6 0.0 slice-start
  21.6 1.1 %gate_up_first.1 = (f32[16,1792]{1,0:T(8,128)S(1)}, f32[16,1792]{1,0:T(8,128)S(1)}) custom-call(bf16[16,1024]{1,0:T(8,128)(2,1)S(1)} %get-tuple-element.41.lifted, bf16[2048,3584]{1,0:T(8,128)(2,1)S(1)} %bitcast.3, bf16[2048,3584]{1,0:T(8,128)(2,1)S(1)} %bitcast.5), custom_call_target="tpu_custom_call" | custom-call | tf_op jit(solution)/shard_map/gate_up_first/pallas_call | solution.py:464
  22.7 0.1 collective-permute-done.9.received
  22.7 1.1 %gate_up_second.1 = (f32[16,2048]{1,0:T(8,128)S(1)}, bf16[16,1920]{1,0:T(8,128)(2,1)S(1)}, bf16[16,1920]{1,0:T(8,128)(2,1)S(1)}) custom-call(f32[16,1024]{1,0:T(8,128)S(1)} %get-tuple-element.40.own, f32[16,1024]{1,0:T(8,128)S(1)} %collective-permute-done.9.received, bf16[2048]{0:T(1024)(128)(2,1)S(1)} %copy-done.2, bf16[2048,3584]{1,0:T(8,128)(2,1)S(1)} %bitcast.3, ...), custom_call_target="tpu_custom_call" | custom-call | flops 40000000000 | bytes 1024 | tf_op jit(solution)/shard_map/gate_up_second/pallas_call | solution.py:470
  23.8 2.0 %collective-permute-start.11 = (bf16[16,1920]{1,0:T(8,128)(2,1)S(1)}, bf16[16,1920]{1,0:T(8,128)(2,1)S(1)}, u32[]{:S(2)}, u32[]{:S(2)}) collective-permute-start(bf16[16,1920]{1,0:T(8,128)(2,1)S(1)} %get-tuple-element.45.refs_0_), channel_id=1, source_target_pairs={{0,8},{4,12},{8,0},{12,4},{1,9},{5,13},{9,1},{13,5},{2,10},{6,14},... | collective-permute-start | bytes 184328 | tf_op jit(solution)/shard_map/ppermute | solution.py:24
  25.9 0.2 collective-permute-start.12
  26.1 1.3 %collective-permute-start.10 = (bf16[16,1920]{1,0:T(8,128)(2,1)S(1)}, bf16[16,1920]{1,0:T(8,128)(2,1)S(1)}, u32[]{:S(2)}, u32[]{:S(2)}) collective-permute-start(bf16[16,1920]{1,0:T(8,128)(2,1)S(1)} %get-tuple-element.46), channel_id=1, source_target_pairs={{0,4},{4,0},{8,12},{12,8},{1,5},{5,1},{9,13},{13,9},{2,6},{6,2},{1... | collective-permute-start | bytes 184328 | tf_op jit(solution)/shard_map/ppermute | solution.py:24
  27.3 2.5 %collective-permute-done.11.refs_2_ = bf16[16,1920]{1,0:T(8,128)(2,1)S(1)} collective-permute-done((bf16[16,1920]{1,0:T(8,128)(2,1)S(1)}, bf16[16,1920]{1,0:T(8,128)(2,1)S(1)}, u32[]{:S(2)}, u32[]{:S(2)}) %collective-permute-start.11) | collective-permute-done | bytes 61472 | tf_op jit(solution)/shard_map/ppermute | solution.py:24
  29.8 2.6 %collective-permute-done.12.refs_3_ = bf16[16,1920]{1,0:T(8,128)(2,1)S(1)} collective-permute-done((bf16[16,1920]{1,0:T(8,128)(2,1)S(1)}, bf16[16,1920]{1,0:T(8,128)(2,1)S(1)}, u32[]{:S(2)}, u32[]{:S(2)}) %collective-permute-start.12) | collective-permute-done | bytes 61472 | tf_op jit(solution)/shard_map/ppermute | solution.py:24
  32.4 0.0 collective-permute-done.10.refs_1_
  32.4 0.1 activation.1.own
  32.5 0.6 %collective-permute-start.15 = (bf16[8,1792]{1,0:T(8,128)(2,1)S(1)}, bf16[8,1792]{1,0:T(8,128)(2,1)S(1)}, u32[]{:S(2)}, u32[]{:S(2)}) collective-permute-start(bf16[8,1792]{1,0:T(8,128)(2,1)S(1)} %activation.1.own), channel_id=1, source_target_pairs={{0,4},{4,0},{8,12},{12,8},{1,5},{5,1},{9,13},{13,9},{2,6},{6,2},{1... | collective-permute-start | bytes 86024 | tf_op jit(solution)/shard_map/ppermute | solution.py:24
  33.1 2.5 %collective-permute-start.14 = (bf16[8,1792]{1,0:T(8,128)(2,1)S(1)}, bf16[8,1792]{1,0:T(8,128)(2,1)S(1)}, u32[]{:S(2)}, u32[]{:S(2)}) collective-permute-start(bf16[8,1792]{1,0:T(8,128)(2,1)S(1)} %activation.1.own), channel_id=1, source_target_pairs={{0,20},{4,16},{8,28},{12,24},{16,4},{20,0},{24,12},{28,8},{1,21},{... | collective-permute-start | bytes 86024 | tf_op jit(solution)/shard_map/ppermute | solution.py:24
  35.6 0.5 %collective-permute-start.13 = (bf16[8,1792]{1,0:T(8,128)(2,1)S(1)}, bf16[8,1792]{1,0:T(8,128)(2,1)S(1)}, u32[]{:S(2)}, u32[]{:S(2)}) collective-permute-start(bf16[8,1792]{1,0:T(8,128)(2,1)S(1)} %activation.1.own), channel_id=1, source_target_pairs={{0,16},{16,0},{1,17},{17,1},{2,18},{18,2},{3,19},{19,3},{4,20},{20... | collective-permute-start | bytes 86024 | tf_op jit(solution)/shard_map/ppermute | solution.py:24
  36.1 0.6 %collective-permute-done.15.received = bf16[8,1792]{1,0:T(8,128)(2,1)S(1)} collective-permute-done((bf16[8,1792]{1,0:T(8,128)(2,1)S(1)}, bf16[8,1792]{1,0:T(8,128)(2,1)S(1)}, u32[]{:S(2)}, u32[]{:S(2)}) %collective-permute-start.15) | collective-permute-done | bytes 28704 | tf_op jit(solution)/shard_map/ppermute | solution.py:24
  36.8 1.1 %down.2.refs_0_ = f32[16,2048]{1,0:T(8,128)S(1)} custom-call(bf16[16,1792]{1,0:T(8,128)(2,1)S(1)} %gather_act.3.act, bf16[3584,2048]{1,0:T(8,128)(2,1)S(1)} %bitcast.1), custom_call_target="tpu_custom_call" | custom-call | tf_op jit(solution)/shard_map/down/pallas_call | solution.py:495
  37.8 0.1 collective-permute-done.14.received
  38.0 1.5 %collective-permute-done.13.own = bf16[8,1792]{1,0:T(8,128)(2,1)S(1)} collective-permute-done((bf16[8,1792]{1,0:T(8,128)(2,1)S(1)}, bf16[8,1792]{1,0:T(8,128)(2,1)S(1)}, u32[]{:S(2)}, u32[]{:S(2)}) %collective-permute-start.13) | collective-permute-done | bytes 28704 | tf_op jit(solution)/shard_map/ppermute | solution.py:24
  39.5 1.1 %down.3.refs_0_ = bf16[16,2048]{1,0:T(8,128)(2,1)S(1)} custom-call(bf16[16,1792]{1,0:T(8,128)(2,1)S(1)} %gather_act.2.act, bf16[3584,2048]{1,0:T(8,128)(2,1)S(1)} %bitcast.1, f32[16,2048]{1,0:T(8,128)S(1)} %down.2.refs_0_), custom_call_target="tpu_custom_call" | custom-call | tf_op jit(solution)/shard_map/down/pallas_call | solution.py:495
  40.5 0.0 collective-permute-start.18
  40.5 0.6 %collective-permute-start.17 = (bf16[16,2048]{1,0:T(8,128)(2,1)S(1)}, bf16[16,2048]{1,0:T(8,128)(2,1)S(1)}, u32[]{:S(2)}, u32[]{:S(2)}) collective-permute-start(bf16[16,2048]{1,0:T(8,128)(2,1)S(1)} %down.3.refs_0_), channel_id=1, source_target_pairs={{0,2},{1,3},{2,0},{3,1},{4,6},{5,7},{6,4},{7,5},{8,10},{9,11},{10,... | collective-permute-start | bytes 196616 | tf_op jit(solution)/shard_map/ppermute | solution.py:24
  41.2 1.2 %collective-permute-start.16 = (bf16[16,2048]{1,0:T(8,128)(2,1)S(1)}, bf16[16,2048]{1,0:T(8,128)(2,1)S(1)}, u32[]{:S(2)}, u32[]{:S(2)}) collective-permute-start(bf16[16,2048]{1,0:T(8,128)(2,1)S(1)} %down.3.refs_0_), channel_id=1, source_target_pairs={{0,1},{1,0},{2,3},{3,2},{4,5},{5,4},{6,7},{7,6},{8,9},{9,8},{10,11... | collective-permute-start | bytes 196616 | tf_op jit(solution)/shard_map/ppermute | solution.py:24
  42.4 2.0 %collective-permute-done.18.refs_3_ = bf16[16,2048]{1,0:T(8,128)(2,1)S(1)} collective-permute-done((bf16[16,2048]{1,0:T(8,128)(2,1)S(1)}, bf16[16,2048]{1,0:T(8,128)(2,1)S(1)}, u32[]{:S(2)}, u32[]{:S(2)}) %collective-permute-start.18) | collective-permute-done | bytes 65568 | tf_op jit(solution)/shard_map/ppermute | solution.py:24
  44.4 1.1 %collective-permute-done.17.refs_2_ = bf16[16,2048]{1,0:T(8,128)(2,1)S(1)} collective-permute-done((bf16[16,2048]{1,0:T(8,128)(2,1)S(1)}, bf16[16,2048]{1,0:T(8,128)(2,1)S(1)}, u32[]{:S(2)}, u32[]{:S(2)}) %collective-permute-start.17) | collective-permute-done | bytes 65568 | tf_op jit(solution)/shard_map/ppermute | solution.py:24
  45.5 0.0 collective-permute-done.16.refs_1_
  45.5 0.7 %final.1 = bf16[2,8,2048]{2,1,0:T(8,128)(2,1)} custom-call(f32[16,2048]{1,0:T(8,128)S(1)} %get-tuple-element.44.mid, bf16[16,2048]{1,0:T(8,128)(2,1)S(1)} %down.3.refs_0_, bf16[16,2048]{1,0:T(8,128)(2,1)S(1)} %collective-permute-done.16.refs_1_, bf16[16,2048]{1,0:T(8,128)(2,1)S(1)} %collective-permute-done.17.refs_2_, ...), custom_call_target="tpu_custom_call" | custom-call | tf_op jit(solution)/shard_map/final/pallas_call | solution.py:509
  (36 shorter events, 0.1 us)
Async XLA Ops:
  1.9 4.7 %collective-permute-start = (bf16[5,8,128]{2,1,0:T(8,128)(2,1)S(1)}, bf16[5,8,128]{2,1,0:T(8,128)(2,1)S(1)}, u32[]{:S(2)}, u32[]{:S(2)}) collective-permute-start(bf16[5,8,128]{2,1,0:T(8,128)(2,1)S(1)} %get-tuple-element.26), channel_id=1, source_target_pairs={{0,2},{1,3},{2,0},{3,1},{4,6},{5,7},{6,4},{7,5},{8,10},{9,11},{10,... | collective-permute-start | bytes 30728 | tf_op jit(solution)/shard_map/ppermute | solution.py:24
  4.9 3.1 %collective-permute-start.1 = (bf16[5,8,128]{2,1,0:T(8,128)(2,1)S(1)}, bf16[5,8,128]{2,1,0:T(8,128)(2,1)S(1)}, u32[]{:S(2)}, u32[]{:S(2)}) collective-permute-start(bf16[5,8,128]{2,1,0:T(8,128)(2,1)S(1)} %get-tuple-element.27), channel_id=1, source_target_pairs={{0,3},{1,2},{2,1},{3,0},{4,7},{5,6},{6,5},{7,4},{8,11},{9,10},{10,... | collective-permute-start | bytes 30728 | tf_op jit(solution)/shard_map/ppermute | solution.py:24
  4.9 16.6 %slice-start.4 = ((s8[14680064]{0:T(1024)(128)(4,1)}), s8[4194304]{0:T(1024)(128)(4,1)S(1)}, s32[]{:S(2)}) async-start(s8[14680064]{0:T(1024)(128)(4,1)} %bitcast.2), calls=%async_computation.4 | async-start | bytes 8388608
  4.9 16.6 %slice-start.8 = ((s8[14680064]{0:T(1024)(128)(4,1)}), s8[4194304]{0:T(1024)(128)(4,1)S(1)}, s32[]{:S(2)}) async-start(s8[14680064]{0:T(1024)(128)(4,1)} %bitcast.4), calls=%async_computation.8 | async-start | bytes 8388608
  5.4 2.6 %collective-permute-start.2 = (bf16[5,8,128]{2,1,0:T(8,128)(2,1)S(1)}, bf16[5,8,128]{2,1,0:T(8,128)(2,1)S(1)}, u32[]{:S(2)}, u32[]{:S(2)}) collective-permute-start(bf16[5,8,128]{2,1,0:T(8,128)(2,1)S(1)} %get-tuple-element.35), channel_id=1, source_target_pairs={{0,1},{1,0},{2,3},{3,2},{4,5},{5,4},{6,7},{7,6},{8,9},{9,8},{10,11... | collective-permute-start | bytes 30728 | tf_op jit(solution)/shard_map/ppermute | solution.py:24
  8.0 8.6 %copy-start = (bf16[1024,2048]{1,0:T(8,128)(2,1)S(1)}, bf16[1024,2048]{1,0:T(8,128)(2,1)}, u32[]{:S(2)}) copy-start(bf16[1024,2048]{1,0:T(8,128)(2,1)} %refs_4_.3) | copy-start | bytes 12582916
  8.0 13.4 %copy-start.1 = (bf16[2,8,2048]{2,1,0:T(8,128)(2,1)S(1)}, bf16[2,8,2048]{2,1,0:T(8,128)(2,1)}, u32[]{:S(2)}) copy-start(bf16[2,8,2048]{2,1,0:T(8,128)(2,1)} %residual.1) | copy-start | bytes 196612
  8.0 13.4 %copy-start.2 = (bf16[2048]{0:T(1024)(128)(2,1)S(1)}, bf16[2048]{0:T(1024)(128)(2,1)}, u32[]{:S(2)}) copy-start(bf16[2048]{0:T(1024)(128)(2,1)} %gains.3) | copy-start | bytes 12292
  8.0 13.5 %slice-start.5 = ((s8[14680064]{0:T(1024)(128)(4,1)}), s8[4194304]{0:T(1024)(128)(4,1)S(1)}, s32[]{:S(2)}) async-start(s8[14680064]{0:T(1024)(128)(4,1)} %bitcast.2), calls=%async_computation.5 | async-start | bytes 8388608
  8.0 13.5 %slice-start.6 = ((s8[14680064]{0:T(1024)(128)(4,1)}), s8[4194304]{0:T(1024)(128)(4,1)S(1)}, s32[]{:S(2)}) async-start(s8[14680064]{0:T(1024)(128)(4,1)} %bitcast.2), calls=%async_computation.6 | async-start | bytes 8388608
  8.0 13.5 %slice-start.7 = ((s8[14680064]{0:T(1024)(128)(4,1)}), s8[2097152]{0:T(1024)(128)(4,1)S(1)}, s32[]{:S(2)}) async-start(s8[14680064]{0:T(1024)(128)(4,1)} %bitcast.2), calls=%async_computation.7 | async-start | bytes 4194304
  8.0 13.5 %slice-start.9 = ((s8[14680064]{0:T(1024)(128)(4,1)}), s8[4194304]{0:T(1024)(128)(4,1)S(1)}, s32[]{:S(2)}) async-start(s8[14680064]{0:T(1024)(128)(4,1)} %bitcast.4), calls=%async_computation.9 | async-start | bytes 8388608
  8.0 13.5 %slice-start.10 = ((s8[14680064]{0:T(1024)(128)(4,1)}), s8[4194304]{0:T(1024)(128)(4,1)S(1)}, s32[]{:S(2)}) async-start(s8[14680064]{0:T(1024)(128)(4,1)} %bitcast.4), calls=%async_computation.10 | async-start | bytes 8388608
  8.1 13.5 %slice-start.11 = ((s8[14680064]{0:T(1024)(128)(4,1)}), s8[2097152]{0:T(1024)(128)(4,1)S(1)}, s32[]{:S(2)}) async-start(s8[14680064]{0:T(1024)(128)(4,1)} %bitcast.4), calls=%async_computation.11 | async-start | bytes 4194304
  8.3 5.6 %collective-permute-start.5 = (bf16[4,1024]{1,0:T(4,128)(2,1)S(1)}, bf16[4,1024]{1,0:T(4,128)(2,1)S(1)}, u32[]{:S(2)}, u32[]{:S(2)}) collective-permute-start(bf16[4,1024]{1,0:T(4,128)(2,1)S(1)} %combine.1.refs_0_), channel_id=1, source_target_pairs={{0,12},{4,8},{8,4},{12,0},{1,13},{5,9},{9,5},{13,1},{2,14},{6,10},... | collective-permute-start | bytes 24584 | tf_op jit(solution)/shard_map/ppermute | solution.py:24
  12.0 4.5 %collective-permute-start.4 = (bf16[4,1024]{1,0:T(4,128)(2,1)S(1)}, bf16[4,1024]{1,0:T(4,128)(2,1)S(1)}, u32[]{:S(2)}, u32[]{:S(2)}) collective-permute-start(bf16[4,1024]{1,0:T(4,128)(2,1)S(1)} %combine.1.refs_0_), channel_id=1, source_target_pairs={{0,8},{4,12},{8,0},{12,4},{1,9},{5,13},{9,1},{13,5},{2,10},{6,14},... | collective-permute-start | bytes 24584 | tf_op jit(solution)/shard_map/ppermute | solution.py:24
  12.0 4.5 %collective-permute-start.3 = (bf16[4,1024]{1,0:T(4,128)(2,1)S(1)}, bf16[4,1024]{1,0:T(4,128)(2,1)S(1)}, u32[]{:S(2)}, u32[]{:S(2)}) collective-permute-start(bf16[4,1024]{1,0:T(4,128)(2,1)S(1)} %combine.1.refs_0_), channel_id=1, source_target_pairs={{0,4},{4,0},{8,12},{12,8},{1,5},{5,1},{9,13},{13,9},{2,6},{6,2},{1... | collective-permute-start | bytes 24584 | tf_op jit(solution)/shard_map/ppermute | solution.py:24
  17.2 3.4 %collective-permute-start.6 = (bf16[16,1024]{1,0:T(8,128)(2,1)S(1)}, bf16[16,1024]{1,0:T(8,128)(2,1)S(1)}, u32[]{:S(2)}, u32[]{:S(2)}) collective-permute-start(bf16[16,1024]{1,0:T(8,128)(2,1)S(1)} %get-tuple-element.37), channel_id=1, source_target_pairs={{0,3},{1,2},{2,1},{3,0},{4,7},{5,6},{6,5},{7,4},{8,11},{9,10},{10,... | collective-permute-start | bytes 98312 | tf_op jit(solution)/shard_map/ppermute | solution.py:24
  17.3 4.0 %collective-permute-start.7 = (bf16[16,1024]{1,0:T(8,128)(2,1)S(1)}, bf16[16,1024]{1,0:T(8,128)(2,1)S(1)}, u32[]{:S(2)}, u32[]{:S(2)}) collective-permute-start(bf16[16,1024]{1,0:T(8,128)(2,1)S(1)} %get-tuple-element.38), channel_id=1, source_target_pairs={{0,2},{1,3},{2,0},{3,1},{4,6},{5,7},{6,4},{7,5},{8,10},{9,11},{10,... | collective-permute-start | bytes 98312 | tf_op jit(solution)/shard_map/ppermute | solution.py:24
  18.0 3.3 %collective-permute-start.8 = (bf16[16,1024]{1,0:T(8,128)(2,1)S(1)}, bf16[16,1024]{1,0:T(8,128)(2,1)S(1)}, u32[]{:S(2)}, u32[]{:S(2)}) collective-permute-start(bf16[16,1024]{1,0:T(8,128)(2,1)S(1)} %get-tuple-element.39), channel_id=1, source_target_pairs={{0,1},{1,0},{2,3},{3,2},{4,5},{5,4},{6,7},{7,6},{8,9},{9,8},{10,11... | collective-permute-start | bytes 98312 | tf_op jit(solution)/shard_map/ppermute | solution.py:24
  21.4 1.3 %collective-permute-start.9 = (f32[16,1024]{1,0:T(8,128)S(1)}, f32[16,1024]{1,0:T(8,128)S(1)}, u32[]{:S(2)}, u32[]{:S(2)}) collective-permute-start(f32[16,1024]{1,0:T(8,128)S(1)} %get-tuple-element.40.own), channel_id=1, source_target_pairs={{0,1},{1,0},{2,3},{3,2},{4,5},{5,4},{6,7},{7,6},{8,9},{9,8},{10,11... | collective-permute-start | bytes 196616 | tf_op jit(solution)/shard_map/ppermute | solution.py:24
  21.6 15.1 %slice-start = ((s8[14680064]{0:T(1024)(128)(4,1)}), s8[4194304]{0:T(1024)(128)(4,1)S(1)}, s32[]{:S(2)}) async-start(s8[14680064]{0:T(1024)(128)(4,1)} %bitcast), calls=%async_computation | async-start | bytes 8388608
  22.7 14.0 %slice-start.1 = ((s8[14680064]{0:T(1024)(128)(4,1)}), s8[4194304]{0:T(1024)(128)(4,1)S(1)}, s32[]{:S(2)}) async-start(s8[14680064]{0:T(1024)(128)(4,1)} %bitcast), calls=%async_computation.1 | async-start | bytes 8388608
  22.7 14.0 %slice-start.2 = ((s8[14680064]{0:T(1024)(128)(4,1)}), s8[4194304]{0:T(1024)(128)(4,1)S(1)}, s32[]{:S(2)}) async-start(s8[14680064]{0:T(1024)(128)(4,1)} %bitcast), calls=%async_computation.2 | async-start | bytes 8388608
  22.7 14.0 %slice-start.3 = ((s8[14680064]{0:T(1024)(128)(4,1)}), s8[2097152]{0:T(1024)(128)(4,1)S(1)}, s32[]{:S(2)}) async-start(s8[14680064]{0:T(1024)(128)(4,1)} %bitcast), calls=%async_computation.3 | async-start | bytes 4194304
  23.8 6.0 %collective-permute-start.11 = (bf16[16,1920]{1,0:T(8,128)(2,1)S(1)}, bf16[16,1920]{1,0:T(8,128)(2,1)S(1)}, u32[]{:S(2)}, u32[]{:S(2)}) collective-permute-start(bf16[16,1920]{1,0:T(8,128)(2,1)S(1)} %get-tuple-element.45.refs_0_), channel_id=1, source_target_pairs={{0,8},{4,12},{8,0},{12,4},{1,9},{5,13},{9,1},{13,5},{2,10},{6,14},... | collective-permute-start | bytes 184328 | tf_op jit(solution)/shard_map/ppermute | solution.py:24
  25.9 6.5 %collective-permute-start.12 = (bf16[16,1920]{1,0:T(8,128)(2,1)S(1)}, bf16[16,1920]{1,0:T(8,128)(2,1)S(1)}, u32[]{:S(2)}, u32[]{:S(2)}) collective-permute-start(bf16[16,1920]{1,0:T(8,128)(2,1)S(1)} %get-tuple-element.46), channel_id=1, source_target_pairs={{0,12},{4,8},{8,4},{12,0},{1,13},{5,9},{9,5},{13,1},{2,14},{6,10},... | collective-permute-start | bytes 184328 | tf_op jit(solution)/shard_map/ppermute | solution.py:24
  26.1 6.3 %collective-permute-start.10 = (bf16[16,1920]{1,0:T(8,128)(2,1)S(1)}, bf16[16,1920]{1,0:T(8,128)(2,1)S(1)}, u32[]{:S(2)}, u32[]{:S(2)}) collective-permute-start(bf16[16,1920]{1,0:T(8,128)(2,1)S(1)} %get-tuple-element.46), channel_id=1, source_target_pairs={{0,4},{4,0},{8,12},{12,8},{1,5},{5,1},{9,13},{13,9},{2,6},{6,2},{1... | collective-permute-start | bytes 184328 | tf_op jit(solution)/shard_map/ppermute | solution.py:24
  32.5 4.2 %collective-permute-start.15 = (bf16[8,1792]{1,0:T(8,128)(2,1)S(1)}, bf16[8,1792]{1,0:T(8,128)(2,1)S(1)}, u32[]{:S(2)}, u32[]{:S(2)}) collective-permute-start(bf16[8,1792]{1,0:T(8,128)(2,1)S(1)} %activation.1.own), channel_id=1, source_target_pairs={{0,4},{4,0},{8,12},{12,8},{1,5},{5,1},{9,13},{13,9},{2,6},{6,2},{1... | collective-permute-start | bytes 86024 | tf_op jit(solution)/shard_map/ppermute | solution.py:24
  33.1 4.8 %collective-permute-start.14 = (bf16[8,1792]{1,0:T(8,128)(2,1)S(1)}, bf16[8,1792]{1,0:T(8,128)(2,1)S(1)}, u32[]{:S(2)}, u32[]{:S(2)}) collective-permute-start(bf16[8,1792]{1,0:T(8,128)(2,1)S(1)} %activation.1.own), channel_id=1, source_target_pairs={{0,20},{4,16},{8,28},{12,24},{16,4},{20,0},{24,12},{28,8},{1,21},{... | collective-permute-start | bytes 86024 | tf_op jit(solution)/shard_map/ppermute | solution.py:24
  35.6 3.9 %collective-permute-start.13 = (bf16[8,1792]{1,0:T(8,128)(2,1)S(1)}, bf16[8,1792]{1,0:T(8,128)(2,1)S(1)}, u32[]{:S(2)}, u32[]{:S(2)}) collective-permute-start(bf16[8,1792]{1,0:T(8,128)(2,1)S(1)} %activation.1.own), channel_id=1, source_target_pairs={{0,16},{16,0},{1,17},{17,1},{2,18},{18,2},{3,19},{19,3},{4,20},{20... | collective-permute-start | bytes 86024 | tf_op jit(solution)/shard_map/ppermute | solution.py:24
  40.5 3.8 %collective-permute-start.18 = (bf16[16,2048]{1,0:T(8,128)(2,1)S(1)}, bf16[16,2048]{1,0:T(8,128)(2,1)S(1)}, u32[]{:S(2)}, u32[]{:S(2)}) collective-permute-start(bf16[16,2048]{1,0:T(8,128)(2,1)S(1)} %down.3.refs_0_), channel_id=1, source_target_pairs={{0,3},{1,2},{2,1},{3,0},{4,7},{5,6},{6,5},{7,4},{8,11},{9,10},{10,... | collective-permute-start | bytes 196616 | tf_op jit(solution)/shard_map/ppermute | solution.py:24
  40.5 5.0 %collective-permute-start.17 = (bf16[16,2048]{1,0:T(8,128)(2,1)S(1)}, bf16[16,2048]{1,0:T(8,128)(2,1)S(1)}, u32[]{:S(2)}, u32[]{:S(2)}) collective-permute-start(bf16[16,2048]{1,0:T(8,128)(2,1)S(1)} %down.3.refs_0_), channel_id=1, source_target_pairs={{0,2},{1,3},{2,0},{3,1},{4,6},{5,7},{6,4},{7,5},{8,10},{9,11},{10,... | collective-permute-start | bytes 196616 | tf_op jit(solution)/shard_map/ppermute | solution.py:24
  41.2 4.3 %collective-permute-start.16 = (bf16[16,2048]{1,0:T(8,128)(2,1)S(1)}, bf16[16,2048]{1,0:T(8,128)(2,1)S(1)}, u32[]{:S(2)}, u32[]{:S(2)}) collective-permute-start(bf16[16,2048]{1,0:T(8,128)(2,1)S(1)} %down.3.refs_0_), channel_id=1, source_target_pairs={{0,1},{1,0},{2,3},{3,2},{4,5},{5,4},{6,7},{7,6},{8,9},{9,8},{10,11... | collective-permute-start | bytes 196616 | tf_op jit(solution)/shard_map/ppermute | solution.py:24

commit v14 on v12

--- a/solution.py
+++ b/solution.py
@@ -235,8 +235,17 @@
     return [refs[order.index(k)] for k in range(len(refs))]
 
 
+def gather_order(groups):
+    return [0, 1, 3, 2] if groups == 4 else list(range(groups))
+
+
+def sum_order(groups):
+    return [0, 3, 1, 2] if groups == 4 else list(range(groups))
+
+
 def out_kernel(groups, *refs):
-    parts, (weight, *outs) = refs[:groups], refs[groups:-3]
+    parts = [refs[gather_order(groups).index(k)] for k in range(groups)]
+    weight, *outs = refs[groups:-3]
     canon, attended, packed = refs[-3:]
     half = packed.shape[2]
     attended[...] = canonical(parts, canon, lax.axis_index("row"))
@@ -286,8 +295,9 @@
 
 
 def lift_second_kernel(
-    own, received, gains, gate_weight, up_weight, gate_first, up_first, mid, keep, send, packed
+    own, received, gains, gate_weight, up_weight, gate_first, up_first, mid, *rest
 ):
+    outs, packed = rest[:-1], rest[-1]
     rows, hidden = gate_first.shape
     half, bit = rows // 2, lax.axis_index("col") & 1
     width = own.shape[1]
@@ -305,12 +315,14 @@
         packed[i, :, hidden:] = jnp.concatenate([sent[part], sent[part]], axis=0)
         packed[i, :, :hidden] = jnp.concatenate([gate[part], up[part]], axis=0)
     bit = lax.axis_index("row") & 1
-    keep[...] = packed[bit].astype(keep.dtype)
-    send[...] = packed[1 - bit].astype(send.dtype)
+    mine, theirs = (packed[i].astype(outs[0].dtype) for i in (bit, 1 - bit))
+    for k, out in enumerate(outs):
+        out[...] = theirs if k % 2 else mine
 
 
 def act_kernel(model, *refs):
-    parts, out = refs[:-1], refs[-1]
+    out = refs[-1]
+    parts = [refs[sum_order(len(refs) - 1).index(k)] for k in range(len(refs) - 1)]
     hidden = parts[0].shape[1] - HD
     cells = parts[0].shape[0] // 2
     values = [p[...].astype(jnp.float32) for p in parts]
@@ -428,7 +440,7 @@
             pltpu.VMEM((2, m, half), f32),
         ],
         name="out_projection",
-    )(*gathered, in_vmem(out_weight))
+    )(*[gathered[k] for k in gather_order(groups)], in_vmem(out_weight))
     partials = [partials[0]] + [partner(partials[k], "col", k) for k in range(1, cols)]
     norm_gain = in_vmem(norm_gain)
     own, own_lifted = call(
@@ -445,21 +457,21 @@
         [VMEM_SPEC] * 3,
         name="gate_up_first",
     )(own_lifted, *weights)
-    mid, keep, send = call(
+    mid, *sums = call(
         lift_second_kernel,
-        [shape((m, width_share), f32)] + [shape((m, hidden + HD), WIRE)] * 2,
+        [shape((m, width_share), f32)] + [shape((m, hidden + HD), WIRE)] * groups,
         [VMEM_SPEC] * 7,
         [pltpu.VMEM((2, m, hidden + HD), f32)],
         flops=40 * 10**9,
         name="gate_up_second",
     )(own, received, norm_gain, *weights, *first)
-    sums = [keep] + [partner((keep, send)[k % 2], "row", k) for k in range(1, groups)]
+    sums = sums[:1] + [partner(sums[k], "row", k) for k in range(1, groups)]
     act = call(
         functools.partial(act_kernel, model),
         shape((m // 2, hidden), bf16),
         [VMEM_SPEC] * groups,
         name="activation",
-    )(*sums)
+    )(*[sums[k] for k in sum_order(groups)])
     down_weight = in_vmem(down_weight)
 
     def down_part(same, from_row, other, before, result):

time: 46.5 us -> 46.7 us (level)
  starting transfers between devices: 18.6 us -> 19.3 us
  waiting for transfers between devices: 18.9 us -> 18.4 us
    ppermute x19, starting transfers between devices: 18.6 us -> 19.3 us  [partner(): lax.ppermute(value, axis, [(i, i ^ k) for i in range(lax.axis_size(axis))])]
    ppermute x19, waiting for transfers between devices: 18.9 us -> 18.4 us  [partner(): lax.ppermute(value, axis, [(i, i ^ k) for i in range(lax.axis_size(axis))])]
  transfers between devices with their start and end apart: 19 -> 19, of which waited for: 14 -> 15; matrix products, arithmetic and copies ran while one was open for 0% -> 0% of each run, Pallas kernels for 6% -> 6%
where the time goes in v14:
time: 46.7 us; the launch traced here: 46.5 us
  starting transfers between devices  19.3 us (41%)
  waiting for transfers between devices  18.4 us (39%)
  Pallas kernels  8.44 us (18%)
    ppermute x19, starting transfers between devices, partner(): lax.ppermute(value, axis, [(i, i ^ k) for i in range(lax.axis_size(axis))])  19.3 us
    ppermute x19, waiting for transfers between devices, partner(): lax.ppermute(value, axis, [(i, i ^ k) for i in range(lax.axis_size(axis))])  18.4 us
    pallas_call x2, Pallas kernels, down_part(): call(functools.partial(down_kernel, other), shape((m, width_share), resul...  2.13 us
    pallas_call x1, Pallas kernels, shards(): call(functools.partial(attention_far_kernel, cols), [message] * (cols //...  1.88 us
    pallas_call x1, Pallas kernels, shards(): call(lift_second_kernel, [shape((m, width_share), f32)] + [shape((m, hidd...  1.09 us
    pallas_call x1, Pallas kernels, shards(): call(lift_first_kernel, [shape((m, hidden), f32)] * 2, [VMEM_SPEC] * 3, n...  1.07 us
  transfers between devices with their start and end apart: 19, of which 15 were waited for; matrix products, arithmetic and copies ran while one was open for 0% of the time, Pallas kernels for 6%

profile of v14, /device:TPU:0, one launch (start us, length us, event | category | flops | bytes accessed | tf_op | source)
XLA Modules:
  0.0 46.5 jit_solution(6863692818024686264)
XLA Ops:
  0.0 1.9 %attention_far.1 = (f32[5,8,128]{2,1,0:T(8,128)S(1)}, f32[5,8,128]{2,1,0:T(8,128)S(1)}, bf16[2,2,4096]{2,1,0:T(2,128)(2,1)S(1)}, bf16[2,2,512]{2,1,0:T(2,128)(2,...) custom-call(bf16[2,2,4096]{2,1,0:T(2,128)(2,1)} %refs_0_.1, ...), custom_call_target="tpu_custom_call" | custom-call | tf_op jit(solution)/shard_map/attention_far/pallas_call | solution.py:407
  1.9 3.0 %collective-permute-start = (f32[5,8,128]{2,1,0:T(8,128)S(1)}, f32[5,8,128]{2,1,0:T(8,128)S(1)}, u32[]{:S(2)}, u32[]{:S(2)}) collective-permute-start(f32[5,8,128]{2,1,0:T(8,128)S(1)} %get-tuple-element.28), channel_id=1, source_target_pairs={{0,2},{1,3},{2,0},{3,1},{4,6},{5,7},{6,4},{7,5},{8,10},{9,11},{10,... | collective-permute-start | bytes 61448 | tf_op jit(solution)/shard_map/ppermute | solution.py:24
  4.9 0.5 %attention_near.1 = (f32[5,8,128]{2,1,0:T(8,128)S(1)}, f32[5,8,128]{2,1,0:T(8,128)S(1)}) custom-call(bf16[2,2,4096]{2,1,0:T(2,128)(2,1)S(1)} %get-tuple-element.30.refs_0_, bf16[2,2,512]{2,1,0:T(2,128)(2,1)S(1)} %get-tuple-element.31.refs_1_, bf16[2,2,512]{2,1,0:T(2,128)(2,1)S(1)} %get-tuple-element.32.refs_2_, ...), custom_call_target="tpu_custom_call" | custom-call | tf_op jit(solution)/shard_map/attention_near/pallas_call | solution.py:416
  5.4 0.2 collective-permute-start.2
  5.7 1.0 %collective-permute-done.refs_0_ = f32[5,8,128]{2,1,0:T(8,128)S(1)} collective-permute-done((f32[5,8,128]{2,1,0:T(8,128)S(1)}, f32[5,8,128]{2,1,0:T(8,128)S(1)}, u32[]{:S(2)}, u32[]{:S(2)}) %collective-permute-start) | collective-permute-done | bytes 20512 | tf_op jit(solution)/shard_map/ppermute | solution.py:24
  6.7 1.4 %collective-permute-done.1.refs_1_ = f32[5,8,128]{2,1,0:T(8,128)S(1)} collective-permute-done((f32[5,8,128]{2,1,0:T(8,128)S(1)}, f32[5,8,128]{2,1,0:T(8,128)S(1)}, u32[]{:S(2)}, u32[]{:S(2)}) %collective-permute-start.1) | collective-permute-done | bytes 20512 | tf_op jit(solution)/shard_map/ppermute | solution.py:24
  8.1 0.0 slice-start.5
  8.2 0.0 slice-start.6
  8.2 0.0 slice-start.7
  8.2 0.0 slice-start.9
  8.2 0.0 slice-start.11
  8.2 0.2 combine.1.refs_0_
  8.4 2.7 %collective-permute-start.5 = (bf16[4,1024]{1,0:T(4,128)(2,1)S(1)}, bf16[4,1024]{1,0:T(4,128)(2,1)S(1)}, u32[]{:S(2)}, u32[]{:S(2)}) collective-permute-start(bf16[4,1024]{1,0:T(4,128)(2,1)S(1)} %combine.1.refs_0_), channel_id=1, source_target_pairs={{0,8},{4,12},{8,0},{12,4},{1,9},{5,13},{9,1},{13,5},{2,10},{6,14},... | collective-permute-start | bytes 24584 | tf_op jit(solution)/shard_map/ppermute | solution.py:24
  11.0 1.3 %collective-permute-start.4 = (bf16[4,1024]{1,0:T(4,128)(2,1)S(1)}, bf16[4,1024]{1,0:T(4,128)(2,1)S(1)}, u32[]{:S(2)}, u32[]{:S(2)}) collective-permute-start(bf16[4,1024]{1,0:T(4,128)(2,1)S(1)} %combine.1.refs_0_), channel_id=1, source_target_pairs={{0,12},{4,8},{8,4},{12,0},{1,13},{5,9},{9,5},{13,1},{2,14},{6,10},... | collective-permute-start | bytes 24584 | tf_op jit(solution)/shard_map/ppermute | solution.py:24
  12.4 0.2 collective-permute-start.3
  12.6 0.4 collective-permute-done.5.refs_3_
  13.0 3.5 %collective-permute-done.4.refs_2_ = bf16[4,1024]{1,0:T(4,128)(2,1)S(1)} collective-permute-done((bf16[4,1024]{1,0:T(4,128)(2,1)S(1)}, bf16[4,1024]{1,0:T(4,128)(2,1)S(1)}, u32[]{:S(2)}, u32[]{:S(2)}) %collective-permute-start.4) | collective-permute-done | bytes 8224 | tf_op jit(solution)/shard_map/ppermute | solution.py:24
  16.5 0.0 collective-permute-done.3.refs_1_
  16.5 0.7 %out_projection.1 = (bf16[16,1024]{1,0:T(8,128)(2,1)S(1)}, bf16[16,1024]{1,0:T(8,128)(2,1)S(1)}, bf16[16,1024]{1,0:T(8,128)(2,1)S(1)}, bf16[16,1024]{1,0:T(8,128)(2,1)S(1)}) custom-call(bf16[4,1024]{1,0:T(4,128)(2,1)S(1)} %combine.1.refs_0_, bf16[4,1024]{1,0:T(4,128)(2,1)S(1)} %collective-permute-done.3.refs_1_, ...), custom_call_target="tpu_custom_call" | custom-call | tf_op jit(solution)/shard_map/out_projection/pallas_call | solution.py:433
  17.2 0.1 collective-permute-start.6
  17.3 0.8 %collective-permute-start.7 = (bf16[16,1024]{1,0:T(8,128)(2,1)S(1)}, bf16[16,1024]{1,0:T(8,128)(2,1)S(1)}, u32[]{:S(2)}, u32[]{:S(2)}) collective-permute-start(bf16[16,1024]{1,0:T(8,128)(2,1)S(1)} %get-tuple-element.40), channel_id=1, source_target_pairs={{0,2},{1,3},{2,0},{3,1},{4,6},{5,7},{6,4},{7,5},{8,10},{9,11},{10,... | collective-permute-start | bytes 98312 | tf_op jit(solution)/shard_map/ppermute | solution.py:24
  18.1 1.0 %collective-permute-start.8 = (bf16[16,1024]{1,0:T(8,128)(2,1)S(1)}, bf16[16,1024]{1,0:T(8,128)(2,1)S(1)}, u32[]{:S(2)}, u32[]{:S(2)}) collective-permute-start(bf16[16,1024]{1,0:T(8,128)(2,1)S(1)} %get-tuple-element.41), channel_id=1, source_target_pairs={{0,1},{1,0},{2,3},{3,2},{4,5},{5,4},{6,7},{7,6},{8,9},{9,8},{10,11... | collective-permute-start | bytes 98312 | tf_op jit(solution)/shard_map/ppermute | solution.py:24
  19.1 1.5 %collective-permute-done.6.refs_1_ = bf16[16,1024]{1,0:T(8,128)(2,1)S(1)} collective-permute-done((bf16[16,1024]{1,0:T(8,128)(2,1)S(1)}, bf16[16,1024]{1,0:T(8,128)(2,1)S(1)}, u32[]{:S(2)}, u32[]{:S(2)}) %collective-permute-start.6) | collective-permute-done | bytes 32800 | tf_op jit(solution)/shard_map/ppermute | solution.py:24
  20.6 0.8 %collective-permute-done.7.refs_2_ = bf16[16,1024]{1,0:T(8,128)(2,1)S(1)} collective-permute-done((bf16[16,1024]{1,0:T(8,128)(2,1)S(1)}, bf16[16,1024]{1,0:T(8,128)(2,1)S(1)}, u32[]{:S(2)}, u32[]{:S(2)}) %collective-permute-start.7) | collective-permute-done | bytes 32800 | tf_op jit(solution)/shard_map/ppermute | solution.py:24
  21.5 0.1 collective-permute-start.9
  21.6 0.0 slice-start
  21.7 1.1 %gate_up_first.1 = (f32[16,1792]{1,0:T(8,128)S(1)}, f32[16,1792]{1,0:T(8,128)S(1)}) custom-call(bf16[16,1024]{1,0:T(8,128)(2,1)S(1)} %get-tuple-element.43.lifted, bf16[2048,3584]{1,0:T(8,128)(2,1)S(1)} %bitcast.3, bf16[2048,3584]{1,0:T(8,128)(2,1)S(1)} %bitcast.5), custom_call_target="tpu_custom_call" | custom-call | tf_op jit(solution)/shard_map/gate_up_first/pallas_call | solution.py:454
  22.7 0.1 collective-permute-done.9.received
  22.8 1.1 %gate_up_second.1 = (f32[16,2048]{1,0:T(8,128)S(1)}, bf16[16,1920]{1,0:T(8,128)(2,1)S(1)}, bf16[16,1920]{1,0:T(8,128)(2,1)S(1)}, bf16[16,1920]{1,0:T(8,128)(2,1)S(1)}, bf16[16,1920]{1,0:T(8,128)(2,1)S(1)}) custom-call(f32[16,1024]{1,0:T(8,128)S(1)} %get-tuple-element.42.own, f32[16,1024]{1,0:T(8,128)S(1)} %collective-permute-done.9.received, ...), custom_call_target="tpu_custom_call" | custom-call | flops 40000000000 | bytes 1024 | tf_op jit(solution)/shard_map/gate_up_second/pallas_call | solution.py:460
  23.9 2.0 %collective-permute-start.10 = (bf16[16,1920]{1,0:T(8,128)(2,1)S(1)}, bf16[16,1920]{1,0:T(8,128)(2,1)S(1)}, u32[]{:S(2)}, u32[]{:S(2)}) collective-permute-start(bf16[16,1920]{1,0:T(8,128)(2,1)S(1)} %get-tuple-element.48), channel_id=1, source_target_pairs={{0,12},{4,8},{8,4},{12,0},{1,13},{5,9},{9,5},{13,1},{2,14},{6,10},... | collective-permute-start | bytes 184328 | tf_op jit(solution)/shard_map/ppermute | solution.py:24
  25.9 2.4 %collective-permute-start.12 = (bf16[16,1920]{1,0:T(8,128)(2,1)S(1)}, bf16[16,1920]{1,0:T(8,128)(2,1)S(1)}, u32[]{:S(2)}, u32[]{:S(2)}) collective-permute-start(bf16[16,1920]{1,0:T(8,128)(2,1)S(1)} %get-tuple-element.50), channel_id=1, source_target_pairs={{0,8},{4,12},{8,0},{12,4},{1,9},{5,13},{9,1},{13,5},{2,10},{6,14},... | collective-permute-start | bytes 184328 | tf_op jit(solution)/shard_map/ppermute | solution.py:24
  28.3 2.3 %collective-permute-done.10.refs_1_ = bf16[16,1920]{1,0:T(8,128)(2,1)S(1)} collective-permute-done((bf16[16,1920]{1,0:T(8,128)(2,1)S(1)}, bf16[16,1920]{1,0:T(8,128)(2,1)S(1)}, u32[]{:S(2)}, u32[]{:S(2)}) %collective-permute-start.10) | collective-permute-done | bytes 61472 | tf_op jit(solution)/shard_map/ppermute | solution.py:24
  30.6 2.0 %collective-permute-done.11.refs_2_ = bf16[16,1920]{1,0:T(8,128)(2,1)S(1)} collective-permute-done((bf16[16,1920]{1,0:T(8,128)(2,1)S(1)}, bf16[16,1920]{1,0:T(8,128)(2,1)S(1)}, u32[]{:S(2)}, u32[]{:S(2)}) %collective-permute-start.11) | collective-permute-done | bytes 61472 | tf_op jit(solution)/shard_map/ppermute | solution.py:24
  32.6 0.1 collective-permute-done.12.refs_3_
  32.7 0.1 activation.1.own
  32.9 0.6 %collective-permute-start.15 = (bf16[8,1792]{1,0:T(8,128)(2,1)S(1)}, bf16[8,1792]{1,0:T(8,128)(2,1)S(1)}, u32[]{:S(2)}, u32[]{:S(2)}) collective-permute-start(bf16[8,1792]{1,0:T(8,128)(2,1)S(1)} %activation.1.own), channel_id=1, source_target_pairs={{0,4},{4,0},{8,12},{12,8},{1,5},{5,1},{9,13},{13,9},{2,6},{6,2},{1... | collective-permute-start | bytes 86024 | tf_op jit(solution)/shard_map/ppermute | solution.py:24
  33.5 2.4 %collective-permute-start.14 = (bf16[8,1792]{1,0:T(8,128)(2,1)S(1)}, bf16[8,1792]{1,0:T(8,128)(2,1)S(1)}, u32[]{:S(2)}, u32[]{:S(2)}) collective-permute-start(bf16[8,1792]{1,0:T(8,128)(2,1)S(1)} %activation.1.own), channel_id=1, source_target_pairs={{0,20},{4,16},{8,28},{12,24},{16,4},{20,0},{24,12},{28,8},{1,21},{... | collective-permute-start | bytes 86024 | tf_op jit(solution)/shard_map/ppermute | solution.py:24
  35.9 0.5 %collective-permute-start.13 = (bf16[8,1792]{1,0:T(8,128)(2,1)S(1)}, bf16[8,1792]{1,0:T(8,128)(2,1)S(1)}, u32[]{:S(2)}, u32[]{:S(2)}) collective-permute-start(bf16[8,1792]{1,0:T(8,128)(2,1)S(1)} %activation.1.own), channel_id=1, source_target_pairs={{0,16},{16,0},{1,17},{17,1},{2,18},{18,2},{3,19},{19,3},{4,20},{20... | collective-permute-start | bytes 86024 | tf_op jit(solution)/shard_map/ppermute | solution.py:24
  36.4 0.5 %collective-permute-done.15.received = bf16[8,1792]{1,0:T(8,128)(2,1)S(1)} collective-permute-done((bf16[8,1792]{1,0:T(8,128)(2,1)S(1)}, bf16[8,1792]{1,0:T(8,128)(2,1)S(1)}, u32[]{:S(2)}, u32[]{:S(2)}) %collective-permute-start.15) | collective-permute-done | bytes 28704 | tf_op jit(solution)/shard_map/ppermute | solution.py:24
  37.1 1.1 %down.2.refs_0_ = f32[16,2048]{1,0:T(8,128)S(1)} custom-call(bf16[16,1792]{1,0:T(8,128)(2,1)S(1)} %gather_act.3.act, bf16[3584,2048]{1,0:T(8,128)(2,1)S(1)} %bitcast.1), custom_call_target="tpu_custom_call" | custom-call | tf_op jit(solution)/shard_map/down/pallas_call | solution.py:485
  38.1 0.2 collective-permute-done.14.received
  38.3 1.4 %collective-permute-done.13.own = bf16[8,1792]{1,0:T(8,128)(2,1)S(1)} collective-permute-done((bf16[8,1792]{1,0:T(8,128)(2,1)S(1)}, bf16[8,1792]{1,0:T(8,128)(2,1)S(1)}, u32[]{:S(2)}, u32[]{:S(2)}) %collective-permute-start.13) | collective-permute-done | bytes 28704 | tf_op jit(solution)/shard_map/ppermute | solution.py:24
  39.8 1.1 %down.3.refs_0_ = bf16[16,2048]{1,0:T(8,128)(2,1)S(1)} custom-call(bf16[16,1792]{1,0:T(8,128)(2,1)S(1)} %gather_act.2.act, bf16[3584,2048]{1,0:T(8,128)(2,1)S(1)} %bitcast.1, f32[16,2048]{1,0:T(8,128)S(1)} %down.2.refs_0_), custom_call_target="tpu_custom_call" | custom-call | tf_op jit(solution)/shard_map/down/pallas_call | solution.py:485
  40.9 0.6 %collective-permute-start.17 = (bf16[16,2048]{1,0:T(8,128)(2,1)S(1)}, bf16[16,2048]{1,0:T(8,128)(2,1)S(1)}, u32[]{:S(2)}, u32[]{:S(2)}) collective-permute-start(bf16[16,2048]{1,0:T(8,128)(2,1)S(1)} %down.3.refs_0_), channel_id=1, source_target_pairs={{0,2},{1,3},{2,0},{3,1},{4,6},{5,7},{6,4},{7,5},{8,10},{9,11},{10,... | collective-permute-start | bytes 196616 | tf_op jit(solution)/shard_map/ppermute | solution.py:24
  41.4 1.3 %collective-permute-start.16 = (bf16[16,2048]{1,0:T(8,128)(2,1)S(1)}, bf16[16,2048]{1,0:T(8,128)(2,1)S(1)}, u32[]{:S(2)}, u32[]{:S(2)}) collective-permute-start(bf16[16,2048]{1,0:T(8,128)(2,1)S(1)} %down.3.refs_0_), channel_id=1, source_target_pairs={{0,1},{1,0},{2,3},{3,2},{4,5},{5,4},{6,7},{7,6},{8,9},{9,8},{10,11... | collective-permute-start | bytes 196616 | tf_op jit(solution)/shard_map/ppermute | solution.py:24
  42.7 2.0 %collective-permute-done.18.refs_3_ = bf16[16,2048]{1,0:T(8,128)(2,1)S(1)} collective-permute-done((bf16[16,2048]{1,0:T(8,128)(2,1)S(1)}, bf16[16,2048]{1,0:T(8,128)(2,1)S(1)}, u32[]{:S(2)}, u32[]{:S(2)}) %collective-permute-start.18) | collective-permute-done | bytes 65568 | tf_op jit(solution)/shard_map/ppermute | solution.py:24
  44.7 1.1 %collective-permute-done.17.refs_2_ = bf16[16,2048]{1,0:T(8,128)(2,1)S(1)} collective-permute-done((bf16[16,2048]{1,0:T(8,128)(2,1)S(1)}, bf16[16,2048]{1,0:T(8,128)(2,1)S(1)}, u32[]{:S(2)}, u32[]{:S(2)}) %collective-permute-start.17) | collective-permute-done | bytes 65568 | tf_op jit(solution)/shard_map/ppermute | solution.py:24
  45.8 0.7 %final.1 = bf16[2,8,2048]{2,1,0:T(8,128)(2,1)} custom-call(f32[16,2048]{1,0:T(8,128)S(1)} %get-tuple-element.46.mid, bf16[16,2048]{1,0:T(8,128)(2,1)S(1)} %down.3.refs_0_, bf16[16,2048]{1,0:T(8,128)(2,1)S(1)} %collective-permute-done.16.refs_1_, bf16[16,2048]{1,0:T(8,128)(2,1)S(1)} %collective-permute-done.17.refs_2_, ...), custom_call_target="tpu_custom_call" | custom-call | tf_op jit(solution)/shard_map/final/pallas_call | solution.py:499
  (36 shorter events, 0.1 us)
Async XLA Ops:
  1.9 4.8 %collective-permute-start = (f32[5,8,128]{2,1,0:T(8,128)S(1)}, f32[5,8,128]{2,1,0:T(8,128)S(1)}, u32[]{:S(2)}, u32[]{:S(2)}) collective-permute-start(f32[5,8,128]{2,1,0:T(8,128)S(1)} %get-tuple-element.28), channel_id=1, source_target_pairs={{0,2},{1,3},{2,0},{3,1},{4,6},{5,7},{6,4},{7,5},{8,10},{9,11},{10,... | collective-permute-start | bytes 61448 | tf_op jit(solution)/shard_map/ppermute | solution.py:24
  4.9 3.2 %collective-permute-start.1 = (f32[5,8,128]{2,1,0:T(8,128)S(1)}, f32[5,8,128]{2,1,0:T(8,128)S(1)}, u32[]{:S(2)}, u32[]{:S(2)}) collective-permute-start(f32[5,8,128]{2,1,0:T(8,128)S(1)} %get-tuple-element.29), channel_id=1, source_target_pairs={{0,3},{1,2},{2,1},{3,0},{4,7},{5,6},{6,5},{7,4},{8,11},{9,10},{10,... | collective-permute-start | bytes 61448 | tf_op jit(solution)/shard_map/ppermute | solution.py:24
  4.9 16.6 %slice-start.4 = ((s8[14680064]{0:T(1024)(128)(4,1)}), s8[4194304]{0:T(1024)(128)(4,1)S(1)}, s32[]{:S(2)}) async-start(s8[14680064]{0:T(1024)(128)(4,1)} %bitcast.2), calls=%async_computation.4 | async-start | bytes 8388608
  4.9 16.6 %slice-start.8 = ((s8[14680064]{0:T(1024)(128)(4,1)}), s8[4194304]{0:T(1024)(128)(4,1)S(1)}, s32[]{:S(2)}) async-start(s8[14680064]{0:T(1024)(128)(4,1)} %bitcast.4), calls=%async_computation.8 | async-start | bytes 8388608
  5.4 2.7 %collective-permute-start.2 = (f32[5,8,128]{2,1,0:T(8,128)S(1)}, f32[5,8,128]{2,1,0:T(8,128)S(1)}, u32[]{:S(2)}, u32[]{:S(2)}) collective-permute-start(f32[5,8,128]{2,1,0:T(8,128)S(1)} %get-tuple-element.37), channel_id=1, source_target_pairs={{0,1},{1,0},{2,3},{3,2},{4,5},{5,4},{6,7},{7,6},{8,9},{9,8},{10,11... | collective-permute-start | bytes 61448 | tf_op jit(solution)/shard_map/ppermute | solution.py:24
  8.1 8.4 %copy-start = (bf16[1024,2048]{1,0:T(8,128)(2,1)S(1)}, bf16[1024,2048]{1,0:T(8,128)(2,1)}, u32[]{:S(2)}) copy-start(bf16[1024,2048]{1,0:T(8,128)(2,1)} %refs_4_.3) | copy-start | bytes 12582916
  8.1 13.3 %copy-start.1 = (bf16[2,8,2048]{2,1,0:T(8,128)(2,1)S(1)}, bf16[2,8,2048]{2,1,0:T(8,128)(2,1)}, u32[]{:S(2)}) copy-start(bf16[2,8,2048]{2,1,0:T(8,128)(2,1)} %residual.1) | copy-start | bytes 196612
  8.1 13.3 %copy-start.2 = (bf16[2048]{0:T(1024)(128)(2,1)S(1)}, bf16[2048]{0:T(1024)(128)(2,1)}, u32[]{:S(2)}) copy-start(bf16[2048]{0:T(1024)(128)(2,1)} %gains.3) | copy-start | bytes 12292
  8.1 13.4 %slice-start.5 = ((s8[14680064]{0:T(1024)(128)(4,1)}), s8[4194304]{0:T(1024)(128)(4,1)S(1)}, s32[]{:S(2)}) async-start(s8[14680064]{0:T(1024)(128)(4,1)} %bitcast.2), calls=%async_computation.5 | async-start | bytes 8388608
  8.2 13.4 %slice-start.6 = ((s8[14680064]{0:T(1024)(128)(4,1)}), s8[4194304]{0:T(1024)(128)(4,1)S(1)}, s32[]{:S(2)}) async-start(s8[14680064]{0:T(1024)(128)(4,1)} %bitcast.2), calls=%async_computation.6 | async-start | bytes 8388608
  8.2 13.4 %slice-start.7 = ((s8[14680064]{0:T(1024)(128)(4,1)}), s8[2097152]{0:T(1024)(128)(4,1)S(1)}, s32[]{:S(2)}) async-start(s8[14680064]{0:T(1024)(128)(4,1)} %bitcast.2), calls=%async_computation.7 | async-start | bytes 4194304
  8.2 13.4 %slice-start.9 = ((s8[14680064]{0:T(1024)(128)(4,1)}), s8[4194304]{0:T(1024)(128)(4,1)S(1)}, s32[]{:S(2)}) async-start(s8[14680064]{0:T(1024)(128)(4,1)} %bitcast.4), calls=%async_computation.9 | async-start | bytes 8388608
  8.2 13.4 %slice-start.10 = ((s8[14680064]{0:T(1024)(128)(4,1)}), s8[4194304]{0:T(1024)(128)(4,1)S(1)}, s32[]{:S(2)}) async-start(s8[14680064]{0:T(1024)(128)(4,1)} %bitcast.4), calls=%async_computation.10 | async-start | bytes 8388608
  8.2 13.4 %slice-start.11 = ((s8[14680064]{0:T(1024)(128)(4,1)}), s8[2097152]{0:T(1024)(128)(4,1)S(1)}, s32[]{:S(2)}) async-start(s8[14680064]{0:T(1024)(128)(4,1)} %bitcast.4), calls=%async_computation.11 | async-start | bytes 4194304
  8.4 4.6 %collective-permute-start.5 = (bf16[4,1024]{1,0:T(4,128)(2,1)S(1)}, bf16[4,1024]{1,0:T(4,128)(2,1)S(1)}, u32[]{:S(2)}, u32[]{:S(2)}) collective-permute-start(bf16[4,1024]{1,0:T(4,128)(2,1)S(1)} %combine.1.refs_0_), channel_id=1, source_target_pairs={{0,8},{4,12},{8,0},{12,4},{1,9},{5,13},{9,1},{13,5},{2,10},{6,14},... | collective-permute-start | bytes 24584 | tf_op jit(solution)/shard_map/ppermute | solution.py:24
  11.0 5.4 %collective-permute-start.4 = (bf16[4,1024]{1,0:T(4,128)(2,1)S(1)}, bf16[4,1024]{1,0:T(4,128)(2,1)S(1)}, u32[]{:S(2)}, u32[]{:S(2)}) collective-permute-start(bf16[4,1024]{1,0:T(4,128)(2,1)S(1)} %combine.1.refs_0_), channel_id=1, source_target_pairs={{0,12},{4,8},{8,4},{12,0},{1,13},{5,9},{9,5},{13,1},{2,14},{6,10},... | collective-permute-start | bytes 24584 | tf_op jit(solution)/shard_map/ppermute | solution.py:24
  12.4 4.1 %collective-permute-start.3 = (bf16[4,1024]{1,0:T(4,128)(2,1)S(1)}, bf16[4,1024]{1,0:T(4,128)(2,1)S(1)}, u32[]{:S(2)}, u32[]{:S(2)}) collective-permute-start(bf16[4,1024]{1,0:T(4,128)(2,1)S(1)} %combine.1.refs_0_), channel_id=1, source_target_pairs={{0,4},{4,0},{8,12},{12,8},{1,5},{5,1},{9,13},{13,9},{2,6},{6,2},{1... | collective-permute-start | bytes 24584 | tf_op jit(solution)/shard_map/ppermute | solution.py:24
  17.2 3.4 %collective-permute-start.6 = (bf16[16,1024]{1,0:T(8,128)(2,1)S(1)}, bf16[16,1024]{1,0:T(8,128)(2,1)S(1)}, u32[]{:S(2)}, u32[]{:S(2)}) collective-permute-start(bf16[16,1024]{1,0:T(8,128)(2,1)S(1)} %get-tuple-element.39), channel_id=1, source_target_pairs={{0,3},{1,2},{2,1},{3,0},{4,7},{5,6},{6,5},{7,4},{8,11},{9,10},{10,... | collective-permute-start | bytes 98312 | tf_op jit(solution)/shard_map/ppermute | solution.py:24
  17.3 4.2 %collective-permute-start.7 = (bf16[16,1024]{1,0:T(8,128)(2,1)S(1)}, bf16[16,1024]{1,0:T(8,128)(2,1)S(1)}, u32[]{:S(2)}, u32[]{:S(2)}) collective-permute-start(bf16[16,1024]{1,0:T(8,128)(2,1)S(1)} %get-tuple-element.40), channel_id=1, source_target_pairs={{0,2},{1,3},{2,0},{3,1},{4,6},{5,7},{6,4},{7,5},{8,10},{9,11},{10,... | collective-permute-start | bytes 98312 | tf_op jit(solution)/shard_map/ppermute | solution.py:24
  18.1 3.3 %collective-permute-start.8 = (bf16[16,1024]{1,0:T(8,128)(2,1)S(1)}, bf16[16,1024]{1,0:T(8,128)(2,1)S(1)}, u32[]{:S(2)}, u32[]{:S(2)}) collective-permute-start(bf16[16,1024]{1,0:T(8,128)(2,1)S(1)} %get-tuple-element.41), channel_id=1, source_target_pairs={{0,1},{1,0},{2,3},{3,2},{4,5},{5,4},{6,7},{7,6},{8,9},{9,8},{10,11... | collective-permute-start | bytes 98312 | tf_op jit(solution)/shard_map/ppermute | solution.py:24
  21.5 1.3 %collective-permute-start.9 = (f32[16,1024]{1,0:T(8,128)S(1)}, f32[16,1024]{1,0:T(8,128)S(1)}, u32[]{:S(2)}, u32[]{:S(2)}) collective-permute-start(f32[16,1024]{1,0:T(8,128)S(1)} %get-tuple-element.42.own), channel_id=1, source_target_pairs={{0,1},{1,0},{2,3},{3,2},{4,5},{5,4},{6,7},{7,6},{8,9},{9,8},{10,11... | collective-permute-start | bytes 196616 | tf_op jit(solution)/shard_map/ppermute | solution.py:24
  21.6 15.4 %slice-start = ((s8[14680064]{0:T(1024)(128)(4,1)}), s8[4194304]{0:T(1024)(128)(4,1)S(1)}, s32[]{:S(2)}) async-start(s8[14680064]{0:T(1024)(128)(4,1)} %bitcast), calls=%async_computation | async-start | bytes 8388608
  22.8 14.2 %slice-start.1 = ((s8[14680064]{0:T(1024)(128)(4,1)}), s8[4194304]{0:T(1024)(128)(4,1)S(1)}, s32[]{:S(2)}) async-start(s8[14680064]{0:T(1024)(128)(4,1)} %bitcast), calls=%async_computation.1 | async-start | bytes 8388608
  22.8 14.2 %slice-start.2 = ((s8[14680064]{0:T(1024)(128)(4,1)}), s8[4194304]{0:T(1024)(128)(4,1)S(1)}, s32[]{:S(2)}) async-start(s8[14680064]{0:T(1024)(128)(4,1)} %bitcast), calls=%async_computation.2 | async-start | bytes 8388608
  22.8 14.2 %slice-start.3 = ((s8[14680064]{0:T(1024)(128)(4,1)}), s8[2097152]{0:T(1024)(128)(4,1)S(1)}, s32[]{:S(2)}) async-start(s8[14680064]{0:T(1024)(128)(4,1)} %bitcast), calls=%async_computation.3 | async-start | bytes 4194304
  23.9 6.7 %collective-permute-start.10 = (bf16[16,1920]{1,0:T(8,128)(2,1)S(1)}, bf16[16,1920]{1,0:T(8,128)(2,1)S(1)}, u32[]{:S(2)}, u32[]{:S(2)}) collective-permute-start(bf16[16,1920]{1,0:T(8,128)(2,1)S(1)} %get-tuple-element.48), channel_id=1, source_target_pairs={{0,12},{4,8},{8,4},{12,0},{1,13},{5,9},{9,5},{13,1},{2,14},{6,10},... | collective-permute-start | bytes 184328 | tf_op jit(solution)/shard_map/ppermute | solution.py:24
  25.9 6.7 %collective-permute-start.11 = (bf16[16,1920]{1,0:T(8,128)(2,1)S(1)}, bf16[16,1920]{1,0:T(8,128)(2,1)S(1)}, u32[]{:S(2)}, u32[]{:S(2)}) collective-permute-start(bf16[16,1920]{1,0:T(8,128)(2,1)S(1)} %get-tuple-element.49), channel_id=1, source_target_pairs={{0,4},{4,0},{8,12},{12,8},{1,5},{5,1},{9,13},{13,9},{2,6},{6,2},{1... | collective-permute-start | bytes 184328 | tf_op jit(solution)/shard_map/ppermute | solution.py:24
  25.9 6.8 %collective-permute-start.12 = (bf16[16,1920]{1,0:T(8,128)(2,1)S(1)}, bf16[16,1920]{1,0:T(8,128)(2,1)S(1)}, u32[]{:S(2)}, u32[]{:S(2)}) collective-permute-start(bf16[16,1920]{1,0:T(8,128)(2,1)S(1)} %get-tuple-element.50), channel_id=1, source_target_pairs={{0,8},{4,12},{8,0},{12,4},{1,9},{5,13},{9,1},{13,5},{2,10},{6,14},... | collective-permute-start | bytes 184328 | tf_op jit(solution)/shard_map/ppermute | solution.py:24
  32.9 4.1 %collective-permute-start.15 = (bf16[8,1792]{1,0:T(8,128)(2,1)S(1)}, bf16[8,1792]{1,0:T(8,128)(2,1)S(1)}, u32[]{:S(2)}, u32[]{:S(2)}) collective-permute-start(bf16[8,1792]{1,0:T(8,128)(2,1)S(1)} %activation.1.own), channel_id=1, source_target_pairs={{0,4},{4,0},{8,12},{12,8},{1,5},{5,1},{9,13},{13,9},{2,6},{6,2},{1... | collective-permute-start | bytes 86024 | tf_op jit(solution)/shard_map/ppermute | solution.py:24
  33.5 4.9 %collective-permute-start.14 = (bf16[8,1792]{1,0:T(8,128)(2,1)S(1)}, bf16[8,1792]{1,0:T(8,128)(2,1)S(1)}, u32[]{:S(2)}, u32[]{:S(2)}) collective-permute-start(bf16[8,1792]{1,0:T(8,128)(2,1)S(1)} %activation.1.own), channel_id=1, source_target_pairs={{0,20},{4,16},{8,28},{12,24},{16,4},{20,0},{24,12},{28,8},{1,21},{... | collective-permute-start | bytes 86024 | tf_op jit(solution)/shard_map/ppermute | solution.py:24
  35.9 3.9 %collective-permute-start.13 = (bf16[8,1792]{1,0:T(8,128)(2,1)S(1)}, bf16[8,1792]{1,0:T(8,128)(2,1)S(1)}, u32[]{:S(2)}, u32[]{:S(2)}) collective-permute-start(bf16[8,1792]{1,0:T(8,128)(2,1)S(1)} %activation.1.own), channel_id=1, source_target_pairs={{0,16},{16,0},{1,17},{17,1},{2,18},{18,2},{3,19},{19,3},{4,20},{20... | collective-permute-start | bytes 86024 | tf_op jit(solution)/shard_map/ppermute | solution.py:24
  40.9 3.8 %collective-permute-start.18 = (bf16[16,2048]{1,0:T(8,128)(2,1)S(1)}, bf16[16,2048]{1,0:T(8,128)(2,1)S(1)}, u32[]{:S(2)}, u32[]{:S(2)}) collective-permute-start(bf16[16,2048]{1,0:T(8,128)(2,1)S(1)} %down.3.refs_0_), channel_id=1, source_target_pairs={{0,3},{1,2},{2,1},{3,0},{4,7},{5,6},{6,5},{7,4},{8,11},{9,10},{10,... | collective-permute-start | bytes 196616 | tf_op jit(solution)/shard_map/ppermute | solution.py:24
  40.9 5.0 %collective-permute-start.17 = (bf16[16,2048]{1,0:T(8,128)(2,1)S(1)}, bf16[16,2048]{1,0:T(8,128)(2,1)S(1)}, u32[]{:S(2)}, u32[]{:S(2)}) collective-permute-start(bf16[16,2048]{1,0:T(8,128)(2,1)S(1)} %down.3.refs_0_), channel_id=1, source_target_pairs={{0,2},{1,3},{2,0},{3,1},{4,6},{5,7},{6,4},{7,5},{8,10},{9,11},{10,... | collective-permute-start | bytes 196616 | tf_op jit(solution)/shard_map/ppermute | solution.py:24
  41.4 4.4 %collective-permute-start.16 = (bf16[16,2048]{1,0:T(8,128)(2,1)S(1)}, bf16[16,2048]{1,0:T(8,128)(2,1)S(1)}, u32[]{:S(2)}, u32[]{:S(2)}) collective-permute-start(bf16[16,2048]{1,0:T(8,128)(2,1)S(1)} %down.3.refs_0_), channel_id=1, source_target_pairs={{0,1},{1,0},{2,3},{3,2},{4,5},{5,4},{6,7},{7,6},{8,9},{9,8},{10,11... | collective-permute-start | bytes 196616 | tf_op jit(solution)/shard_map/ppermute | solution.py:24

commit v15 on v12

--- a/solution.py
+++ b/solution.py
@@ -345,15 +345,37 @@
     over_columns(out.shape[1], body)
 
 
+def down_half_kernel(other, flip, act, weight, *refs):
+    first, out = refs[:-1], refs[-1]
+    hidden, half = act.shape[1], out.shape[1]
+    start = 0
+    if weight.shape[0] > hidden:
+        start = pl.multiple_of(jnp.bitwise_xor(lax.axis_index("side"), other) * hidden, 128)
+    lanes = lanes_of(jnp.bitwise_xor(lax.axis_index("col") & 1, flip), half)
+    product = dot(act[...], weight[pl.ds(start, hidden), lanes])
+    for ref in first:
+        product = product + ref[:, lanes]
+    out[...] = product.astype(out.dtype)
+
+
+def add_kernel(first, second, out):
+    out[...] = (first[...].astype(jnp.float32) + second[...].astype(jnp.float32)).astype(out.dtype)
+
+
 def final_kernel(groups, mid, *refs):
     parts, out = refs[:-1], refs[-1]
-    total = mid[...] + tree_sum([p[...].astype(jnp.float32) for p in parts])
+    half = parts[0].shape[1]
+    bit = lax.axis_index("col") & 1
     here = out.shape[1] // groups
-    for t in range(TOKENS):
-        block = [
-            total[(r * TOKENS + t) * here : (r * TOKENS + t + 1) * here] for r in range(groups)
-        ]
-        out[t] = jnp.concatenate(block, axis=0).astype(out.dtype)
+    parts = [p[...].astype(jnp.float32) for p in parts]
+    for i in range(2):
+        lanes = lanes_of(jnp.bitwise_xor(bit, i), half)
+        total = mid[:, lanes] + tree_sum(parts[i::2])
+        for t in range(TOKENS):
+            block = [
+                total[(r * TOKENS + t) * here : (r * TOKENS + t + 1) * here] for r in range(groups)
+            ]
+            out[t, :, lanes] = jnp.concatenate(block, axis=0).astype(out.dtype)
 
 
 def shards(
@@ -462,28 +484,40 @@
     )(*sums)
     down_weight = in_vmem(down_weight)
 
-    def down_part(same, from_row, other, before, result):
-        rows = call(
+    def gather_act(own_rows, other_rows):
+        return call(
             gather_kernel,
             shape((m, hidden), bf16),
             [VMEM_SPEC] * 2,
             [pltpu.VMEM((2, m // 2, hidden), f32)],
             name="gather_act",
-        )(same, from_row)
+        )(own_rows, other_rows)
+
+    rows, first, other = gather_act(act, partner(act, "row", 1)), [], 0
+    if split > 1:
+        first, other = [
+            call(
+                functools.partial(down_kernel, 0),
+                shape((m, width_share), f32),
+                [VMEM_SPEC] * 2,
+                name="down_first",
+            )(rows, down_weight)
+        ], 1
+        far = partner(act, ("side", "row"), groups + 1)
+        rows = gather_act(partner(act, "side", 1), far)
+
+    def down_half(flip, result):
         return call(
-            functools.partial(down_kernel, other),
-            shape((m, width_share), result),
-            [VMEM_SPEC] * (2 + len(before)),
-            name="down",
-        )(rows, down_weight, *before)
-
-    near = partner(act, "row", 1)
-    if split > 1:
-        first = down_part(act, near, 0, [], f32)
-        far = partner(act, ("side", "row"), groups + 1)
-        down = down_part(partner(act, "side", 1), far, 1, [first], WIRE)
-    else:
-        down = down_part(act, near, 0, [], WIRE)
+            functools.partial(down_half_kernel, other, flip),
+            shape((m, half), result),
+            [VMEM_SPEC] * (2 + len(first)),
+            name="down_theirs" if flip else "down_mine",
+        )(rows, down_weight, *first)
+
+    theirs = partner(down_half(1, WIRE), "col", 1)
+    down = call(add_kernel, shape((m, half), WIRE), [VMEM_SPEC] * 2, name="down_add")(
+        down_half(0, f32), theirs
+    )
     return call(
         functools.partial(final_kernel, groups),
         shape((TOKENS, total_rows, width_share), bf16),

time: 46.5 us -> 46.8 us (level)
    pallas_call x4 -> x6, Pallas kernels: 2.17 us -> 2.3 us  [the longest x2 1.19 us: down_half(): call(functools.partial(down_half_kernel, other, flip), shape((m, half), r...]
    ppermute x19 -> x20, waiting for transfers between devices: 18.9 us -> 19 us  [partner(): lax.ppermute(value, axis, [(i, i ^ k) for i in range(lax.axis_size(axis))])]
    ppermute x19 -> x20, starting transfers between devices: 18.6 us -> 18.7 us  [partner(): lax.ppermute(value, axis, [(i, i ^ k) for i in range(lax.axis_size(axis))])]
  transfers between devices with their start and end apart: 19 -> 20, of which waited for: 14 -> 15; matrix products, arithmetic and copies ran while one was open for 0% -> 0% of each run, Pallas kernels for 6% -> 7%
where the time goes in v15:
time: 46.8 us; the launch traced here: 46.6 us
  waiting for transfers between devices  19 us (41%)
  starting transfers between devices  18.7 us (40%)
  Pallas kernels  8.54 us (18%)
    ppermute x20, waiting for transfers between devices, partner(): lax.ppermute(value, axis, [(i, i ^ k) for i in range(lax.axis_size(axis))])  19 us
    ppermute x20, starting transfers between devices, partner(): lax.ppermute(value, axis, [(i, i ^ k) for i in range(lax.axis_size(axis))])  18.7 us
    pallas_call x1, Pallas kernels, shards(): call(functools.partial(attention_far_kernel, cols), [message] * (cols //...  1.88 us
    pallas_call x2, Pallas kernels, down_half(): call(functools.partial(down_half_kernel, other, flip), shape((m, half), r...  1.19 us
    pallas_call x1, Pallas kernels, shards(): call(lift_second_kernel, [shape((m, width_share), f32)] + [shape((m, hidd...  1.08 us
    pallas_call x1, Pallas kernels, shards(): call(lift_first_kernel, [shape((m, hidden), f32)] * 2, [VMEM_SPEC] * 3, n...  1.07 us
    pallas_call x1, Pallas kernels, shards(): call(functools.partial(down_kernel, 0), shape((m, width_share), f32), [VM...  1.06 us
  transfers between devices with their start and end apart: 20, of which 15 were waited for; matrix products, arithmetic and copies ran while one was open for 0% of the time, Pallas kernels for 7%

profile of v15, /device:TPU:0, one launch (start us, length us, event | category | flops | bytes accessed | tf_op | source)
XLA Modules:
  0.0 46.6 jit_solution(15752810057465605971)
XLA Ops:
  0.0 1.9 %attention_far.1 = (f32[5,8,128]{2,1,0:T(8,128)S(1)}, f32[5,8,128]{2,1,0:T(8,128)S(1)}, bf16[2,2,4096]{2,1,0:T(2,128)(2,1)S(1)}, bf16[2,2,512]{2,1,0:T(2,128)(2,...) custom-call(bf16[2,2,4096]{2,1,0:T(2,128)(2,1)} %refs_0_.1, ...), custom_call_target="tpu_custom_call" | custom-call | tf_op jit(solution)/shard_map/attention_far/pallas_call | solution.py:417
  1.9 3.0 %collective-permute-start = (f32[5,8,128]{2,1,0:T(8,128)S(1)}, f32[5,8,128]{2,1,0:T(8,128)S(1)}, u32[]{:S(2)}, u32[]{:S(2)}) collective-permute-start(f32[5,8,128]{2,1,0:T(8,128)S(1)} %get-tuple-element.26), channel_id=1, source_target_pairs={{0,2},{1,3},{2,0},{3,1},{4,6},{5,7},{6,4},{7,5},{8,10},{9,11},{10,... | collective-permute-start | bytes 61448 | tf_op jit(solution)/shard_map/ppermute | solution.py:24
  4.9 0.0 collective-permute-start.1
  4.9 0.5 %attention_near.1 = (f32[5,8,128]{2,1,0:T(8,128)S(1)}, f32[5,8,128]{2,1,0:T(8,128)S(1)}) custom-call(bf16[2,2,4096]{2,1,0:T(2,128)(2,1)S(1)} %get-tuple-element.28.refs_0_, bf16[2,2,512]{2,1,0:T(2,128)(2,1)S(1)} %get-tuple-element.29.refs_1_, bf16[2,2,512]{2,1,0:T(2,128)(2,1)S(1)} %get-tuple-element.30.refs_2_, ...), custom_call_target="tpu_custom_call" | custom-call | tf_op jit(solution)/shard_map/attention_near/pallas_call | solution.py:426
  5.4 0.2 collective-permute-start.2
  5.7 1.0 %collective-permute-done.refs_0_ = f32[5,8,128]{2,1,0:T(8,128)S(1)} collective-permute-done((f32[5,8,128]{2,1,0:T(8,128)S(1)}, f32[5,8,128]{2,1,0:T(8,128)S(1)}, u32[]{:S(2)}, u32[]{:S(2)}) %collective-permute-start) | collective-permute-done | bytes 20512 | tf_op jit(solution)/shard_map/ppermute | solution.py:24
  6.7 1.4 %collective-permute-done.1.refs_1_ = f32[5,8,128]{2,1,0:T(8,128)S(1)} collective-permute-done((f32[5,8,128]{2,1,0:T(8,128)S(1)}, f32[5,8,128]{2,1,0:T(8,128)S(1)}, u32[]{:S(2)}, u32[]{:S(2)}) %collective-permute-start.1) | collective-permute-done | bytes 20512 | tf_op jit(solution)/shard_map/ppermute | solution.py:24
  8.1 0.0 collective-permute-done.2.refs_3_
  8.1 0.0 slice-start.5
  8.2 0.0 slice-start.9
  8.2 0.2 combine.1.refs_0_
  8.4 3.7 %collective-permute-start.5 = (bf16[4,1024]{1,0:T(4,128)(2,1)S(1)}, bf16[4,1024]{1,0:T(4,128)(2,1)S(1)}, u32[]{:S(2)}, u32[]{:S(2)}) collective-permute-start(bf16[4,1024]{1,0:T(4,128)(2,1)S(1)} %combine.1.refs_0_), channel_id=1, source_target_pairs={{0,12},{4,8},{8,4},{12,0},{1,13},{5,9},{9,5},{13,1},{2,14},{6,10},... | collective-permute-start | bytes 24584 | tf_op jit(solution)/shard_map/ppermute | solution.py:24
  12.1 0.8 %collective-permute-start.3 = (bf16[4,1024]{1,0:T(4,128)(2,1)S(1)}, bf16[4,1024]{1,0:T(4,128)(2,1)S(1)}, u32[]{:S(2)}, u32[]{:S(2)}) collective-permute-start(bf16[4,1024]{1,0:T(4,128)(2,1)S(1)} %combine.1.refs_0_), channel_id=1, source_target_pairs={{0,4},{4,0},{8,12},{12,8},{1,5},{5,1},{9,13},{13,9},{2,6},{6,2},{1... | collective-permute-start | bytes 24584 | tf_op jit(solution)/shard_map/ppermute | solution.py:24
  12.8 1.1 %collective-permute-done.5.refs_3_ = bf16[4,1024]{1,0:T(4,128)(2,1)S(1)} collective-permute-done((bf16[4,1024]{1,0:T(4,128)(2,1)S(1)}, bf16[4,1024]{1,0:T(4,128)(2,1)S(1)}, u32[]{:S(2)}, u32[]{:S(2)}) %collective-permute-start.5) | collective-permute-done | bytes 8224 | tf_op jit(solution)/shard_map/ppermute | solution.py:24
  14.0 2.6 %collective-permute-done.4.refs_2_ = bf16[4,1024]{1,0:T(4,128)(2,1)S(1)} collective-permute-done((bf16[4,1024]{1,0:T(4,128)(2,1)S(1)}, bf16[4,1024]{1,0:T(4,128)(2,1)S(1)}, u32[]{:S(2)}, u32[]{:S(2)}) %collective-permute-start.4) | collective-permute-done | bytes 8224 | tf_op jit(solution)/shard_map/ppermute | solution.py:24
  16.6 0.7 %out_projection.1 = (bf16[16,1024]{1,0:T(8,128)(2,1)S(1)}, bf16[16,1024]{1,0:T(8,128)(2,1)S(1)}, bf16[16,1024]{1,0:T(8,128)(2,1)S(1)}, bf16[16,1024]{1,0:T(8,128)(2,1)S(1)}) custom-call(bf16[4,1024]{1,0:T(4,128)(2,1)S(1)} %combine.1.refs_0_, bf16[4,1024]{1,0:T(4,128)(2,1)S(1)} %collective-permute-done.3.refs_1_, ...), custom_call_target="tpu_custom_call" | custom-call | tf_op jit(solution)/shard_map/out_projection/pallas_call | solution.py:443
  17.3 0.1 collective-permute-start.6
  17.4 0.8 %collective-permute-start.7 = (bf16[16,1024]{1,0:T(8,128)(2,1)S(1)}, bf16[16,1024]{1,0:T(8,128)(2,1)S(1)}, u32[]{:S(2)}, u32[]{:S(2)}) collective-permute-start(bf16[16,1024]{1,0:T(8,128)(2,1)S(1)} %get-tuple-element.38), channel_id=1, source_target_pairs={{0,2},{1,3},{2,0},{3,1},{4,6},{5,7},{6,4},{7,5},{8,10},{9,11},{10,... | collective-permute-start | bytes 98312 | tf_op jit(solution)/shard_map/ppermute | solution.py:24
  18.2 1.0 %collective-permute-start.8 = (bf16[16,1024]{1,0:T(8,128)(2,1)S(1)}, bf16[16,1024]{1,0:T(8,128)(2,1)S(1)}, u32[]{:S(2)}, u32[]{:S(2)}) collective-permute-start(bf16[16,1024]{1,0:T(8,128)(2,1)S(1)} %get-tuple-element.39), channel_id=1, source_target_pairs={{0,1},{1,0},{2,3},{3,2},{4,5},{5,4},{6,7},{7,6},{8,9},{9,8},{10,11... | collective-permute-start | bytes 98312 | tf_op jit(solution)/shard_map/ppermute | solution.py:24
  19.2 1.5 %collective-permute-done.6.refs_1_ = bf16[16,1024]{1,0:T(8,128)(2,1)S(1)} collective-permute-done((bf16[16,1024]{1,0:T(8,128)(2,1)S(1)}, bf16[16,1024]{1,0:T(8,128)(2,1)S(1)}, u32[]{:S(2)}, u32[]{:S(2)}) %collective-permute-start.6) | collective-permute-done | bytes 32800 | tf_op jit(solution)/shard_map/ppermute | solution.py:24
  20.7 0.8 %collective-permute-done.7.refs_2_ = bf16[16,1024]{1,0:T(8,128)(2,1)S(1)} collective-permute-done((bf16[16,1024]{1,0:T(8,128)(2,1)S(1)}, bf16[16,1024]{1,0:T(8,128)(2,1)S(1)}, u32[]{:S(2)}, u32[]{:S(2)}) %collective-permute-start.7) | collective-permute-done | bytes 32800 | tf_op jit(solution)/shard_map/ppermute | solution.py:24
  21.6 0.1 collective-permute-start.9
  21.8 0.0 slice-start
  21.8 1.1 %gate_up_first.1 = (f32[16,1792]{1,0:T(8,128)S(1)}, f32[16,1792]{1,0:T(8,128)S(1)}) custom-call(bf16[16,1024]{1,0:T(8,128)(2,1)S(1)} %get-tuple-element.41.lifted, bf16[2048,3584]{1,0:T(8,128)(2,1)S(1)} %bitcast.3, bf16[2048,3584]{1,0:T(8,128)(2,1)S(1)} %bitcast.5), custom_call_target="tpu_custom_call" | custom-call | tf_op jit(solution)/shard_map/gate_up_first/pallas_call | solution.py:464
  22.8 0.1 collective-permute-done.9.received
  22.9 1.1 %gate_up_second.1 = (f32[16,2048]{1,0:T(8,128)S(1)}, bf16[16,1920]{1,0:T(8,128)(2,1)S(1)}, bf16[16,1920]{1,0:T(8,128)(2,1)S(1)}) custom-call(f32[16,1024]{1,0:T(8,128)S(1)} %get-tuple-element.40.own, f32[16,1024]{1,0:T(8,128)S(1)} %collective-permute-done.9.received, bf16[2048]{0:T(1024)(128)(2,1)S(1)} %copy-done.2, bf16[2048,3584]{1,0:T(8,128)(2,1)S(1)} %bitcast.3, ...), custom_call_target="tpu_custom_call" | custom-call | flops 40000000000 | bytes 1024 | tf_op jit(solution)/shard_map/gate_up_second/pallas_call | solution.py:470
  24.0 2.0 %collective-permute-start.11 = (bf16[16,1920]{1,0:T(8,128)(2,1)S(1)}, bf16[16,1920]{1,0:T(8,128)(2,1)S(1)}, u32[]{:S(2)}, u32[]{:S(2)}) collective-permute-start(bf16[16,1920]{1,0:T(8,128)(2,1)S(1)} %get-tuple-element.45.refs_0_), channel_id=1, source_target_pairs={{0,8},{4,12},{8,0},{12,4},{1,9},{5,13},{9,1},{13,5},{2,10},{6,14},... | collective-permute-start | bytes 184328 | tf_op jit(solution)/shard_map/ppermute | solution.py:24
  26.0 0.1 collective-permute-start.12
  26.1 1.4 %collective-permute-start.10 = (bf16[16,1920]{1,0:T(8,128)(2,1)S(1)}, bf16[16,1920]{1,0:T(8,128)(2,1)S(1)}, u32[]{:S(2)}, u32[]{:S(2)}) collective-permute-start(bf16[16,1920]{1,0:T(8,128)(2,1)S(1)} %get-tuple-element.46), channel_id=1, source_target_pairs={{0,4},{4,0},{8,12},{12,8},{1,5},{5,1},{9,13},{13,9},{2,6},{6,2},{1... | collective-permute-start | bytes 184328 | tf_op jit(solution)/shard_map/ppermute | solution.py:24
  27.5 2.4 %collective-permute-done.11.refs_2_ = bf16[16,1920]{1,0:T(8,128)(2,1)S(1)} collective-permute-done((bf16[16,1920]{1,0:T(8,128)(2,1)S(1)}, bf16[16,1920]{1,0:T(8,128)(2,1)S(1)}, u32[]{:S(2)}, u32[]{:S(2)}) %collective-permute-start.11) | collective-permute-done | bytes 61472 | tf_op jit(solution)/shard_map/ppermute | solution.py:24
  29.9 2.7 %collective-permute-done.12.refs_3_ = bf16[16,1920]{1,0:T(8,128)(2,1)S(1)} collective-permute-done((bf16[16,1920]{1,0:T(8,128)(2,1)S(1)}, bf16[16,1920]{1,0:T(8,128)(2,1)S(1)}, u32[]{:S(2)}, u32[]{:S(2)}) %collective-permute-start.12) | collective-permute-done | bytes 61472 | tf_op jit(solution)/shard_map/ppermute | solution.py:24
  32.6 0.1 activation.1.own
  32.7 0.6 %collective-permute-start.15 = (bf16[8,1792]{1,0:T(8,128)(2,1)S(1)}, bf16[8,1792]{1,0:T(8,128)(2,1)S(1)}, u32[]{:S(2)}, u32[]{:S(2)}) collective-permute-start(bf16[8,1792]{1,0:T(8,128)(2,1)S(1)} %activation.1.own), channel_id=1, source_target_pairs={{0,4},{4,0},{8,12},{12,8},{1,5},{5,1},{9,13},{13,9},{2,6},{6,2},{1... | collective-permute-start | bytes 86024 | tf_op jit(solution)/shard_map/ppermute | solution.py:24
  33.3 2.5 %collective-permute-start.14 = (bf16[8,1792]{1,0:T(8,128)(2,1)S(1)}, bf16[8,1792]{1,0:T(8,128)(2,1)S(1)}, u32[]{:S(2)}, u32[]{:S(2)}) collective-permute-start(bf16[8,1792]{1,0:T(8,128)(2,1)S(1)} %activation.1.own), channel_id=1, source_target_pairs={{0,20},{4,16},{8,28},{12,24},{16,4},{20,0},{24,12},{28,8},{1,21},{... | collective-permute-start | bytes 86024 | tf_op jit(solution)/shard_map/ppermute | solution.py:24
  35.7 0.5 %collective-permute-start.13 = (bf16[8,1792]{1,0:T(8,128)(2,1)S(1)}, bf16[8,1792]{1,0:T(8,128)(2,1)S(1)}, u32[]{:S(2)}, u32[]{:S(2)}) collective-permute-start(bf16[8,1792]{1,0:T(8,128)(2,1)S(1)} %activation.1.own), channel_id=1, source_target_pairs={{0,16},{16,0},{1,17},{17,1},{2,18},{18,2},{3,19},{19,3},{4,20},{20... | collective-permute-start | bytes 86024 | tf_op jit(solution)/shard_map/ppermute | solution.py:24
  36.3 0.6 %collective-permute-done.15.received = bf16[8,1792]{1,0:T(8,128)(2,1)S(1)} collective-permute-done((bf16[8,1792]{1,0:T(8,128)(2,1)S(1)}, bf16[8,1792]{1,0:T(8,128)(2,1)S(1)}, u32[]{:S(2)}, u32[]{:S(2)}) %collective-permute-start.15) | collective-permute-done | bytes 28704 | tf_op jit(solution)/shard_map/ppermute | solution.py:24
  37.0 1.1 %down_first.1.refs_0_ = f32[16,2048]{1,0:T(8,128)S(1)} custom-call(bf16[16,1792]{1,0:T(8,128)(2,1)S(1)} %gather_act.3.act, bf16[3584,2048]{1,0:T(8,128)(2,1)S(1)} %bitcast.1), custom_call_target="tpu_custom_call" | custom-call | tf_op jit(solution)/shard_map/down_first/pallas_call | solution.py:499
  38.0 0.1 collective-permute-done.14.received
  38.1 1.5 %collective-permute-done.13.own = bf16[8,1792]{1,0:T(8,128)(2,1)S(1)} collective-permute-done((bf16[8,1792]{1,0:T(8,128)(2,1)S(1)}, bf16[8,1792]{1,0:T(8,128)(2,1)S(1)}, u32[]{:S(2)}, u32[]{:S(2)}) %collective-permute-start.13) | collective-permute-done | bytes 28704 | tf_op jit(solution)/shard_map/ppermute | solution.py:24
  39.6 0.6 %down_theirs.1 = bf16[16,1024]{1,0:T(8,128)(2,1)S(1)} custom-call(bf16[16,1792]{1,0:T(8,128)(2,1)S(1)} %gather_act.2.act, bf16[3584,2048]{1,0:T(8,128)(2,1)S(1)} %bitcast.1, f32[16,2048]{1,0:T(8,128)S(1)} %down_first.1.refs_0_), custom_call_target="tpu_custom_call" | custom-call | tf_op jit(solution)/shard_map/down_theirs/pallas_call | solution.py:510
  40.2 0.6 %down_mine.1.first = f32[16,1024]{1,0:T(8,128)S(1)} custom-call(bf16[16,1792]{1,0:T(8,128)(2,1)S(1)} %gather_act.2.act, bf16[3584,2048]{1,0:T(8,128)(2,1)S(1)} %bitcast.1, f32[16,2048]{1,0:T(8,128)S(1)} %down_first.1.refs_0_), custom_call_target="tpu_custom_call" | custom-call | tf_op jit(solution)/shard_map/down_mine/pallas_call | solution.py:510
  40.8 0.6 %collective-permute-done.16.second = bf16[16,1024]{1,0:T(8,128)(2,1)S(1)} collective-permute-done((bf16[16,1024]{1,0:T(8,128)(2,1)S(1)}, bf16[16,1024]{1,0:T(8,128)(2,1)S(1)}, u32[]{:S(2)}, u32[]{:S(2)}) %collective-permute-start.16) | collective-permute-done | bytes 32800 | tf_op jit(solution)/shard_map/ppermute | solution.py:24
  41.5 0.4 collective-permute-start.19
  41.9 1.4 %collective-permute-start.18 = (bf16[16,1024]{1,0:T(8,128)(2,1)S(1)}, bf16[16,1024]{1,0:T(8,128)(2,1)S(1)}, u32[]{:S(2)}, u32[]{:S(2)}) collective-permute-start(bf16[16,1024]{1,0:T(8,128)(2,1)S(1)} %down_add.1.refs_0_), channel_id=1, source_target_pairs={{0,2},{1,3},{2,0},{3,1},{4,6},{5,7},{6,4},{7,5},{8,10},{9,11},{10,... | collective-permute-start | bytes 98312 | tf_op jit(solution)/shard_map/ppermute | solution.py:24
  43.3 0.1 collective-permute-start.17
  43.4 1.5 %collective-permute-done.19.refs_3_ = bf16[16,1024]{1,0:T(8,128)(2,1)S(1)} collective-permute-done((bf16[16,1024]{1,0:T(8,128)(2,1)S(1)}, bf16[16,1024]{1,0:T(8,128)(2,1)S(1)}, u32[]{:S(2)}, u32[]{:S(2)}) %collective-permute-start.19) | collective-permute-done | bytes 32800 | tf_op jit(solution)/shard_map/ppermute | solution.py:24
  44.9 1.0 %collective-permute-done.18.refs_2_ = bf16[16,1024]{1,0:T(8,128)(2,1)S(1)} collective-permute-done((bf16[16,1024]{1,0:T(8,128)(2,1)S(1)}, bf16[16,1024]{1,0:T(8,128)(2,1)S(1)}, u32[]{:S(2)}, u32[]{:S(2)}) %collective-permute-start.18) | collective-permute-done | bytes 32800 | tf_op jit(solution)/shard_map/ppermute | solution.py:24
  45.9 0.7 %final.1 = bf16[2,8,2048]{2,1,0:T(8,128)(2,1)} custom-call(f32[16,2048]{1,0:T(8,128)S(1)} %get-tuple-element.44.mid, bf16[16,1024]{1,0:T(8,128)(2,1)S(1)} %down_add.1.refs_0_, bf16[16,1024]{1,0:T(8,128)(2,1)S(1)} %collective-permute-done.17.refs_1_, bf16[16,1024]{1,0:T(8,128)(2,1)S(1)} %collective-permute-done.18.refs_2_, ...), custom_call_target="tpu_custom_call" | custom-call | tf_op jit(solution)/shard_map/final/pallas_call | solution.py:521
  (40 shorter events, 0.2 us)
Async XLA Ops:
  1.9 4.8 %collective-permute-start = (f32[5,8,128]{2,1,0:T(8,128)S(1)}, f32[5,8,128]{2,1,0:T(8,128)S(1)}, u32[]{:S(2)}, u32[]{:S(2)}) collective-permute-start(f32[5,8,128]{2,1,0:T(8,128)S(1)} %get-tuple-element.26), channel_id=1, source_target_pairs={{0,2},{1,3},{2,0},{3,1},{4,6},{5,7},{6,4},{7,5},{8,10},{9,11},{10,... | collective-permute-start | bytes 61448 | tf_op jit(solution)/shard_map/ppermute | solution.py:24
  4.9 3.2 %collective-permute-start.1 = (f32[5,8,128]{2,1,0:T(8,128)S(1)}, f32[5,8,128]{2,1,0:T(8,128)S(1)}, u32[]{:S(2)}, u32[]{:S(2)}) collective-permute-start(f32[5,8,128]{2,1,0:T(8,128)S(1)} %get-tuple-element.27), channel_id=1, source_target_pairs={{0,3},{1,2},{2,1},{3,0},{4,7},{5,6},{6,5},{7,4},{8,11},{9,10},{10,... | collective-permute-start | bytes 61448 | tf_op jit(solution)/shard_map/ppermute | solution.py:24
  4.9 16.7 %slice-start.4 = ((s8[14680064]{0:T(1024)(128)(4,1)}), s8[4194304]{0:T(1024)(128)(4,1)S(1)}, s32[]{:S(2)}) async-start(s8[14680064]{0:T(1024)(128)(4,1)} %bitcast.2), calls=%async_computation.4 | async-start | bytes 8388608
  4.9 16.8 %slice-start.8 = ((s8[14680064]{0:T(1024)(128)(4,1)}), s8[4194304]{0:T(1024)(128)(4,1)S(1)}, s32[]{:S(2)}) async-start(s8[14680064]{0:T(1024)(128)(4,1)} %bitcast.4), calls=%async_computation.8 | async-start | bytes 8388608
  5.4 2.7 %collective-permute-start.2 = (f32[5,8,128]{2,1,0:T(8,128)S(1)}, f32[5,8,128]{2,1,0:T(8,128)S(1)}, u32[]{:S(2)}, u32[]{:S(2)}) collective-permute-start(f32[5,8,128]{2,1,0:T(8,128)S(1)} %get-tuple-element.35), channel_id=1, source_target_pairs={{0,1},{1,0},{2,3},{3,2},{4,5},{5,4},{6,7},{7,6},{8,9},{9,8},{10,11... | collective-permute-start | bytes 61448 | tf_op jit(solution)/shard_map/ppermute | solution.py:24
  8.1 8.5 %copy-start = (bf16[1024,2048]{1,0:T(8,128)(2,1)S(1)}, bf16[1024,2048]{1,0:T(8,128)(2,1)}, u32[]{:S(2)}) copy-start(bf16[1024,2048]{1,0:T(8,128)(2,1)} %refs_4_.3) | copy-start | bytes 12582916
  8.1 13.4 %copy-start.1 = (bf16[2,8,2048]{2,1,0:T(8,128)(2,1)S(1)}, bf16[2,8,2048]{2,1,0:T(8,128)(2,1)}, u32[]{:S(2)}) copy-start(bf16[2,8,2048]{2,1,0:T(8,128)(2,1)} %residual.1) | copy-start | bytes 196612
  8.1 13.4 %copy-start.2 = (bf16[2048]{0:T(1024)(128)(2,1)S(1)}, bf16[2048]{0:T(1024)(128)(2,1)}, u32[]{:S(2)}) copy-start(bf16[2048]{0:T(1024)(128)(2,1)} %gains.3) | copy-start | bytes 12292
  8.1 13.5 %slice-start.5 = ((s8[14680064]{0:T(1024)(128)(4,1)}), s8[4194304]{0:T(1024)(128)(4,1)S(1)}, s32[]{:S(2)}) async-start(s8[14680064]{0:T(1024)(128)(4,1)} %bitcast.2), calls=%async_computation.5 | async-start | bytes 8388608
  8.2 13.5 %slice-start.6 = ((s8[14680064]{0:T(1024)(128)(4,1)}), s8[4194304]{0:T(1024)(128)(4,1)S(1)}, s32[]{:S(2)}) async-start(s8[14680064]{0:T(1024)(128)(4,1)} %bitcast.2), calls=%async_computation.6 | async-start | bytes 8388608
  8.2 13.5 %slice-start.7 = ((s8[14680064]{0:T(1024)(128)(4,1)}), s8[2097152]{0:T(1024)(128)(4,1)S(1)}, s32[]{:S(2)}) async-start(s8[14680064]{0:T(1024)(128)(4,1)} %bitcast.2), calls=%async_computation.7 | async-start | bytes 4194304
  8.2 13.5 %slice-start.9 = ((s8[14680064]{0:T(1024)(128)(4,1)}), s8[4194304]{0:T(1024)(128)(4,1)S(1)}, s32[]{:S(2)}) async-start(s8[14680064]{0:T(1024)(128)(4,1)} %bitcast.4), calls=%async_computation.9 | async-start | bytes 8388608
  8.2 13.5 %slice-start.10 = ((s8[14680064]{0:T(1024)(128)(4,1)}), s8[4194304]{0:T(1024)(128)(4,1)S(1)}, s32[]{:S(2)}) async-start(s8[14680064]{0:T(1024)(128)(4,1)} %bitcast.4), calls=%async_computation.10 | async-start | bytes 8388608
  8.2 13.5 %slice-start.11 = ((s8[14680064]{0:T(1024)(128)(4,1)}), s8[2097152]{0:T(1024)(128)(4,1)S(1)}, s32[]{:S(2)}) async-start(s8[14680064]{0:T(1024)(128)(4,1)} %bitcast.4), calls=%async_computation.11 | async-start | bytes 4194304
  8.4 5.6 %collective-permute-start.5 = (bf16[4,1024]{1,0:T(4,128)(2,1)S(1)}, bf16[4,1024]{1,0:T(4,128)(2,1)S(1)}, u32[]{:S(2)}, u32[]{:S(2)}) collective-permute-start(bf16[4,1024]{1,0:T(4,128)(2,1)S(1)} %combine.1.refs_0_), channel_id=1, source_target_pairs={{0,12},{4,8},{8,4},{12,0},{1,13},{5,9},{9,5},{13,1},{2,14},{6,10},... | collective-permute-start | bytes 24584 | tf_op jit(solution)/shard_map/ppermute | solution.py:24
  12.1 4.5 %collective-permute-start.4 = (bf16[4,1024]{1,0:T(4,128)(2,1)S(1)}, bf16[4,1024]{1,0:T(4,128)(2,1)S(1)}, u32[]{:S(2)}, u32[]{:S(2)}) collective-permute-start(bf16[4,1024]{1,0:T(4,128)(2,1)S(1)} %combine.1.refs_0_), channel_id=1, source_target_pairs={{0,8},{4,12},{8,0},{12,4},{1,9},{5,13},{9,1},{13,5},{2,10},{6,14},... | collective-permute-start | bytes 24584 | tf_op jit(solution)/shard_map/ppermute | solution.py:24
  12.1 4.5 %collective-permute-start.3 = (bf16[4,1024]{1,0:T(4,128)(2,1)S(1)}, bf16[4,1024]{1,0:T(4,128)(2,1)S(1)}, u32[]{:S(2)}, u32[]{:S(2)}) collective-permute-start(bf16[4,1024]{1,0:T(4,128)(2,1)S(1)} %combine.1.refs_0_), channel_id=1, source_target_pairs={{0,4},{4,0},{8,12},{12,8},{1,5},{5,1},{9,13},{13,9},{2,6},{6,2},{1... | collective-permute-start | bytes 24584 | tf_op jit(solution)/shard_map/ppermute | solution.py:24
  17.3 3.4 %collective-permute-start.6 = (bf16[16,1024]{1,0:T(8,128)(2,1)S(1)}, bf16[16,1024]{1,0:T(8,128)(2,1)S(1)}, u32[]{:S(2)}, u32[]{:S(2)}) collective-permute-start(bf16[16,1024]{1,0:T(8,128)(2,1)S(1)} %get-tuple-element.37), channel_id=1, source_target_pairs={{0,3},{1,2},{2,1},{3,0},{4,7},{5,6},{6,5},{7,4},{8,11},{9,10},{10,... | collective-permute-start | bytes 98312 | tf_op jit(solution)/shard_map/ppermute | solution.py:24
  17.4 4.2 %collective-permute-start.7 = (bf16[16,1024]{1,0:T(8,128)(2,1)S(1)}, bf16[16,1024]{1,0:T(8,128)(2,1)S(1)}, u32[]{:S(2)}, u32[]{:S(2)}) collective-permute-start(bf16[16,1024]{1,0:T(8,128)(2,1)S(1)} %get-tuple-element.38), channel_id=1, source_target_pairs={{0,2},{1,3},{2,0},{3,1},{4,6},{5,7},{6,4},{7,5},{8,10},{9,11},{10,... | collective-permute-start | bytes 98312 | tf_op jit(solution)/shard_map/ppermute | solution.py:24
  18.2 3.3 %collective-permute-start.8 = (bf16[16,1024]{1,0:T(8,128)(2,1)S(1)}, bf16[16,1024]{1,0:T(8,128)(2,1)S(1)}, u32[]{:S(2)}, u32[]{:S(2)}) collective-permute-start(bf16[16,1024]{1,0:T(8,128)(2,1)S(1)} %get-tuple-element.39), channel_id=1, source_target_pairs={{0,1},{1,0},{2,3},{3,2},{4,5},{5,4},{6,7},{7,6},{8,9},{9,8},{10,11... | collective-permute-start | bytes 98312 | tf_op jit(solution)/shard_map/ppermute | solution.py:24
  21.6 1.3 %collective-permute-start.9 = (f32[16,1024]{1,0:T(8,128)S(1)}, f32[16,1024]{1,0:T(8,128)S(1)}, u32[]{:S(2)}, u32[]{:S(2)}) collective-permute-start(f32[16,1024]{1,0:T(8,128)S(1)} %get-tuple-element.40.own), channel_id=1, source_target_pairs={{0,1},{1,0},{2,3},{3,2},{4,5},{5,4},{6,7},{7,6},{8,9},{9,8},{10,11... | collective-permute-start | bytes 196616 | tf_op jit(solution)/shard_map/ppermute | solution.py:24
  21.8 15.1 %slice-start = ((s8[14680064]{0:T(1024)(128)(4,1)}), s8[4194304]{0:T(1024)(128)(4,1)S(1)}, s32[]{:S(2)}) async-start(s8[14680064]{0:T(1024)(128)(4,1)} %bitcast), calls=%async_computation | async-start | bytes 8388608
  22.9 14.0 %slice-start.1 = ((s8[14680064]{0:T(1024)(128)(4,1)}), s8[4194304]{0:T(1024)(128)(4,1)S(1)}, s32[]{:S(2)}) async-start(s8[14680064]{0:T(1024)(128)(4,1)} %bitcast), calls=%async_computation.1 | async-start | bytes 8388608
  22.9 14.0 %slice-start.2 = ((s8[14680064]{0:T(1024)(128)(4,1)}), s8[4194304]{0:T(1024)(128)(4,1)S(1)}, s32[]{:S(2)}) async-start(s8[14680064]{0:T(1024)(128)(4,1)} %bitcast), calls=%async_computation.2 | async-start | bytes 8388608
  22.9 14.0 %slice-start.3 = ((s8[14680064]{0:T(1024)(128)(4,1)}), s8[2097152]{0:T(1024)(128)(4,1)S(1)}, s32[]{:S(2)}) async-start(s8[14680064]{0:T(1024)(128)(4,1)} %bitcast), calls=%async_computation.3 | async-start | bytes 4194304
  24.0 5.9 %collective-permute-start.11 = (bf16[16,1920]{1,0:T(8,128)(2,1)S(1)}, bf16[16,1920]{1,0:T(8,128)(2,1)S(1)}, u32[]{:S(2)}, u32[]{:S(2)}) collective-permute-start(bf16[16,1920]{1,0:T(8,128)(2,1)S(1)} %get-tuple-element.45.refs_0_), channel_id=1, source_target_pairs={{0,8},{4,12},{8,0},{12,4},{1,9},{5,13},{9,1},{13,5},{2,10},{6,14},... | collective-permute-start | bytes 184328 | tf_op jit(solution)/shard_map/ppermute | solution.py:24
  26.0 6.5 %collective-permute-start.12 = (bf16[16,1920]{1,0:T(8,128)(2,1)S(1)}, bf16[16,1920]{1,0:T(8,128)(2,1)S(1)}, u32[]{:S(2)}, u32[]{:S(2)}) collective-permute-start(bf16[16,1920]{1,0:T(8,128)(2,1)S(1)} %get-tuple-element.46), channel_id=1, source_target_pairs={{0,12},{4,8},{8,4},{12,0},{1,13},{5,9},{9,5},{13,1},{2,14},{6,10},... | collective-permute-start | bytes 184328 | tf_op jit(solution)/shard_map/ppermute | solution.py:24
  26.1 6.4 %collective-permute-start.10 = (bf16[16,1920]{1,0:T(8,128)(2,1)S(1)}, bf16[16,1920]{1,0:T(8,128)(2,1)S(1)}, u32[]{:S(2)}, u32[]{:S(2)}) collective-permute-start(bf16[16,1920]{1,0:T(8,128)(2,1)S(1)} %get-tuple-element.46), channel_id=1, source_target_pairs={{0,4},{4,0},{8,12},{12,8},{1,5},{5,1},{9,13},{13,9},{2,6},{6,2},{1... | collective-permute-start | bytes 184328 | tf_op jit(solution)/shard_map/ppermute | solution.py:24
  32.7 4.2 %collective-permute-start.15 = (bf16[8,1792]{1,0:T(8,128)(2,1)S(1)}, bf16[8,1792]{1,0:T(8,128)(2,1)S(1)}, u32[]{:S(2)}, u32[]{:S(2)}) collective-permute-start(bf16[8,1792]{1,0:T(8,128)(2,1)S(1)} %activation.1.own), channel_id=1, source_target_pairs={{0,4},{4,0},{8,12},{12,8},{1,5},{5,1},{9,13},{13,9},{2,6},{6,2},{1... | collective-permute-start | bytes 86024 | tf_op jit(solution)/shard_map/ppermute | solution.py:24
  33.3 4.8 %collective-permute-start.14 = (bf16[8,1792]{1,0:T(8,128)(2,1)S(1)}, bf16[8,1792]{1,0:T(8,128)(2,1)S(1)}, u32[]{:S(2)}, u32[]{:S(2)}) collective-permute-start(bf16[8,1792]{1,0:T(8,128)(2,1)S(1)} %activation.1.own), channel_id=1, source_target_pairs={{0,20},{4,16},{8,28},{12,24},{16,4},{20,0},{24,12},{28,8},{1,21},{... | collective-permute-start | bytes 86024 | tf_op jit(solution)/shard_map/ppermute | solution.py:24
  35.7 3.9 %collective-permute-start.13 = (bf16[8,1792]{1,0:T(8,128)(2,1)S(1)}, bf16[8,1792]{1,0:T(8,128)(2,1)S(1)}, u32[]{:S(2)}, u32[]{:S(2)}) collective-permute-start(bf16[8,1792]{1,0:T(8,128)(2,1)S(1)} %activation.1.own), channel_id=1, source_target_pairs={{0,16},{16,0},{1,17},{17,1},{2,18},{18,2},{3,19},{19,3},{4,20},{20... | collective-permute-start | bytes 86024 | tf_op jit(solution)/shard_map/ppermute | solution.py:24
  40.2 1.2 %collective-permute-start.16 = (bf16[16,1024]{1,0:T(8,128)(2,1)S(1)}, bf16[16,1024]{1,0:T(8,128)(2,1)S(1)}, u32[]{:S(2)}, u32[]{:S(2)}) collective-permute-start(bf16[16,1024]{1,0:T(8,128)(2,1)S(1)} %down_theirs.1), channel_id=1, source_target_pairs={{0,1},{1,0},{2,3},{3,2},{4,5},{5,4},{6,7},{7,6},{8,9},{9,8},{10,11... | collective-permute-start | bytes 98312 | tf_op jit(solution)/shard_map/ppermute | solution.py:24
  41.5 3.4 %collective-permute-start.19 = (bf16[16,1024]{1,0:T(8,128)(2,1)S(1)}, bf16[16,1024]{1,0:T(8,128)(2,1)S(1)}, u32[]{:S(2)}, u32[]{:S(2)}) collective-permute-start(bf16[16,1024]{1,0:T(8,128)(2,1)S(1)} %down_add.1.refs_0_), channel_id=1, source_target_pairs={{0,3},{1,2},{2,1},{3,0},{4,7},{5,6},{6,5},{7,4},{8,11},{9,10},{10,... | collective-permute-start | bytes 98312 | tf_op jit(solution)/shard_map/ppermute | solution.py:24
  41.9 4.0 %collective-permute-start.18 = (bf16[16,1024]{1,0:T(8,128)(2,1)S(1)}, bf16[16,1024]{1,0:T(8,128)(2,1)S(1)}, u32[]{:S(2)}, u32[]{:S(2)}) collective-permute-start(bf16[16,1024]{1,0:T(8,128)(2,1)S(1)} %down_add.1.refs_0_), channel_id=1, source_target_pairs={{0,2},{1,3},{2,0},{3,1},{4,6},{5,7},{6,4},{7,5},{8,10},{9,11},{10,... | collective-permute-start | bytes 98312 | tf_op jit(solution)/shard_map/ppermute | solution.py:24
  43.3 2.6 %collective-permute-start.17 = (bf16[16,1024]{1,0:T(8,128)(2,1)S(1)}, bf16[16,1024]{1,0:T(8,128)(2,1)S(1)}, u32[]{:S(2)}, u32[]{:S(2)}) collective-permute-start(bf16[16,1024]{1,0:T(8,128)(2,1)S(1)} %down_add.1.refs_0_), channel_id=1, source_target_pairs={{0,1},{1,0},{2,3},{3,2},{4,5},{5,4},{6,7},{7,6},{8,9},{9,8},{10,11... | collective-permute-start | bytes 98312 | tf_op jit(solution)/shard_map/ppermute | solution.py:24

commit v16 on v13

--- a/solution.py
+++ b/solution.py
@@ -48,7 +48,7 @@
     return first, second, value - first - second
 
 
-def call(kernel, out_shape, in_specs, scratch=(), limit=4, name=None, flops=None):
+def call(kernel, out_shape, in_specs, scratch=(), limit=4, name=None, flops=None, out_specs=None):
     cost = None
     if flops is not None:
         cost = pl.CostEstimate(flops=flops, bytes_accessed=1024, transcendentals=0)
@@ -56,7 +56,7 @@
         kernel,
         out_shape=out_shape,
         in_specs=in_specs,
-        out_specs=jax.tree.map(lambda _: VMEM_SPEC, out_shape),
+        out_specs=out_specs or jax.tree.map(lambda _: VMEM_SPEC, out_shape),
         scratch_shapes=list(scratch),
         compiler_params=pltpu.CompilerParams(vmem_limit_bytes=limit * MIB),
         cost_estimate=cost,
@@ -364,14 +364,19 @@
 
 
 def final_kernel(groups, mid, *refs):
-    parts, out = refs[:-1], refs[-1]
+    parts, (out, held, sems) = refs[:-3], refs[-3:]
     total = mid[...] + tree_sum([p[...].astype(jnp.float32) for p in parts])
     here = out.shape[1] // groups
+    copies = []
     for t in range(TOKENS):
         block = [
             total[(r * TOKENS + t) * here : (r * TOKENS + t + 1) * here] for r in range(groups)
         ]
-        out[t] = jnp.concatenate(block, axis=0).astype(out.dtype)
+        held[t] = jnp.concatenate(block, axis=0).astype(out.dtype)
+        copies.append(pltpu.make_async_copy(held.at[t], out.at[t], sems.at[t]))
+        copies[t].start()
+    for copy in copies:
+        copy.wait()
 
 
 def shards(
@@ -506,11 +511,14 @@
         down = down_part(partner(act, "side", 1), far, 1, [first], WIRE)
     else:
         down = down_part(act, near, 0, [], WIRE)
+    result = shape((TOKENS, total_rows, width_share), bf16)
     return call(
         functools.partial(final_kernel, groups),
-        shape((TOKENS, total_rows, width_share), bf16),
+        result,
         [VMEM_SPEC] * (cols + 1),
+        [pltpu.VMEM(result.shape, bf16), pltpu.SemaphoreType.DMA((TOKENS,))],
         name="final",
+        out_specs=ANY_SPEC,
     )(mid, *spread(down, "col"))
 
 

time: 46.3 us -> 46.3 us (level)
  no operation moved by 1% of the time
where the time goes in v16:
time: 46.3 us; the launch traced here: 46.2 us
  waiting for transfers between devices  18.7 us (40%)
  starting transfers between devices  18.6 us (40%)
  Pallas kernels  8.49 us (18%)
    ppermute x19, waiting for transfers between devices, partner(): lax.ppermute(value, axis, [(i, i ^ k) for i in range(lax.axis_size(axis))])  18.7 us
    ppermute x19, starting transfers between devices, partner(): lax.ppermute(value, axis, [(i, i ^ k) for i in range(lax.axis_size(axis))])  18.6 us
    pallas_call x2, Pallas kernels, down_part(): call(functools.partial(down_kernel, other), shape((m, width_share), resul...  2.13 us
    pallas_call x1, Pallas kernels, shards(): call(functools.partial(attention_far_kernel, cols), [message] * (cols //...  1.85 us
    pallas_call x1, Pallas kernels, shards(): call(lift_second_kernel, [shape((m, width_share), f32)] + [shape((m, hidd...  1.08 us
    pallas_call x1, Pallas kernels, shards(): call(lift_first_kernel, [shape((m, hidden), f32)] * 2, [VMEM_SPEC] * 3, n...  1.07 us
  transfers between devices with their start and end apart: 19, of which 14 were waited for; matrix products, arithmetic and copies ran while one was open for 0% of the time, Pallas kernels for 6%

profile of v16, /device:TPU:0, one launch (start us, length us, event | category | flops | bytes accessed | tf_op | source)
XLA Modules:
  0.0 46.2 jit_solution(11162643546971503601)
XLA Ops:
  0.0 1.9 %attention_far.1 = (bf16[5,8,128]{2,1,0:T(8,128)(2,1)S(1)}, bf16[5,8,128]{2,1,0:T(8,128)(2,1)S(1)}, bf16[2,2,4096]{2,1,0:T(2,128)(2,1)S(1)}, bf16[2,2,512]{2,1,0...) custom-call(bf16[2,2,4096]{2,1,0:T(2,128)(2,1)} %refs_0_.1, ...), custom_call_target="tpu_custom_call" | custom-call | tf_op jit(solution)/shard_map/attention_far/pallas_call | solution.py:418
  1.9 3.0 %collective-permute-start = (bf16[5,8,128]{2,1,0:T(8,128)(2,1)S(1)}, bf16[5,8,128]{2,1,0:T(8,128)(2,1)S(1)}, u32[]{:S(2)}, u32[]{:S(2)}) collective-permute-start(bf16[5,8,128]{2,1,0:T(8,128)(2,1)S(1)} %get-tuple-element.26), channel_id=1, source_target_pairs={{0,2},{1,3},{2,0},{3,1},{4,6},{5,7},{6,4},{7,5},{8,10},{9,11},{10,... | collective-permute-start | bytes 30728 | tf_op jit(solution)/shard_map/ppermute | solution.py:24
  4.9 0.5 %attention_near.1 = (bf16[5,8,128]{2,1,0:T(8,128)(2,1)S(1)}, bf16[5,8,128]{2,1,0:T(8,128)(2,1)S(1)}) custom-call(bf16[2,2,4096]{2,1,0:T(2,128)(2,1)S(1)} %get-tuple-element.28.refs_0_, bf16[2,2,512]{2,1,0:T(2,128)(2,1)S(1)} %get-tuple-element.29.refs_1_, bf16[2,2,512]{2,1,0:T(2,128)(2,1)S(1)} %get-tuple-element.30.refs_2_, ...), custom_call_target="tpu_custom_call" | custom-call | tf_op jit(solution)/shard_map/attention_near/pallas_call | solution.py:431
  5.4 0.2 collective-permute-start.2
  5.6 0.9 %collective-permute-done.refs_0_ = bf16[5,8,128]{2,1,0:T(8,128)(2,1)S(1)} collective-permute-done((bf16[5,8,128]{2,1,0:T(8,128)(2,1)S(1)}, bf16[5,8,128]{2,1,0:T(8,128)(2,1)S(1)}, u32[]{:S(2)}, u32[]{:S(2)}) %collective-permute-start) | collective-permute-done | bytes 10272 | tf_op jit(solution)/shard_map/ppermute | solution.py:24
  6.5 1.4 %collective-permute-done.1.refs_1_ = bf16[5,8,128]{2,1,0:T(8,128)(2,1)S(1)} collective-permute-done((bf16[5,8,128]{2,1,0:T(8,128)(2,1)S(1)}, bf16[5,8,128]{2,1,0:T(8,128)(2,1)S(1)}, u32[]{:S(2)}, u32[]{:S(2)}) %collective-permute-start.1) | collective-permute-done | bytes 10272 | tf_op jit(solution)/shard_map/ppermute | solution.py:24
  8.0 0.0 collective-permute-done.2.refs_3_
  8.0 0.0 slice-start.5
  8.0 0.0 slice-start.6
  8.0 0.0 slice-start.9
  8.0 0.0 slice-start.10
  8.1 0.0 slice-start.11
  8.1 0.2 combine.1.refs_0_
  8.3 3.7 %collective-permute-start.5 = (bf16[4,1024]{1,0:T(4,128)(2,1)S(1)}, bf16[4,1024]{1,0:T(4,128)(2,1)S(1)}, u32[]{:S(2)}, u32[]{:S(2)}) collective-permute-start(bf16[4,1024]{1,0:T(4,128)(2,1)S(1)} %combine.1.refs_0_), channel_id=1, source_target_pairs={{0,12},{4,8},{8,4},{12,0},{1,13},{5,9},{9,5},{13,1},{2,14},{6,10},... | collective-permute-start | bytes 24584 | tf_op jit(solution)/shard_map/ppermute | solution.py:24
  12.0 0.0 collective-permute-start.4
  12.0 0.8 %collective-permute-start.3 = (bf16[4,1024]{1,0:T(4,128)(2,1)S(1)}, bf16[4,1024]{1,0:T(4,128)(2,1)S(1)}, u32[]{:S(2)}, u32[]{:S(2)}) collective-permute-start(bf16[4,1024]{1,0:T(4,128)(2,1)S(1)} %combine.1.refs_0_), channel_id=1, source_target_pairs={{0,4},{4,0},{8,12},{12,8},{1,5},{5,1},{9,13},{13,9},{2,6},{6,2},{1... | collective-permute-start | bytes 24584 | tf_op jit(solution)/shard_map/ppermute | solution.py:24
  12.8 1.1 %collective-permute-done.5.refs_3_ = bf16[4,1024]{1,0:T(4,128)(2,1)S(1)} collective-permute-done((bf16[4,1024]{1,0:T(4,128)(2,1)S(1)}, bf16[4,1024]{1,0:T(4,128)(2,1)S(1)}, u32[]{:S(2)}, u32[]{:S(2)}) %collective-permute-start.5) | collective-permute-done | bytes 8224 | tf_op jit(solution)/shard_map/ppermute | solution.py:24
  13.9 2.6 %collective-permute-done.4.refs_2_ = bf16[4,1024]{1,0:T(4,128)(2,1)S(1)} collective-permute-done((bf16[4,1024]{1,0:T(4,128)(2,1)S(1)}, bf16[4,1024]{1,0:T(4,128)(2,1)S(1)}, u32[]{:S(2)}, u32[]{:S(2)}) %collective-permute-start.4) | collective-permute-done | bytes 8224 | tf_op jit(solution)/shard_map/ppermute | solution.py:24
  16.5 0.7 %out_projection.1 = (bf16[16,1024]{1,0:T(8,128)(2,1)S(1)}, bf16[16,1024]{1,0:T(8,128)(2,1)S(1)}, bf16[16,1024]{1,0:T(8,128)(2,1)S(1)}, bf16[16,1024]{1,0:T(8,128)(2,1)S(1)}) custom-call(bf16[4,1024]{1,0:T(4,128)(2,1)S(1)} %combine.1.refs_0_, bf16[4,1024]{1,0:T(4,128)(2,1)S(1)} %collective-permute-done.3.refs_1_, ...), custom_call_target="tpu_custom_call" | custom-call | tf_op jit(solution)/shard_map/out_projection/pallas_call | solution.py:448
  17.2 0.1 collective-permute-start.6
  17.3 0.7 %collective-permute-start.7 = (bf16[16,1024]{1,0:T(8,128)(2,1)S(1)}, bf16[16,1024]{1,0:T(8,128)(2,1)S(1)}, u32[]{:S(2)}, u32[]{:S(2)}) collective-permute-start(bf16[16,1024]{1,0:T(8,128)(2,1)S(1)} %get-tuple-element.38), channel_id=1, source_target_pairs={{0,2},{1,3},{2,0},{3,1},{4,6},{5,7},{6,4},{7,5},{8,10},{9,11},{10,... | collective-permute-start | bytes 98312 | tf_op jit(solution)/shard_map/ppermute | solution.py:24
  18.0 1.1 %collective-permute-start.8 = (bf16[16,1024]{1,0:T(8,128)(2,1)S(1)}, bf16[16,1024]{1,0:T(8,128)(2,1)S(1)}, u32[]{:S(2)}, u32[]{:S(2)}) collective-permute-start(bf16[16,1024]{1,0:T(8,128)(2,1)S(1)} %get-tuple-element.39), channel_id=1, source_target_pairs={{0,1},{1,0},{2,3},{3,2},{4,5},{5,4},{6,7},{7,6},{8,9},{9,8},{10,11... | collective-permute-start | bytes 98312 | tf_op jit(solution)/shard_map/ppermute | solution.py:24
  19.1 1.5 %collective-permute-done.6.refs_1_ = bf16[16,1024]{1,0:T(8,128)(2,1)S(1)} collective-permute-done((bf16[16,1024]{1,0:T(8,128)(2,1)S(1)}, bf16[16,1024]{1,0:T(8,128)(2,1)S(1)}, u32[]{:S(2)}, u32[]{:S(2)}) %collective-permute-start.6) | collective-permute-done | bytes 32800 | tf_op jit(solution)/shard_map/ppermute | solution.py:24
  20.6 0.7 %collective-permute-done.7.refs_2_ = bf16[16,1024]{1,0:T(8,128)(2,1)S(1)} collective-permute-done((bf16[16,1024]{1,0:T(8,128)(2,1)S(1)}, bf16[16,1024]{1,0:T(8,128)(2,1)S(1)}, u32[]{:S(2)}, u32[]{:S(2)}) %collective-permute-start.7) | collective-permute-done | bytes 32800 | tf_op jit(solution)/shard_map/ppermute | solution.py:24
  21.4 0.1 collective-permute-start.9
  21.6 0.0 slice-start
  21.6 1.1 %gate_up_first.1 = (f32[16,1792]{1,0:T(8,128)S(1)}, f32[16,1792]{1,0:T(8,128)S(1)}) custom-call(bf16[16,1024]{1,0:T(8,128)(2,1)S(1)} %get-tuple-element.41.lifted, bf16[2048,3584]{1,0:T(8,128)(2,1)S(1)} %bitcast.3, bf16[2048,3584]{1,0:T(8,128)(2,1)S(1)} %bitcast.5), custom_call_target="tpu_custom_call" | custom-call | tf_op jit(solution)/shard_map/gate_up_first/pallas_call | solution.py:469
  22.7 0.1 collective-permute-done.9.received
  22.7 1.1 %gate_up_second.1 = (f32[16,2048]{1,0:T(8,128)S(1)}, bf16[16,1920]{1,0:T(8,128)(2,1)S(1)}, bf16[16,1920]{1,0:T(8,128)(2,1)S(1)}) custom-call(f32[16,1024]{1,0:T(8,128)S(1)} %get-tuple-element.40.own, f32[16,1024]{1,0:T(8,128)S(1)} %collective-permute-done.9.received, bf16[2048]{0:T(1024)(128)(2,1)S(1)} %copy-done.2, bf16[2048,3584]{1,0:T(8,128)(2,1)S(1)} %bitcast.3, ...), custom_call_target="tpu_custom_call" | custom-call | flops 40000000000 | bytes 1024 | tf_op jit(solution)/shard_map/gate_up_second/pallas_call | solution.py:475
  23.8 2.0 %collective-permute-start.11 = (bf16[16,1920]{1,0:T(8,128)(2,1)S(1)}, bf16[16,1920]{1,0:T(8,128)(2,1)S(1)}, u32[]{:S(2)}, u32[]{:S(2)}) collective-permute-start(bf16[16,1920]{1,0:T(8,128)(2,1)S(1)} %get-tuple-element.45.refs_0_), channel_id=1, source_target_pairs={{0,8},{4,12},{8,0},{12,4},{1,9},{5,13},{9,1},{13,5},{2,10},{6,14},... | collective-permute-start | bytes 184328 | tf_op jit(solution)/shard_map/ppermute | solution.py:24
  25.9 0.2 collective-permute-start.12
  26.1 1.3 %collective-permute-start.10 = (bf16[16,1920]{1,0:T(8,128)(2,1)S(1)}, bf16[16,1920]{1,0:T(8,128)(2,1)S(1)}, u32[]{:S(2)}, u32[]{:S(2)}) collective-permute-start(bf16[16,1920]{1,0:T(8,128)(2,1)S(1)} %get-tuple-element.46), channel_id=1, source_target_pairs={{0,4},{4,0},{8,12},{12,8},{1,5},{5,1},{9,13},{13,9},{2,6},{6,2},{1... | collective-permute-start | bytes 184328 | tf_op jit(solution)/shard_map/ppermute | solution.py:24
  27.3 2.5 %collective-permute-done.11.refs_2_ = bf16[16,1920]{1,0:T(8,128)(2,1)S(1)} collective-permute-done((bf16[16,1920]{1,0:T(8,128)(2,1)S(1)}, bf16[16,1920]{1,0:T(8,128)(2,1)S(1)}, u32[]{:S(2)}, u32[]{:S(2)}) %collective-permute-start.11) | collective-permute-done | bytes 61472 | tf_op jit(solution)/shard_map/ppermute | solution.py:24
  29.8 2.6 %collective-permute-done.12.refs_3_ = bf16[16,1920]{1,0:T(8,128)(2,1)S(1)} collective-permute-done((bf16[16,1920]{1,0:T(8,128)(2,1)S(1)}, bf16[16,1920]{1,0:T(8,128)(2,1)S(1)}, u32[]{:S(2)}, u32[]{:S(2)}) %collective-permute-start.12) | collective-permute-done | bytes 61472 | tf_op jit(solution)/shard_map/ppermute | solution.py:24
  32.4 0.1 activation.1.own
  32.5 0.6 %collective-permute-start.15 = (bf16[8,1792]{1,0:T(8,128)(2,1)S(1)}, bf16[8,1792]{1,0:T(8,128)(2,1)S(1)}, u32[]{:S(2)}, u32[]{:S(2)}) collective-permute-start(bf16[8,1792]{1,0:T(8,128)(2,1)S(1)} %activation.1.own), channel_id=1, source_target_pairs={{0,4},{4,0},{8,12},{12,8},{1,5},{5,1},{9,13},{13,9},{2,6},{6,2},{1... | collective-permute-start | bytes 86024 | tf_op jit(solution)/shard_map/ppermute | solution.py:24
  33.1 2.5 %collective-permute-start.14 = (bf16[8,1792]{1,0:T(8,128)(2,1)S(1)}, bf16[8,1792]{1,0:T(8,128)(2,1)S(1)}, u32[]{:S(2)}, u32[]{:S(2)}) collective-permute-start(bf16[8,1792]{1,0:T(8,128)(2,1)S(1)} %activation.1.own), channel_id=1, source_target_pairs={{0,20},{4,16},{8,28},{12,24},{16,4},{20,0},{24,12},{28,8},{1,21},{... | collective-permute-start | bytes 86024 | tf_op jit(solution)/shard_map/ppermute | solution.py:24
  35.6 0.5 %collective-permute-start.13 = (bf16[8,1792]{1,0:T(8,128)(2,1)S(1)}, bf16[8,1792]{1,0:T(8,128)(2,1)S(1)}, u32[]{:S(2)}, u32[]{:S(2)}) collective-permute-start(bf16[8,1792]{1,0:T(8,128)(2,1)S(1)} %activation.1.own), channel_id=1, source_target_pairs={{0,16},{16,0},{1,17},{17,1},{2,18},{18,2},{3,19},{19,3},{4,20},{20... | collective-permute-start | bytes 86024 | tf_op jit(solution)/shard_map/ppermute | solution.py:24
  36.1 0.6 %collective-permute-done.15.received = bf16[8,1792]{1,0:T(8,128)(2,1)S(1)} collective-permute-done((bf16[8,1792]{1,0:T(8,128)(2,1)S(1)}, bf16[8,1792]{1,0:T(8,128)(2,1)S(1)}, u32[]{:S(2)}, u32[]{:S(2)}) %collective-permute-start.15) | collective-permute-done | bytes 28704 | tf_op jit(solution)/shard_map/ppermute | solution.py:24
  36.8 1.1 %down.2.refs_0_ = f32[16,2048]{1,0:T(8,128)S(1)} custom-call(bf16[16,1792]{1,0:T(8,128)(2,1)S(1)} %gather_act.3.act, bf16[3584,2048]{1,0:T(8,128)(2,1)S(1)} %bitcast.1), custom_call_target="tpu_custom_call" | custom-call | tf_op jit(solution)/shard_map/down/pallas_call | solution.py:500
  37.8 0.1 collective-permute-done.14.received
  38.0 1.5 %collective-permute-done.13.own = bf16[8,1792]{1,0:T(8,128)(2,1)S(1)} collective-permute-done((bf16[8,1792]{1,0:T(8,128)(2,1)S(1)}, bf16[8,1792]{1,0:T(8,128)(2,1)S(1)}, u32[]{:S(2)}, u32[]{:S(2)}) %collective-permute-start.13) | collective-permute-done | bytes 28704 | tf_op jit(solution)/shard_map/ppermute | solution.py:24
  39.5 1.1 %down.3.refs_0_ = bf16[16,2048]{1,0:T(8,128)(2,1)S(1)} custom-call(bf16[16,1792]{1,0:T(8,128)(2,1)S(1)} %gather_act.2.act, bf16[3584,2048]{1,0:T(8,128)(2,1)S(1)} %bitcast.1, f32[16,2048]{1,0:T(8,128)S(1)} %down.2.refs_0_), custom_call_target="tpu_custom_call" | custom-call | tf_op jit(solution)/shard_map/down/pallas_call | solution.py:500
  40.5 0.6 %collective-permute-start.17 = (bf16[16,2048]{1,0:T(8,128)(2,1)S(1)}, bf16[16,2048]{1,0:T(8,128)(2,1)S(1)}, u32[]{:S(2)}, u32[]{:S(2)}) collective-permute-start(bf16[16,2048]{1,0:T(8,128)(2,1)S(1)} %down.3.refs_0_), channel_id=1, source_target_pairs={{0,2},{1,3},{2,0},{3,1},{4,6},{5,7},{6,4},{7,5},{8,10},{9,11},{10,... | collective-permute-start | bytes 196616 | tf_op jit(solution)/shard_map/ppermute | solution.py:24
  41.2 1.2 %collective-permute-start.16 = (bf16[16,2048]{1,0:T(8,128)(2,1)S(1)}, bf16[16,2048]{1,0:T(8,128)(2,1)S(1)}, u32[]{:S(2)}, u32[]{:S(2)}) collective-permute-start(bf16[16,2048]{1,0:T(8,128)(2,1)S(1)} %down.3.refs_0_), channel_id=1, source_target_pairs={{0,1},{1,0},{2,3},{3,2},{4,5},{5,4},{6,7},{7,6},{8,9},{9,8},{10,11... | collective-permute-start | bytes 196616 | tf_op jit(solution)/shard_map/ppermute | solution.py:24
  42.4 2.0 %collective-permute-done.18.refs_3_ = bf16[16,2048]{1,0:T(8,128)(2,1)S(1)} collective-permute-done((bf16[16,2048]{1,0:T(8,128)(2,1)S(1)}, bf16[16,2048]{1,0:T(8,128)(2,1)S(1)}, u32[]{:S(2)}, u32[]{:S(2)}) %collective-permute-start.18) | collective-permute-done | bytes 65568 | tf_op jit(solution)/shard_map/ppermute | solution.py:24
  44.4 1.1 %collective-permute-done.17.refs_2_ = bf16[16,2048]{1,0:T(8,128)(2,1)S(1)} collective-permute-done((bf16[16,2048]{1,0:T(8,128)(2,1)S(1)}, bf16[16,2048]{1,0:T(8,128)(2,1)S(1)}, u32[]{:S(2)}, u32[]{:S(2)}) %collective-permute-start.17) | collective-permute-done | bytes 65568 | tf_op jit(solution)/shard_map/ppermute | solution.py:24
  45.5 0.7 %final.1 = bf16[2,8,2048]{2,1,0:T(8,128)(2,1)} custom-call(f32[16,2048]{1,0:T(8,128)S(1)} %get-tuple-element.44.mid, bf16[16,2048]{1,0:T(8,128)(2,1)S(1)} %down.3.refs_0_, bf16[16,2048]{1,0:T(8,128)(2,1)S(1)} %collective-permute-done.16.refs_1_, bf16[16,2048]{1,0:T(8,128)(2,1)S(1)} %collective-permute-done.17.refs_2_, ...), custom_call_target="tpu_custom_call" | custom-call | tf_op jit(solution)/shard_map/final/pallas_call | solution.py:515
  (36 shorter events, 0.1 us)
Async XLA Ops:
  1.9 4.7 %collective-permute-start = (bf16[5,8,128]{2,1,0:T(8,128)(2,1)S(1)}, bf16[5,8,128]{2,1,0:T(8,128)(2,1)S(1)}, u32[]{:S(2)}, u32[]{:S(2)}) collective-permute-start(bf16[5,8,128]{2,1,0:T(8,128)(2,1)S(1)} %get-tuple-element.26), channel_id=1, source_target_pairs={{0,2},{1,3},{2,0},{3,1},{4,6},{5,7},{6,4},{7,5},{8,10},{9,11},{10,... | collective-permute-start | bytes 30728 | tf_op jit(solution)/shard_map/ppermute | solution.py:24
  4.9 3.1 %collective-permute-start.1 = (bf16[5,8,128]{2,1,0:T(8,128)(2,1)S(1)}, bf16[5,8,128]{2,1,0:T(8,128)(2,1)S(1)}, u32[]{:S(2)}, u32[]{:S(2)}) collective-permute-start(bf16[5,8,128]{2,1,0:T(8,128)(2,1)S(1)} %get-tuple-element.27), channel_id=1, source_target_pairs={{0,3},{1,2},{2,1},{3,0},{4,7},{5,6},{6,5},{7,4},{8,11},{9,10},{10,... | collective-permute-start | bytes 30728 | tf_op jit(solution)/shard_map/ppermute | solution.py:24
  4.9 16.6 %slice-start.4 = ((s8[14680064]{0:T(1024)(128)(4,1)}), s8[4194304]{0:T(1024)(128)(4,1)S(1)}, s32[]{:S(2)}) async-start(s8[14680064]{0:T(1024)(128)(4,1)} %bitcast.2), calls=%async_computation.4 | async-start | bytes 8388608
  4.9 16.6 %slice-start.8 = ((s8[14680064]{0:T(1024)(128)(4,1)}), s8[4194304]{0:T(1024)(128)(4,1)S(1)}, s32[]{:S(2)}) async-start(s8[14680064]{0:T(1024)(128)(4,1)} %bitcast.4), calls=%async_computation.8 | async-start | bytes 8388608
  5.4 2.6 %collective-permute-start.2 = (bf16[5,8,128]{2,1,0:T(8,128)(2,1)S(1)}, bf16[5,8,128]{2,1,0:T(8,128)(2,1)S(1)}, u32[]{:S(2)}, u32[]{:S(2)}) collective-permute-start(bf16[5,8,128]{2,1,0:T(8,128)(2,1)S(1)} %get-tuple-element.35), channel_id=1, source_target_pairs={{0,1},{1,0},{2,3},{3,2},{4,5},{5,4},{6,7},{7,6},{8,9},{9,8},{10,11... | collective-permute-start | bytes 30728 | tf_op jit(solution)/shard_map/ppermute | solution.py:24
  8.0 8.6 %copy-start = (bf16[1024,2048]{1,0:T(8,128)(2,1)S(1)}, bf16[1024,2048]{1,0:T(8,128)(2,1)}, u32[]{:S(2)}) copy-start(bf16[1024,2048]{1,0:T(8,128)(2,1)} %refs_4_.3) | copy-start | bytes 12582916
  8.0 13.4 %copy-start.1 = (bf16[2,8,2048]{2,1,0:T(8,128)(2,1)S(1)}, bf16[2,8,2048]{2,1,0:T(8,128)(2,1)}, u32[]{:S(2)}) copy-start(bf16[2,8,2048]{2,1,0:T(8,128)(2,1)} %residual.1) | copy-start | bytes 196612
  8.0 13.4 %copy-start.2 = (bf16[2048]{0:T(1024)(128)(2,1)S(1)}, bf16[2048]{0:T(1024)(128)(2,1)}, u32[]{:S(2)}) copy-start(bf16[2048]{0:T(1024)(128)(2,1)} %gains.3) | copy-start | bytes 12292
  8.0 13.5 %slice-start.5 = ((s8[14680064]{0:T(1024)(128)(4,1)}), s8[4194304]{0:T(1024)(128)(4,1)S(1)}, s32[]{:S(2)}) async-start(s8[14680064]{0:T(1024)(128)(4,1)} %bitcast.2), calls=%async_computation.5 | async-start | bytes 8388608
  8.0 13.5 %slice-start.6 = ((s8[14680064]{0:T(1024)(128)(4,1)}), s8[4194304]{0:T(1024)(128)(4,1)S(1)}, s32[]{:S(2)}) async-start(s8[14680064]{0:T(1024)(128)(4,1)} %bitcast.2), calls=%async_computation.6 | async-start | bytes 8388608
  8.0 13.5 %slice-start.7 = ((s8[14680064]{0:T(1024)(128)(4,1)}), s8[2097152]{0:T(1024)(128)(4,1)S(1)}, s32[]{:S(2)}) async-start(s8[14680064]{0:T(1024)(128)(4,1)} %bitcast.2), calls=%async_computation.7 | async-start | bytes 4194304
  8.0 13.5 %slice-start.9 = ((s8[14680064]{0:T(1024)(128)(4,1)}), s8[4194304]{0:T(1024)(128)(4,1)S(1)}, s32[]{:S(2)}) async-start(s8[14680064]{0:T(1024)(128)(4,1)} %bitcast.4), calls=%async_computation.9 | async-start | bytes 8388608
  8.0 13.5 %slice-start.10 = ((s8[14680064]{0:T(1024)(128)(4,1)}), s8[4194304]{0:T(1024)(128)(4,1)S(1)}, s32[]{:S(2)}) async-start(s8[14680064]{0:T(1024)(128)(4,1)} %bitcast.4), calls=%async_computation.10 | async-start | bytes 8388608
  8.1 13.5 %slice-start.11 = ((s8[14680064]{0:T(1024)(128)(4,1)}), s8[2097152]{0:T(1024)(128)(4,1)S(1)}, s32[]{:S(2)}) async-start(s8[14680064]{0:T(1024)(128)(4,1)} %bitcast.4), calls=%async_computation.11 | async-start | bytes 4194304
  8.3 5.6 %collective-permute-start.5 = (bf16[4,1024]{1,0:T(4,128)(2,1)S(1)}, bf16[4,1024]{1,0:T(4,128)(2,1)S(1)}, u32[]{:S(2)}, u32[]{:S(2)}) collective-permute-start(bf16[4,1024]{1,0:T(4,128)(2,1)S(1)} %combine.1.refs_0_), channel_id=1, source_target_pairs={{0,12},{4,8},{8,4},{12,0},{1,13},{5,9},{9,5},{13,1},{2,14},{6,10},... | collective-permute-start | bytes 24584 | tf_op jit(solution)/shard_map/ppermute | solution.py:24
  12.0 4.5 %collective-permute-start.4 = (bf16[4,1024]{1,0:T(4,128)(2,1)S(1)}, bf16[4,1024]{1,0:T(4,128)(2,1)S(1)}, u32[]{:S(2)}, u32[]{:S(2)}) collective-permute-start(bf16[4,1024]{1,0:T(4,128)(2,1)S(1)} %combine.1.refs_0_), channel_id=1, source_target_pairs={{0,8},{4,12},{8,0},{12,4},{1,9},{5,13},{9,1},{13,5},{2,10},{6,14},... | collective-permute-start | bytes 24584 | tf_op jit(solution)/shard_map/ppermute | solution.py:24
  12.0 4.5 %collective-permute-start.3 = (bf16[4,1024]{1,0:T(4,128)(2,1)S(1)}, bf16[4,1024]{1,0:T(4,128)(2,1)S(1)}, u32[]{:S(2)}, u32[]{:S(2)}) collective-permute-start(bf16[4,1024]{1,0:T(4,128)(2,1)S(1)} %combine.1.refs_0_), channel_id=1, source_target_pairs={{0,4},{4,0},{8,12},{12,8},{1,5},{5,1},{9,13},{13,9},{2,6},{6,2},{1... | collective-permute-start | bytes 24584 | tf_op jit(solution)/shard_map/ppermute | solution.py:24
  17.2 3.4 %collective-permute-start.6 = (bf16[16,1024]{1,0:T(8,128)(2,1)S(1)}, bf16[16,1024]{1,0:T(8,128)(2,1)S(1)}, u32[]{:S(2)}, u32[]{:S(2)}) collective-permute-start(bf16[16,1024]{1,0:T(8,128)(2,1)S(1)} %get-tuple-element.37), channel_id=1, source_target_pairs={{0,3},{1,2},{2,1},{3,0},{4,7},{5,6},{6,5},{7,4},{8,11},{9,10},{10,... | collective-permute-start | bytes 98312 | tf_op jit(solution)/shard_map/ppermute | solution.py:24
  17.3 4.0 %collective-permute-start.7 = (bf16[16,1024]{1,0:T(8,128)(2,1)S(1)}, bf16[16,1024]{1,0:T(8,128)(2,1)S(1)}, u32[]{:S(2)}, u32[]{:S(2)}) collective-permute-start(bf16[16,1024]{1,0:T(8,128)(2,1)S(1)} %get-tuple-element.38), channel_id=1, source_target_pairs={{0,2},{1,3},{2,0},{3,1},{4,6},{5,7},{6,4},{7,5},{8,10},{9,11},{10,... | collective-permute-start | bytes 98312 | tf_op jit(solution)/shard_map/ppermute | solution.py:24
  18.0 3.3 %collective-permute-start.8 = (bf16[16,1024]{1,0:T(8,128)(2,1)S(1)}, bf16[16,1024]{1,0:T(8,128)(2,1)S(1)}, u32[]{:S(2)}, u32[]{:S(2)}) collective-permute-start(bf16[16,1024]{1,0:T(8,128)(2,1)S(1)} %get-tuple-element.39), channel_id=1, source_target_pairs={{0,1},{1,0},{2,3},{3,2},{4,5},{5,4},{6,7},{7,6},{8,9},{9,8},{10,11... | collective-permute-start | bytes 98312 | tf_op jit(solution)/shard_map/ppermute | solution.py:24
  21.4 1.3 %collective-permute-start.9 = (f32[16,1024]{1,0:T(8,128)S(1)}, f32[16,1024]{1,0:T(8,128)S(1)}, u32[]{:S(2)}, u32[]{:S(2)}) collective-permute-start(f32[16,1024]{1,0:T(8,128)S(1)} %get-tuple-element.40.own), channel_id=1, source_target_pairs={{0,1},{1,0},{2,3},{3,2},{4,5},{5,4},{6,7},{7,6},{8,9},{9,8},{10,11... | collective-permute-start | bytes 196616 | tf_op jit(solution)/shard_map/ppermute | solution.py:24
  21.6 15.1 %slice-start = ((s8[14680064]{0:T(1024)(128)(4,1)}), s8[4194304]{0:T(1024)(128)(4,1)S(1)}, s32[]{:S(2)}) async-start(s8[14680064]{0:T(1024)(128)(4,1)} %bitcast), calls=%async_computation | async-start | bytes 8388608
  22.7 14.0 %slice-start.1 = ((s8[14680064]{0:T(1024)(128)(4,1)}), s8[4194304]{0:T(1024)(128)(4,1)S(1)}, s32[]{:S(2)}) async-start(s8[14680064]{0:T(1024)(128)(4,1)} %bitcast), calls=%async_computation.1 | async-start | bytes 8388608
  22.7 14.0 %slice-start.2 = ((s8[14680064]{0:T(1024)(128)(4,1)}), s8[4194304]{0:T(1024)(128)(4,1)S(1)}, s32[]{:S(2)}) async-start(s8[14680064]{0:T(1024)(128)(4,1)} %bitcast), calls=%async_computation.2 | async-start | bytes 8388608
  22.7 14.0 %slice-start.3 = ((s8[14680064]{0:T(1024)(128)(4,1)}), s8[2097152]{0:T(1024)(128)(4,1)S(1)}, s32[]{:S(2)}) async-start(s8[14680064]{0:T(1024)(128)(4,1)} %bitcast), calls=%async_computation.3 | async-start | bytes 4194304
  23.8 6.0 %collective-permute-start.11 = (bf16[16,1920]{1,0:T(8,128)(2,1)S(1)}, bf16[16,1920]{1,0:T(8,128)(2,1)S(1)}, u32[]{:S(2)}, u32[]{:S(2)}) collective-permute-start(bf16[16,1920]{1,0:T(8,128)(2,1)S(1)} %get-tuple-element.45.refs_0_), channel_id=1, source_target_pairs={{0,8},{4,12},{8,0},{12,4},{1,9},{5,13},{9,1},{13,5},{2,10},{6,14},... | collective-permute-start | bytes 184328 | tf_op jit(solution)/shard_map/ppermute | solution.py:24
  25.9 6.5 %collective-permute-start.12 = (bf16[16,1920]{1,0:T(8,128)(2,1)S(1)}, bf16[16,1920]{1,0:T(8,128)(2,1)S(1)}, u32[]{:S(2)}, u32[]{:S(2)}) collective-permute-start(bf16[16,1920]{1,0:T(8,128)(2,1)S(1)} %get-tuple-element.46), channel_id=1, source_target_pairs={{0,12},{4,8},{8,4},{12,0},{1,13},{5,9},{9,5},{13,1},{2,14},{6,10},... | collective-permute-start | bytes 184328 | tf_op jit(solution)/shard_map/ppermute | solution.py:24
  26.1 6.3 %collective-permute-start.10 = (bf16[16,1920]{1,0:T(8,128)(2,1)S(1)}, bf16[16,1920]{1,0:T(8,128)(2,1)S(1)}, u32[]{:S(2)}, u32[]{:S(2)}) collective-permute-start(bf16[16,1920]{1,0:T(8,128)(2,1)S(1)} %get-tuple-element.46), channel_id=1, source_target_pairs={{0,4},{4,0},{8,12},{12,8},{1,5},{5,1},{9,13},{13,9},{2,6},{6,2},{1... | collective-permute-start | bytes 184328 | tf_op jit(solution)/shard_map/ppermute | solution.py:24
  32.5 4.2 %collective-permute-start.15 = (bf16[8,1792]{1,0:T(8,128)(2,1)S(1)}, bf16[8,1792]{1,0:T(8,128)(2,1)S(1)}, u32[]{:S(2)}, u32[]{:S(2)}) collective-permute-start(bf16[8,1792]{1,0:T(8,128)(2,1)S(1)} %activation.1.own), channel_id=1, source_target_pairs={{0,4},{4,0},{8,12},{12,8},{1,5},{5,1},{9,13},{13,9},{2,6},{6,2},{1... | collective-permute-start | bytes 86024 | tf_op jit(solution)/shard_map/ppermute | solution.py:24
  33.1 4.8 %collective-permute-start.14 = (bf16[8,1792]{1,0:T(8,128)(2,1)S(1)}, bf16[8,1792]{1,0:T(8,128)(2,1)S(1)}, u32[]{:S(2)}, u32[]{:S(2)}) collective-permute-start(bf16[8,1792]{1,0:T(8,128)(2,1)S(1)} %activation.1.own), channel_id=1, source_target_pairs={{0,20},{4,16},{8,28},{12,24},{16,4},{20,0},{24,12},{28,8},{1,21},{... | collective-permute-start | bytes 86024 | tf_op jit(solution)/shard_map/ppermute | solution.py:24
  35.6 3.9 %collective-permute-start.13 = (bf16[8,1792]{1,0:T(8,128)(2,1)S(1)}, bf16[8,1792]{1,0:T(8,128)(2,1)S(1)}, u32[]{:S(2)}, u32[]{:S(2)}) collective-permute-start(bf16[8,1792]{1,0:T(8,128)(2,1)S(1)} %activation.1.own), channel_id=1, source_target_pairs={{0,16},{16,0},{1,17},{17,1},{2,18},{18,2},{3,19},{19,3},{4,20},{20... | collective-permute-start | bytes 86024 | tf_op jit(solution)/shard_map/ppermute | solution.py:24
  40.5 3.8 %collective-permute-start.18 = (bf16[16,2048]{1,0:T(8,128)(2,1)S(1)}, bf16[16,2048]{1,0:T(8,128)(2,1)S(1)}, u32[]{:S(2)}, u32[]{:S(2)}) collective-permute-start(bf16[16,2048]{1,0:T(8,128)(2,1)S(1)} %down.3.refs_0_), channel_id=1, source_target_pairs={{0,3},{1,2},{2,1},{3,0},{4,7},{5,6},{6,5},{7,4},{8,11},{9,10},{10,... | collective-permute-start | bytes 196616 | tf_op jit(solution)/shard_map/ppermute | solution.py:24
  40.5 5.0 %collective-permute-start.17 = (bf16[16,2048]{1,0:T(8,128)(2,1)S(1)}, bf16[16,2048]{1,0:T(8,128)(2,1)S(1)}, u32[]{:S(2)}, u32[]{:S(2)}) collective-permute-start(bf16[16,2048]{1,0:T(8,128)(2,1)S(1)} %down.3.refs_0_), channel_id=1, source_target_pairs={{0,2},{1,3},{2,0},{3,1},{4,6},{5,7},{6,4},{7,5},{8,10},{9,11},{10,... | collective-permute-start | bytes 196616 | tf_op jit(solution)/shard_map/ppermute | solution.py:24
  41.2 4.3 %collective-permute-start.16 = (bf16[16,2048]{1,0:T(8,128)(2,1)S(1)}, bf16[16,2048]{1,0:T(8,128)(2,1)S(1)}, u32[]{:S(2)}, u32[]{:S(2)}) collective-permute-start(bf16[16,2048]{1,0:T(8,128)(2,1)S(1)} %down.3.refs_0_), channel_id=1, source_target_pairs={{0,1},{1,0},{2,3},{3,2},{4,5},{5,4},{6,7},{7,6},{8,9},{9,8},{10,11... | collective-permute-start | bytes 196616 | tf_op jit(solution)/shard_map/ppermute | solution.py:24
